TPU v7x, 32 devices: a whole 2x2x4 slice. The times are simulated.
32 devices in a mesh: heads: 16 (over z, x, core), frames: 2 (over y).
Axes of the slice: x: 2, y: 2, z: 4, core: 2. Of those that a mesh axis runs over, the one named last changes fastest.
Arguments:
- query: bfloat16 [4096, 2048], P(('frames', 'heads'))
- keys: bfloat16 [4096, 2048], P(('frames', 'heads'))
- values: bfloat16 [4096, 2048], P(('frames', 'heads')), may hold values from -6 to 6
- query_tan: bfloat16 [4096, 2048], P(('frames', 'heads')), may hold values from -6 to 6
- keys_tan: bfloat16 [4096, 2048], P(('frames', 'heads')), may hold values from -6 to 6
- values_tan: bfloat16 [4096, 2048], P(('frames', 'heads')), may hold values from -6 to 6
- neighbors: int32 [16, 4], P('frames'), may hold values from 0 to 15, as said below
Outputs:
- attended: bfloat16 [4096, 2048], P(('frames', 'heads'))
- attended_tan: bfloat16 [4096, 2048], P(('frames', 'heads'))
Inputs may be any that keep to these rules, and one draw needn't show every extreme that they name: `neighbors`: entry 0 of row b is b itself; the other entries are min(max(b + o, 0), 15) for distinct nonzero offsets o between -4 and 4.
All inputs are finite; a program needn't handle non-finite values.
Results may differ from a plain program's by a relative error of at most 0.028.
Values may be sent and summed in bfloat16 or wider, within the bound.
No kernel may reach another device: no remote copies, remote signals or barrier semaphores. Data moves between devices by JAX's collectives and lax.ppermute only.
A program may use at most 192 MiB of HBM per device.

v0:
```python
import jax
import jax.numpy as jnp
from jax import lax
from jax.sharding import PartitionSpec as P

BQ = 256
WK = 4
HB = 4


def extended(array, sides, width):
    for axis, dim in sides:
        devices, length = (lax.axis_size(axis), array.shape[dim])
        up = [(i, (i + 1) % devices) for i in range(devices - 1)]
        down = [(j, i) for i, j in up]
        last = lax.slice_in_dim(array, length - width, length, axis=dim)
        initial = lax.slice_in_dim(array, 0, width, axis=dim)
        before = lax.ppermute(last, axis, up)
        after = lax.ppermute(initial, axis, down)
        array = jnp.concatenate([before, array, after], axis=dim)
    return array


def widen_keys(keys_h, values_h, keys_tanh, values_tanh):
    stacked = jnp.stack([keys_h, values_h, keys_tanh, values_tanh], axis=0)
    return extended(stacked, (("frames", 1),), HB * BQ)


def attend(query_h, query_tanh, padded, neighbors):
    rows, width = query_h.shape
    blocks = rows // BQ
    scale = width ** (-0.5)
    tiles = padded.reshape(4, blocks + 2 * HB, BQ, width)
    local = neighbors - lax.axis_index("frames") * blocks + HB
    chosen = tiles[:, local].reshape(4, blocks, WK * BQ, width)
    k_win, v_win, kt_win, vt_win = (chosen[0], chosen[1], chosen[2], chosen[3])
    q_rows = query_h.reshape(blocks, BQ, width)
    qt_rows = query_tanh.reshape(blocks, BQ, width)
    scores = jnp.einsum("nqd,nkd->nqk", q_rows, k_win, preferred_element_type=jnp.float32) * scale
    probs = jax.nn.softmax(scores, axis=-1)
    probs16 = probs.astype(jnp.bfloat16)
    out = jnp.einsum("nqk,nkd->nqd", probs16, v_win, preferred_element_type=jnp.float32)
    score_tan = (
        jnp.einsum("nqd,nkd->nqk", qt_rows, k_win, preferred_element_type=jnp.float32)
        + jnp.einsum("nqd,nkd->nqk", q_rows, kt_win, preferred_element_type=jnp.float32)
    ) * scale
    weighted = probs * score_tan
    mean_tan = jnp.sum(weighted, axis=-1, keepdims=True)
    weighted16 = weighted.astype(jnp.bfloat16)
    tan = (
        jnp.einsum("nqk,nkd->nqd", probs16, vt_win, preferred_element_type=jnp.float32)
        + jnp.einsum("nqk,nkd->nqd", weighted16, v_win, preferred_element_type=jnp.float32)
        - mean_tan * out
    )
    return (
        out.reshape(rows, width).astype(jnp.bfloat16),
        tan.reshape(rows, width).astype(jnp.bfloat16),
    )


def per_device(query, keys, values, query_tan, keys_tan, values_tan, neighbors):
    query_h, keys_h, values_h, query_tanh, keys_tanh, values_tanh = (
        lax.all_to_all(query, "heads", split_axis=1, concat_axis=0, tiled=True),
        lax.all_to_all(keys, "heads", split_axis=1, concat_axis=0, tiled=True),
        lax.all_to_all(values, "heads", split_axis=1, concat_axis=0, tiled=True),
        lax.all_to_all(query_tan, "heads", split_axis=1, concat_axis=0, tiled=True),
        lax.all_to_all(keys_tan, "heads", split_axis=1, concat_axis=0, tiled=True),
        lax.all_to_all(values_tan, "heads", split_axis=1, concat_axis=0, tiled=True),
    )
    padded = widen_keys(keys_h, values_h, keys_tanh, values_tanh)
    out_h, tan_h = attend(query_h, query_tanh, padded, neighbors)
    attended, attended_tan = (
        lax.all_to_all(out_h, "heads", split_axis=0, concat_axis=1, tiled=True),
        lax.all_to_all(tan_h, "heads", split_axis=0, concat_axis=1, tiled=True),
    )
    return (attended, attended_tan)


def solution(mesh):
    return jax.shard_map(
        per_device,
        mesh=mesh,
        in_specs=(
            P(("frames", "heads"), None),
            P(("frames", "heads"), None),
            P(("frames", "heads"), None),
            P(("frames", "heads"), None),
            P(("frames", "heads"), None),
            P(("frames", "heads"), None),
            P("frames", None),
        ),
        out_specs=(P(("frames", "heads"), None), P(("frames", "heads"), None)),
        check_vma=False,
    )
```

profile of v0, /device:TPU:0, one launch (start us, length us, event | category | flops | bytes accessed | tf_op | source)
XLA Modules:
  0.0 219.2 jit_solution(13128405073210604041)
XLA Ops:
  0.6 0.0 copy-start
  0.6 0.0 copy-start.5
  0.7 0.0 copy-start.6
  0.7 2.2 copy.26
  2.8 7.4 %all-to-all-start = ((bf16[128,16,128]{0,2,1:T(8,128)(2,1)}), bf16[128,16,128]{0,2,1:T(8,128)(2,1)S(1)}, u32[]{:S(2)}, u32[]{:S(2)}) async-start(bf16[128,16,128]{0,2,1:T(8,128)(2,1)} %bitcast), calls=%async_computation | async-start | bytes 1048576 | tf_op jit(solution)/shard_map/all_to_all | solution.py:64
  10.2 2.0 copy.28
  12.2 12.4 %all-to-all-done = bf16[128,16,128]{0,2,1:T(8,128)(2,1)S(1)} async-done(((bf16[128,16,128]{0,2,1:T(8,128)(2,1)}), bf16[128,16,128]{0,2,1:T(8,128)(2,1)S(1)}, u32[]{:S(2)}, u32[]{:S(2)}) %all-to-all-start) | async-done | bytes 524320 | tf_op jit(solution)/shard_map/all_to_all | solution.py:64
  24.7 4.1 %all-to-all-start.1 = ((bf16[128,16,128]{0,2,1:T(8,128)(2,1)}), bf16[128,16,128]{0,2,1:T(8,128)(2,1)S(1)}, u32[]{:S(2)}, u32[]{:S(2)}) async-start(bf16[128,16,128]{0,2,1:T(8,128)(2,1)} %bitcast.3), calls=%async_computation.1 | async-start | bytes 1048576 | tf_op jit(solution)/shard_map/all_to_all | solution.py:65
  28.8 0.0 copy-done.5
  28.8 1.0 copy.30
  29.8 13.5 %all-to-all-done.1 = bf16[128,16,128]{0,2,1:T(8,128)(2,1)S(1)} async-done(((bf16[128,16,128]{0,2,1:T(8,128)(2,1)}), bf16[128,16,128]{0,2,1:T(8,128)(2,1)S(1)}, u32[]{:S(2)}, u32[]{:S(2)}) %all-to-all-start.1) | async-done | bytes 524320 | tf_op jit(solution)/shard_map/all_to_all | solution.py:65
  43.2 4.1 %all-to-all-start.2 = ((bf16[128,16,128]{0,2,1:T(8,128)(2,1)}), bf16[128,16,128]{0,2,1:T(8,128)(2,1)S(1)}, u32[]{:S(2)}, u32[]{:S(2)}) async-start(bf16[128,16,128]{0,2,1:T(8,128)(2,1)} %bitcast.6), calls=%async_computation.2 | async-start | bytes 1048576 | tf_op jit(solution)/shard_map/all_to_all | solution.py:67
  47.3 0.0 copy-done.6
  47.3 1.0 copy.32
  48.3 13.5 %all-to-all-done.2 = bf16[128,16,128]{0,2,1:T(8,128)(2,1)S(1)} async-done(((bf16[128,16,128]{0,2,1:T(8,128)(2,1)}), bf16[128,16,128]{0,2,1:T(8,128)(2,1)S(1)}, u32[]{:S(2)}, u32[]{:S(2)}) %all-to-all-start.2) | async-done | bytes 524320 | tf_op jit(solution)/shard_map/all_to_all | solution.py:67
  61.8 4.1 %all-to-all-start.3 = ((bf16[128,16,128]{0,2,1:T(8,128)(2,1)}), bf16[128,16,128]{0,2,1:T(8,128)(2,1)S(1)}, u32[]{:S(2)}, u32[]{:S(2)}) async-start(bf16[128,16,128]{0,2,1:T(8,128)(2,1)} %bitcast.9), calls=%async_computation.3 | async-start | bytes 1048576 | tf_op jit(solution)/shard_map/all_to_all | solution.py:68
  65.9 0.3 copy.27
  66.2 0.3 copy.29
  66.5 0.3 copy.31
  66.8 13.6 %all-to-all-done.3 = bf16[128,16,128]{0,2,1:T(8,128)(2,1)S(1)} async-done(((bf16[128,16,128]{0,2,1:T(8,128)(2,1)}), bf16[128,16,128]{0,2,1:T(8,128)(2,1)S(1)}, u32[]{:S(2)}, u32[]{:S(2)}) %all-to-all-start.3) | async-done | bytes 524320 | tf_op jit(solution)/shard_map/all_to_all | solution.py:68
  80.4 0.3 copy.33
  80.7 0.3 pad_maximum_fusion.1
  80.9 0.0 copy-start.8
  80.9 0.0 copy-start.7
  81.0 1.5 fusion.23
  82.4 4.4 %collective-permute-start = (bf16[4,1024,128]{2,1,0:T(8,128)(2,1)}, bf16[4,1024,128]{2,1,0:T(8,128)(2,1)}, u32[]{:S(2)}, u32[]{:S(2)}) collective-permute-start(bf16[4,1024,128]{2,1,0:T(8,128)(2,1)} %get-tuple-element.6), channel_id=1, source_target_pairs={{0,1},{2,3},{4,5},{6,7},{8,9},{10,11},{12,13},{14,15},{16,17},{18,... | collective-permute-start | bytes 3145736 | tf_op jit(solution)/shard_map/ppermute | solution.py:18
  86.9 1.3 collective-permute-start.1
  88.1 0.0 copy-done
  88.2 0.9 copy_bitcast_fusion.3
  89.1 4.1 %all-to-all-start.6 = ((bf16[128,16,128]{2,0,1:T(8,128)(2,1)}), bf16[128,16,128]{2,0,1:T(8,128)(2,1)S(1)}, u32[]{:S(2)}, u32[]{:S(2)}) async-start(bf16[128,16,128]{2,0,1:T(8,128)(2,1)} %copy_bitcast_fusion.3), calls=%async_computation.6 | async-start | bytes 1048576 | tf_op jit(solution)/shard_map/all_to_all | solution.py:66
  93.2 0.0 copy-done.8
  93.2 0.1 copy.34
  93.3 0.1 reshape.66
  93.4 0.0 copy-done.7
  93.4 0.9 copy_bitcast_fusion.4
  94.3 14.4 %collective-permute-done = bf16[4,1024,128]{2,1,0:T(8,128)(2,1)} collective-permute-done((bf16[4,1024,128]{2,1,0:T(8,128)(2,1)}, bf16[4,1024,128]{2,1,0:T(8,128)(2,1)}, u32[]{:S(2)}, u32[]{:S(2)}) %collective-permute-start) | collective-permute-done | bytes 1048608 | tf_op jit(solution)/shard_map/ppermute | solution.py:18
  108.8 5.1 %collective-permute-done.1 = bf16[4,1024,128]{2,1,0:T(8,128)(2,1)} collective-permute-done((bf16[4,1024,128]{2,1,0:T(8,128)(2,1)}, bf16[4,1024,128]{2,1,0:T(8,128)(2,1)}, u32[]{:S(2)}, u32[]{:S(2)}) %collective-permute-start.1) | collective-permute-done | bytes 1048608 | tf_op jit(solution)/shard_map/ppermute | solution.py:19
  113.9 11.2 %pad_maximum_fusion = bf16[4,4096,128]{2,1,0:T(8,128)(2,1)} fusion(bf16[4,1024,128]{2,1,0:T(8,128)(2,1)} %collective-permute-done.1, bf16[1,2048,128]{2,1,0:T(8,128)(2,1)S(1)} %bitcast.95, bf16[1,2048,128]{2,1,0:T(8,128)(2,1)S(1)} %bitcast.93, bf16[1,2048,128]{2,1,0:T(8,128)(2,1)S(1)} %bitcast.91, bf16[1,2048,128]{2,1,0:T(8,128)(2,1)S(1)} %bitcast.89, ...), kind=kLoop, calls=%fused_computation.9 | loop fusion | flops 25165824 | bytes 8388608 | tf_op jit(solution)/shard_map/concatenate | solution.py:20
  125.1 7.2 %gather_fusion = bf16[32,4,256,128]{3,2,1,0:T(8,128)(2,1)} fusion(bf16[4,16,256,128]{3,2,1,0:T(8,128)(2,1)} %bitcast.78, s32[1024]{0:T(1024)S(1)} %pad_clamp_fusion), kind=kCustom, calls=%fused_computation | custom fusion | bytes 16777344 | tf_op jit(solution)/shard_map/gather | solution.py:35
  132.3 7.8 %copy.55 = bf16[8,4,4,256,128]{4,3,1,0,2:T(8,128)(2,1)} copy(bf16[8,4,4,256,128]{4,3,2,1,0:T(8,128)(2,1)} %bitcast.79) | data formatting | bytes 16777216 | tf_op jit(solution)/shard_map/gather | solution.py:35
  140.0 0.0 all-to-all-done.6
  140.0 4.4 %all-to-all-start.4 = ((bf16[128,16,128]{2,0,1:T(8,128)(2,1)}), bf16[128,16,128]{2,0,1:T(8,128)(2,1)S(1)}, u32[]{:S(2)}, u32[]{:S(2)}) async-start(bf16[128,16,128]{2,0,1:T(8,128)(2,1)} %copy_bitcast_fusion.4), calls=%async_computation.4 | async-start | bytes 1048576 | tf_op jit(solution)/shard_map/all_to_all | solution.py:63
  144.4 5.2 %fusion.22 = (bf16[1,8,4,256,128]{4,3,2,1,0:T(8,128)(2,1)}, bf16[1,8,4,256,128]{4,3,2,1,0:T(8,128)(2,1)}, bf16[1,8,4,256,128]{4,3,2,1,0:T(8,128)(2,1)S(1)}, bf16[1,8,4,256,128]{4,3,2,1,0:T(8,128)(2,1)S(1)}) fusion(bf16[4,8,4,256,128]{4,3,2,1,0:T(8,128)(2,1)} %bitcast.80), kind=kLoop, calls=%fused_computation.27 | loop fusion | bytes 16777216 | tf_op jit(solution)/shard_map/slice | solution.py:36
  149.6 1.3 copy-done.3
  151.0 4.5 %fusion.28 = f32[8,1024,256]{2,1,0:T(8,128)} fusion(bf16[8,1024,128]{2,1,0:T(8,128)(2,1)S(1)} %bitcast.86, bf16[8,256,128]{2,1,0:T(8,128)(2,1)S(1)} %bitcast.102), kind=kOutput, calls=%fused_computation.33 | convolution fusion | flops 536870912 | bytes 11010048 | tf_op jit(solution)/shard_map/nqd,nkd->nqk/dot_general | solution.py:44
  155.4 3.4 %all-to-all-done.4 = bf16[128,16,128]{2,0,1:T(8,128)(2,1)S(1)} async-done(((bf16[128,16,128]{2,0,1:T(8,128)(2,1)}), bf16[128,16,128]{2,0,1:T(8,128)(2,1)S(1)}, u32[]{:S(2)}, u32[]{:S(2)}) %all-to-all-start.4) | async-done | bytes 524320 | tf_op jit(solution)/shard_map/all_to_all | solution.py:63
  158.9 7.5 %fusion.24 = (f32[8,256]{1,0:T(8,128)S(1)}, f32[8,256,1024]{1,2,0:T(8,128)}) fusion(bf16[8,1024,128]{2,1,0:T(8,128)(2,1)} %bitcast.87, bf16[8,256,128]{2,1,0:T(8,128)(2,1)S(1)} %bitcast.103), kind=kOutput, calls=%fused_computation.29 | convolution fusion | flops 543163392 | bytes 11018240 | tf_op jit(solution)/shard_map/sub | solution.py:40
  166.4 4.2 %fusion.9 = bf16[8,256,1024]{1,2,0:T(8,128)(2,1)S(1)} fusion(f32[8,256,1024]{1,2,0:T(8,128)} %get-tuple-element.9, f32[8,256]{1,0:T(8,128)S(1)} %get-tuple-element.8), kind=kLoop, calls=%fused_computation.14 | loop fusion | flops 4194304 | bytes 12591104 | tf_op jit(solution)/shard_map/convert_element_type | solution.py:41
  170.6 0.0 copy-done.2
  170.6 0.0 slice-start
  170.6 1.4 fusion.27
  172.1 0.0 copy-start.4
  172.1 0.0 slice-start.1
  172.1 2.3 %fusion.25 = (bf16[8,256,128]{2,1,0:T(8,128)(2,1)}, f32[8,256,128]{2,1,0:T(8,128)S(1)}) fusion(bf16[8,256,1024]{1,2,0:T(8,128)(2,1)S(1)} %fusion.9, bf16[8,1024,128]{2,1,0:T(8,128)(2,1)S(1)} %bitcast.81), kind=kOutput, calls=%fused_computation.30 | convolution fusion | flops 537133056 | bytes 7864320 | tf_op jit(solution)/shard_map/nqk,nkd->nqd/dot_general | solution.py:42
  174.4 0.0 slice-done
  174.4 0.9 slice-done.1
  175.3 4.6 %fusion.26 = (f32[8,256]{1,0:T(8,128)S(1)}, bf16[8,256,1024]{1,2,0:T(8,128)(2,1)S(1)}) fusion(f32[8,1024,256]{2,1,0:T(8,128)S(1)} %bitcast.84, bf16[8,1024,128]{2,1,0:T(8,128)(2,1)S(1)} %bitcast.101, bf16[8,256,128]{2,1,0:T(8,128)(2,1)S(1)} %bitcast.104, f32[8,256,1024]{1,2,0:T(8,128)} %get-tuple-element.9, f32[8,256]{1,0:T(8,128)S(1)} %get-tuple-element.8), kind=kOutput, calls=%fused_computation.31 | convolution fusion | flops 549451776 | bytes 23609344 | tf_op jit(solution)/shard_map/nqd,nkd->nqk/dot_general | solution.py:45
  179.8 0.0 copy-start.1
  179.8 1.5 fusion.16
  181.4 18.4 %all_to_all.128 = bf16[16,128,128]{2,1,0:T(8,128)(2,1)S(1)} all-to-all(bf16[16,128,128]{2,1,0:T(8,128)(2,1)S(1)} %bitcast.96), channel_id=1, replica_groups=mesh['heads'=16,'frames'=2] {'heads'}, dimensions={0} | all-to-all | bytes 1048576 | tf_op jit(solution)/shard_map/all_to_all | solution.py:74
  199.7 4.1 %all-to-all-start.5 = ((bf16[16,128,128]{2,1,0:T(8,128)(2,1)}), bf16[16,128,128]{2,1,0:T(8,128)(2,1)S(1)}, u32[]{:S(2)}, u32[]{:S(2)}) async-start(bf16[16,128,128]{2,1,0:T(8,128)(2,1)} %bitcast.20), calls=%async_computation.5 | async-start | bytes 1048576 | tf_op jit(solution)/shard_map/all_to_all | solution.py:73
  203.8 0.9 copy_bitcast_fusion.1
  204.7 13.6 %all-to-all-done.5 = bf16[16,128,128]{2,1,0:T(8,128)(2,1)S(1)} async-done(((bf16[16,128,128]{2,1,0:T(8,128)(2,1)}), bf16[16,128,128]{2,1,0:T(8,128)(2,1)S(1)}, u32[]{:S(2)}, u32[]{:S(2)}) %all-to-all-start.5) | async-done | bytes 524320 | tf_op jit(solution)/shard_map/all_to_all | solution.py:73
  218.3 0.9 copy_bitcast_fusion.2
  (7 shorter events, 0.0 us)
Async XLA Ops:
  0.6 87.5 %copy-start = (bf16[128,2048]{1,0:T(8,128)(2,1)S(1)}, bf16[128,2048]{1,0:T(8,128)(2,1)}, u32[]{:S(2)}) copy-start(bf16[128,2048]{1,0:T(8,128)(2,1)} %param.10) | copy-start | bytes 1572868
  0.6 28.1 %copy-start.5 = (bf16[128,2048]{1,0:T(8,128)(2,1)S(1)}, bf16[128,2048]{1,0:T(8,128)(2,1)}, u32[]{:S(2)}) copy-start(bf16[128,2048]{1,0:T(8,128)(2,1)} %param.11) | copy-start | bytes 1572868
  0.7 46.7 %copy-start.6 = (bf16[128,2048]{1,0:T(8,128)(2,1)S(1)}, bf16[128,2048]{1,0:T(8,128)(2,1)}, u32[]{:S(2)}) copy-start(bf16[128,2048]{1,0:T(8,128)(2,1)} %param.12) | copy-start | bytes 1572868
  2.8 21.8 %all-to-all-start = ((bf16[128,16,128]{0,2,1:T(8,128)(2,1)}), bf16[128,16,128]{0,2,1:T(8,128)(2,1)S(1)}, u32[]{:S(2)}, u32[]{:S(2)}) async-start(bf16[128,16,128]{0,2,1:T(8,128)(2,1)} %bitcast), calls=%async_computation | async-start | bytes 1048576 | tf_op jit(solution)/shard_map/all_to_all | solution.py:64
  24.7 18.6 %all-to-all-start.1 = ((bf16[128,16,128]{0,2,1:T(8,128)(2,1)}), bf16[128,16,128]{0,2,1:T(8,128)(2,1)S(1)}, u32[]{:S(2)}, u32[]{:S(2)}) async-start(bf16[128,16,128]{0,2,1:T(8,128)(2,1)} %bitcast.3), calls=%async_computation.1 | async-start | bytes 1048576 | tf_op jit(solution)/shard_map/all_to_all | solution.py:65
  43.2 18.6 %all-to-all-start.2 = ((bf16[128,16,128]{0,2,1:T(8,128)(2,1)}), bf16[128,16,128]{0,2,1:T(8,128)(2,1)S(1)}, u32[]{:S(2)}, u32[]{:S(2)}) async-start(bf16[128,16,128]{0,2,1:T(8,128)(2,1)} %bitcast.6), calls=%async_computation.2 | async-start | bytes 1048576 | tf_op jit(solution)/shard_map/all_to_all | solution.py:67
  61.8 18.6 %all-to-all-start.3 = ((bf16[128,16,128]{0,2,1:T(8,128)(2,1)}), bf16[128,16,128]{0,2,1:T(8,128)(2,1)S(1)}, u32[]{:S(2)}, u32[]{:S(2)}) async-start(bf16[128,16,128]{0,2,1:T(8,128)(2,1)} %bitcast.9), calls=%async_computation.3 | async-start | bytes 1048576 | tf_op jit(solution)/shard_map/all_to_all | solution.py:68
  80.9 12.3 %copy-start.8 = (s32[8,4]{0,1:T(4,128)S(1)}, s32[8,4]{0,1:T(4,128)}, u32[]{:S(2)}) copy-start(s32[8,4]{0,1:T(4,128)} %param.13) | copy-start | bytes 388
  80.9 12.4 %copy-start.7 = (bf16[128,2048]{1,0:T(8,128)(2,1)S(1)}, bf16[128,2048]{1,0:T(8,128)(2,1)}, u32[]{:S(2)}) copy-start(bf16[128,2048]{1,0:T(8,128)(2,1)} %param.7) | copy-start | bytes 1572868
  82.4 26.3 %collective-permute-start = (bf16[4,1024,128]{2,1,0:T(8,128)(2,1)}, bf16[4,1024,128]{2,1,0:T(8,128)(2,1)}, u32[]{:S(2)}, u32[]{:S(2)}) collective-permute-start(bf16[4,1024,128]{2,1,0:T(8,128)(2,1)} %get-tuple-element.6), channel_id=1, source_target_pairs={{0,1},{2,3},{4,5},{6,7},{8,9},{10,11},{12,13},{14,15},{16,17},{18,... | collective-permute-start | bytes 3145736 | tf_op jit(solution)/shard_map/ppermute | solution.py:18
  86.9 27.0 %collective-permute-start.1 = (bf16[4,1024,128]{2,1,0:T(8,128)(2,1)}, bf16[4,1024,128]{2,1,0:T(8,128)(2,1)}, u32[]{:S(2)}, u32[]{:S(2)}) collective-permute-start(bf16[4,1024,128]{2,1,0:T(8,128)(2,1)} %get-tuple-element.7), channel_id=1, source_target_pairs={{1,0},{3,2},{5,4},{7,6},{9,8},{11,10},{13,12},{15,14},{17,16},{19,... | collective-permute-start | bytes 3145736 | tf_op jit(solution)/shard_map/ppermute | solution.py:19
  89.1 50.9 %all-to-all-start.6 = ((bf16[128,16,128]{2,0,1:T(8,128)(2,1)}), bf16[128,16,128]{2,0,1:T(8,128)(2,1)S(1)}, u32[]{:S(2)}, u32[]{:S(2)}) async-start(bf16[128,16,128]{2,0,1:T(8,128)(2,1)} %copy_bitcast_fusion.3), calls=%async_computation.6 | async-start | bytes 1048576 | tf_op jit(solution)/shard_map/all_to_all | solution.py:66
  140.0 18.9 %all-to-all-start.4 = ((bf16[128,16,128]{2,0,1:T(8,128)(2,1)}), bf16[128,16,128]{2,0,1:T(8,128)(2,1)S(1)}, u32[]{:S(2)}, u32[]{:S(2)}) async-start(bf16[128,16,128]{2,0,1:T(8,128)(2,1)} %copy_bitcast_fusion.4), calls=%async_computation.4 | async-start | bytes 1048576 | tf_op jit(solution)/shard_map/all_to_all | solution.py:63
  149.6 1.3 copy-start.3
  166.4 4.3 %copy-start.2 = (bf16[1,8,4,256,128]{4,3,2,1,0:T(8,128)(2,1)S(1)}, bf16[1,8,4,256,128]{4,3,2,1,0:T(8,128)(2,1)}, u32[]{:S(2)}) copy-start(bf16[1,8,4,256,128]{4,3,2,1,0:T(8,128)(2,1)} %get-tuple-element.3) | copy-start | bytes 6291460
  170.6 3.8 %slice-start = ((s8[8388608]{0:T(1024)(128)(4,1)}), s8[4194304]{0:T(1024)(128)(4,1)S(1)}, s32[]{:S(2)}) async-start(s8[8388608]{0:T(1024)(128)(4,1)} %bitcast.83), calls=%async_computation.8 | async-start | bytes 8388608
  172.1 2.3 %copy-start.4 = (bf16[1,8,4,256,128]{4,3,2,1,0:T(8,128)(2,1)S(1)}, bf16[1,8,4,256,128]{4,3,2,1,0:T(8,128)(2,1)}, u32[]{:S(2)}) copy-start(bf16[1,8,4,256,128]{4,3,2,1,0:T(8,128)(2,1)} %get-tuple-element.2) | copy-start | bytes 6291460
  172.1 3.2 %slice-start.1 = ((s8[8388608]{0:T(1024)(128)(4,1)}), s8[4194304]{0:T(1024)(128)(4,1)S(1)}, s32[]{:S(2)}) async-start(s8[8388608]{0:T(1024)(128)(4,1)} %bitcast.83), calls=%async_computation.9 | async-start | bytes 8388608
  179.8 39.4 %copy-start.1 = (bf16[128,2048]{1,0:T(8,128)(2,1)S(1)}, bf16[128,2048]{1,0:T(8,128)(2,1)}, u32[]{:S(2)}) copy-start(bf16[128,2048]{1,0:T(8,128)(2,1)} %param.10) | copy-start | bytes 1572868
  199.7 18.6 %all-to-all-start.5 = ((bf16[16,128,128]{2,1,0:T(8,128)(2,1)}), bf16[16,128,128]{2,1,0:T(8,128)(2,1)S(1)}, u32[]{:S(2)}, u32[]{:S(2)}) async-start(bf16[16,128,128]{2,1,0:T(8,128)(2,1)} %bitcast.20), calls=%async_computation.5 | async-start | bytes 1048576 | tf_op jit(solution)/shard_map/all_to_all | solution.py:73
where the time goes:
time: 220 us; the launch traced here: 219 us
  waiting for transfers between devices  89.5 us (41%)
  starting transfers between devices  37.9 us (17%)
  local copies, waits for them, and re-layouts  35 us (16%)
  matrix products  21.7 us (10%)
  blocking collectives  18.4 us (8%)
  other arithmetic  15.7 us (7%)
    all_to_all x1, blocking collectives, per_device(): lax.all_to_all(tan_h, 'heads', split_axis=0, concat_axis=1, tiled=True)  18.4 us
    gather x2, local copies, waits for them, and re-layouts, attend(): chosen = tiles[:, local].reshape(4, blocks, WK * BQ, width)  15 us
    ppermute x1, waiting for transfers between devices, extended(): before = lax.ppermute(last, axis, up)  14.4 us
    all_to_all x1, waiting for transfers between devices, per_device(): lax.all_to_all(values_tan, 'heads', split_axis=1, concat_axis=0, tiled=True)  13.6 us
    all_to_all x1, waiting for transfers between devices, per_device(): lax.all_to_all(out_h, 'heads', split_axis=0, concat_axis=1, tiled=True)  13.6 us
    all_to_all x1, waiting for transfers between devices, per_device(): lax.all_to_all(values, 'heads', split_axis=1, concat_axis=0, tiled=True)  13.5 us
    all_to_all x1, waiting for transfers between devices, per_device(): lax.all_to_all(keys_tan, 'heads', split_axis=1, concat_axis=0, tiled=True)  13.5 us
    all_to_all x1, waiting for transfers between devices, per_device(): lax.all_to_all(keys, 'heads', split_axis=1, concat_axis=0, tiled=True)  12.4 us
  transfers between devices with their start and end apart: 9, of which 8 were waited for; matrix products, arithmetic and copies ran while one was open for 20% of the time, Pallas kernels for 0%

commit v1 on v0

v1 whole, which is shorter than its diff:
```python
import functools
import math

import jax
import jax.numpy as jnp
from jax import lax
from jax.experimental import pallas as pl
from jax.experimental.pallas import tpu as pltpu
from jax.sharding import PartitionSpec as P

BQ = 256
WK = 4
HB = 4
HALO = HB * BQ


def attend_kernel(table, q_ref, kv_hbm, *rest, halos, hd):
    halo_hbm, (o_ref, kv, sem) = rest[:halos], rest[halos:]
    step = pl.program_id(0)
    rows = kv_hbm.shape[0]

    @pl.when(step == 0)
    def load():
        copies = [pltpu.make_async_copy(kv_hbm, kv.at[pl.ds(0, rows)], sem.at[0])]
        for i, ref in enumerate(halo_hbm):
            copies.append(
                pltpu.make_async_copy(ref, kv.at[pl.ds(rows + i * HALO, HALO)], sem.at[1 + i])
            )
        for copy in copies:
            copy.start()
        for copy in copies:
            copy.wait()

    scale = hd ** (-0.5)
    factor = scale * math.log2(math.e)
    trans = (((1,), (1,)), ((), ()))
    both = q_ref[...]
    query = both[:, :hd]
    starts = [pl.multiple_of(table[step * WK + w] * BQ, BQ) for w in range(WK)]
    scores, tans = [], []
    for start in starts:
        keys = kv[pl.ds(start, BQ), : 2 * hd]
        scores.append(
            lax.dot_general(query, keys[:, hd:], trans, preferred_element_type=jnp.float32)
        )
        tans.append(lax.dot_general(both, keys, trans, preferred_element_type=jnp.float32))
    top = functools.reduce(jnp.maximum, scores)
    top = jnp.max(top, axis=1, keepdims=True) * factor
    probs = [jnp.exp2(s * factor - top) for s in scores]
    weighted = [p * t for p, t in zip(probs, tans)]
    total = jnp.sum(functools.reduce(jnp.add, probs), axis=1, keepdims=True)
    mean = jnp.sum(functools.reduce(jnp.add, weighted), axis=1, keepdims=True)
    main, side = 0.0, 0.0
    for start, p, w in zip(starts, probs, weighted):
        vals = kv[pl.ds(start, BQ), 2 * hd :]
        main += jnp.dot(p.astype(jnp.bfloat16), vals, preferred_element_type=jnp.float32)
        side += jnp.dot(w.astype(jnp.bfloat16), vals[:, :hd], preferred_element_type=jnp.float32)
    inverse = 1.0 / total
    out = main[:, :hd] * inverse
    tan = (main[:, hd:] + scale * side) * inverse - (scale * mean * inverse) * out
    o_ref[:, :hd] = out.astype(jnp.bfloat16)
    o_ref[:, hd:] = tan.astype(jnp.bfloat16)


def attend(table, q_pair, kv, halos):
    rows, width = q_pair.shape
    hd = width // 2
    blocks = rows // BQ
    total = rows + len(halos) * HALO
    elements = rows * WK * BQ
    return pl.pallas_call(
        functools.partial(attend_kernel, halos=len(halos), hd=hd),
        grid_spec=pltpu.PrefetchScalarGridSpec(
            num_scalar_prefetch=1,
            grid=(blocks,),
            in_specs=[pl.BlockSpec((BQ, width), lambda i, t: (i, 0))]
            + [pl.BlockSpec(memory_space=pl.ANY)] * (1 + len(halos)),
            out_specs=pl.BlockSpec((BQ, width), lambda i, t: (i, 0)),
            scratch_shapes=[
                pltpu.VMEM((total, 4 * hd), jnp.bfloat16),
                pltpu.SemaphoreType.DMA((1 + len(halos),)),
            ],
        ),
        out_shape=jax.ShapeDtypeStruct((rows, width), jnp.bfloat16),
        compiler_params=pltpu.CompilerParams(vmem_limit_bytes=32 * 1024 * 1024),
        cost_estimate=pl.CostEstimate(
            flops=12 * elements * hd,
            bytes_accessed=2 * (total * 4 * hd + 2 * rows * width),
            transcendentals=elements,
        ),
    )(table, q_pair, kv, *halos)


def to_heads(arrays, devices):
    tokens, columns = arrays[0].shape
    hd = columns // devices
    parts = [a.reshape(tokens, devices, hd).transpose(1, 0, 2) for a in arrays]
    sent = jnp.concatenate(parts, axis=2)
    got = lax.all_to_all(sent, "heads", split_axis=0, concat_axis=0, tiled=True)
    return got.reshape(devices * tokens, len(arrays) * hd)


def exchange(kv, frame, frames):
    rows = kv.shape[0]
    halos = []
    for first in (0, 1):
        pairs = [(i, i + 1) for i in range(first, frames - 1, 2)]
        if not pairs:
            continue
        start = jnp.where(frame % 2 == first, rows - HALO, 0)
        edge = lax.dynamic_slice_in_dim(kv, start, HALO, axis=0)
        halos.append(lax.ppermute(edge, "frames", pairs + [(j, i) for i, j in pairs]))
    return halos


def slots(neighbors, frame, blocks):
    local = neighbors - frame * blocks
    even = frame % 2 == 0
    before = blocks + jnp.where(even, HB, 0) + local + HB
    after = blocks + jnp.where(even, 0, HB) + local - blocks
    return jnp.where(local < 0, before, jnp.where(local >= blocks, after, local)).reshape(-1)


def per_device(query, keys, values, query_tan, keys_tan, values_tan, neighbors):
    devices, frames = lax.axis_size("heads"), lax.axis_size("frames")
    frame = lax.axis_index("frames")
    tokens, columns = query.shape
    hd = columns // devices
    kv = to_heads([keys_tan, keys, values, values_tan], devices)
    halos = exchange(kv, frame, frames)
    q_pair = to_heads([query, query_tan], devices)
    table = slots(neighbors, frame, neighbors.shape[0])
    pair = attend(table, q_pair, kv, halos).reshape(devices, tokens, 2 * hd)
    back = lax.all_to_all(pair, "heads", split_axis=0, concat_axis=0, tiled=True)
    back = back.reshape(devices, tokens, 2, hd).transpose(2, 1, 0, 3)
    back = back.reshape(2, tokens, columns)
    return back[0], back[1]


def solution(mesh):
    own = P(("frames", "heads"), None)
    return jax.shard_map(
        per_device,
        mesh=mesh,
        in_specs=(own,) * 6 + (P("frames", None),),
        out_specs=(own, own),
        check_vma=False,
    )
```

time: 220 us -> 137 us (0.62)
  local copies, waits for them, and re-layouts: 35 us -> 8.17 us
  waiting for transfers between devices: 89.5 us -> 62.7 us
  matrix products: 21.7 us -> 0 us
  starting transfers between devices: 37.9 us -> 20.3 us
  other arithmetic: 15.7 us -> 2.75 us
  blocking collectives: 18.4 us -> 30.4 us
  Pallas kernels: 0 us -> 11.2 us
    ppermute x2 -> x1, waiting for transfers between devices: 19.5 us -> 3.81 us  [exchange(): lax.ppermute(edge, 'frames', pairs + [(j, i) for i, j in pairs])]
    gather x2 -> x0, local copies, waits for them, and re-layouts: 15 us -> none  [attend(): chosen = tiles[:, local].reshape(4, blocks, WK * BQ, width)]
    dot_general x5 -> x0, matrix products: 14.3 us -> none  [the longest x1 4.55 us: attend(): jnp.einsum('nqd,nkd->nqk', q_rows, kt_win, preferred_element_type=jnp.flo...]
    all_to_all x7 -> x2, starting transfers between devices: 32.2 us -> 18.8 us  [to_heads(): got = lax.all_to_all(sent, 'heads', split_axis=0, concat_axis=0, tiled=True)]
    all_to_all x1, blocking collectives: 18.4 us -> 30.4 us  [per_device(): lax.all_to_all(pair, 'heads', split_axis=0, concat_axis=0, tiled=True)]
    pallas_call x0 -> x1, Pallas kernels: none -> 11.2 us  [attend(): pl.pallas_call(functools.partial(attend_kernel, halos=len(halos), hd=hd),...]
    all_to_all x7 -> x2, waiting for transfers between devices: 70 us -> 58.9 us  [to_heads(): got = lax.all_to_all(sent, 'heads', split_axis=0, concat_axis=0, tiled=True)]
    concatenate x1 -> x2, other arithmetic: 11.2 us -> 2.75 us  [to_heads(): sent = jnp.concatenate(parts, axis=2)]
  transfers between devices with their start and end apart: 9 -> 3, of which waited for: 8 -> 3; matrix products, arithmetic and copies ran while one was open for 20% -> 3% of each run, Pallas kernels for 0% -> 0%
where the time goes in v1:
time: 137 us; the launch traced here: 136 us
  waiting for transfers between devices  62.7 us (46%)
  blocking collectives  30.4 us (22%)
  starting transfers between devices  20.3 us (15%)
  Pallas kernels  11.2 us (8%)
  local copies, waits for them, and re-layouts  8.17 us (6%)
  other arithmetic  2.75 us (2%)
    all_to_all x2, waiting for transfers between devices, to_heads(): got = lax.all_to_all(sent, 'heads', split_axis=0, concat_axis=0, tiled=True)  58.9 us
    all_to_all x1, blocking collectives, per_device(): lax.all_to_all(pair, 'heads', split_axis=0, concat_axis=0, tiled=True)  30.4 us
    all_to_all x2, starting transfers between devices, to_heads(): got = lax.all_to_all(sent, 'heads', split_axis=0, concat_axis=0, tiled=True)  18.8 us
    pallas_call x1, Pallas kernels, attend(): pl.pallas_call(functools.partial(attend_kernel, halos=len(halos), hd=hd),...  11.2 us
    ppermute x1, waiting for transfers between devices, exchange(): lax.ppermute(edge, 'frames', pairs + [(j, i) for i, j in pairs])  3.81 us
    transpose x3, local copies, waits for them, and re-layouts, to_heads(): parts = [a.reshape(tokens, devices, hd).transpose(1, 0, 2) for a in arrays]  2.9 us
    unnamed x12, local copies, waits for them, and re-layouts  2.9 us
    concatenate x2, other arithmetic, to_heads(): sent = jnp.concatenate(parts, axis=2)  2.75 us
  transfers between devices with their start and end apart: 3, of which 3 were waited for; matrix products, arithmetic and copies ran while one was open for 3% of the time, Pallas kernels for 0%

profile of v1, /device:TPU:0, one launch (start us, length us, event | category | flops | bytes accessed | tf_op | source)
XLA Modules:
  0.0 136.2 jit_solution(14649925181190264809)
XLA Ops:
  0.6 0.0 copy-start
  0.6 0.0 copy-start.1
  0.7 0.0 copy-start.2
  0.7 1.0 copy-done
  1.7 1.3 bitcast_bitcast_fusion
  3.0 0.0 copy-done.1
  3.0 0.0 copy-done.2
  3.0 0.3 bitcast_bitcast_fusion.2
  3.3 1.6 %pad_maximum_fusion = bf16[16,128,512]{2,1,0:T(8,128)(2,1)} fusion(bf16[16,128,128]{2,1,0:T(8,128)(2,1)S(1)} %get-tuple-element.6, bf16[16,128,128]{2,1,0:T(8,128)(2,1)S(1)} %get-tuple-element.7, bf16[16,128,128]{2,1,0:T(8,128)(2,1)S(1)} %get-tuple-element.8, bf16[16,128,128]{2,1,0:T(8,128)(2,1)S(1)} %get-tuple-element.9), kind=kLoop, calls=%fused_computation | loop fusion | flops 8388608 | bytes 4194304 | tf_op jit(solution)/shard_map/concatenate | solution.py:98
  4.9 0.0 copy-start.3
  4.9 7.5 %all-to-all-start.1 = ((bf16[16,128,512]{2,1,0:T(8,128)(2,1)}), bf16[16,128,512]{2,1,0:T(8,128)(2,1)S(1)}, u32[]{:S(2)}, u32[]{:S(2)}) async-start(bf16[16,128,512]{2,1,0:T(8,128)(2,1)} %pad_maximum_fusion), calls=%async_computation.1 | async-start | bytes 4194304 | tf_op jit(solution)/shard_map/all_to_all | solution.py:99
  12.4 0.0 copy-done.3
  12.4 1.3 bitcast_bitcast_fusion.4
  13.8 1.1 pad_maximum_fusion.1
  14.9 0.0 copy-start.4
  14.9 38.6 %all-to-all-done.1 = bf16[16,128,512]{2,1,0:T(8,128)(2,1)S(1)} async-done(((bf16[16,128,512]{2,1,0:T(8,128)(2,1)}), bf16[16,128,512]{2,1,0:T(8,128)(2,1)S(1)}, u32[]{:S(2)}, u32[]{:S(2)}) %all-to-all-start.1) | async-done | bytes 2097184 | tf_op jit(solution)/shard_map/all_to_all | solution.py:99
  53.5 11.3 %all-to-all-start = ((bf16[16,128,256]{2,1,0:T(8,128)(2,1)}), bf16[16,128,256]{2,1,0:T(8,128)(2,1)}, u32[]{:S(2)}, u32[]{:S(2)}) async-start(bf16[16,128,256]{2,1,0:T(8,128)(2,1)} %pad_maximum_fusion.1), calls=%async_computation | async-start | bytes 2097152 | tf_op jit(solution)/shard_map/all_to_all | solution.py:99
  64.8 1.1 constant_dynamic-slice_fusion
  65.9 1.5 %collective-permute-start = (bf16[1024,512]{1,0:T(8,128)(2,1)}, bf16[1024,512]{1,0:T(8,128)(2,1)}, u32[]{:S(2)}, u32[]{:S(2)}) collective-permute-start(bf16[1024,512]{1,0:T(8,128)(2,1)} %constant_dynamic-slice_fusion), channel_id=1, source_target_pairs={{0,1},{1,0},{2,3},{3,2},{4,5},{5,4},{6,7},{7,6},{8,9},{9,8},{10,11... | collective-permute-start | bytes 3145736 | tf_op jit(solution)/shard_map/ppermute | solution.py:112
  67.4 0.0 copy-done.4
  67.4 0.1 copy.17
  67.5 0.1 reshape.42.table
  67.6 20.2 %all-to-all-done = bf16[16,128,256]{2,1,0:T(8,128)(2,1)} async-done(((bf16[16,128,256]{2,1,0:T(8,128)(2,1)}), bf16[16,128,256]{2,1,0:T(8,128)(2,1)}, u32[]{:S(2)}, u32[]{:S(2)}) %all-to-all-start) | async-done | bytes 1048608 | tf_op jit(solution)/shard_map/all_to_all | solution.py:99
  87.8 3.8 %collective-permute-done.rest_0_ = bf16[1024,512]{1,0:T(8,128)(2,1)} collective-permute-done((bf16[1024,512]{1,0:T(8,128)(2,1)}, bf16[1024,512]{1,0:T(8,128)(2,1)}, u32[]{:S(2)}, u32[]{:S(2)}) %collective-permute-start) | collective-permute-done | bytes 1048608 | tf_op jit(solution)/shard_map/ppermute | solution.py:112
  91.6 11.2 %shard_map.86 = bf16[2048,256]{1,0:T(8,128)(2,1)S(1)} custom-call(s32[32]{0:T(128)S(1)} %reshape.42.table, bf16[2048,256]{1,0:T(8,128)(2,1)} %bitcast.2.q_ref, bf16[2048,512]{1,0:T(8,128)(2,1)S(1)} %bitcast.59, bf16[1024,512]{1,0:T(8,128)(2,1)} %collective-permute-done.rest_0_), custom_call_target="tpu_custom_call" | custom-call | flops 3221225472 | bytes 5242880 | tf_op jit(solution)/shard_map/pallas_call | solution.py:71
  102.8 30.4 %all_to_all.15 = bf16[16,128,256]{2,1,0:T(8,128)(2,1)S(1)} all-to-all(bf16[16,128,256]{2,1,0:T(8,128)(2,1)S(1)} %bitcast.60), channel_id=1, replica_groups=mesh['heads'=16,'frames'=2] {'heads'}, dimensions={0} | all-to-all | bytes 2097152 | tf_op jit(solution)/shard_map/all_to_all | solution.py:134
  133.2 0.3 reshape.52
  133.4 0.7 copy.42
  134.1 0.2 fusion.1
  134.3 0.9 copy.43
  135.3 0.9 copy.44
  (1 shorter events, 0.0 us)
Async XLA Ops:
  0.6 1.0 copy-start
  0.6 2.4 %copy-start.1 = (bf16[128,2048]{1,0:T(8,128)(2,1)S(1)}, bf16[128,2048]{1,0:T(8,128)(2,1)}, u32[]{:S(2)}) copy-start(bf16[128,2048]{1,0:T(8,128)(2,1)} %param.11) | copy-start | bytes 1572868
  0.7 2.4 %copy-start.2 = (bf16[128,2048]{1,0:T(8,128)(2,1)S(1)}, bf16[128,2048]{1,0:T(8,128)(2,1)}, u32[]{:S(2)}) copy-start(bf16[128,2048]{1,0:T(8,128)(2,1)} %param.8) | copy-start | bytes 1572868
  4.9 7.5 %copy-start.3 = (bf16[128,2048]{1,0:T(8,128)(2,1)S(1)}, bf16[128,2048]{1,0:T(8,128)(2,1)}, u32[]{:S(2)}) copy-start(bf16[128,2048]{1,0:T(8,128)(2,1)} %param.7) | copy-start | bytes 1572868
  4.9 48.6 %all-to-all-start.1 = ((bf16[16,128,512]{2,1,0:T(8,128)(2,1)}), bf16[16,128,512]{2,1,0:T(8,128)(2,1)S(1)}, u32[]{:S(2)}, u32[]{:S(2)}) async-start(bf16[16,128,512]{2,1,0:T(8,128)(2,1)} %pad_maximum_fusion), calls=%async_computation.1 | async-start | bytes 4194304 | tf_op jit(solution)/shard_map/all_to_all | solution.py:99
  14.9 52.5 %copy-start.4 = (s32[8,4]{0,1:T(4,128)S(1)}, s32[8,4]{0,1:T(4,128)}, u32[]{:S(2)}) copy-start(s32[8,4]{0,1:T(4,128)} %param.13) | copy-start | bytes 388
  53.5 34.3 %all-to-all-start = ((bf16[16,128,256]{2,1,0:T(8,128)(2,1)}), bf16[16,128,256]{2,1,0:T(8,128)(2,1)}, u32[]{:S(2)}, u32[]{:S(2)}) async-start(bf16[16,128,256]{2,1,0:T(8,128)(2,1)} %pad_maximum_fusion.1), calls=%async_computation | async-start | bytes 2097152 | tf_op jit(solution)/shard_map/all_to_all | solution.py:99
  65.9 25.7 %collective-permute-start = (bf16[1024,512]{1,0:T(8,128)(2,1)}, bf16[1024,512]{1,0:T(8,128)(2,1)}, u32[]{:S(2)}, u32[]{:S(2)}) collective-permute-start(bf16[1024,512]{1,0:T(8,128)(2,1)} %constant_dynamic-slice_fusion), channel_id=1, source_target_pairs={{0,1},{1,0},{2,3},{3,2},{4,5},{5,4},{6,7},{7,6},{8,9},{9,8},{10,11... | collective-permute-start | bytes 3145736 | tf_op jit(solution)/shard_map/ppermute | solution.py:112

commit v2 on v1

v2 whole, which is shorter than its diff:
```python
import functools
import math

import jax
import jax.numpy as jnp
from jax import lax
from jax.experimental import pallas as pl
from jax.experimental.pallas import tpu as pltpu
from jax.sharding import PartitionSpec as P

BQ = 256
WK = 4
HB = 4
VMEM_LIMIT = 32 * 1024 * 1024
ANY = pl.BlockSpec(memory_space=pl.ANY)
VMEM = pl.BlockSpec(memory_space=pltpu.VMEM)
SMEM = pl.BlockSpec(memory_space=pltpu.SMEM)


def finish(copies):
    for copy in copies:
        copy.start()
    for copy in copies:
        copy.wait()


def pack_kernel(me, *refs, count, hd):
    arrays, pieces, sems = refs[:count], refs[count:-1], refs[-1]
    copies = []
    for k, piece in enumerate(pieces):
        column = pl.multiple_of((me[0] ^ k) * hd, hd)
        for a, array in enumerate(arrays):
            source = array.at[:, pl.ds(column, hd)]
            copies.append(
                pltpu.make_async_copy(source, piece.at[:, pl.ds(a * hd, hd)], sems.at[k, a])
            )
    finish(copies)


def pack(me, arrays, devices):
    tokens, columns = arrays[0].shape
    hd, count = columns // devices, len(arrays)
    piece = jax.ShapeDtypeStruct((tokens, count * hd), jnp.bfloat16)
    size = 2 * tokens * columns * count
    return pl.pallas_call(
        functools.partial(pack_kernel, count=count, hd=hd),
        in_specs=[SMEM] + [ANY] * count,
        out_specs=[ANY] * devices,
        out_shape=[piece] * devices,
        scratch_shapes=[pltpu.SemaphoreType.DMA((devices, count))],
        cost_estimate=pl.CostEstimate(flops=0, bytes_accessed=2 * size, transcendentals=0),
    )(me, *arrays)


def unpack_kernel(me, *refs, count, hd):
    pieces, arrays, sems = refs[: -count - 1], refs[-count - 1 : -1], refs[-1]
    copies = []
    for k, piece in enumerate(pieces):
        column = pl.multiple_of((me[0] ^ k) * hd, hd)
        for a, array in enumerate(arrays):
            target = array.at[:, pl.ds(column, hd)]
            copies.append(
                pltpu.make_async_copy(piece.at[:, pl.ds(a * hd, hd)], target, sems.at[k, a])
            )
    finish(copies)


def unpack(me, pieces, count):
    tokens, width = pieces[0].shape
    devices, hd = len(pieces), width // count
    array = jax.ShapeDtypeStruct((tokens, devices * hd), jnp.bfloat16)
    size = 2 * tokens * width * devices
    return pl.pallas_call(
        functools.partial(unpack_kernel, count=count, hd=hd),
        in_specs=[SMEM] + [ANY] * devices,
        out_specs=[ANY] * count,
        out_shape=[array] * count,
        scratch_shapes=[pltpu.SemaphoreType.DMA((devices, count))],
        cost_estimate=pl.CostEstimate(flops=0, bytes_accessed=2 * size, transcendentals=0),
    )(me, *pieces)


def edge_kernel(group, *refs):
    pieces, out, sems = refs[:-2], refs[-2], refs[-1]
    tokens = pieces[0].shape[0]
    per = out.shape[0] // tokens
    for g in range(len(pieces) // per):

        @pl.when(group[0] == g)
        def copy(g=g):
            finish(
                [
                    pltpu.make_async_copy(
                        pieces[g * per + i], out.at[pl.ds(i * tokens, tokens)], sems.at[i]
                    )
                    for i in range(per)
                ]
            )


def edge(group, pieces):
    tokens, width = pieces[0].shape
    rows = HB * BQ
    return pl.pallas_call(
        edge_kernel,
        in_specs=[SMEM] + [ANY] * len(pieces),
        out_specs=ANY,
        out_shape=jax.ShapeDtypeStruct((rows, width), jnp.bfloat16),
        scratch_shapes=[pltpu.SemaphoreType.DMA((rows // tokens,))],
        cost_estimate=pl.CostEstimate(
            flops=0, bytes_accessed=4 * rows * width, transcendentals=0
        ),
    )(group, *pieces)


def attend_kernel(table, *refs, count, own, halos, hd, first):
    q_refs, refs = refs[:count], refs[count:]
    pieces, refs = refs[:own], refs[own:]
    halo_refs, refs = refs[:halos], refs[halos:]
    outs, kv, sems = refs[:count], refs[count], refs[count + 1]
    tokens = q_refs[0].shape[0]
    per = BQ // tokens
    copies, row = [], 0
    for i, ref in enumerate(pieces + halo_refs):
        rows = ref.shape[0]
        copies.append(pltpu.make_async_copy(ref, kv.at[pl.ds(row, rows)], sems.at[i]))
        row += rows
    finish(copies)

    scale = hd ** (-0.5)
    factor = scale * math.log2(math.e)
    trans = (((1,), (1,)), ((), ()))
    for b in range(count // per):
        both = jnp.concatenate([q_refs[b * per + i][...] for i in range(per)], axis=0)
        query = both[:, :hd]
        starts = [pl.multiple_of(table[first + b, w] * BQ, BQ) for w in range(WK)]
        scores, tans = [], []
        for start in starts:
            keys = kv[pl.ds(start, BQ), : 2 * hd]
            scores.append(
                lax.dot_general(query, keys[:, hd:], trans, preferred_element_type=jnp.float32)
            )
            tans.append(lax.dot_general(both, keys, trans, preferred_element_type=jnp.float32))
        top = functools.reduce(jnp.maximum, scores)
        top = jnp.max(top, axis=1, keepdims=True) * factor
        probs = [jnp.exp2(s * factor - top) for s in scores]
        weighted = [p * t for p, t in zip(probs, tans)]
        total = jnp.sum(functools.reduce(jnp.add, probs), axis=1, keepdims=True)
        mean = jnp.sum(functools.reduce(jnp.add, weighted), axis=1, keepdims=True)
        main, side = 0.0, 0.0
        for start, p, w in zip(starts, probs, weighted):
            vals = kv[pl.ds(start, BQ), 2 * hd :]
            main += jnp.dot(p.astype(jnp.bfloat16), vals, preferred_element_type=jnp.float32)
            side += jnp.dot(
                w.astype(jnp.bfloat16), vals[:, :hd], preferred_element_type=jnp.float32
            )
        inverse = 1.0 / total
        out = main[:, :hd] * inverse
        tan = (main[:, hd:] + scale * side) * inverse - (scale * mean * inverse) * out
        out, tan = out.astype(jnp.bfloat16), tan.astype(jnp.bfloat16)
        for i in range(per):
            outs[b * per + i][:, :hd] = out[i * tokens : (i + 1) * tokens]
            outs[b * per + i][:, hd:] = tan[i * tokens : (i + 1) * tokens]


def attend(table, first, queries, pieces, halos):
    tokens, width = queries[0].shape
    hd = width // 2
    total = sum(a.shape[0] for a in pieces) + sum(a.shape[0] for a in halos)
    rows = tokens * len(queries)
    elements = rows * WK * BQ
    return pl.pallas_call(
        functools.partial(
            attend_kernel,
            count=len(queries),
            own=len(pieces),
            halos=len(halos),
            hd=hd,
            first=first,
        ),
        in_specs=[SMEM] + [VMEM] * len(queries) + [ANY] * (len(pieces) + len(halos)),
        out_specs=[VMEM] * len(queries),
        out_shape=[jax.ShapeDtypeStruct((tokens, width), jnp.bfloat16)] * len(queries),
        scratch_shapes=[
            pltpu.VMEM((total, 4 * hd), jnp.bfloat16),
            pltpu.SemaphoreType.DMA((len(pieces) + len(halos),)),
        ],
        compiler_params=pltpu.CompilerParams(vmem_limit_bytes=VMEM_LIMIT),
        cost_estimate=pl.CostEstimate(
            flops=12 * elements * hd,
            bytes_accessed=2 * (total * 4 * hd + 2 * rows * width),
            transcendentals=elements,
        ),
    )(table, *queries, *pieces, *halos)


def send(pieces, slots, devices):
    got = {}
    for k in slots:
        pairs = [(i, i ^ k) for i in range(devices)]
        got[k] = lax.ppermute(pieces[k], "heads", pairs) if k else pieces[k]
    return got


def per_device(query, keys, values, query_tan, keys_tan, values_tan, neighbors):
    devices, frames = lax.axis_size("heads"), lax.axis_size("frames")
    index, frame = lax.axis_index("heads"), lax.axis_index("frames")
    tokens = query.shape[0]
    blocks = neighbors.shape[0]
    per = BQ // tokens
    me = index.reshape(1).astype(jnp.int32)
    chip = index // per
    far = list(range(devices // 2, devices))
    near = list(range(devices // 2 - 1, -1, -1))

    sent = pack(me, [keys_tan, keys, values, values_tan], devices)
    got = send(sent, far + near, devices)
    kv = [got[k] for k in range(devices)]
    q_sent = pack(me, [query, query_tan], devices)
    q_got = send(q_sent, far + near, devices)

    halos = []
    for first in (0, 1):
        pairs = [(i, i + 1) for i in range(first, frames - 1, 2)]
        if not pairs:
            continue
        group = jnp.where(frame % 2 == first, blocks // HB - 1, 0) ^ (chip // HB)
        outer = edge(group.reshape(1).astype(jnp.int32), kv)
        halos.append(lax.ppermute(outer, "frames", pairs + [(j, i) for i, j in pairs]))

    local = neighbors - frame * blocks
    even = frame % 2 == 0
    before = blocks + jnp.where(even, HB, 0) + ((local + blocks) ^ chip) % HB
    after = blocks + jnp.where(even, 0, HB) + ((local - blocks) ^ chip) % HB
    table = jnp.where(local < 0, before, jnp.where(local >= blocks, after, local ^ chip))
    table = table[jnp.arange(blocks) ^ chip]

    half = blocks // 2
    outs = {}
    for low, high in ((half, half + half // 2), (half + half // 2, blocks), (0, half)):
        slots = range(low * per, high * per)
        done = attend(table, low, [q_got[k] for k in slots], kv, halos)
        outs.update(send(dict(zip(slots, done)), slots, devices))
    return unpack(me, [outs[k] for k in range(devices)], 2)


def solution(mesh):
    own = P(("frames", "heads"), None)
    return jax.shard_map(
        per_device,
        mesh=mesh,
        in_specs=(own,) * 6 + (P("frames", None),),
        out_specs=(own, own),
        check_vma=False,
    )
```

time: 137 us -> 308 us (2.25)
  Pallas kernels: 11.2 us -> 183 us
  starting transfers between devices: 20.3 us -> 76.9 us
  blocking collectives: 30.4 us -> 0 us
  waiting for transfers between devices: 62.7 us -> 36.3 us
    pallas_call x1 -> x7, Pallas kernels: 11.2 us -> 183 us  [the longest x2 98.4 us: pack(): pl.pallas_call(functools.partial(pack_kernel, count=count, hd=hd), in_spe...]
    ppermute x1 -> x46, starting transfers between devices: 1.52 us -> 76.9 us  [the longest x45 75.4 us: send(): got[k] = lax.ppermute(pieces[k], 'heads', pairs) if k else pieces[k]]
    all_to_all x2 -> x0, waiting for transfers between devices: 58.9 us -> none  [to_heads(): got = lax.all_to_all(sent, 'heads', split_axis=0, concat_axis=0, tiled=True)]
    ppermute x1 -> x46, waiting for transfers between devices: 3.81 us -> 36.3 us  [the longest x45 36.3 us: send(): got[k] = lax.ppermute(pieces[k], 'heads', pairs) if k else pieces[k]]
    all_to_all x1 -> x0, blocking collectives: 30.4 us -> none  [per_device(): lax.all_to_all(pair, 'heads', split_axis=0, concat_axis=0, tiled=True)]
    all_to_all x2 -> x0, starting transfers between devices: 18.8 us -> none  [to_heads(): got = lax.all_to_all(sent, 'heads', split_axis=0, concat_axis=0, tiled=True)]
    unnamed x12 -> x123, local copies, waits for them, and re-layouts: 2.9 us -> 9.82 us
  transfers between devices with their start and end apart: 3 -> 46, of which waited for: 3 -> 15; matrix products, arithmetic and copies ran while one was open for 3% -> 0% of each run, Pallas kernels for 0% -> 17%
where the time goes in v2:
time: 308 us
  Pallas kernels  183 us (59%)
  starting transfers between devices  76.9 us (25%)
  waiting for transfers between devices  36.3 us (12%)
  local copies, waits for them, and re-layouts  10.4 us (3%)
    pallas_call x2, Pallas kernels, pack(): pl.pallas_call(functools.partial(pack_kernel, count=count, hd=hd), in_spe...  98.4 us
    ppermute x45, starting transfers between devices, send(): got[k] = lax.ppermute(pieces[k], 'heads', pairs) if k else pieces[k]  75.4 us
    ppermute x45, waiting for transfers between devices, send(): got[k] = lax.ppermute(pieces[k], 'heads', pairs) if k else pieces[k]  36.3 us
    pallas_call x1, Pallas kernels, unpack(): pl.pallas_call(functools.partial(unpack_kernel, count=count, hd=hd), in_s...  33.1 us
    pallas_call x1, Pallas kernels, edge(): pl.pallas_call(edge_kernel, in_specs=[SMEM] + [ANY] * len(pieces), out_sp...  32.9 us
    pallas_call x3, Pallas kernels, attend(): pl.pallas_call(functools.partial(attend_kernel, count=len(queries), own=l...  18.5 us
    unnamed x123, local copies, waits for them, and re-layouts  9.82 us
  transfers between devices with their start and end apart: 46, of which 15 were waited for; matrix products, arithmetic and copies ran while one was open for 0% of the time, Pallas kernels for 17%

profile of v2, /device:TPU:0, one launch (start us, length us, event | category | flops | bytes accessed | tf_op | source)
XLA Modules:
  0.0 308.0 jit_solution(8183950684053427614)
XLA Ops:
  0.6 65.2 %shard_map.87 = (bf16[128,512]{1,0:T(8,128)(2,1)}, bf16[128,512]{1,0:T(8,128)(2,1)}, bf16[128,512]{1,0:T(8,128)(2,1)}, bf16[128,512]{1,0:T(8,128)(2,1)}, bf16[12...) custom-call(s32[1]{0:T(128)} %bitcast.me, ...), custom_call_target="tpu_custom_call" | custom-call | bytes 4194304 | tf_op jit(solution)/shard_map/pallas_call | solution.py:45
  65.9 3.1 %collective-permute-start.10 = (bf16[128,512]{1,0:T(8,128)(2,1)}, bf16[128,512]{1,0:T(8,128)(2,1)S(1)}, u32[]{:S(2)}, u32[]{:S(2)}) collective-permute-start(bf16[128,512]{1,0:T(8,128)(2,1)} %get-tuple-element.62), channel_id=1, source_target_pairs={{0,8},{2,10},{4,12},{6,14},{8,0},{10,2},{12,4},{14,6},{16,24},{18,... | collective-permute-start | bytes 393224 | tf_op jit(solution)/shard_map/ppermute | solution.py:201
  69.0 2.1 collective-permute-start.12
  71.1 0.6 collective-permute-start.13
  71.7 2.7 collective-permute-start.14
  74.4 1.6 collective-permute-done.11.refs_5_.refs_13_.refs_9_
  76.0 9.0 %collective-permute-start.16 = (bf16[128,512]{1,0:T(8,128)(2,1)}, bf16[128,512]{1,0:T(8,128)(2,1)S(1)}, u32[]{:S(2)}, u32[]{:S(2)}) collective-permute-start(bf16[128,512]{1,0:T(8,128)(2,1)} %get-tuple-element.68), channel_id=1, source_target_pairs={{0,20},{2,22},{4,16},{6,18},{8,28},{10,30},{12,24},{14,26},{16,4},... | collective-permute-start | bytes 393224 | tf_op jit(solution)/shard_map/ppermute | solution.py:201
  84.9 0.7 collective-permute-done.12.refs_6_.refs_14_.refs_10_
  85.7 1.6 collective-permute-done.13.refs_7_.refs_15_.refs_11_
  87.2 3.2 %collective-permute-start.18 = (bf16[128,512]{1,0:T(8,128)(2,1)}, bf16[128,512]{1,0:T(8,128)(2,1)S(1)}, u32[]{:S(2)}, u32[]{:S(2)}) collective-permute-start(bf16[128,512]{1,0:T(8,128)(2,1)} %get-tuple-element.70), channel_id=1, source_target_pairs={{0,24},{2,26},{4,28},{6,30},{8,16},{10,18},{12,20},{14,22},{16,8},... | collective-permute-start | bytes 393224 | tf_op jit(solution)/shard_map/ppermute | solution.py:201
  90.4 1.0 collective-permute-start.19
  91.4 3.4 %collective-permute-start.20 = (bf16[128,512]{1,0:T(8,128)(2,1)}, bf16[128,512]{1,0:T(8,128)(2,1)S(1)}, u32[]{:S(2)}, u32[]{:S(2)}) collective-permute-start(bf16[128,512]{1,0:T(8,128)(2,1)} %get-tuple-element.72), channel_id=1, source_target_pairs={{0,28},{2,30},{4,24},{6,26},{8,20},{10,22},{12,16},{14,18},{16,12}... | collective-permute-start | bytes 393224 | tf_op jit(solution)/shard_map/ppermute | solution.py:201
  94.8 11.9 %collective-permute-done.16.refs_10_.refs_18_.refs_14_ = bf16[128,512]{1,0:T(8,128)(2,1)S(1)} collective-permute-done((bf16[128,512]{1,0:T(8,128)(2,1)}, bf16[128,512]{1,0:T(8,128)(2,1)S(1)}, u32[]{:S(2)}, u32[]{:S(2)}) %collective-permute-start.16) | collective-permute-done | bytes 131104 | tf_op jit(solution)/shard_map/ppermute | solution.py:201
  106.7 0.9 collective-permute-start.21
  107.6 1.8 collective-permute-done.17.refs_11_.refs_19_.refs_15_
  109.5 0.6 collective-permute-start.8
  110.2 1.1 collective-permute-start.9
  111.3 4.2 %collective-permute-done.21.refs_15_.refs_23_.refs_19_ = bf16[128,512]{1,0:T(8,128)(2,1)S(1)} collective-permute-done((bf16[128,512]{1,0:T(8,128)(2,1)}, bf16[128,512]{1,0:T(8,128)(2,1)S(1)}, u32[]{:S(2)}, u32[]{:S(2)}) %collective-permute-start.21) | collective-permute-done | bytes 131104 | tf_op jit(solution)/shard_map/ppermute | solution.py:201
  115.5 2.9 collective-permute-done.8.refs_2_.refs_10_.refs_6_
  118.4 2.7 collective-permute-done.9.refs_3_.refs_11_.refs_7_
  121.7 32.9 %shard_map.88 = bf16[1024,512]{1,0:T(8,128)(2,1)} custom-call(s32[1]{0:T(128)} %bitcast.2.group, bf16[128,512]{1,0:T(8,128)(2,1)} %get-tuple-element.58.refs_0_.refs_8_.refs_4_, bf16[128,512]{1,0:T(8,128)(2,1)} %copy-done.30, bf16[128,512]{1,0:T(8,128)(2,1)} %copy-done.32, bf16[128,512]{1,0:T(8,128)(2,1)} %copy-done.34, bf16[128,512]{1,0:T(8,128)(2,1)} %copy-done.1, ...), custom_call_target="tpu_custom_call" | custom-call | bytes 2097152 | tf_op jit(solution)/shard_map/pallas_call | solution.py:104
  154.7 1.6 collective-permute-start.22
  156.3 33.2 %shard_map.86 = (bf16[128,256]{1,0:T(8,128)(2,1)}, bf16[128,256]{1,0:T(8,128)(2,1)}, bf16[128,256]{1,0:T(8,128)(2,1)}, bf16[128,256]{1,0:T(8,128)(2,1)}, bf16[12...) custom-call(s32[1]{0:T(128)} %bitcast.me, ...), custom_call_target="tpu_custom_call" | custom-call | bytes 2097152 | tf_op jit(solution)/shard_map/pallas_call | solution.py:45
  189.5 1.1 collective-permute-start.38
  190.6 1.9 collective-permute-start.39
  192.5 1.0 collective-permute-start.40
  193.5 4.0 %collective-permute-start.41 = (bf16[128,256]{1,0:T(8,128)(2,1)}, bf16[128,256]{1,0:T(8,128)(2,1)S(1)}, u32[]{:S(2)}, u32[]{:S(2)}) collective-permute-start(bf16[128,256]{1,0:T(8,128)(2,1)} %get-tuple-element.93), channel_id=1, source_target_pairs={{0,30},{2,28},{4,26},{6,24},{8,22},{10,20},{12,18},{14,16},{16,14}... | collective-permute-start | bytes 196616 | tf_op jit(solution)/shard_map/ppermute | solution.py:201
  197.5 0.7 copy-done.54
  198.3 3.9 %collective-permute-start.30 = (bf16[128,256]{1,0:T(8,128)(2,1)}, bf16[128,256]{1,0:T(8,128)(2,1)S(1)}, u32[]{:S(2)}, u32[]{:S(2)}) collective-permute-start(bf16[128,256]{1,0:T(8,128)(2,1)} %get-tuple-element.82), channel_id=1, source_target_pairs={{0,16},{2,18},{4,20},{6,22},{8,24},{10,26},{12,28},{14,30},{16,0},... | collective-permute-start | bytes 196616 | tf_op jit(solution)/shard_map/ppermute | solution.py:201
  202.8 1.1 collective-permute-start.31
  203.8 3.5 %collective-permute-start.32 = (bf16[128,256]{1,0:T(8,128)(2,1)}, bf16[128,256]{1,0:T(8,128)(2,1)S(1)}, u32[]{:S(2)}, u32[]{:S(2)}) collective-permute-start(bf16[128,256]{1,0:T(8,128)(2,1)} %get-tuple-element.84), channel_id=1, source_target_pairs={{0,20},{2,22},{4,16},{6,18},{8,28},{10,30},{12,24},{14,26},{16,4},... | collective-permute-start | bytes 196616 | tf_op jit(solution)/shard_map/ppermute | solution.py:201
  207.3 3.0 collective-permute-start.33
  210.4 2.4 collective-permute-done.30.refs_0_
  212.8 0.8 collective-permute-start.1
  213.7 0.9 copy-done.16
  214.6 0.9 copy-done.19
  215.5 0.9 copy-done.22
  216.4 0.9 copy-done.25
  217.3 0.9 copy-done.28
  218.2 0.9 copy-done.31
  219.1 0.9 copy-done.33
  220.0 0.9 copy-done.35
  220.9 5.8 %shard_map.91 = (bf16[128,256]{1,0:T(8,128)(2,1)S(1)}, bf16[128,256]{1,0:T(8,128)(2,1)S(1)}, bf16[128,256]{1,0:T(8,128)(2,1)S(1)}, bf16[128,256]{1,0:T(8,128)(2,1)S(1)}) custom-call(s32[8,4]{1,0:T(8,128)S(1)} %gather_fusion, bf16[128,256]{1,0:T(8,128)(2,1)S(1)} %collective-permute-done.38.refs_0_, bf16[128,256]{1,0:T(8,128)(2,1)S(1)} %collective-permute-done.39.refs_1_, ...), custom_call_target="tpu_custom_call" | custom-call | flops 805306368 | bytes 3670016 | tf_op jit(solution)/shard_map/pallas_call | solution.py:172
  226.7 1.1 collective-permute-start.2
  227.9 1.7 collective-permute-start.4
  229.6 0.6 collective-permute-start.5
  230.2 2.2 collective-permute-start.6
  232.4 5.6 %shard_map.90 = (bf16[128,256]{1,0:T(8,128)(2,1)S(1)}, bf16[128,256]{1,0:T(8,128)(2,1)S(1)}, bf16[128,256]{1,0:T(8,128)(2,1)S(1)}, bf16[128,256]{1,0:T(8,128)(2,1)S(1)}) custom-call(s32[8,4]{1,0:T(8,128)S(1)} %gather_fusion, bf16[128,256]{1,0:T(8,128)(2,1)S(1)} %collective-permute-done.30.refs_0_, bf16[128,256]{1,0:T(8,128)(2,1)S(1)} %collective-permute-done.31.refs_1_, ...), custom_call_target="tpu_custom_call" | custom-call | flops 805306368 | bytes 3670016 | tf_op jit(solution)/shard_map/pallas_call | solution.py:172
  238.0 0.9 collective-permute-start.42
  238.9 2.7 collective-permute-start.43
  241.6 0.6 collective-permute-start.44
  242.2 3.9 %collective-permute-start.45 = (bf16[128,256]{1,0:T(8,128)(2,1)S(1)}, bf16[128,256]{1,0:T(8,128)(2,1)S(1)}, u32[]{:S(2)}, u32[]{:S(2)}) collective-permute-start(bf16[128,256]{1,0:T(8,128)(2,1)S(1)} %get-tuple-element.97), channel_id=1, source_target_pairs={{0,30},{2,28},{4,26},{6,24},{8,22},{10,20},{12,18},{14,16},{16,14}... | collective-permute-start | bytes 196616 | tf_op jit(solution)/shard_map/ppermute | solution.py:201
  246.1 7.2 %shard_map.89 = (bf16[128,256]{1,0:T(8,128)(2,1)S(1)}, bf16[128,256]{1,0:T(8,128)(2,1)S(1)}, bf16[128,256]{1,0:T(8,128)(2,1)S(1)}, bf16[128,256]{1,0:T(8,128)(2,...) custom-call(s32[8,4]{1,0:T(8,128)S(1)} %gather_fusion, ...), custom_call_target="tpu_custom_call" | custom-call | flops 1610612736 | bytes 4194304 | tf_op jit(solution)/shard_map/pallas_call | solution.py:172
  253.3 0.6 copy-done.37
  254.0 2.6 collective-permute-start.35
  256.5 0.6 collective-permute-start.36
  257.1 3.0 collective-permute-start.37
  260.5 0.7 collective-permute-start.24
  261.6 2.5 collective-permute-start.25
  264.1 1.5 collective-permute-done.36.refs_10_
  266.1 2.6 collective-permute-start.28
  268.7 1.3 collective-permute-start.29
  270.5 3.4 %collective-permute-done.28.refs_6_ = bf16[128,256]{1,0:T(8,128)(2,1)S(1)} collective-permute-done((bf16[128,256]{1,0:T(8,128)(2,1)S(1)}, bf16[128,256]{1,0:T(8,128)(2,1)S(1)}, u32[]{:S(2)}, u32[]{:S(2)}) %collective-permute-start.28) | collective-permute-done | bytes 65568 | tf_op jit(solution)/shard_map/ppermute | solution.py:201
  274.7 33.1 %shard_map.92 = (bf16[128,2048]{1,0:T(8,128)(2,1)}, bf16[128,2048]{1,0:T(8,128)(2,1)}) custom-call(s32[1]{0:T(128)} %bitcast.me, bf16[128,256]{1,0:T(8,128)(2,1)} %copy-done.37, bf16[128,256]{1,0:T(8,128)(2,1)} %copy-done.47, bf16[128,256]{1,0:T(8,128)(2,1)} %copy-done.48, bf16[128,256]{1,0:T(8,128)(2,1)} %copy-done.49, bf16[128,256]{1,0:T(8,128)(2,1)} %copy-done.50, ...), custom_call_target="tpu_custom_call" | custom-call | bytes 2097152 | tf_op jit(solution)/shard_map/pallas_call | solution.py:73
  (162 shorter events, 3.9 us)
Async XLA Ops:
  65.9 8.5 %collective-permute-start.10 = (bf16[128,512]{1,0:T(8,128)(2,1)}, bf16[128,512]{1,0:T(8,128)(2,1)S(1)}, u32[]{:S(2)}, u32[]{:S(2)}) collective-permute-start(bf16[128,512]{1,0:T(8,128)(2,1)} %get-tuple-element.62), channel_id=1, source_target_pairs={{0,8},{2,10},{4,12},{6,14},{8,0},{10,2},{12,4},{14,6},{16,24},{18,... | collective-permute-start | bytes 393224 | tf_op jit(solution)/shard_map/ppermute | solution.py:201
  69.0 7.0 %collective-permute-start.11 = (bf16[128,512]{1,0:T(8,128)(2,1)}, bf16[128,512]{1,0:T(8,128)(2,1)S(1)}, u32[]{:S(2)}, u32[]{:S(2)}) collective-permute-start(bf16[128,512]{1,0:T(8,128)(2,1)} %get-tuple-element.63), channel_id=1, source_target_pairs={{0,10},{2,8},{4,14},{6,12},{8,2},{10,0},{12,6},{14,4},{16,26},{18,... | collective-permute-start | bytes 393224 | tf_op jit(solution)/shard_map/ppermute | solution.py:201
  69.0 16.7 %collective-permute-start.12 = (bf16[128,512]{1,0:T(8,128)(2,1)}, bf16[128,512]{1,0:T(8,128)(2,1)S(1)}, u32[]{:S(2)}, u32[]{:S(2)}) collective-permute-start(bf16[128,512]{1,0:T(8,128)(2,1)} %get-tuple-element.64), channel_id=1, source_target_pairs={{0,12},{2,14},{4,8},{6,10},{8,4},{10,6},{12,0},{14,2},{16,28},{18,... | collective-permute-start | bytes 393224 | tf_op jit(solution)/shard_map/ppermute | solution.py:201
  71.1 16.2 %collective-permute-start.13 = (bf16[128,512]{1,0:T(8,128)(2,1)}, bf16[128,512]{1,0:T(8,128)(2,1)S(1)}, u32[]{:S(2)}, u32[]{:S(2)}) collective-permute-start(bf16[128,512]{1,0:T(8,128)(2,1)} %get-tuple-element.65), channel_id=1, source_target_pairs={{0,14},{2,12},{4,10},{6,8},{8,6},{10,4},{12,2},{14,0},{16,30},{18,... | collective-permute-start | bytes 393224 | tf_op jit(solution)/shard_map/ppermute | solution.py:201
  71.7 18.7 %collective-permute-start.14 = (bf16[128,512]{1,0:T(8,128)(2,1)}, bf16[128,512]{1,0:T(8,128)(2,1)S(1)}, u32[]{:S(2)}, u32[]{:S(2)}) collective-permute-start(bf16[128,512]{1,0:T(8,128)(2,1)} %get-tuple-element.66), channel_id=1, source_target_pairs={{0,16},{2,18},{4,20},{6,22},{8,24},{10,26},{12,28},{14,30},{16,0},... | collective-permute-start | bytes 393224 | tf_op jit(solution)/shard_map/ppermute | solution.py:201
  74.4 46.7 %copy-start.1 = (bf16[128,512]{1,0:T(8,128)(2,1)}, bf16[128,512]{1,0:T(8,128)(2,1)S(1)}, u32[]{:S(2)}) copy-start(bf16[128,512]{1,0:T(8,128)(2,1)S(1)} %collective-permute-done.10.refs_4_.refs_12_.refs_8_) | copy-start | bytes 393220
  74.4 17.0 %collective-permute-start.15 = (bf16[128,512]{1,0:T(8,128)(2,1)}, bf16[128,512]{1,0:T(8,128)(2,1)S(1)}, u32[]{:S(2)}, u32[]{:S(2)}) collective-permute-start(bf16[128,512]{1,0:T(8,128)(2,1)} %get-tuple-element.67), channel_id=1, source_target_pairs={{0,18},{2,16},{4,22},{6,20},{8,26},{10,24},{12,30},{14,28},{16,2},... | collective-permute-start | bytes 393224 | tf_op jit(solution)/shard_map/ppermute | solution.py:201
  76.0 45.1 %copy-start.3 = (bf16[128,512]{1,0:T(8,128)(2,1)}, bf16[128,512]{1,0:T(8,128)(2,1)S(1)}, u32[]{:S(2)}) copy-start(bf16[128,512]{1,0:T(8,128)(2,1)S(1)} %collective-permute-done.11.refs_5_.refs_13_.refs_9_) | copy-start | bytes 393220
  76.0 30.7 %collective-permute-start.16 = (bf16[128,512]{1,0:T(8,128)(2,1)}, bf16[128,512]{1,0:T(8,128)(2,1)S(1)}, u32[]{:S(2)}, u32[]{:S(2)}) collective-permute-start(bf16[128,512]{1,0:T(8,128)(2,1)} %get-tuple-element.68), channel_id=1, source_target_pairs={{0,20},{2,22},{4,16},{6,18},{8,28},{10,30},{12,24},{14,26},{16,4},... | collective-permute-start | bytes 393224 | tf_op jit(solution)/shard_map/ppermute | solution.py:201
  85.7 35.5 %copy-start.5 = (bf16[128,512]{1,0:T(8,128)(2,1)}, bf16[128,512]{1,0:T(8,128)(2,1)S(1)}, u32[]{:S(2)}) copy-start(bf16[128,512]{1,0:T(8,128)(2,1)S(1)} %collective-permute-done.12.refs_6_.refs_14_.refs_10_) | copy-start | bytes 393220
  85.7 23.8 %collective-permute-start.17 = (bf16[128,512]{1,0:T(8,128)(2,1)}, bf16[128,512]{1,0:T(8,128)(2,1)S(1)}, u32[]{:S(2)}, u32[]{:S(2)}) collective-permute-start(bf16[128,512]{1,0:T(8,128)(2,1)} %get-tuple-element.69), channel_id=1, source_target_pairs={{0,22},{2,20},{4,18},{6,16},{8,30},{10,28},{12,26},{14,24},{16,6},... | collective-permute-start | bytes 393224 | tf_op jit(solution)/shard_map/ppermute | solution.py:201
  87.2 33.9 %copy-start.7 = (bf16[128,512]{1,0:T(8,128)(2,1)}, bf16[128,512]{1,0:T(8,128)(2,1)S(1)}, u32[]{:S(2)}) copy-start(bf16[128,512]{1,0:T(8,128)(2,1)S(1)} %collective-permute-done.13.refs_7_.refs_15_.refs_11_) | copy-start | bytes 393220
  87.2 22.3 %collective-permute-start.18 = (bf16[128,512]{1,0:T(8,128)(2,1)}, bf16[128,512]{1,0:T(8,128)(2,1)S(1)}, u32[]{:S(2)}, u32[]{:S(2)}) collective-permute-start(bf16[128,512]{1,0:T(8,128)(2,1)} %get-tuple-element.70), channel_id=1, source_target_pairs={{0,24},{2,26},{4,28},{6,30},{8,16},{10,18},{12,20},{14,22},{16,8},... | collective-permute-start | bytes 393224 | tf_op jit(solution)/shard_map/ppermute | solution.py:201
  90.4 30.7 %copy-start.9 = (bf16[128,512]{1,0:T(8,128)(2,1)}, bf16[128,512]{1,0:T(8,128)(2,1)S(1)}, u32[]{:S(2)}) copy-start(bf16[128,512]{1,0:T(8,128)(2,1)S(1)} %collective-permute-done.14.refs_8_.refs_16_.refs_12_) | copy-start | bytes 393220
  90.4 19.8 %collective-permute-start.19 = (bf16[128,512]{1,0:T(8,128)(2,1)}, bf16[128,512]{1,0:T(8,128)(2,1)S(1)}, u32[]{:S(2)}, u32[]{:S(2)}) collective-permute-start(bf16[128,512]{1,0:T(8,128)(2,1)} %get-tuple-element.71), channel_id=1, source_target_pairs={{0,26},{2,24},{4,30},{6,28},{8,18},{10,16},{12,22},{14,20},{16,10}... | collective-permute-start | bytes 393224 | tf_op jit(solution)/shard_map/ppermute | solution.py:201
  91.4 29.8 %copy-start.11 = (bf16[128,512]{1,0:T(8,128)(2,1)}, bf16[128,512]{1,0:T(8,128)(2,1)S(1)}, u32[]{:S(2)}) copy-start(bf16[128,512]{1,0:T(8,128)(2,1)S(1)} %collective-permute-done.15.refs_9_.refs_17_.refs_13_) | copy-start | bytes 393220
  91.4 19.9 %collective-permute-start.20 = (bf16[128,512]{1,0:T(8,128)(2,1)}, bf16[128,512]{1,0:T(8,128)(2,1)S(1)}, u32[]{:S(2)}, u32[]{:S(2)}) collective-permute-start(bf16[128,512]{1,0:T(8,128)(2,1)} %get-tuple-element.72), channel_id=1, source_target_pairs={{0,28},{2,30},{4,24},{6,26},{8,20},{10,22},{12,16},{14,18},{16,12}... | collective-permute-start | bytes 393224 | tf_op jit(solution)/shard_map/ppermute | solution.py:201
  106.7 8.7 %collective-permute-start.21 = (bf16[128,512]{1,0:T(8,128)(2,1)}, bf16[128,512]{1,0:T(8,128)(2,1)S(1)}, u32[]{:S(2)}, u32[]{:S(2)}) collective-permute-start(bf16[128,512]{1,0:T(8,128)(2,1)} %get-tuple-element.73), channel_id=1, source_target_pairs={{0,30},{2,28},{4,26},{6,24},{8,22},{10,20},{12,18},{14,16},{16,14}... | collective-permute-start | bytes 393224 | tf_op jit(solution)/shard_map/ppermute | solution.py:201
  109.4 6.0 %collective-permute-start.7 = (bf16[128,512]{1,0:T(8,128)(2,1)}, bf16[128,512]{1,0:T(8,128)(2,1)S(1)}, u32[]{:S(2)}, u32[]{:S(2)}) collective-permute-start(bf16[128,512]{1,0:T(8,128)(2,1)} %get-tuple-element.59), channel_id=1, source_target_pairs={{0,2},{2,0},{4,6},{6,4},{8,10},{10,8},{12,14},{14,12},{16,18},{18,... | collective-permute-start | bytes 393224 | tf_op jit(solution)/shard_map/ppermute | solution.py:201
  109.5 8.9 %collective-permute-start.8 = (bf16[128,512]{1,0:T(8,128)(2,1)}, bf16[128,512]{1,0:T(8,128)(2,1)S(1)}, u32[]{:S(2)}, u32[]{:S(2)}) collective-permute-start(bf16[128,512]{1,0:T(8,128)(2,1)} %get-tuple-element.60), channel_id=1, source_target_pairs={{0,4},{2,6},{4,0},{6,2},{8,12},{10,14},{12,8},{14,10},{16,20},{18,... | collective-permute-start | bytes 393224 | tf_op jit(solution)/shard_map/ppermute | solution.py:201
  110.2 10.9 %collective-permute-start.9 = (bf16[128,512]{1,0:T(8,128)(2,1)}, bf16[128,512]{1,0:T(8,128)(2,1)S(1)}, u32[]{:S(2)}, u32[]{:S(2)}) collective-permute-start(bf16[128,512]{1,0:T(8,128)(2,1)} %get-tuple-element.61), channel_id=1, source_target_pairs={{0,6},{2,4},{4,2},{6,0},{8,14},{10,12},{12,10},{14,8},{16,22},{18,... | collective-permute-start | bytes 393224 | tf_op jit(solution)/shard_map/ppermute | solution.py:201
  154.7 58.1 %collective-permute-start.22 = (bf16[1024,512]{1,0:T(8,128)(2,1)}, bf16[1024,512]{1,0:T(8,128)(2,1)S(1)}, u32[]{:S(2)}, u32[]{:S(2)}) collective-permute-start(bf16[1024,512]{1,0:T(8,128)(2,1)} %shard_map.88), channel_id=1, source_target_pairs={{0,1},{1,0},{2,3},{3,2},{4,5},{5,4},{6,7},{7,6},{8,9},{9,8},{10,11... | collective-permute-start | bytes 3145736 | tf_op jit(solution)/shard_map/ppermute | solution.py:229
  156.2 57.4 %copy-start = (bf16[128,512]{1,0:T(8,128)(2,1)S(1)}, bf16[128,512]{1,0:T(8,128)(2,1)}, u32[]{:S(2)}) copy-start(bf16[128,512]{1,0:T(8,128)(2,1)} %get-tuple-element.58.refs_0_.refs_8_.refs_4_) | copy-start | bytes 393220
  156.2 57.4 %copy-start.2 = (bf16[128,512]{1,0:T(8,128)(2,1)S(1)}, bf16[128,512]{1,0:T(8,128)(2,1)}, u32[]{:S(2)}) copy-start(bf16[128,512]{1,0:T(8,128)(2,1)} %copy-done.1) | copy-start | bytes 393220
  156.2 57.4 %copy-start.4 = (bf16[128,512]{1,0:T(8,128)(2,1)S(1)}, bf16[128,512]{1,0:T(8,128)(2,1)}, u32[]{:S(2)}) copy-start(bf16[128,512]{1,0:T(8,128)(2,1)} %copy-done.3) | copy-start | bytes 393220
  156.3 57.4 %copy-start.6 = (bf16[128,512]{1,0:T(8,128)(2,1)S(1)}, bf16[128,512]{1,0:T(8,128)(2,1)}, u32[]{:S(2)}) copy-start(bf16[128,512]{1,0:T(8,128)(2,1)} %copy-done.5) | copy-start | bytes 393220
  156.3 57.4 %copy-start.8 = (bf16[128,512]{1,0:T(8,128)(2,1)S(1)}, bf16[128,512]{1,0:T(8,128)(2,1)}, u32[]{:S(2)}) copy-start(bf16[128,512]{1,0:T(8,128)(2,1)} %copy-done.7) | copy-start | bytes 393220
  156.3 57.4 %copy-start.10 = (bf16[128,512]{1,0:T(8,128)(2,1)S(1)}, bf16[128,512]{1,0:T(8,128)(2,1)}, u32[]{:S(2)}) copy-start(bf16[128,512]{1,0:T(8,128)(2,1)} %copy-done.9) | copy-start | bytes 393220
  156.3 57.4 %copy-start.12 = (bf16[128,512]{1,0:T(8,128)(2,1)S(1)}, bf16[128,512]{1,0:T(8,128)(2,1)}, u32[]{:S(2)}) copy-start(bf16[128,512]{1,0:T(8,128)(2,1)} %copy-done.11) | copy-start | bytes 393220
  156.3 57.4 %copy-start.14 = (bf16[128,512]{1,0:T(8,128)(2,1)S(1)}, bf16[128,512]{1,0:T(8,128)(2,1)}, u32[]{:S(2)}) copy-start(bf16[128,512]{1,0:T(8,128)(2,1)} %copy-done.13) | copy-start | bytes 393220
  189.5 8.8 %collective-permute-start.38 = (bf16[128,256]{1,0:T(8,128)(2,1)}, bf16[128,256]{1,0:T(8,128)(2,1)S(1)}, u32[]{:S(2)}, u32[]{:S(2)}) collective-permute-start(bf16[128,256]{1,0:T(8,128)(2,1)} %get-tuple-element.90), channel_id=1, source_target_pairs={{0,24},{2,26},{4,28},{6,30},{8,16},{10,18},{12,20},{14,22},{16,8},... | collective-permute-start | bytes 196616 | tf_op jit(solution)/shard_map/ppermute | solution.py:201
  190.6 12.2 %collective-permute-start.39 = (bf16[128,256]{1,0:T(8,128)(2,1)}, bf16[128,256]{1,0:T(8,128)(2,1)S(1)}, u32[]{:S(2)}, u32[]{:S(2)}) collective-permute-start(bf16[128,256]{1,0:T(8,128)(2,1)} %get-tuple-element.91), channel_id=1, source_target_pairs={{0,26},{2,24},{4,30},{6,28},{8,18},{10,16},{12,22},{14,20},{16,10}... | collective-permute-start | bytes 196616 | tf_op jit(solution)/shard_map/ppermute | solution.py:201
  192.5 11.3 %collective-permute-start.40 = (bf16[128,256]{1,0:T(8,128)(2,1)}, bf16[128,256]{1,0:T(8,128)(2,1)S(1)}, u32[]{:S(2)}, u32[]{:S(2)}) collective-permute-start(bf16[128,256]{1,0:T(8,128)(2,1)} %get-tuple-element.92), channel_id=1, source_target_pairs={{0,28},{2,30},{4,24},{6,26},{8,20},{10,22},{12,16},{14,18},{16,12}... | collective-permute-start | bytes 196616 | tf_op jit(solution)/shard_map/ppermute | solution.py:201
  193.5 13.8 %collective-permute-start.41 = (bf16[128,256]{1,0:T(8,128)(2,1)}, bf16[128,256]{1,0:T(8,128)(2,1)S(1)}, u32[]{:S(2)}, u32[]{:S(2)}) collective-permute-start(bf16[128,256]{1,0:T(8,128)(2,1)} %get-tuple-element.93), channel_id=1, source_target_pairs={{0,30},{2,28},{4,26},{6,24},{8,22},{10,20},{12,18},{14,16},{16,14}... | collective-permute-start | bytes 196616 | tf_op jit(solution)/shard_map/ppermute | solution.py:201
  198.3 14.5 %collective-permute-start.30 = (bf16[128,256]{1,0:T(8,128)(2,1)}, bf16[128,256]{1,0:T(8,128)(2,1)S(1)}, u32[]{:S(2)}, u32[]{:S(2)}) collective-permute-start(bf16[128,256]{1,0:T(8,128)(2,1)} %get-tuple-element.82), channel_id=1, source_target_pairs={{0,16},{2,18},{4,20},{6,22},{8,24},{10,26},{12,28},{14,30},{16,0},... | collective-permute-start | bytes 196616 | tf_op jit(solution)/shard_map/ppermute | solution.py:201
  202.8 23.9 %collective-permute-start.31 = (bf16[128,256]{1,0:T(8,128)(2,1)}, bf16[128,256]{1,0:T(8,128)(2,1)S(1)}, u32[]{:S(2)}, u32[]{:S(2)}) collective-permute-start(bf16[128,256]{1,0:T(8,128)(2,1)} %get-tuple-element.83), channel_id=1, source_target_pairs={{0,18},{2,16},{4,22},{6,20},{8,26},{10,24},{12,30},{14,28},{16,2},... | collective-permute-start | bytes 196616 | tf_op jit(solution)/shard_map/ppermute | solution.py:201
  203.8 24.0 %collective-permute-start.32 = (bf16[128,256]{1,0:T(8,128)(2,1)}, bf16[128,256]{1,0:T(8,128)(2,1)S(1)}, u32[]{:S(2)}, u32[]{:S(2)}) collective-permute-start(bf16[128,256]{1,0:T(8,128)(2,1)} %get-tuple-element.84), channel_id=1, source_target_pairs={{0,20},{2,22},{4,16},{6,18},{8,28},{10,30},{12,24},{14,26},{16,4},... | collective-permute-start | bytes 196616 | tf_op jit(solution)/shard_map/ppermute | solution.py:201
  207.3 20.6 %collective-permute-start.33 = (bf16[128,256]{1,0:T(8,128)(2,1)}, bf16[128,256]{1,0:T(8,128)(2,1)S(1)}, u32[]{:S(2)}, u32[]{:S(2)}) collective-permute-start(bf16[128,256]{1,0:T(8,128)(2,1)} %get-tuple-element.85), channel_id=1, source_target_pairs={{0,22},{2,20},{4,18},{6,16},{8,30},{10,28},{12,26},{14,24},{16,6},... | collective-permute-start | bytes 196616 | tf_op jit(solution)/shard_map/ppermute | solution.py:201
  212.8 16.8 %collective-permute-start = (bf16[128,256]{1,0:T(8,128)(2,1)}, bf16[128,256]{1,0:T(8,128)(2,1)S(1)}, u32[]{:S(2)}, u32[]{:S(2)}) collective-permute-start(bf16[128,256]{1,0:T(8,128)(2,1)} %get-tuple-element.51), channel_id=1, source_target_pairs={{0,2},{2,0},{4,6},{6,4},{8,10},{10,8},{12,14},{14,12},{16,18},{18,... | collective-permute-start | bytes 196616 | tf_op jit(solution)/shard_map/ppermute | solution.py:201
  212.8 17.4 %collective-permute-start.1 = (bf16[128,256]{1,0:T(8,128)(2,1)S(1)}, bf16[128,256]{1,0:T(8,128)(2,1)S(1)}, u32[]{:S(2)}, u32[]{:S(2)}) collective-permute-start(bf16[128,256]{1,0:T(8,128)(2,1)S(1)} %copy-done.60), channel_id=1, source_target_pairs={{0,4},{2,6},{4,0},{6,2},{8,12},{10,14},{12,8},{14,10},{16,20},{18,... | collective-permute-start | bytes 196616 | tf_op jit(solution)/shard_map/ppermute | solution.py:201
  226.7 11.2 %collective-permute-start.2 = (bf16[128,256]{1,0:T(8,128)(2,1)S(1)}, bf16[128,256]{1,0:T(8,128)(2,1)S(1)}, u32[]{:S(2)}, u32[]{:S(2)}) collective-permute-start(bf16[128,256]{1,0:T(8,128)(2,1)S(1)} %copy-done.59), channel_id=1, source_target_pairs={{0,6},{2,4},{4,2},{6,0},{8,14},{10,12},{12,10},{14,8},{16,22},{18,... | collective-permute-start | bytes 196616 | tf_op jit(solution)/shard_map/ppermute | solution.py:201
  227.9 11.0 %collective-permute-start.3 = (bf16[128,256]{1,0:T(8,128)(2,1)S(1)}, bf16[128,256]{1,0:T(8,128)(2,1)S(1)}, u32[]{:S(2)}, u32[]{:S(2)}) collective-permute-start(bf16[128,256]{1,0:T(8,128)(2,1)S(1)} %copy-done.58), channel_id=1, source_target_pairs={{0,8},{2,10},{4,12},{6,14},{8,0},{10,2},{12,4},{14,6},{16,24},{18,... | collective-permute-start | bytes 196616 | tf_op jit(solution)/shard_map/ppermute | solution.py:201
  227.9 13.7 %collective-permute-start.4 = (bf16[128,256]{1,0:T(8,128)(2,1)S(1)}, bf16[128,256]{1,0:T(8,128)(2,1)S(1)}, u32[]{:S(2)}, u32[]{:S(2)}) collective-permute-start(bf16[128,256]{1,0:T(8,128)(2,1)S(1)} %copy-done.57), channel_id=1, source_target_pairs={{0,10},{2,8},{4,14},{6,12},{8,2},{10,0},{12,6},{14,4},{16,26},{18,... | collective-permute-start | bytes 196616 | tf_op jit(solution)/shard_map/ppermute | solution.py:201
  229.6 12.6 %collective-permute-start.5 = (bf16[128,256]{1,0:T(8,128)(2,1)S(1)}, bf16[128,256]{1,0:T(8,128)(2,1)S(1)}, u32[]{:S(2)}, u32[]{:S(2)}) collective-permute-start(bf16[128,256]{1,0:T(8,128)(2,1)S(1)} %copy-done.56), channel_id=1, source_target_pairs={{0,12},{2,14},{4,8},{6,10},{8,4},{10,6},{12,0},{14,2},{16,28},{18,... | collective-permute-start | bytes 196616 | tf_op jit(solution)/shard_map/ppermute | solution.py:201
  230.2 15.9 %copy-start.23 = (bf16[128,512]{1,0:T(8,128)(2,1)S(1)}, bf16[128,512]{1,0:T(8,128)(2,1)}, u32[]{:S(2)}) copy-start(bf16[128,512]{1,0:T(8,128)(2,1)} %copy-done.21) | copy-start | bytes 393220
  230.2 15.8 %collective-permute-start.6 = (bf16[128,256]{1,0:T(8,128)(2,1)S(1)}, bf16[128,256]{1,0:T(8,128)(2,1)S(1)}, u32[]{:S(2)}, u32[]{:S(2)}) collective-permute-start(bf16[128,256]{1,0:T(8,128)(2,1)S(1)} %copy-done.55), channel_id=1, source_target_pairs={{0,14},{2,12},{4,10},{6,8},{8,6},{10,4},{12,2},{14,0},{16,30},{18,... | collective-permute-start | bytes 196616 | tf_op jit(solution)/shard_map/ppermute | solution.py:201
  238.0 16.0 %collective-permute-start.42 = (bf16[128,256]{1,0:T(8,128)(2,1)S(1)}, bf16[128,256]{1,0:T(8,128)(2,1)S(1)}, u32[]{:S(2)}, u32[]{:S(2)}) collective-permute-start(bf16[128,256]{1,0:T(8,128)(2,1)S(1)} %get-tuple-element.94), channel_id=1, source_target_pairs={{0,24},{2,26},{4,28},{6,30},{8,16},{10,18},{12,20},{14,22},{16,8},... | collective-permute-start | bytes 196616 | tf_op jit(solution)/shard_map/ppermute | solution.py:201
  238.9 17.6 %collective-permute-start.43 = (bf16[128,256]{1,0:T(8,128)(2,1)S(1)}, bf16[128,256]{1,0:T(8,128)(2,1)S(1)}, u32[]{:S(2)}, u32[]{:S(2)}) collective-permute-start(bf16[128,256]{1,0:T(8,128)(2,1)S(1)} %get-tuple-element.95), channel_id=1, source_target_pairs={{0,26},{2,24},{4,30},{6,28},{8,18},{10,16},{12,22},{14,20},{16,10}... | collective-permute-start | bytes 196616 | tf_op jit(solution)/shard_map/ppermute | solution.py:201
  241.6 15.6 %collective-permute-start.44 = (bf16[128,256]{1,0:T(8,128)(2,1)S(1)}, bf16[128,256]{1,0:T(8,128)(2,1)S(1)}, u32[]{:S(2)}, u32[]{:S(2)}) collective-permute-start(bf16[128,256]{1,0:T(8,128)(2,1)S(1)} %get-tuple-element.96), channel_id=1, source_target_pairs={{0,28},{2,30},{4,24},{6,26},{8,20},{10,22},{12,16},{14,18},{16,12}... | collective-permute-start | bytes 196616 | tf_op jit(solution)/shard_map/ppermute | solution.py:201
  242.2 17.9 %collective-permute-start.45 = (bf16[128,256]{1,0:T(8,128)(2,1)S(1)}, bf16[128,256]{1,0:T(8,128)(2,1)S(1)}, u32[]{:S(2)}, u32[]{:S(2)}) collective-permute-start(bf16[128,256]{1,0:T(8,128)(2,1)S(1)} %get-tuple-element.97), channel_id=1, source_target_pairs={{0,30},{2,28},{4,26},{6,24},{8,22},{10,20},{12,18},{14,16},{16,14}... | collective-permute-start | bytes 196616 | tf_op jit(solution)/shard_map/ppermute | solution.py:201
  246.1 14.4 %collective-permute-start.34 = (bf16[128,256]{1,0:T(8,128)(2,1)S(1)}, bf16[128,256]{1,0:T(8,128)(2,1)S(1)}, u32[]{:S(2)}, u32[]{:S(2)}) collective-permute-start(bf16[128,256]{1,0:T(8,128)(2,1)S(1)} %get-tuple-element.86), channel_id=1, source_target_pairs={{0,16},{2,18},{4,20},{6,22},{8,24},{10,26},{12,28},{14,30},{16,0},... | collective-permute-start | bytes 196616 | tf_op jit(solution)/shard_map/ppermute | solution.py:201
  254.0 20.2 %copy-start.39 = (bf16[128,256]{1,0:T(8,128)(2,1)}, bf16[128,256]{1,0:T(8,128)(2,1)S(1)}, u32[]{:S(2)}) copy-start(bf16[128,256]{1,0:T(8,128)(2,1)S(1)} %collective-permute-done.42.refs_12_) | copy-start | bytes 196612
  254.0 7.6 %collective-permute-start.35 = (bf16[128,256]{1,0:T(8,128)(2,1)S(1)}, bf16[128,256]{1,0:T(8,128)(2,1)S(1)}, u32[]{:S(2)}, u32[]{:S(2)}) collective-permute-start(bf16[128,256]{1,0:T(8,128)(2,1)S(1)} %get-tuple-element.87), channel_id=1, source_target_pairs={{0,18},{2,16},{4,22},{6,20},{8,26},{10,24},{12,30},{14,28},{16,2},... | collective-permute-start | bytes 196616 | tf_op jit(solution)/shard_map/ppermute | solution.py:201
  256.5 17.6 %copy-start.40 = (bf16[128,256]{1,0:T(8,128)(2,1)}, bf16[128,256]{1,0:T(8,128)(2,1)S(1)}, u32[]{:S(2)}) copy-start(bf16[128,256]{1,0:T(8,128)(2,1)S(1)} %collective-permute-done.43.refs_13_) | copy-start | bytes 196612
  256.5 9.1 %collective-permute-start.36 = (bf16[128,256]{1,0:T(8,128)(2,1)S(1)}, bf16[128,256]{1,0:T(8,128)(2,1)S(1)}, u32[]{:S(2)}, u32[]{:S(2)}) collective-permute-start(bf16[128,256]{1,0:T(8,128)(2,1)S(1)} %get-tuple-element.88), channel_id=1, source_target_pairs={{0,20},{2,22},{4,16},{6,18},{8,28},{10,30},{12,24},{14,26},{16,4},... | collective-permute-start | bytes 196616 | tf_op jit(solution)/shard_map/ppermute | solution.py:201
  257.1 17.0 %copy-start.41 = (bf16[128,256]{1,0:T(8,128)(2,1)}, bf16[128,256]{1,0:T(8,128)(2,1)S(1)}, u32[]{:S(2)}) copy-start(bf16[128,256]{1,0:T(8,128)(2,1)S(1)} %collective-permute-done.44.refs_14_) | copy-start | bytes 196612
  257.1 8.9 %collective-permute-start.37 = (bf16[128,256]{1,0:T(8,128)(2,1)S(1)}, bf16[128,256]{1,0:T(8,128)(2,1)S(1)}, u32[]{:S(2)}, u32[]{:S(2)}) collective-permute-start(bf16[128,256]{1,0:T(8,128)(2,1)S(1)} %get-tuple-element.89), channel_id=1, source_target_pairs={{0,22},{2,20},{4,18},{6,16},{8,30},{10,28},{12,26},{14,24},{16,6},... | collective-permute-start | bytes 196616 | tf_op jit(solution)/shard_map/ppermute | solution.py:201
  260.1 5.9 %collective-permute-start.23 = (bf16[128,256]{1,0:T(8,128)(2,1)S(1)}, bf16[128,256]{1,0:T(8,128)(2,1)S(1)}, u32[]{:S(2)}, u32[]{:S(2)}) collective-permute-start(bf16[128,256]{1,0:T(8,128)(2,1)S(1)} %get-tuple-element.75), channel_id=1, source_target_pairs={{0,2},{2,0},{4,6},{6,4},{8,10},{10,8},{12,14},{14,12},{16,18},{18,... | collective-permute-start | bytes 196616 | tf_op jit(solution)/shard_map/ppermute | solution.py:201
  260.5 8.2 %collective-permute-start.24 = (bf16[128,256]{1,0:T(8,128)(2,1)S(1)}, bf16[128,256]{1,0:T(8,128)(2,1)S(1)}, u32[]{:S(2)}, u32[]{:S(2)}) collective-permute-start(bf16[128,256]{1,0:T(8,128)(2,1)S(1)} %get-tuple-element.76), channel_id=1, source_target_pairs={{0,4},{2,6},{4,0},{6,2},{8,12},{10,14},{12,8},{14,10},{16,20},{18,... | collective-permute-start | bytes 196616 | tf_op jit(solution)/shard_map/ppermute | solution.py:201
  261.6 8.4 %collective-permute-start.25 = (bf16[128,256]{1,0:T(8,128)(2,1)S(1)}, bf16[128,256]{1,0:T(8,128)(2,1)S(1)}, u32[]{:S(2)}, u32[]{:S(2)}) collective-permute-start(bf16[128,256]{1,0:T(8,128)(2,1)S(1)} %get-tuple-element.77), channel_id=1, source_target_pairs={{0,6},{2,4},{4,2},{6,0},{8,14},{10,12},{12,10},{14,8},{16,22},{18,... | collective-permute-start | bytes 196616 | tf_op jit(solution)/shard_map/ppermute | solution.py:201
  265.6 4.9 %collective-permute-start.26 = (bf16[128,256]{1,0:T(8,128)(2,1)S(1)}, bf16[128,256]{1,0:T(8,128)(2,1)S(1)}, u32[]{:S(2)}, u32[]{:S(2)}) collective-permute-start(bf16[128,256]{1,0:T(8,128)(2,1)S(1)} %get-tuple-element.78), channel_id=1, source_target_pairs={{0,8},{2,10},{4,12},{6,14},{8,0},{10,2},{12,4},{14,6},{16,24},{18,... | collective-permute-start | bytes 196616 | tf_op jit(solution)/shard_map/ppermute | solution.py:201
  266.1 4.4 %collective-permute-start.27 = (bf16[128,256]{1,0:T(8,128)(2,1)S(1)}, bf16[128,256]{1,0:T(8,128)(2,1)S(1)}, u32[]{:S(2)}, u32[]{:S(2)}) collective-permute-start(bf16[128,256]{1,0:T(8,128)(2,1)S(1)} %get-tuple-element.79), channel_id=1, source_target_pairs={{0,10},{2,8},{4,14},{6,12},{8,2},{10,0},{12,6},{14,4},{16,26},{18,... | collective-permute-start | bytes 196616 | tf_op jit(solution)/shard_map/ppermute | solution.py:201
  266.1 7.8 %collective-permute-start.28 = (bf16[128,256]{1,0:T(8,128)(2,1)S(1)}, bf16[128,256]{1,0:T(8,128)(2,1)S(1)}, u32[]{:S(2)}, u32[]{:S(2)}) collective-permute-start(bf16[128,256]{1,0:T(8,128)(2,1)S(1)} %get-tuple-element.80), channel_id=1, source_target_pairs={{0,12},{2,14},{4,8},{6,10},{8,4},{10,6},{12,0},{14,2},{16,28},{18,... | collective-permute-start | bytes 196616 | tf_op jit(solution)/shard_map/ppermute | solution.py:201
  268.7 5.4 %collective-permute-start.29 = (bf16[128,256]{1,0:T(8,128)(2,1)S(1)}, bf16[128,256]{1,0:T(8,128)(2,1)S(1)}, u32[]{:S(2)}, u32[]{:S(2)}) collective-permute-start(bf16[128,256]{1,0:T(8,128)(2,1)S(1)} %get-tuple-element.81), channel_id=1, source_target_pairs={{0,14},{2,12},{4,10},{6,8},{8,6},{10,4},{12,2},{14,0},{16,30},{18,... | collective-permute-start | bytes 196616 | tf_op jit(solution)/shard_map/ppermute | solution.py:201
  (43 other events, 309.2 us)

commit v3 on v0

v3 whole, which is shorter than its diff:
```python
import functools
import math

import jax
import jax.numpy as jnp
from jax import lax
from jax.experimental import pallas as pl
from jax.experimental.pallas import tpu as pltpu
from jax.sharding import PartitionSpec as P

BQ = 256
WK = 4
HB = 4
PAIR = 2
PARAMS = pltpu.CompilerParams(vmem_limit_bytes=32 * 1024 * 1024)
ANY = pl.BlockSpec(memory_space=pl.ANY)
VMEM = pl.BlockSpec(memory_space=pltpu.VMEM)
SMEM = pl.BlockSpec(memory_space=pltpu.SMEM)


def moves(size):
    return pl.CostEstimate(flops=0, bytes_accessed=2 * size, transcendentals=0)


def pack_kernel(chip, *refs, counts, slots, hd):
    total = sum(counts)
    arrays, pieces = refs[:total], refs[total : total + slots * len(counts)]
    held, sems = refs[-2], refs[-1]
    copies = [pltpu.make_async_copy(a, held.at[i], sems.at[i]) for i, a in enumerate(arrays)]
    for copy in copies:
        copy.start()
    base = 0
    for g, count in enumerate(counts):
        for a in range(count):
            copies[base + a].wait()
            for k in range(slots):
                for h in range(PAIR):
                    column = pl.multiple_of(((chip[0] ^ k) * PAIR + h) * hd, hd)
                    target = (h * count + a) * hd
                    pieces[g * slots + k][:, target : target + hd] = held[
                        base + a, :, pl.ds(column, hd)
                    ]
        base += count


def pack(chip, groups, devices):
    arrays = [a for group in groups for a in group]
    tokens, columns = arrays[0].shape
    hd, slots = columns // devices, devices // PAIR
    counts = tuple(len(group) for group in groups)
    shapes = [
        jax.ShapeDtypeStruct((tokens, PAIR * count * hd), jnp.bfloat16)
        for count in counts
        for _ in range(slots)
    ]
    done = pl.pallas_call(
        functools.partial(pack_kernel, counts=counts, slots=slots, hd=hd),
        in_specs=[SMEM] + [ANY] * len(arrays),
        out_specs=[VMEM] * len(shapes),
        out_shape=shapes,
        scratch_shapes=[
            pltpu.VMEM((len(arrays), tokens, columns), jnp.bfloat16),
            pltpu.SemaphoreType.DMA((len(arrays),)),
        ],
        compiler_params=PARAMS,
        cost_estimate=moves(2 * tokens * columns * len(arrays)),
    )(chip, *arrays)
    return [done[g * slots : (g + 1) * slots] for g in range(len(groups))]


def unpack_kernel(chip, *refs, count, hd):
    pieces, arrays = refs[:-count], refs[-count:]
    for k, piece in enumerate(pieces):
        for h in range(PAIR):
            column = pl.multiple_of(((chip[0] ^ k) * PAIR + h) * hd, hd)
            for a, array in enumerate(arrays):
                source = (h * count + a) * hd
                array[:, pl.ds(column, hd)] = piece[:, source : source + hd]


def unpack(chip, pieces, count):
    tokens, width = pieces[0].shape
    hd = width // (PAIR * count)
    array = jax.ShapeDtypeStruct((tokens, len(pieces) * PAIR * hd), jnp.bfloat16)
    return pl.pallas_call(
        functools.partial(unpack_kernel, count=count, hd=hd),
        in_specs=[SMEM] + [VMEM] * len(pieces),
        out_specs=[VMEM] * count,
        out_shape=[array] * count,
        compiler_params=PARAMS,
        cost_estimate=moves(2 * tokens * width * len(pieces)),
    )(chip, *pieces)


def join_kernel(groups, *refs, slots):
    pieces, own, edges = refs[:slots], refs[slots], refs[slots + 1 :]
    for k, piece in enumerate(pieces):
        own[k] = piece[...]
    for e, out in enumerate(edges):
        for i in range(HB):
            out[i] = own[groups[e] * HB + i]


def join(groups, pieces):
    tokens, width = pieces[0].shape
    count = groups.shape[0]
    return pl.pallas_call(
        functools.partial(join_kernel, slots=len(pieces)),
        in_specs=[SMEM] + [VMEM] * len(pieces),
        out_specs=[VMEM] * (1 + count),
        out_shape=[jax.ShapeDtypeStruct((len(pieces), tokens, width), jnp.bfloat16)]
        + [jax.ShapeDtypeStruct((HB, tokens, width), jnp.bfloat16)] * count,
        compiler_params=PARAMS,
        cost_estimate=moves(2 * (len(pieces) + count * HB) * tokens * width),
    )(groups, *pieces)


def attend_slot(table, slot, q_ref, kv, out_ref, hd):
    tokens = q_ref.shape[0]
    scale = hd ** (-0.5)
    factor = scale * math.log2(math.e)
    trans = (((1,), (1,)), ((), ()))
    blocks = [table[slot, w] for w in range(WK)]
    for h in range(PAIR):
        both = q_ref[:, 2 * h * hd : 2 * (h + 1) * hd]
        query = both[:, :hd]
        left = jnp.concatenate([jnp.zeros_like(query), query], axis=1)
        left = jnp.concatenate([left, both], axis=0)
        low = 4 * h * hd
        scores, tans = [], []
        for block in blocks:
            keys = kv[block, :, :, low : low + 2 * hd].reshape(BQ, 2 * hd)
            product = lax.dot_general(left, keys, trans, preferred_element_type=jnp.float32)
            scores.append(product[:tokens])
            tans.append(product[tokens:])
        top = functools.reduce(jnp.maximum, scores)
        top = jnp.max(top, axis=1, keepdims=True) * factor
        probs = [jnp.exp2(s * factor - top) for s in scores]
        weighted = [p * t for p, t in zip(probs, tans)]
        total = jnp.sum(functools.reduce(jnp.add, probs), axis=1, keepdims=True)
        mean = jnp.sum(functools.reduce(jnp.add, weighted), axis=1, keepdims=True)
        mixed = jnp.zeros((2 * tokens, 2 * hd), jnp.float32)
        for block, p, w in zip(blocks, probs, weighted):
            vals = kv[block, :, :, low + 2 * hd : low + 4 * hd].reshape(BQ, 2 * hd)
            right = jnp.concatenate([p.astype(jnp.bfloat16), w.astype(jnp.bfloat16)], axis=0)
            mixed += jnp.dot(right, vals, preferred_element_type=jnp.float32)
        inverse = 1.0 / total
        out = mixed[:tokens, :hd] * inverse
        tan = (mixed[:tokens, hd:] + scale * mixed[tokens:, :hd]) * inverse
        tan = tan - (scale * mean * inverse) * out
        out_ref[:, 2 * h * hd : (2 * h + 1) * hd] = out.astype(jnp.bfloat16)
        out_ref[:, (2 * h + 1) * hd : 2 * (h + 1) * hd] = tan.astype(jnp.bfloat16)


def first_kernel(table, *refs, count, sources, hd, first):
    q_refs, refs = refs[:count], refs[count:]
    mine, other, refs = refs[:sources], refs[sources : 2 * sources], refs[2 * sources :]
    outs, kv = refs[:count], refs[count]
    row = 0
    for a, b in zip(mine, other):
        for i in range(a.shape[0]):
            kv[row + i, 0] = a[i]
            kv[row + i, 1] = b[i]
        row += a.shape[0]
    for i in range(count):
        attend_slot(table, first + i, q_refs[i], kv, outs[i], hd)


def next_kernel(table, *refs, count, hd, first):
    q_refs, kv, outs = refs[:count], refs[count], refs[count + 1 :]
    for i in range(count):
        attend_slot(table, first + i, q_refs[i], kv, outs[i], hd)


def hold_kernel(*refs):
    del refs


def hold(array, others):
    return pl.pallas_call(
        hold_kernel,
        in_specs=[ANY] * (1 + len(others)),
        out_specs=ANY,
        out_shape=jax.ShapeDtypeStruct(array.shape, array.dtype),
        input_output_aliases={0: 0},
        cost_estimate=moves(0),
    )(array, *others)


def cost(slots, tokens, hd, size):
    elements = slots * PAIR * tokens * WK * BQ
    return pl.CostEstimate(
        flops=16 * elements * hd, bytes_accessed=size, transcendentals=elements
    )


def attend_first(table, first, queries, mine, other):
    tokens, width = queries[0].shape
    hd = width // (2 * PAIR)
    total = sum(a.shape[0] for a in mine)
    count = len(queries)
    kv = jax.ShapeDtypeStruct((total, PAIR, tokens, 2 * width), jnp.bfloat16)
    done = pl.pallas_call(
        functools.partial(first_kernel, count=count, sources=len(mine), hd=hd, first=first),
        in_specs=[SMEM] + [VMEM] * (count + 2 * len(mine)),
        out_specs=[VMEM] * (count + 1),
        out_shape=[jax.ShapeDtypeStruct((tokens, width), jnp.bfloat16)] * count + [kv],
        compiler_params=PARAMS,
        cost_estimate=cost(count, tokens, hd, 2 * kv.size * 2),
    )(table, *queries, *mine, *other)
    return done[:count], done[count]


def attend_next(table, first, queries, kv):
    tokens, width = queries[0].shape
    hd = width // (2 * PAIR)
    count = len(queries)
    return pl.pallas_call(
        functools.partial(next_kernel, count=count, hd=hd, first=first),
        in_specs=[SMEM] + [VMEM] * (count + 1),
        out_specs=[VMEM] * count,
        out_shape=[jax.ShapeDtypeStruct((tokens, width), jnp.bfloat16)] * count,
        compiler_params=PARAMS,
        cost_estimate=cost(count, tokens, hd, 2 * kv.size),
    )(table, *queries, kv)


def send(pieces, order, devices):
    got = {}
    for k in order:
        pairs = [(i, i ^ (k * PAIR)) for i in range(devices)]
        got[k] = lax.ppermute(pieces[k], "heads", pairs) if k else pieces[k]
    return got


def per_device(query, keys, values, query_tan, keys_tan, values_tan, neighbors):
    devices, frames = lax.axis_size("heads"), lax.axis_size("frames")
    frame = lax.axis_index("frames")
    chip = lax.axis_index("heads") // PAIR
    blocks = neighbors.shape[0]
    half = blocks // 2
    far, near = list(range(half, blocks)), list(range(1, half))
    order = [k for pair in zip(far, near + [0]) for k in pair]

    groups = [[keys_tan, keys, values, values_tan], [query, query_tan]]
    chip_ref = chip.reshape(1).astype(jnp.int32)
    kv_sent, q_sent = pack(chip_ref, groups, devices)
    got = send(kv_sent, order, devices)
    q_got = send(q_sent, order, devices)

    rounds = []
    for first in (0, 1):
        pairs = [(i, i + 1) for i in range(first, frames - 1, 2)]
        if pairs:
            rounds.append((first, pairs + [(j, i) for i, j in pairs]))
    outer = [
        jnp.where(frame % 2 == first, blocks // HB - 1, 0) ^ (chip // HB) for first, _ in rounds
    ]
    joined = join(jnp.stack(outer).astype(jnp.int32), [got[k] for k in range(blocks)])
    mine = [joined[0]]
    for (_, pairs), edge in zip(rounds, joined[1:]):
        halo = lax.ppermute(edge, "frames", pairs)
        mine.append(hold(halo, [q_got[k] for k in range(1, blocks)]))
    swap = [(i, i ^ 1) for i in range(devices)]
    other = [lax.ppermute(a, "heads", swap) for a in mine]

    local = neighbors - frame * blocks
    even = frame % 2 == 0
    before = blocks + jnp.where(even, HB, 0) + ((local + blocks) ^ chip) % HB
    after = blocks + jnp.where(even, 0, HB) + ((local - blocks) ^ chip) % HB
    table = jnp.where(local < 0, before, jnp.where(local >= blocks, after, local ^ chip))
    table = table[jnp.arange(blocks) ^ chip]

    quarter = half // 2
    queries = [q_got[k] for k in range(blocks)]
    outs = {}
    done, kv = attend_first(table, half, queries[half : half + quarter], mine, other)
    outs.update(enumerate(done, half))
    done = attend_next(table, half + quarter, queries[half + quarter :], kv)
    outs.update(enumerate(done, half + quarter))
    done = attend_next(table, 0, queries[:half], kv)
    outs.update(enumerate(done))
    back = send(outs, far + near + [0], devices)
    return unpack(chip_ref, [back[k] for k in range(blocks)], 2)


def solution(mesh):
    own = P(("frames", "heads"), None)
    return jax.shard_map(
        per_device,
        mesh=mesh,
        in_specs=(own,) * 6 + (P("frames", None),),
        out_specs=(own, own),
        check_vma=False,
    )
```

time: 220 us -> 151 us (0.69)
  waiting for transfers between devices: 89.5 us -> 66.3 us
  matrix products: 21.7 us -> 0 us
  blocking collectives: 18.4 us -> 0 us
  other arithmetic: 15.7 us -> 0.03 us
  local copies, waits for them, and re-layouts: 35 us -> 19.8 us
  Pallas kernels: 0 us -> 13.9 us
  starting transfers between devices: 37.9 us -> 49.9 us
    all_to_all x7 -> x0, waiting for transfers between devices: 70 us -> none  [the longest x1 13.6 us: per_device(): lax.all_to_all(values_tan, 'heads', split_axis=1, concat_axis=0, tiled=True)]
    ppermute x2 -> x24, waiting for transfers between devices: 19.5 us -> 66.3 us  [the longest x21 64.1 us: send(): got[k] = lax.ppermute(pieces[k], 'heads', pairs) if k else pieces[k]]
    ppermute x2 -> x24, starting transfers between devices: 5.69 us -> 49.9 us  [the longest x21 48.3 us: send(): got[k] = lax.ppermute(pieces[k], 'heads', pairs) if k else pieces[k]]
    all_to_all x7 -> x0, starting transfers between devices: 32.2 us -> none  [the longest x1 7.36 us: per_device(): lax.all_to_all(keys, 'heads', split_axis=1, concat_axis=0, tiled=True)]
    all_to_all x1 -> x0, blocking collectives: 18.4 us -> none  [per_device(): lax.all_to_all(tan_h, 'heads', split_axis=0, concat_axis=1, tiled=True)]
    gather x2 -> x1, local copies, waits for them, and re-layouts: 15 us -> 0.56 us  [per_device(): table = table[jnp.arange(blocks) ^ chip]]
    dot_general x5 -> x0, matrix products: 14.3 us -> none  [the longest x1 4.55 us: attend(): jnp.einsum('nqd,nkd->nqk', q_rows, kt_win, preferred_element_type=jnp.flo...]
    pallas_call x0 -> x7, Pallas kernels: none -> 13.9 us  [the longest x2 6.62 us: attend_next(): pl.pallas_call(functools.partial(next_kernel, count=count, hd=hd, first=f...]
  transfers between devices with their start and end apart: 9 -> 24, of which waited for: 8 -> 12; matrix products, arithmetic and copies ran while one was open for 20% -> 0% of each run, Pallas kernels for 0% -> 2%
where the time goes in v3:
time: 151 us
  waiting for transfers between devices  66.3 us (44%)
  starting transfers between devices  49.9 us (33%)
  local copies, waits for them, and re-layouts  19.8 us (13%)
  Pallas kernels  13.9 us (9%)
    ppermute x21, waiting for transfers between devices, send(): got[k] = lax.ppermute(pieces[k], 'heads', pairs) if k else pieces[k]  64.1 us
    ppermute x21, starting transfers between devices, send(): got[k] = lax.ppermute(pieces[k], 'heads', pairs) if k else pieces[k]  48.3 us
    unnamed x79, local copies, waits for them, and re-layouts  19.2 us
    pallas_call x2, Pallas kernels, attend_next(): pl.pallas_call(functools.partial(next_kernel, count=count, hd=hd, first=f...  6.62 us
    pallas_call x1, Pallas kernels, attend_first(): pl.pallas_call(functools.partial(first_kernel, count=count, sources=len(m...  4.05 us
  transfers between devices with their start and end apart: 24, of which 12 were waited for; matrix products, arithmetic and copies ran while one was open for 0% of the time, Pallas kernels for 2%

profile of v3, /device:TPU:0, one launch (start us, length us, event | category | flops | bytes accessed | tf_op | source)
XLA Modules:
  0.0 150.8 jit_solution(11913584223483860406)
XLA Ops:
  0.7 1.0 copy-done.10
  1.7 1.0 copy-done.11
  2.7 1.0 copy-done.12
  3.8 1.0 copy-done.13
  4.8 1.0 copy-done.14
  5.9 1.0 copy-done.15
  6.9 1.8 %shard_map.86 = (bf16[128,1024]{1,0:T(8,128)(2,1)S(1)}, bf16[128,1024]{1,0:T(8,128)(2,1)S(1)}, bf16[128,1024]{1,0:T(8,128)(2,1)S(1)}, bf16[128,1024]{1,0:T(8,128...) custom-call(s32[1]{0:T(128)} %bitcast.chip, ...), custom_call_target="tpu_custom_call" | custom-call | bytes 6291456 | tf_op jit(solution)/shard_map/pallas_call | solution.py:56
  8.7 0.6 copy-done.28
  9.4 0.6 copy-done.30
  10.0 0.6 copy-done.32
  10.7 0.7 copy-done.34
  11.3 0.6 copy-done.36
  12.0 2.9 %collective-permute-start.5 = (bf16[128,1024]{1,0:T(8,128)(2,1)S(1)}, bf16[128,1024]{1,0:T(8,128)(2,1)S(1)}, u32[]{:S(2)}, u32[]{:S(2)}) collective-permute-start(bf16[128,1024]{1,0:T(8,128)(2,1)S(1)} %get-tuple-element.36), channel_id=1, source_target_pairs={{0,4},{2,6},{4,0},{6,2},{8,12},{10,14},{12,8},{14,10},{16,20},{18,... | collective-permute-start | bytes 786440 | tf_op jit(solution)/shard_map/ppermute | solution.py:232
  14.9 1.6 %collective-permute-start.6 = (bf16[128,1024]{1,0:T(8,128)(2,1)S(1)}, bf16[128,1024]{1,0:T(8,128)(2,1)S(1)}, u32[]{:S(2)}, u32[]{:S(2)}) collective-permute-start(bf16[128,1024]{1,0:T(8,128)(2,1)S(1)} %get-tuple-element.37), channel_id=1, source_target_pairs={{0,8},{2,10},{4,12},{6,14},{8,0},{10,2},{12,4},{14,6},{16,24},{18,... | collective-permute-start | bytes 786440 | tf_op jit(solution)/shard_map/ppermute | solution.py:232
  16.5 3.0 %collective-permute-start.8 = (bf16[128,1024]{1,0:T(8,128)(2,1)S(1)}, bf16[128,1024]{1,0:T(8,128)(2,1)S(1)}, u32[]{:S(2)}, u32[]{:S(2)}) collective-permute-start(bf16[128,1024]{1,0:T(8,128)(2,1)S(1)} %get-tuple-element.39), channel_id=1, source_target_pairs={{0,16},{2,18},{4,20},{6,22},{8,24},{10,26},{12,28},{14,30},{16,0},... | collective-permute-start | bytes 786440 | tf_op jit(solution)/shard_map/ppermute | solution.py:232
  19.5 1.3 collective-permute-start.9
  20.8 0.5 collective-permute-done.5.refs_1_
  21.2 3.9 %collective-permute-start.10 = (bf16[128,1024]{1,0:T(8,128)(2,1)S(1)}, bf16[128,1024]{1,0:T(8,128)(2,1)S(1)}, u32[]{:S(2)}, u32[]{:S(2)}) collective-permute-start(bf16[128,1024]{1,0:T(8,128)(2,1)S(1)} %get-tuple-element.41), channel_id=1, source_target_pairs={{0,24},{2,26},{4,28},{6,30},{8,16},{10,18},{12,20},{14,22},{16,8},... | collective-permute-start | bytes 786440 | tf_op jit(solution)/shard_map/ppermute | solution.py:232
  25.1 9.3 %collective-permute-done.6.refs_2_ = bf16[128,1024]{1,0:T(8,128)(2,1)S(1)} collective-permute-done((bf16[128,1024]{1,0:T(8,128)(2,1)S(1)}, bf16[128,1024]{1,0:T(8,128)(2,1)S(1)}, u32[]{:S(2)}, u32[]{:S(2)}) %collective-permute-start.6) | collective-permute-done | bytes 262176 | tf_op jit(solution)/shard_map/ppermute | solution.py:232
  34.4 1.1 collective-permute-start.11
  35.5 2.2 %collective-permute-done.7.refs_3_ = bf16[128,1024]{1,0:T(8,128)(2,1)S(1)} collective-permute-done((bf16[128,1024]{1,0:T(8,128)(2,1)S(1)}, bf16[128,1024]{1,0:T(8,128)(2,1)S(1)}, u32[]{:S(2)}, u32[]{:S(2)}) %collective-permute-start.7) | collective-permute-done | bytes 262176 | tf_op jit(solution)/shard_map/ppermute | solution.py:232
  37.7 18.3 %collective-permute-done.9.refs_5_ = bf16[128,1024]{1,0:T(8,128)(2,1)S(1)} collective-permute-done((bf16[128,1024]{1,0:T(8,128)(2,1)S(1)}, bf16[128,1024]{1,0:T(8,128)(2,1)S(1)}, u32[]{:S(2)}, u32[]{:S(2)}) %collective-permute-start.9) | collective-permute-done | bytes 262176 | tf_op jit(solution)/shard_map/ppermute | solution.py:232
  56.1 0.7 copy-done.16
  56.8 0.7 copy-done.18
  57.5 0.7 copy-done.20
  58.2 0.9 copy-done.17
  59.1 0.9 copy-done.19
  60.1 0.9 copy-done.21
  61.0 0.0 copy-start.38
  61.0 0.2 shard_map.87
  61.3 1.6 %collective-permute-start.12 = (bf16[4,128,1024]{2,1,0:T(8,128)(2,1)S(1)}, bf16[4,128,1024]{2,1,0:T(8,128)(2,1)S(1)}, u32[]{:S(2)}, u32[]{:S(2)}) collective-permute-start(bf16[4,128,1024]{2,1,0:T(8,128)(2,1)S(1)} %get-tuple-element.44), channel_id=1, source_target_pairs={{0,1},{1,0},{2,3},{3,2},{4,5},{5,4},{6,7},{7,6},{8,9},{9,8},{10,11... | collective-permute-start | bytes 3145736 | tf_op jit(solution)/shard_map/ppermute | solution.py:262
  62.8 0.0 collective-permute-start.15
  62.8 0.5 collective-permute-start
  63.4 8.6 %collective-permute-start.1 = (bf16[128,512]{1,0:T(8,128)(2,1)}, bf16[128,512]{1,0:T(8,128)(2,1)S(1)}, u32[]{:S(2)}, u32[]{:S(2)}) collective-permute-start(bf16[128,512]{1,0:T(8,128)(2,1)} %get-tuple-element.31), channel_id=1, source_target_pairs={{0,8},{2,10},{4,12},{6,14},{8,0},{10,2},{12,4},{14,6},{16,24},{18,... | collective-permute-start | bytes 393224 | tf_op jit(solution)/shard_map/ppermute | solution.py:232
  72.0 0.7 collective-permute-start.2
  72.7 6.6 %collective-permute-start.3 = (bf16[128,512]{1,0:T(8,128)(2,1)S(1)}, bf16[128,512]{1,0:T(8,128)(2,1)S(1)}, u32[]{:S(2)}, u32[]{:S(2)}) collective-permute-start(bf16[128,512]{1,0:T(8,128)(2,1)S(1)} %copy-done.37), channel_id=1, source_target_pairs={{0,16},{2,18},{4,20},{6,22},{8,24},{10,26},{12,28},{14,30},{16,0},... | collective-permute-start | bytes 393224 | tf_op jit(solution)/shard_map/ppermute | solution.py:232
  79.3 2.3 %collective-permute-start.4 = (bf16[128,512]{1,0:T(8,128)(2,1)S(1)}, bf16[128,512]{1,0:T(8,128)(2,1)S(1)}, u32[]{:S(2)}, u32[]{:S(2)}) collective-permute-start(bf16[128,512]{1,0:T(8,128)(2,1)S(1)} %copy-done.35), channel_id=1, source_target_pairs={{0,20},{2,22},{4,16},{6,18},{8,28},{10,30},{12,24},{14,26},{16,4},... | collective-permute-start | bytes 393224 | tf_op jit(solution)/shard_map/ppermute | solution.py:232
  81.7 4.5 %collective-permute-start.13 = (bf16[128,512]{1,0:T(8,128)(2,1)S(1)}, bf16[128,512]{1,0:T(8,128)(2,1)S(1)}, u32[]{:S(2)}, u32[]{:S(2)}) collective-permute-start(bf16[128,512]{1,0:T(8,128)(2,1)S(1)} %copy-done.33), channel_id=1, source_target_pairs={{0,24},{2,26},{4,28},{6,30},{8,16},{10,18},{12,20},{14,22},{16,8},... | collective-permute-start | bytes 393224 | tf_op jit(solution)/shard_map/ppermute | solution.py:232
  86.2 8.6 %collective-permute-done.3.refs_4_.refs_0_ = bf16[128,512]{1,0:T(8,128)(2,1)S(1)} collective-permute-done((bf16[128,512]{1,0:T(8,128)(2,1)S(1)}, bf16[128,512]{1,0:T(8,128)(2,1)S(1)}, u32[]{:S(2)}, u32[]{:S(2)}) %collective-permute-start.3) | collective-permute-done | bytes 131104 | tf_op jit(solution)/shard_map/ppermute | solution.py:232
  94.8 0.1 collective-permute-start.14
  94.8 0.8 collective-permute-done.4.refs_5_.refs_1_
  95.7 6.8 %collective-permute-done.14.refs_7_.refs_1_ = bf16[128,512]{1,0:T(8,128)(2,1)S(1)} collective-permute-done((bf16[128,512]{1,0:T(8,128)(2,1)S(1)}, bf16[128,512]{1,0:T(8,128)(2,1)S(1)}, u32[]{:S(2)}, u32[]{:S(2)}) %collective-permute-start.14) | collective-permute-done | bytes 131104 | tf_op jit(solution)/shard_map/ppermute | solution.py:232
  102.5 0.6 copy-done.4
  103.1 1.0 copy-done
  104.1 0.1 copy.10
  104.2 0.6 gather_fusion
  104.8 2.2 %collective-permute-done.16.refs_5_ = bf16[4,128,1024]{2,1,0:T(8,128)(2,1)S(1)} collective-permute-done((bf16[4,128,1024]{2,1,0:T(8,128)(2,1)}, bf16[4,128,1024]{2,1,0:T(8,128)(2,1)S(1)}, u32[]{:S(2)}, u32[]{:S(2)}) %collective-permute-start.16) | collective-permute-done | bytes 1048608 | tf_op jit(solution)/shard_map/ppermute | solution.py:265
  107.0 1.2 copy-done.1
  108.2 0.9 copy-done.7
  109.1 0.9 copy-done.9
  110.0 4.0 %shard_map.89 = (bf16[128,512]{1,0:T(8,128)(2,1)S(1)}, bf16[128,512]{1,0:T(8,128)(2,1)S(1)}, bf16[12,2,128,1024]{3,2,1,0:T(8,128)(2,1)S(1)}) custom-call(s32[8,4]{1,0:T(8,128)S(1)} %gather_fusion, bf16[128,512]{1,0:T(8,128)(2,1)S(1)} %copy-done.7, bf16[128,512]{1,0:T(8,128)(2,1)S(1)} %copy-done.9, bf16[8,128,1024]{2,1,0:T(8,128)(2,1)S(1)} %get-tuple-element.43.refs_2_, ...), custom_call_target="tpu_custom_call" | custom-call | flops 1073741824 | bytes 12582912 | tf_op jit(solution)/shard_map/pallas_call | solution.py:203
  114.2 4.0 %shard_map.90 = (bf16[128,512]{1,0:T(8,128)(2,1)S(1)}, bf16[128,512]{1,0:T(8,128)(2,1)S(1)}, bf16[128,512]{1,0:T(8,128)(2,1)S(1)}, bf16[128,512]{1,0:T(8,128)(2,1)S(1)}) custom-call(s32[8,4]{1,0:T(8,128)S(1)} %gather_fusion, bf16[128,512]{1,0:T(8,128)(2,1)S(1)} %copy-done.29, bf16[128,512]{1,0:T(8,128)(2,1)S(1)} %copy-done.23, ...), custom_call_target="tpu_custom_call" | custom-call | flops 2147483648 | bytes 6291456 | tf_op jit(solution)/shard_map/pallas_call | solution.py:218
  118.2 0.1 collective-permute-start.17
  118.2 1.9 %collective-permute-start.18 = (bf16[128,512]{1,0:T(8,128)(2,1)S(1)}, bf16[128,512]{1,0:T(8,128)(2,1)S(1)}, u32[]{:S(2)}, u32[]{:S(2)}) collective-permute-start(bf16[128,512]{1,0:T(8,128)(2,1)S(1)} %get-tuple-element.50), channel_id=1, source_target_pairs={{0,8},{2,10},{4,12},{6,14},{8,0},{10,2},{12,4},{14,6},{16,24},{18,... | collective-permute-start | bytes 393224 | tf_op jit(solution)/shard_map/ppermute | solution.py:232
  120.1 1.6 %collective-permute-start.19 = (bf16[128,512]{1,0:T(8,128)(2,1)S(1)}, bf16[128,512]{1,0:T(8,128)(2,1)S(1)}, u32[]{:S(2)}, u32[]{:S(2)}) collective-permute-start(bf16[128,512]{1,0:T(8,128)(2,1)S(1)} %get-tuple-element.51), channel_id=1, source_target_pairs={{0,12},{2,14},{4,8},{6,10},{8,4},{10,6},{12,0},{14,2},{16,28},{18,... | collective-permute-start | bytes 393224 | tf_op jit(solution)/shard_map/ppermute | solution.py:232
  121.7 2.6 %shard_map.91 = (bf16[128,512]{1,0:T(8,128)(2,1)S(1)}, bf16[128,512]{1,0:T(8,128)(2,1)S(1)}) custom-call(s32[8,4]{1,0:T(8,128)S(1)} %gather_fusion, bf16[128,512]{1,0:T(8,128)(2,1)S(1)} %copy-done.3, bf16[128,512]{1,0:T(8,128)(2,1)S(1)} %copy-done.5, bf16[12,2,128,1024]{3,2,1,0:T(8,128)(2,1)S(1)} %get-tuple-element.47.refs_4_.refs_2_), custom_call_target="tpu_custom_call" | custom-call | flops 1073741824 | bytes 6291456 | tf_op jit(solution)/shard_map/pallas_call | solution.py:218
  124.4 0.1 collective-permute-start.22
  124.4 3.3 %collective-permute-start.23 = (bf16[128,512]{1,0:T(8,128)(2,1)S(1)}, bf16[128,512]{1,0:T(8,128)(2,1)S(1)}, u32[]{:S(2)}, u32[]{:S(2)}) collective-permute-start(bf16[128,512]{1,0:T(8,128)(2,1)S(1)} %get-tuple-element.55), channel_id=1, source_target_pairs={{0,28},{2,30},{4,24},{6,26},{8,20},{10,22},{12,16},{14,18},{16,12}... | collective-permute-start | bytes 393224 | tf_op jit(solution)/shard_map/ppermute | solution.py:232
  127.8 4.3 %collective-permute-start.21 = (bf16[128,512]{1,0:T(8,128)(2,1)S(1)}, bf16[128,512]{1,0:T(8,128)(2,1)S(1)}, u32[]{:S(2)}, u32[]{:S(2)}) collective-permute-start(bf16[128,512]{1,0:T(8,128)(2,1)S(1)} %get-tuple-element.53), channel_id=1, source_target_pairs={{0,20},{2,22},{4,16},{6,18},{8,28},{10,30},{12,24},{14,26},{16,4},... | collective-permute-start | bytes 393224 | tf_op jit(solution)/shard_map/ppermute | solution.py:232
  132.1 0.6 collective-permute-done.22.refs_6_
  132.7 2.3 %collective-permute-done.23.refs_7_ = bf16[128,512]{1,0:T(8,128)(2,1)S(1)} collective-permute-done((bf16[128,512]{1,0:T(8,128)(2,1)S(1)}, bf16[128,512]{1,0:T(8,128)(2,1)S(1)}, u32[]{:S(2)}, u32[]{:S(2)}) %collective-permute-start.23) | collective-permute-done | bytes 131104 | tf_op jit(solution)/shard_map/ppermute | solution.py:232
  135.0 12.1 %collective-permute-done.20.refs_4_ = bf16[128,512]{1,0:T(8,128)(2,1)S(1)} collective-permute-done((bf16[128,512]{1,0:T(8,128)(2,1)S(1)}, bf16[128,512]{1,0:T(8,128)(2,1)S(1)}, u32[]{:S(2)}, u32[]{:S(2)}) %collective-permute-start.20) | collective-permute-done | bytes 131104 | tf_op jit(solution)/shard_map/ppermute | solution.py:232
  147.1 2.4 %collective-permute-done.21.refs_5_ = bf16[128,512]{1,0:T(8,128)(2,1)S(1)} collective-permute-done((bf16[128,512]{1,0:T(8,128)(2,1)S(1)}, bf16[128,512]{1,0:T(8,128)(2,1)S(1)}, u32[]{:S(2)}, u32[]{:S(2)}) %collective-permute-start.21) | collective-permute-done | bytes 131104 | tf_op jit(solution)/shard_map/ppermute | solution.py:232
  149.5 1.3 shard_map.92
  (74 shorter events, 0.2 us)
Async XLA Ops:
  0.6 1.0 copy-start.10
  1.7 1.0 copy-start.11
  2.7 1.0 copy-start.12
  3.8 1.0 copy-start.13
  4.8 1.0 copy-start.14
  5.9 1.0 copy-start.15
  8.7 0.6 copy-start.28
  9.4 0.6 copy-start.30
  10.0 0.6 copy-start.32
  10.6 0.7 copy-start.34
  11.3 0.7 copy-start.36
  12.0 9.2 %collective-permute-start.5 = (bf16[128,1024]{1,0:T(8,128)(2,1)S(1)}, bf16[128,1024]{1,0:T(8,128)(2,1)S(1)}, u32[]{:S(2)}, u32[]{:S(2)}) collective-permute-start(bf16[128,1024]{1,0:T(8,128)(2,1)S(1)} %get-tuple-element.36), channel_id=1, source_target_pairs={{0,4},{2,6},{4,0},{6,2},{8,12},{10,14},{12,8},{14,10},{16,20},{18,... | collective-permute-start | bytes 786440 | tf_op jit(solution)/shard_map/ppermute | solution.py:232
  14.9 19.5 %collective-permute-start.6 = (bf16[128,1024]{1,0:T(8,128)(2,1)S(1)}, bf16[128,1024]{1,0:T(8,128)(2,1)S(1)}, u32[]{:S(2)}, u32[]{:S(2)}) collective-permute-start(bf16[128,1024]{1,0:T(8,128)(2,1)S(1)} %get-tuple-element.37), channel_id=1, source_target_pairs={{0,8},{2,10},{4,12},{6,14},{8,0},{10,2},{12,4},{14,6},{16,24},{18,... | collective-permute-start | bytes 786440 | tf_op jit(solution)/shard_map/ppermute | solution.py:232
  16.5 21.2 %collective-permute-start.7 = (bf16[128,1024]{1,0:T(8,128)(2,1)S(1)}, bf16[128,1024]{1,0:T(8,128)(2,1)S(1)}, u32[]{:S(2)}, u32[]{:S(2)}) collective-permute-start(bf16[128,1024]{1,0:T(8,128)(2,1)S(1)} %get-tuple-element.38), channel_id=1, source_target_pairs={{0,12},{2,14},{4,8},{6,10},{8,4},{10,6},{12,0},{14,2},{16,28},{18,... | collective-permute-start | bytes 786440 | tf_op jit(solution)/shard_map/ppermute | solution.py:232
  16.5 21.2 %collective-permute-start.8 = (bf16[128,1024]{1,0:T(8,128)(2,1)S(1)}, bf16[128,1024]{1,0:T(8,128)(2,1)S(1)}, u32[]{:S(2)}, u32[]{:S(2)}) collective-permute-start(bf16[128,1024]{1,0:T(8,128)(2,1)S(1)} %get-tuple-element.39), channel_id=1, source_target_pairs={{0,16},{2,18},{4,20},{6,22},{8,24},{10,26},{12,28},{14,30},{16,0},... | collective-permute-start | bytes 786440 | tf_op jit(solution)/shard_map/ppermute | solution.py:232
  19.5 36.6 %collective-permute-start.9 = (bf16[128,1024]{1,0:T(8,128)(2,1)S(1)}, bf16[128,1024]{1,0:T(8,128)(2,1)S(1)}, u32[]{:S(2)}, u32[]{:S(2)}) collective-permute-start(bf16[128,1024]{1,0:T(8,128)(2,1)S(1)} %get-tuple-element.40), channel_id=1, source_target_pairs={{0,20},{2,22},{4,16},{6,18},{8,28},{10,30},{12,24},{14,26},{16,4},... | collective-permute-start | bytes 786440 | tf_op jit(solution)/shard_map/ppermute | solution.py:232
  21.2 35.6 %collective-permute-start.10 = (bf16[128,1024]{1,0:T(8,128)(2,1)S(1)}, bf16[128,1024]{1,0:T(8,128)(2,1)S(1)}, u32[]{:S(2)}, u32[]{:S(2)}) collective-permute-start(bf16[128,1024]{1,0:T(8,128)(2,1)S(1)} %get-tuple-element.41), channel_id=1, source_target_pairs={{0,24},{2,26},{4,28},{6,30},{8,16},{10,18},{12,20},{14,22},{16,8},... | collective-permute-start | bytes 786440 | tf_op jit(solution)/shard_map/ppermute | solution.py:232
  34.4 23.1 %collective-permute-start.11 = (bf16[128,1024]{1,0:T(8,128)(2,1)S(1)}, bf16[128,1024]{1,0:T(8,128)(2,1)S(1)}, u32[]{:S(2)}, u32[]{:S(2)}) collective-permute-start(bf16[128,1024]{1,0:T(8,128)(2,1)S(1)} %get-tuple-element.42), channel_id=1, source_target_pairs={{0,28},{2,30},{4,24},{6,26},{8,20},{10,22},{12,16},{14,18},{16,12}... | collective-permute-start | bytes 786440 | tf_op jit(solution)/shard_map/ppermute | solution.py:232
  56.1 0.7 copy-start.16
  56.8 0.7 copy-start.18
  57.5 0.7 copy-start.20
  58.2 0.9 copy-start.17
  59.1 0.9 copy-start.19
  60.1 0.9 copy-start.21
  61.0 11.7 %copy-start.37 = (bf16[128,512]{1,0:T(8,128)(2,1)S(1)}, bf16[128,512]{1,0:T(8,128)(2,1)}, u32[]{:S(2)}) copy-start(bf16[128,512]{1,0:T(8,128)(2,1)} %copy-done.36) | copy-start | bytes 393220
  61.0 18.3 %copy-start.35 = (bf16[128,512]{1,0:T(8,128)(2,1)S(1)}, bf16[128,512]{1,0:T(8,128)(2,1)}, u32[]{:S(2)}) copy-start(bf16[128,512]{1,0:T(8,128)(2,1)} %copy-done.34) | copy-start | bytes 393220
  61.0 20.6 %copy-start.33 = (bf16[128,512]{1,0:T(8,128)(2,1)S(1)}, bf16[128,512]{1,0:T(8,128)(2,1)}, u32[]{:S(2)}) copy-start(bf16[128,512]{1,0:T(8,128)(2,1)} %copy-done.32) | copy-start | bytes 393220
  61.0 33.7 %copy-start.31 = (bf16[128,512]{1,0:T(8,128)(2,1)S(1)}, bf16[128,512]{1,0:T(8,128)(2,1)}, u32[]{:S(2)}) copy-start(bf16[128,512]{1,0:T(8,128)(2,1)} %copy-done.30) | copy-start | bytes 393220
  61.0 43.1 %copy-start.38 = (s32[8,4]{0,1:T(4,128)S(1)}, s32[8,4]{0,1:T(4,128)}, u32[]{:S(2)}) copy-start(s32[8,4]{0,1:T(4,128)} %param.13) | copy-start | bytes 388
  61.3 41.2 %collective-permute-start.12 = (bf16[4,128,1024]{2,1,0:T(8,128)(2,1)S(1)}, bf16[4,128,1024]{2,1,0:T(8,128)(2,1)S(1)}, u32[]{:S(2)}, u32[]{:S(2)}) collective-permute-start(bf16[4,128,1024]{2,1,0:T(8,128)(2,1)S(1)} %get-tuple-element.44), channel_id=1, source_target_pairs={{0,1},{1,0},{2,3},{3,2},{4,5},{5,4},{6,7},{7,6},{8,9},{9,8},{10,11... | collective-permute-start | bytes 3145736 | tf_op jit(solution)/shard_map/ppermute | solution.py:262
  62.8 44.2 %collective-permute-start.15 = (bf16[8,128,1024]{2,1,0:T(8,128)(2,1)S(1)}, bf16[8,128,1024]{2,1,0:T(8,128)(2,1)}, u32[]{:S(2)}, u32[]{:S(2)}) collective-permute-start(bf16[8,128,1024]{2,1,0:T(8,128)(2,1)S(1)} %get-tuple-element.43.refs_2_), channel_id=1, source_target_pairs={{0,2},{2,0},{4,6},{6,4},{8,10},{10,8},{12,14},{14,12},{16,18},{18,... | collective-permute-start | bytes 6291464 | tf_op jit(solution)/shard_map/ppermute | solution.py:265
  62.8 9.9 %collective-permute-start = (bf16[128,512]{1,0:T(8,128)(2,1)S(1)}, bf16[128,512]{1,0:T(8,128)(2,1)S(1)}, u32[]{:S(2)}, u32[]{:S(2)}) collective-permute-start(bf16[128,512]{1,0:T(8,128)(2,1)S(1)} %get-tuple-element.30), channel_id=1, source_target_pairs={{0,4},{2,6},{4,0},{6,2},{8,12},{10,14},{12,8},{14,10},{16,20},{18,... | collective-permute-start | bytes 393224 | tf_op jit(solution)/shard_map/ppermute | solution.py:232
  63.4 15.9 %collective-permute-start.1 = (bf16[128,512]{1,0:T(8,128)(2,1)}, bf16[128,512]{1,0:T(8,128)(2,1)S(1)}, u32[]{:S(2)}, u32[]{:S(2)}) collective-permute-start(bf16[128,512]{1,0:T(8,128)(2,1)} %get-tuple-element.31), channel_id=1, source_target_pairs={{0,8},{2,10},{4,12},{6,14},{8,0},{10,2},{12,4},{14,6},{16,24},{18,... | collective-permute-start | bytes 393224 | tf_op jit(solution)/shard_map/ppermute | solution.py:232
  72.0 9.6 %collective-permute-start.2 = (bf16[128,512]{1,0:T(8,128)(2,1)}, bf16[128,512]{1,0:T(8,128)(2,1)S(1)}, u32[]{:S(2)}, u32[]{:S(2)}) collective-permute-start(bf16[128,512]{1,0:T(8,128)(2,1)} %get-tuple-element.32), channel_id=1, source_target_pairs={{0,12},{2,14},{4,8},{6,10},{8,4},{10,6},{12,0},{14,2},{16,28},{18,... | collective-permute-start | bytes 393224 | tf_op jit(solution)/shard_map/ppermute | solution.py:232
  72.7 6.6 %copy-start.22 = (bf16[128,512]{1,0:T(8,128)(2,1)}, bf16[128,512]{1,0:T(8,128)(2,1)S(1)}, u32[]{:S(2)}) copy-start(bf16[128,512]{1,0:T(8,128)(2,1)S(1)} %collective-permute-done.refs_1_) | copy-start | bytes 393220
  72.7 22.0 %collective-permute-start.3 = (bf16[128,512]{1,0:T(8,128)(2,1)S(1)}, bf16[128,512]{1,0:T(8,128)(2,1)S(1)}, u32[]{:S(2)}, u32[]{:S(2)}) collective-permute-start(bf16[128,512]{1,0:T(8,128)(2,1)S(1)} %copy-done.37), channel_id=1, source_target_pairs={{0,16},{2,18},{4,20},{6,22},{8,24},{10,26},{12,28},{14,30},{16,0},... | collective-permute-start | bytes 393224 | tf_op jit(solution)/shard_map/ppermute | solution.py:232
  79.3 2.4 %copy-start.24 = (bf16[128,512]{1,0:T(8,128)(2,1)}, bf16[128,512]{1,0:T(8,128)(2,1)S(1)}, u32[]{:S(2)}) copy-start(bf16[128,512]{1,0:T(8,128)(2,1)S(1)} %collective-permute-done.1.refs_2_) | copy-start | bytes 393220
  79.3 16.4 %collective-permute-start.4 = (bf16[128,512]{1,0:T(8,128)(2,1)S(1)}, bf16[128,512]{1,0:T(8,128)(2,1)S(1)}, u32[]{:S(2)}, u32[]{:S(2)}) collective-permute-start(bf16[128,512]{1,0:T(8,128)(2,1)S(1)} %copy-done.35), channel_id=1, source_target_pairs={{0,20},{2,22},{4,16},{6,18},{8,28},{10,30},{12,24},{14,26},{16,4},... | collective-permute-start | bytes 393224 | tf_op jit(solution)/shard_map/ppermute | solution.py:232
  81.7 13.1 %copy-start.26 = (bf16[128,512]{1,0:T(8,128)(2,1)}, bf16[128,512]{1,0:T(8,128)(2,1)S(1)}, u32[]{:S(2)}) copy-start(bf16[128,512]{1,0:T(8,128)(2,1)S(1)} %collective-permute-done.2.refs_3_) | copy-start | bytes 393220
  81.7 14.0 %collective-permute-start.13 = (bf16[128,512]{1,0:T(8,128)(2,1)S(1)}, bf16[128,512]{1,0:T(8,128)(2,1)S(1)}, u32[]{:S(2)}, u32[]{:S(2)}) collective-permute-start(bf16[128,512]{1,0:T(8,128)(2,1)S(1)} %copy-done.33), channel_id=1, source_target_pairs={{0,24},{2,26},{4,28},{6,30},{8,16},{10,18},{12,20},{14,22},{16,8},... | collective-permute-start | bytes 393224 | tf_op jit(solution)/shard_map/ppermute | solution.py:232
  94.7 7.7 %copy-start.6 = (bf16[128,512]{1,0:T(8,128)(2,1)}, bf16[128,512]{1,0:T(8,128)(2,1)S(1)}, u32[]{:S(2)}) copy-start(bf16[128,512]{1,0:T(8,128)(2,1)S(1)} %collective-permute-done.3.refs_4_.refs_0_) | copy-start | bytes 393220
  94.8 7.7 %collective-permute-start.14 = (bf16[128,512]{1,0:T(8,128)(2,1)S(1)}, bf16[128,512]{1,0:T(8,128)(2,1)S(1)}, u32[]{:S(2)}, u32[]{:S(2)}) collective-permute-start(bf16[128,512]{1,0:T(8,128)(2,1)S(1)} %copy-done.31), channel_id=1, source_target_pairs={{0,28},{2,30},{4,24},{6,26},{8,20},{10,22},{12,16},{14,18},{16,12}... | collective-permute-start | bytes 393224 | tf_op jit(solution)/shard_map/ppermute | solution.py:232
  95.7 6.8 %copy-start.8 = (bf16[128,512]{1,0:T(8,128)(2,1)}, bf16[128,512]{1,0:T(8,128)(2,1)S(1)}, u32[]{:S(2)}) copy-start(bf16[128,512]{1,0:T(8,128)(2,1)S(1)} %collective-permute-done.4.refs_5_.refs_1_) | copy-start | bytes 393220
  95.7 6.8 %copy-start.2 = (bf16[128,512]{1,0:T(8,128)(2,1)}, bf16[128,512]{1,0:T(8,128)(2,1)S(1)}, u32[]{:S(2)}) copy-start(bf16[128,512]{1,0:T(8,128)(2,1)S(1)} %collective-permute-done.13.refs_6_.refs_0_) | copy-start | bytes 393220
  102.5 0.7 copy-start.4
  103.1 1.0 copy-start
  104.1 2.9 %collective-permute-start.16 = (bf16[4,128,1024]{2,1,0:T(8,128)(2,1)}, bf16[4,128,1024]{2,1,0:T(8,128)(2,1)S(1)}, u32[]{:S(2)}, u32[]{:S(2)}) collective-permute-start(bf16[4,128,1024]{2,1,0:T(8,128)(2,1)} %shard_map.88.refs_3_), channel_id=1, source_target_pairs={{0,2},{2,0},{4,6},{6,4},{8,10},{10,8},{12,14},{14,12},{16,18},{18,... | collective-permute-start | bytes 3145736 | tf_op jit(solution)/shard_map/ppermute | solution.py:265
  107.0 1.2 copy-start.1
  108.2 0.9 copy-start.7
  109.1 0.9 copy-start.9
  110.0 4.1 %copy-start.23 = (bf16[128,512]{1,0:T(8,128)(2,1)S(1)}, bf16[128,512]{1,0:T(8,128)(2,1)}, u32[]{:S(2)}) copy-start(bf16[128,512]{1,0:T(8,128)(2,1)} %copy-done.22) | copy-start | bytes 393220
  110.0 4.1 %copy-start.25 = (bf16[128,512]{1,0:T(8,128)(2,1)S(1)}, bf16[128,512]{1,0:T(8,128)(2,1)}, u32[]{:S(2)}) copy-start(bf16[128,512]{1,0:T(8,128)(2,1)} %copy-done.24) | copy-start | bytes 393220
  110.0 4.1 %copy-start.27 = (bf16[128,512]{1,0:T(8,128)(2,1)S(1)}, bf16[128,512]{1,0:T(8,128)(2,1)}, u32[]{:S(2)}) copy-start(bf16[128,512]{1,0:T(8,128)(2,1)} %copy-done.26) | copy-start | bytes 393220
  110.0 4.1 %copy-start.29 = (bf16[128,512]{1,0:T(8,128)(2,1)S(1)}, bf16[128,512]{1,0:T(8,128)(2,1)}, u32[]{:S(2)}) copy-start(bf16[128,512]{1,0:T(8,128)(2,1)} %copy-done.28) | copy-start | bytes 393220
  114.1 7.6 %copy-start.3 = (bf16[128,512]{1,0:T(8,128)(2,1)S(1)}, bf16[128,512]{1,0:T(8,128)(2,1)}, u32[]{:S(2)}) copy-start(bf16[128,512]{1,0:T(8,128)(2,1)} %copy-done.2) | copy-start | bytes 393220
  114.1 7.6 %copy-start.5 = (bf16[128,512]{1,0:T(8,128)(2,1)S(1)}, bf16[128,512]{1,0:T(8,128)(2,1)}, u32[]{:S(2)}) copy-start(bf16[128,512]{1,0:T(8,128)(2,1)} %copy-done.4) | copy-start | bytes 393220
  118.2 9.6 %collective-permute-start.17 = (bf16[128,512]{1,0:T(8,128)(2,1)S(1)}, bf16[128,512]{1,0:T(8,128)(2,1)S(1)}, u32[]{:S(2)}, u32[]{:S(2)}) collective-permute-start(bf16[128,512]{1,0:T(8,128)(2,1)S(1)} %get-tuple-element.49), channel_id=1, source_target_pairs={{0,4},{2,6},{4,0},{6,2},{8,12},{10,14},{12,8},{14,10},{16,20},{18,... | collective-permute-start | bytes 393224 | tf_op jit(solution)/shard_map/ppermute | solution.py:232
  118.2 9.5 %collective-permute-start.18 = (bf16[128,512]{1,0:T(8,128)(2,1)S(1)}, bf16[128,512]{1,0:T(8,128)(2,1)S(1)}, u32[]{:S(2)}, u32[]{:S(2)}) collective-permute-start(bf16[128,512]{1,0:T(8,128)(2,1)S(1)} %get-tuple-element.50), channel_id=1, source_target_pairs={{0,8},{2,10},{4,12},{6,14},{8,0},{10,2},{12,4},{14,6},{16,24},{18,... | collective-permute-start | bytes 393224 | tf_op jit(solution)/shard_map/ppermute | solution.py:232
  120.1 11.9 %collective-permute-start.19 = (bf16[128,512]{1,0:T(8,128)(2,1)S(1)}, bf16[128,512]{1,0:T(8,128)(2,1)S(1)}, u32[]{:S(2)}, u32[]{:S(2)}) collective-permute-start(bf16[128,512]{1,0:T(8,128)(2,1)S(1)} %get-tuple-element.51), channel_id=1, source_target_pairs={{0,12},{2,14},{4,8},{6,10},{8,4},{10,6},{12,0},{14,2},{16,28},{18,... | collective-permute-start | bytes 393224 | tf_op jit(solution)/shard_map/ppermute | solution.py:232
  124.4 8.4 %collective-permute-start.22 = (bf16[128,512]{1,0:T(8,128)(2,1)S(1)}, bf16[128,512]{1,0:T(8,128)(2,1)S(1)}, u32[]{:S(2)}, u32[]{:S(2)}) collective-permute-start(bf16[128,512]{1,0:T(8,128)(2,1)S(1)} %get-tuple-element.54), channel_id=1, source_target_pairs={{0,24},{2,26},{4,28},{6,30},{8,16},{10,18},{12,20},{14,22},{16,8},... | collective-permute-start | bytes 393224 | tf_op jit(solution)/shard_map/ppermute | solution.py:232
  124.4 10.6 %collective-permute-start.23 = (bf16[128,512]{1,0:T(8,128)(2,1)S(1)}, bf16[128,512]{1,0:T(8,128)(2,1)S(1)}, u32[]{:S(2)}, u32[]{:S(2)}) collective-permute-start(bf16[128,512]{1,0:T(8,128)(2,1)S(1)} %get-tuple-element.55), channel_id=1, source_target_pairs={{0,28},{2,30},{4,24},{6,26},{8,20},{10,22},{12,16},{14,18},{16,12}... | collective-permute-start | bytes 393224 | tf_op jit(solution)/shard_map/ppermute | solution.py:232
  127.8 19.3 %collective-permute-start.20 = (bf16[128,512]{1,0:T(8,128)(2,1)S(1)}, bf16[128,512]{1,0:T(8,128)(2,1)S(1)}, u32[]{:S(2)}, u32[]{:S(2)}) collective-permute-start(bf16[128,512]{1,0:T(8,128)(2,1)S(1)} %get-tuple-element.52), channel_id=1, source_target_pairs={{0,16},{2,18},{4,20},{6,22},{8,24},{10,26},{12,28},{14,30},{16,0},... | collective-permute-start | bytes 393224 | tf_op jit(solution)/shard_map/ppermute | solution.py:232
  127.8 21.8 %collective-permute-start.21 = (bf16[128,512]{1,0:T(8,128)(2,1)S(1)}, bf16[128,512]{1,0:T(8,128)(2,1)S(1)}, u32[]{:S(2)}, u32[]{:S(2)}) collective-permute-start(bf16[128,512]{1,0:T(8,128)(2,1)S(1)} %get-tuple-element.53), channel_id=1, source_target_pairs={{0,20},{2,22},{4,16},{6,18},{8,28},{10,30},{12,24},{14,26},{16,4},... | collective-permute-start | bytes 393224 | tf_op jit(solution)/shard_map/ppermute | solution.py:232

commit v4 on v0

v4 whole, which is shorter than its diff:
```python
import functools
import math

import jax
import jax.numpy as jnp
from jax import lax
from jax.experimental import pallas as pl
from jax.experimental.pallas import tpu as pltpu
from jax.sharding import PartitionSpec as P

BQ = 256
WK = 4
HB = 4
PAIR = 2
PARAMS = pltpu.CompilerParams(vmem_limit_bytes=40 * 1024 * 1024)
ANY = pl.BlockSpec(memory_space=pl.ANY)
HBM = pl.BlockSpec(memory_space=pltpu.HBM)
SMEM = pl.BlockSpec(memory_space=pltpu.SMEM)
FREE = pl.CostEstimate(flops=0, bytes_accessed=0, transcendentals=0)


def half(*shape):
    return pltpu.HBM(shape, jnp.bfloat16)


def pin(*arrays):
    return [pltpu.with_memory_space_constraint(a, pltpu.HBM) for a in arrays]


def hold_kernel(*refs):
    del refs


def hold(array, others, micros=0):
    return pl.pallas_call(
        hold_kernel,
        in_specs=[ANY] * (1 + len(others)),
        out_specs=ANY,
        out_shape=jax.ShapeDtypeStruct(array.shape, array.dtype),
        input_output_aliases={0: 0},
        cost_estimate=pl.CostEstimate(
            flops=0, bytes_accessed=3_000_000 * micros, transcendentals=0
        ),
    )(array, *others)


def pack_kernel(chip, *refs, count, slots, hd):
    arrays, pieces = refs[:count], refs[count : count + slots]
    held, staged, sems, out_sems = refs[-4:]
    copies = [pltpu.make_async_copy(a, held.at[i], sems.at[i]) for i, a in enumerate(arrays)]
    for copy in copies:
        copy.start()
    for copy in copies:
        copy.wait()
    sends = []
    for k in range(slots):
        for h in range(PAIR):
            column = pl.multiple_of(((chip[0] ^ k) * PAIR + h) * hd, hd)
            for a in range(count):
                target = (h * count + a) * hd
                staged[k, :, target : target + hd] = held[a, :, pl.ds(column, hd)]
        sends.append(pltpu.make_async_copy(staged.at[k], pieces[k], out_sems.at[k]))
        sends[-1].start()
    for copy in sends:
        copy.wait()


def pack(chip, arrays, devices):
    tokens, columns = arrays[0].shape
    hd, slots, count = columns // devices, devices // PAIR, len(arrays)
    width = PAIR * count * hd
    return pl.pallas_call(
        functools.partial(pack_kernel, count=count, slots=slots, hd=hd),
        in_specs=[SMEM] + [HBM] * count,
        out_specs=[HBM] * slots,
        out_shape=[half(tokens, width)] * slots,
        scratch_shapes=[
            pltpu.VMEM((count, tokens, columns), jnp.bfloat16),
            pltpu.VMEM((slots, tokens, width), jnp.bfloat16),
            pltpu.SemaphoreType.DMA((count,)),
            pltpu.SemaphoreType.DMA((slots,)),
        ],
        compiler_params=PARAMS,
        cost_estimate=FREE,
    )(chip, *pin(*arrays))


def unpack_kernel(chip, *refs, order, count, hd):
    slots = len(order)
    pieces, arrays = refs[:slots], refs[slots : slots + count]
    held, staged, sems, out_sems = refs[-4:]
    copies = [pltpu.make_async_copy(p, held.at[k], sems.at[k]) for k, p in zip(order, pieces)]
    for copy in copies:
        copy.start()
    for k, copy in zip(order, copies):
        copy.wait()
        for h in range(PAIR):
            column = pl.multiple_of(((chip[0] ^ k) * PAIR + h) * hd, hd)
            for a in range(count):
                source = (h * count + a) * hd
                staged[a, :, pl.ds(column, hd)] = held[k, :, source : source + hd]
    sends = [pltpu.make_async_copy(staged.at[a], r, out_sems.at[a]) for a, r in enumerate(arrays)]
    for copy in sends:
        copy.start()
    for copy in sends:
        copy.wait()


def unpack(chip, pieces, count, order):
    tokens, width = pieces[0].shape
    slots, hd = len(pieces), width // (PAIR * count)
    columns = slots * PAIR * hd
    return pl.pallas_call(
        functools.partial(unpack_kernel, order=order, count=count, hd=hd),
        in_specs=[SMEM] + [ANY] * slots,
        out_specs=[HBM] * count,
        out_shape=[half(tokens, columns)] * count,
        scratch_shapes=[
            pltpu.VMEM((slots, tokens, width), jnp.bfloat16),
            pltpu.VMEM((count, tokens, columns), jnp.bfloat16),
            pltpu.SemaphoreType.DMA((slots,)),
            pltpu.SemaphoreType.DMA((count,)),
        ],
        compiler_params=PARAMS,
        cost_estimate=FREE,
    )(chip, *(pieces[k] for k in order))


def join_kernel(groups, *refs, order, edges):
    slots = len(order)
    pieces, outs = refs[:slots], refs[slots : slots + 1 + edges]
    held, sems, out_sems = refs[-3:]
    copies = [pltpu.make_async_copy(p, held.at[k], sems.at[k]) for k, p in zip(order, pieces)]
    for copy in copies:
        copy.start()
    for copy in copies:
        copy.wait()
    sends = [
        pltpu.make_async_copy(
            held.at[pl.ds(groups[e] * HB, HB)], outs[1 + e], out_sems.at[1 + e]
        )
        for e in range(edges)
    ]
    sends.append(pltpu.make_async_copy(held, outs[0], out_sems.at[0]))
    for copy in sends:
        copy.start()
    for copy in sends:
        copy.wait()


def join(groups, pieces, order):
    tokens, width = pieces[0].shape
    slots, edges = len(pieces), groups.shape[0]
    return pl.pallas_call(
        functools.partial(join_kernel, order=order, edges=edges),
        in_specs=[SMEM] + [ANY] * slots,
        out_specs=[HBM] * (1 + edges),
        out_shape=[half(slots, tokens, width)] + [half(HB, tokens, width)] * edges,
        scratch_shapes=[
            pltpu.VMEM((slots, tokens, width), jnp.bfloat16),
            pltpu.SemaphoreType.DMA((slots,)),
            pltpu.SemaphoreType.DMA((1 + edges,)),
        ],
        compiler_params=PARAMS,
        cost_estimate=FREE,
    )(groups, *(pieces[k] for k in order))


def attend_head(blocks, both, kv, low, hd):
    tokens = both.shape[0]
    scale = hd ** (-0.5)
    factor = scale * math.log2(math.e)
    trans = (((1,), (1,)), ((), ()))
    query = both[:, :hd]
    left = jnp.concatenate([jnp.zeros_like(query), query], axis=1)
    left = jnp.concatenate([left, both], axis=0)
    scores, tans = [], []
    for block in blocks:
        keys = kv[block, :, :, low : low + 2 * hd].reshape(BQ, 2 * hd)
        product = lax.dot_general(left, keys, trans, preferred_element_type=jnp.float32)
        scores.append(product[:tokens])
        tans.append(product[tokens:])
    top = functools.reduce(jnp.maximum, scores)
    top = jnp.max(top, axis=1, keepdims=True) * factor
    probs = [jnp.exp2(s * factor - top) for s in scores]
    weighted = [p * t for p, t in zip(probs, tans)]
    total = jnp.sum(functools.reduce(jnp.add, probs), axis=1, keepdims=True)
    mean = jnp.sum(functools.reduce(jnp.add, weighted), axis=1, keepdims=True)
    mixed = jnp.zeros((2 * tokens, 2 * hd), jnp.float32)
    for block, p, w in zip(blocks, probs, weighted):
        vals = kv[block, :, :, low + 2 * hd : low + 4 * hd].reshape(BQ, 2 * hd)
        right = jnp.concatenate([p.astype(jnp.bfloat16), w.astype(jnp.bfloat16)], axis=0)
        mixed += jnp.dot(right, vals, preferred_element_type=jnp.float32)
    inverse = 1.0 / total
    out = mixed[:tokens, :hd] * inverse
    tan = (mixed[:tokens, hd:] + scale * mixed[tokens:, :hd]) * inverse
    tan = tan - (scale * mean * inverse) * out
    return out.astype(jnp.bfloat16), tan.astype(jnp.bfloat16)


def attend_kernel(table, *refs, count, sources, hd, first):
    q_refs, refs = refs[:count], refs[count:]
    parts, refs = refs[: 2 * sources], refs[2 * sources :]
    outs = refs[-6 - count : -6]
    queries, kv, staged, q_sems, kv_sems, out_sems = refs[-6:]
    copies = []
    for i, ref in enumerate(q_refs):
        copies.append(pltpu.make_async_copy(ref, queries.at[i], q_sems.at[i]))
    for core in range(PAIR):
        row = 0
        for i in range(sources):
            ref = parts[core * sources + i]
            target = kv.at[pl.ds(row, ref.shape[0]), core]
            copies.append(
                pltpu.make_async_copy(ref, target, kv_sems.at[core * sources + i])
            )
            row += ref.shape[0]
    for copy in copies:
        copy.start()
    for copy in copies:
        copy.wait()
    sends = []
    for i in range(count):
        blocks = [table[first + i, w] for w in range(WK)]
        for h in range(PAIR):
            both = queries[i, :, 2 * h * hd : 2 * (h + 1) * hd]
            out, tan = attend_head(blocks, both, kv, 4 * h * hd, hd)
            staged[i, :, 2 * h * hd : (2 * h + 1) * hd] = out
            staged[i, :, (2 * h + 1) * hd : 2 * (h + 1) * hd] = tan
        sends.append(pltpu.make_async_copy(staged.at[i], outs[i], out_sems.at[i]))
        sends[-1].start()
    for copy in sends:
        copy.wait()


def attend(table, first, queries, mine, other, later):
    tokens, width = queries[0].shape
    hd, count, sources = width // (2 * PAIR), len(queries), len(mine)
    total = sum(a.shape[0] for a in mine)
    return pl.pallas_call(
        functools.partial(attend_kernel, count=count, sources=sources, hd=hd, first=first),
        in_specs=[SMEM] + [ANY] * (count + 2 * sources + len(later)),
        out_specs=[HBM] * count,
        out_shape=[half(tokens, width)] * count,
        scratch_shapes=[
            pltpu.VMEM((count, tokens, width), jnp.bfloat16),
            pltpu.VMEM((total, PAIR, tokens, 2 * width), jnp.bfloat16),
            pltpu.VMEM((count, tokens, width), jnp.bfloat16),
            pltpu.SemaphoreType.DMA((count,)),
            pltpu.SemaphoreType.DMA((2 * sources,)),
            pltpu.SemaphoreType.DMA((count,)),
        ],
        compiler_params=PARAMS,
        cost_estimate=FREE,
    )(table, *queries, *mine, *other, *later)


def send(pieces, devices):
    got = {}
    for k in range(devices // PAIR):
        pairs = [(i, i ^ (k * PAIR)) for i in range(devices)]
        got[k] = lax.ppermute(pieces[k], "heads", pairs) if k else pieces[k]
    return got


def per_device(query, keys, values, query_tan, keys_tan, values_tan, neighbors):
    devices, frames = lax.axis_size("heads"), lax.axis_size("frames")
    frame = lax.axis_index("frames")
    chip = lax.axis_index("heads") // PAIR
    blocks = neighbors.shape[0]
    middle = blocks // 2
    order = list(range(middle, blocks)) + list(range(middle))

    chip_ref = chip.reshape(1).astype(jnp.int32)
    got = send(pack(chip_ref, [keys_tan, keys, values, values_tan], devices), devices)
    q_got = send(pack(chip_ref, [query, query_tan], devices), devices)

    rounds = []
    for first in (0, 1):
        pairs = [(i, i + 1) for i in range(first, frames - 1, 2)]
        if pairs:
            rounds.append((first, pairs + [(j, i) for i, j in pairs]))
    outer = [
        jnp.where(frame % 2 == first, blocks // HB - 1, 0) ^ (chip // HB) for first, _ in rounds
    ]
    joined = join(jnp.stack(outer).astype(jnp.int32), got, order)
    mine = [joined[0]]
    for (_, pairs), edge in zip(rounds, joined[1:]):
        halo = lax.ppermute(edge, "frames", pairs)
        mine.append(hold(halo, [q_got[k] for k in order]))
    swap = [(i, i ^ 1) for i in range(devices)]
    other = [lax.ppermute(a, "heads", swap) for a in mine]

    local = neighbors - frame * blocks
    even = frame % 2 == 0
    before = blocks + jnp.where(even, HB, 0) + ((local + blocks) ^ chip) % HB
    after = blocks + jnp.where(even, 0, HB) + ((local - blocks) ^ chip) % HB
    table = jnp.where(local < 0, before, jnp.where(local >= blocks, after, local ^ chip))
    table = table[jnp.arange(blocks) ^ chip]

    far, near = range(middle, blocks), range(middle)
    outs, done = {}, []
    for part in (far, near):
        done = attend(table, part[0], [q_got[k] for k in part], mine, other, done)
        outs.update(zip(part, done))
    back = send(outs, devices)
    for k in near:
        back[k] = hold(back[k], [back[j] for j in far], 5)
    return unpack(chip_ref, back, 2, order)


def solution(mesh):
    own = P(("frames", "heads"), None)
    return jax.shard_map(
        per_device,
        mesh=mesh,
        in_specs=(own,) * 6 + (P("frames", None),),
        out_specs=(own, own),
        check_vma=False,
    )
```

time: 220 us -> 157 us (0.71)
  Pallas kernels: 0 us -> 24.4 us
  matrix products: 21.7 us -> 0 us
  local copies, waits for them, and re-layouts: 35 us -> 16.4 us
  blocking collectives: 18.4 us -> 0 us
  waiting for transfers between devices: 89.5 us -> 72.2 us
  other arithmetic: 15.7 us -> 0.03 us
  starting transfers between devices: 37.9 us -> 41.4 us
    all_to_all x7 -> x0, waiting for transfers between devices: 70 us -> none  [the longest x1 13.6 us: per_device(): lax.all_to_all(values_tan, 'heads', split_axis=1, concat_axis=0, tiled=True)]
    ppermute x2 -> x24, waiting for transfers between devices: 19.5 us -> 72.2 us  [the longest x21 70 us: send(): got[k] = lax.ppermute(pieces[k], 'heads', pairs) if k else pieces[k]]
    ppermute x2 -> x24, starting transfers between devices: 5.69 us -> 41.4 us  [the longest x21 39.8 us: send(): got[k] = lax.ppermute(pieces[k], 'heads', pairs) if k else pieces[k]]
    all_to_all x7 -> x0, starting transfers between devices: 32.2 us -> none  [the longest x1 7.36 us: per_device(): lax.all_to_all(keys, 'heads', split_axis=1, concat_axis=0, tiled=True)]
    pallas_call x0 -> x11, Pallas kernels: none -> 24.4 us  [the longest x2 14.4 us: attend(): pl.pallas_call(functools.partial(attend_kernel, count=count, sources=sour...]
    all_to_all x1 -> x0, blocking collectives: 18.4 us -> none  [per_device(): lax.all_to_all(tan_h, 'heads', split_axis=0, concat_axis=1, tiled=True)]
    gather x2 -> x1, local copies, waits for them, and re-layouts: 15 us -> 0.56 us  [per_device(): table = table[jnp.arange(blocks) ^ chip]]
    dot_general x5 -> x0, matrix products: 14.3 us -> none  [the longest x1 4.55 us: attend(): jnp.einsum('nqd,nkd->nqk', q_rows, kt_win, preferred_element_type=jnp.flo...]
  transfers between devices with their start and end apart: 9 -> 24, of which waited for: 8 -> 11; matrix products, arithmetic and copies ran while one was open for 20% -> 0% of each run, Pallas kernels for 0% -> 2%
where the time goes in v4:
time: 157 us; the launch traced here: 155 us
  waiting for transfers between devices  72.2 us (46%)
  starting transfers between devices  41.4 us (26%)
  Pallas kernels  24.4 us (16%)
  local copies, waits for them, and re-layouts  16.4 us (10%)
    ppermute x21, waiting for transfers between devices, send(): got[k] = lax.ppermute(pieces[k], 'heads', pairs) if k else pieces[k]  70 us
    ppermute x21, starting transfers between devices, send(): got[k] = lax.ppermute(pieces[k], 'heads', pairs) if k else pieces[k]  39.8 us
    unnamed x79, local copies, waits for them, and re-layouts  15.8 us
    pallas_call x2, Pallas kernels, attend(): pl.pallas_call(functools.partial(attend_kernel, count=count, sources=sour...  14.4 us
    pallas_call x2, Pallas kernels, pack(): pl.pallas_call(functools.partial(pack_kernel, count=count, slots=slots, h...  5.4 us
  transfers between devices with their start and end apart: 24, of which 11 were waited for; matrix products, arithmetic and copies ran while one was open for 0% of the time, Pallas kernels for 2%

profile of v4, /device:TPU:0, one launch (start us, length us, event | category | flops | bytes accessed | tf_op | source)
XLA Modules:
  0.0 155.4 jit_solution(280750624530142347)
XLA Ops:
  0.6 3.0 %shard_map.87 = (bf16[128,1024]{1,0:T(8,128)(2,1)}, bf16[128,1024]{1,0:T(8,128)(2,1)}, bf16[128,1024]{1,0:T(8,128)(2,1)}, bf16[128,1024]{1,0:T(8,128)(2,1)}, bf1...) custom-call(s32[1]{0:T(128)} %bitcast.chip, ...), custom_call_target="tpu_custom_call" | custom-call | tf_op jit(solution)/shard_map/pallas_call | solution.py:72
  3.7 4.1 %collective-permute-start.4 = (bf16[128,1024]{1,0:T(8,128)(2,1)}, bf16[128,1024]{1,0:T(8,128)(2,1)S(1)}, u32[]{:S(2)}, u32[]{:S(2)}) collective-permute-start(bf16[128,1024]{1,0:T(8,128)(2,1)} %get-tuple-element.32), channel_id=1, source_target_pairs={{0,16},{2,18},{4,20},{6,22},{8,24},{10,26},{12,28},{14,30},{16,0},... | collective-permute-start | bytes 786440 | tf_op jit(solution)/shard_map/ppermute | solution.py:262
  7.8 1.3 collective-permute-start.5
  9.0 3.6 %collective-permute-start.6 = (bf16[128,1024]{1,0:T(8,128)(2,1)}, bf16[128,1024]{1,0:T(8,128)(2,1)S(1)}, u32[]{:S(2)}, u32[]{:S(2)}) collective-permute-start(bf16[128,1024]{1,0:T(8,128)(2,1)} %get-tuple-element.34), channel_id=1, source_target_pairs={{0,24},{2,26},{4,28},{6,30},{8,16},{10,18},{12,20},{14,22},{16,8},... | collective-permute-start | bytes 786440 | tf_op jit(solution)/shard_map/ppermute | solution.py:262
  12.6 1.7 %collective-permute-start.8 = (bf16[128,1024]{1,0:T(8,128)(2,1)}, bf16[128,1024]{1,0:T(8,128)(2,1)S(1)}, u32[]{:S(2)}, u32[]{:S(2)}) collective-permute-start(bf16[128,1024]{1,0:T(8,128)(2,1)} %get-tuple-element.37), channel_id=1, source_target_pairs={{0,4},{2,6},{4,0},{6,2},{8,12},{10,14},{12,8},{14,10},{16,20},{18,... | collective-permute-start | bytes 786440 | tf_op jit(solution)/shard_map/ppermute | solution.py:262
  14.3 23.3 %collective-permute-done.4.refs_0_ = bf16[128,1024]{1,0:T(8,128)(2,1)S(1)} collective-permute-done((bf16[128,1024]{1,0:T(8,128)(2,1)}, bf16[128,1024]{1,0:T(8,128)(2,1)S(1)}, u32[]{:S(2)}, u32[]{:S(2)}) %collective-permute-start.4) | collective-permute-done | bytes 262176 | tf_op jit(solution)/shard_map/ppermute | solution.py:262
  37.6 0.1 collective-permute-start.9
  37.7 6.8 %collective-permute-done.5.refs_1_ = bf16[128,1024]{1,0:T(8,128)(2,1)S(1)} collective-permute-done((bf16[128,1024]{1,0:T(8,128)(2,1)}, bf16[128,1024]{1,0:T(8,128)(2,1)S(1)}, u32[]{:S(2)}, u32[]{:S(2)}) %collective-permute-start.5) | collective-permute-done | bytes 262176 | tf_op jit(solution)/shard_map/ppermute | solution.py:262
  44.5 0.0 collective-permute-done.8.refs_5_
  44.5 3.5 %collective-permute-done.9.refs_6_ = bf16[128,1024]{1,0:T(8,128)(2,1)S(1)} collective-permute-done((bf16[128,1024]{1,0:T(8,128)(2,1)}, bf16[128,1024]{1,0:T(8,128)(2,1)S(1)}, u32[]{:S(2)}, u32[]{:S(2)}) %collective-permute-start.9) | collective-permute-done | bytes 262176 | tf_op jit(solution)/shard_map/ppermute | solution.py:262
  48.1 6.5 %collective-permute-done.10.refs_7_ = bf16[128,1024]{1,0:T(8,128)(2,1)S(1)} collective-permute-done((bf16[128,1024]{1,0:T(8,128)(2,1)}, bf16[128,1024]{1,0:T(8,128)(2,1)S(1)}, u32[]{:S(2)}, u32[]{:S(2)}) %collective-permute-start.10) | collective-permute-done | bytes 262176 | tf_op jit(solution)/shard_map/ppermute | solution.py:262
  54.6 0.9 copy-done.33
  55.5 1.9 %shard_map.88 = (bf16[8,128,1024]{2,1,0:T(8,128)(2,1)}, bf16[4,128,1024]{2,1,0:T(8,128)(2,1)}) custom-call(s32[1]{0:T(128)} %bitcast.2.groups, bf16[128,1024]{1,0:T(8,128)(2,1)S(1)} %collective-permute-done.4.refs_0_, bf16[128,1024]{1,0:T(8,128)(2,1)S(1)} %collective-permute-done.5.refs_1_, bf16[128,1024]{1,0:T(8,128)(2,1)S(1)} %collective-permute-done.6.refs_2_, ...), custom_call_target="tpu_custom_call" | custom-call | tf_op jit(solution)/shard_map/pallas_call | solution.py:154
  57.4 1.6 %collective-permute-start.11 = (bf16[4,128,1024]{2,1,0:T(8,128)(2,1)}, bf16[4,128,1024]{2,1,0:T(8,128)(2,1)S(1)}, u32[]{:S(2)}, u32[]{:S(2)}) collective-permute-start(bf16[4,128,1024]{2,1,0:T(8,128)(2,1)} %get-tuple-element.41), channel_id=1, source_target_pairs={{0,1},{1,0},{2,3},{3,2},{4,5},{5,4},{6,7},{7,6},{8,9},{9,8},{10,11... | collective-permute-start | bytes 3145736 | tf_op jit(solution)/shard_map/ppermute | solution.py:289
  59.0 0.0 collective-permute-start.15
  59.0 2.4 %shard_map.86 = (bf16[128,512]{1,0:T(8,128)(2,1)}, bf16[128,512]{1,0:T(8,128)(2,1)}, bf16[128,512]{1,0:T(8,128)(2,1)}, bf16[128,512]{1,0:T(8,128)(2,1)}, bf16[12...) custom-call(s32[1]{0:T(128)} %bitcast.chip, ...), custom_call_target="tpu_custom_call" | custom-call | tf_op jit(solution)/shard_map/pallas_call | solution.py:72
  61.5 5.2 %collective-permute-start = (bf16[128,512]{1,0:T(8,128)(2,1)}, bf16[128,512]{1,0:T(8,128)(2,1)S(1)}, u32[]{:S(2)}, u32[]{:S(2)}) collective-permute-start(bf16[128,512]{1,0:T(8,128)(2,1)} %get-tuple-element.28), channel_id=1, source_target_pairs={{0,16},{2,18},{4,20},{6,22},{8,24},{10,26},{12,28},{14,30},{16,0},... | collective-permute-start | bytes 393224 | tf_op jit(solution)/shard_map/ppermute | solution.py:262
  66.7 1.0 collective-permute-start.1
  67.7 0.8 collective-permute-start.2
  68.5 11.1 %collective-permute-done.refs_1_.refs_0_ = bf16[128,512]{1,0:T(8,128)(2,1)S(1)} collective-permute-done((bf16[128,512]{1,0:T(8,128)(2,1)}, bf16[128,512]{1,0:T(8,128)(2,1)S(1)}, u32[]{:S(2)}, u32[]{:S(2)}) %collective-permute-start) | collective-permute-done | bytes 131104 | tf_op jit(solution)/shard_map/ppermute | solution.py:262
  79.7 1.8 %collective-permute-start.3 = (bf16[128,512]{1,0:T(8,128)(2,1)}, bf16[128,512]{1,0:T(8,128)(2,1)S(1)}, u32[]{:S(2)}, u32[]{:S(2)}) collective-permute-start(bf16[128,512]{1,0:T(8,128)(2,1)} %get-tuple-element.31), channel_id=1, source_target_pairs={{0,28},{2,30},{4,24},{6,26},{8,20},{10,22},{12,16},{14,18},{16,12}... | collective-permute-start | bytes 393224 | tf_op jit(solution)/shard_map/ppermute | solution.py:262
  81.4 2.0 %collective-permute-done.1.refs_2_.refs_1_ = bf16[128,512]{1,0:T(8,128)(2,1)S(1)} collective-permute-done((bf16[128,512]{1,0:T(8,128)(2,1)}, bf16[128,512]{1,0:T(8,128)(2,1)S(1)}, u32[]{:S(2)}, u32[]{:S(2)}) %collective-permute-start.1) | collective-permute-done | bytes 131104 | tf_op jit(solution)/shard_map/ppermute | solution.py:262
  83.4 0.5 collective-permute-start.12
  83.9 0.0 collective-permute-done.2.refs_3_.refs_2_
  83.9 4.7 %collective-permute-start.13 = (bf16[128,512]{1,0:T(8,128)(2,1)}, bf16[128,512]{1,0:T(8,128)(2,1)S(1)}, u32[]{:S(2)}, u32[]{:S(2)}) collective-permute-start(bf16[128,512]{1,0:T(8,128)(2,1)} %get-tuple-element.44), channel_id=1, source_target_pairs={{0,8},{2,10},{4,12},{6,14},{8,0},{10,2},{12,4},{14,6},{16,24},{18,... | collective-permute-start | bytes 393224 | tf_op jit(solution)/shard_map/ppermute | solution.py:262
  88.7 3.4 %collective-permute-start.14 = (bf16[128,512]{1,0:T(8,128)(2,1)}, bf16[128,512]{1,0:T(8,128)(2,1)S(1)}, u32[]{:S(2)}, u32[]{:S(2)}) collective-permute-start(bf16[128,512]{1,0:T(8,128)(2,1)} %get-tuple-element.45), channel_id=1, source_target_pairs={{0,12},{2,14},{4,8},{6,10},{8,4},{10,6},{12,0},{14,2},{16,28},{18,... | collective-permute-start | bytes 393224 | tf_op jit(solution)/shard_map/ppermute | solution.py:262
  92.0 0.0 collective-permute-done.13.refs_7_.refs_2_
  92.1 3.7 %collective-permute-done.14.refs_8_.refs_3_ = bf16[128,512]{1,0:T(8,128)(2,1)S(1)} collective-permute-done((bf16[128,512]{1,0:T(8,128)(2,1)}, bf16[128,512]{1,0:T(8,128)(2,1)S(1)}, u32[]{:S(2)}, u32[]{:S(2)}) %collective-permute-start.14) | collective-permute-done | bytes 131104 | tf_op jit(solution)/shard_map/ppermute | solution.py:262
  95.8 0.6 copy-done.16
  96.4 0.4 copy-done
  96.8 0.0 collective-permute-start.16
  96.8 0.1 copy.14
  96.9 0.6 gather_fusion
  97.4 2.2 %collective-permute-done.16.refs_7_ = bf16[4,128,1024]{2,1,0:T(8,128)(2,1)S(1)} collective-permute-done((bf16[4,128,1024]{2,1,0:T(8,128)(2,1)}, bf16[4,128,1024]{2,1,0:T(8,128)(2,1)S(1)}, u32[]{:S(2)}, u32[]{:S(2)}) %collective-permute-start.16) | collective-permute-done | bytes 1048608 | tf_op jit(solution)/shard_map/ppermute | solution.py:292
  99.6 0.0 collective-permute-done.15.refs_6_
  99.6 1.2 copy-done.1
  100.9 0.9 copy-done.19
  101.8 0.9 copy-done.21
  102.7 0.9 copy-done.23
  103.6 0.9 copy-done.25
  104.5 7.2 %shard_map.90 = (bf16[128,512]{1,0:T(8,128)(2,1)}, bf16[128,512]{1,0:T(8,128)(2,1)}, bf16[128,512]{1,0:T(8,128)(2,1)}, bf16[128,512]{1,0:T(8,128)(2,1)}) custom-call(s32[8,4]{1,0:T(8,128)S(1)} %gather_fusion, bf16[128,512]{1,0:T(8,128)(2,1)S(1)} %copy-done.19, bf16[128,512]{1,0:T(8,128)(2,1)S(1)} %copy-done.21, bf16[128,512]{1,0:T(8,128)(2,1)S(1)} %copy-done.23, ...), custom_call_target="tpu_custom_call" | custom-call | tf_op jit(solution)/shard_map/pallas_call | solution.py:240
  111.7 0.9 copy-done.34
  112.6 0.9 copy-done.35
  113.5 0.9 copy-done.36
  114.5 0.9 copy-done.37
  115.4 7.2 %shard_map.91 = (bf16[128,512]{1,0:T(8,128)(2,1)}, bf16[128,512]{1,0:T(8,128)(2,1)}, bf16[128,512]{1,0:T(8,128)(2,1)}, bf16[128,512]{1,0:T(8,128)(2,1)}) custom-call(s32[8,4]{1,0:T(8,128)S(1)} %gather_fusion, bf16[128,512]{1,0:T(8,128)(2,1)S(1)} %copy-done.11, bf16[128,512]{1,0:T(8,128)(2,1)S(1)} %copy-done.13, bf16[128,512]{1,0:T(8,128)(2,1)S(1)} %copy-done.15, ...), custom_call_target="tpu_custom_call" | custom-call | tf_op jit(solution)/shard_map/pallas_call | solution.py:240
  122.6 2.7 %collective-permute-start.23 = (bf16[128,512]{1,0:T(8,128)(2,1)}, bf16[128,512]{1,0:T(8,128)(2,1)S(1)}, u32[]{:S(2)}, u32[]{:S(2)}) collective-permute-start(bf16[128,512]{1,0:T(8,128)(2,1)} %get-tuple-element.53), channel_id=1, source_target_pairs={{0,12},{2,14},{4,8},{6,10},{8,4},{10,6},{12,0},{14,2},{16,28},{18,... | collective-permute-start | bytes 393224 | tf_op jit(solution)/shard_map/ppermute | solution.py:262
  125.2 0.0 collective-permute-start.17
  125.2 3.9 %collective-permute-start.18 = (bf16[128,512]{1,0:T(8,128)(2,1)S(1)}, bf16[128,512]{1,0:T(8,128)(2,1)S(1)}, u32[]{:S(2)}, u32[]{:S(2)}) collective-permute-start(bf16[128,512]{1,0:T(8,128)(2,1)S(1)} %copy-done.36), channel_id=1, source_target_pairs={{0,20},{2,22},{4,16},{6,18},{8,28},{10,30},{12,24},{14,26},{16,4},... | collective-permute-start | bytes 393224 | tf_op jit(solution)/shard_map/ppermute | solution.py:262
  129.1 0.8 collective-permute-start.19
  129.9 3.0 %collective-permute-start.20 = (bf16[128,512]{1,0:T(8,128)(2,1)S(1)}, bf16[128,512]{1,0:T(8,128)(2,1)S(1)}, u32[]{:S(2)}, u32[]{:S(2)}) collective-permute-start(bf16[128,512]{1,0:T(8,128)(2,1)S(1)} %copy-done.34), channel_id=1, source_target_pairs={{0,28},{2,30},{4,24},{6,26},{8,20},{10,22},{12,16},{14,18},{16,12}... | collective-permute-start | bytes 393224 | tf_op jit(solution)/shard_map/ppermute | solution.py:262
  132.9 10.8 %collective-permute-done.17.refs_1_.refs_0_ = bf16[128,512]{1,0:T(8,128)(2,1)S(1)} collective-permute-done((bf16[128,512]{1,0:T(8,128)(2,1)S(1)}, bf16[128,512]{1,0:T(8,128)(2,1)S(1)}, u32[]{:S(2)}, u32[]{:S(2)}) %collective-permute-start.17) | collective-permute-done | bytes 131104 | tf_op jit(solution)/shard_map/ppermute | solution.py:262
  143.7 1.3 collective-permute-start.21
  145.0 2.2 %collective-permute-done.18.refs_2_.refs_1_ = bf16[128,512]{1,0:T(8,128)(2,1)S(1)} collective-permute-done((bf16[128,512]{1,0:T(8,128)(2,1)S(1)}, bf16[128,512]{1,0:T(8,128)(2,1)S(1)}, u32[]{:S(2)}, u32[]{:S(2)}) %collective-permute-start.18) | collective-permute-done | bytes 131104 | tf_op jit(solution)/shard_map/ppermute | solution.py:262
  147.2 0.6 copy-done.5
  147.8 0.0 copy-done.7
  147.9 0.6 copy-done.9
  148.6 0.6 copy-done.29
  149.2 0.1 collective-permute-done.21.refs_0_
  149.3 0.6 copy-done.31
  150.0 0.9 copy-done.26
  150.9 0.9 copy-done.30
  151.8 0.9 copy-done.32
  152.7 2.7 %shard_map.96 = (bf16[128,2048]{1,0:T(8,128)(2,1)}, bf16[128,2048]{1,0:T(8,128)(2,1)}) custom-call(s32[1]{0:T(128)} %bitcast.chip, bf16[128,512]{1,0:T(8,128)(2,1)S(1)} %copy-done.4, bf16[128,512]{1,0:T(8,128)(2,1)S(1)} %copy-done.6, bf16[128,512]{1,0:T(8,128)(2,1)S(1)} %copy-done.8, bf16[128,512]{1,0:T(8,128)(2,1)S(1)} %copy-done.10, ...), custom_call_target="tpu_custom_call" | custom-call | tf_op jit(solution)/shard_map/pallas_call | solution.py:113
  (78 shorter events, 0.2 us)
Async XLA Ops:
  3.7 33.9 %collective-permute-start.4 = (bf16[128,1024]{1,0:T(8,128)(2,1)}, bf16[128,1024]{1,0:T(8,128)(2,1)S(1)}, u32[]{:S(2)}, u32[]{:S(2)}) collective-permute-start(bf16[128,1024]{1,0:T(8,128)(2,1)} %get-tuple-element.32), channel_id=1, source_target_pairs={{0,16},{2,18},{4,20},{6,22},{8,24},{10,26},{12,28},{14,30},{16,0},... | collective-permute-start | bytes 786440 | tf_op jit(solution)/shard_map/ppermute | solution.py:262
  7.8 36.8 %collective-permute-start.5 = (bf16[128,1024]{1,0:T(8,128)(2,1)}, bf16[128,1024]{1,0:T(8,128)(2,1)S(1)}, u32[]{:S(2)}, u32[]{:S(2)}) collective-permute-start(bf16[128,1024]{1,0:T(8,128)(2,1)} %get-tuple-element.33), channel_id=1, source_target_pairs={{0,20},{2,22},{4,16},{6,18},{8,28},{10,30},{12,24},{14,26},{16,4},... | collective-permute-start | bytes 786440 | tf_op jit(solution)/shard_map/ppermute | solution.py:262
  9.0 35.5 %collective-permute-start.6 = (bf16[128,1024]{1,0:T(8,128)(2,1)}, bf16[128,1024]{1,0:T(8,128)(2,1)S(1)}, u32[]{:S(2)}, u32[]{:S(2)}) collective-permute-start(bf16[128,1024]{1,0:T(8,128)(2,1)} %get-tuple-element.34), channel_id=1, source_target_pairs={{0,24},{2,26},{4,28},{6,30},{8,16},{10,18},{12,20},{14,22},{16,8},... | collective-permute-start | bytes 786440 | tf_op jit(solution)/shard_map/ppermute | solution.py:262
  12.6 31.9 %collective-permute-start.7 = (bf16[128,1024]{1,0:T(8,128)(2,1)}, bf16[128,1024]{1,0:T(8,128)(2,1)S(1)}, u32[]{:S(2)}, u32[]{:S(2)}) collective-permute-start(bf16[128,1024]{1,0:T(8,128)(2,1)} %get-tuple-element.35), channel_id=1, source_target_pairs={{0,28},{2,30},{4,24},{6,26},{8,20},{10,22},{12,16},{14,18},{16,12}... | collective-permute-start | bytes 786440 | tf_op jit(solution)/shard_map/ppermute | solution.py:262
  12.6 31.9 %collective-permute-start.8 = (bf16[128,1024]{1,0:T(8,128)(2,1)}, bf16[128,1024]{1,0:T(8,128)(2,1)S(1)}, u32[]{:S(2)}, u32[]{:S(2)}) collective-permute-start(bf16[128,1024]{1,0:T(8,128)(2,1)} %get-tuple-element.37), channel_id=1, source_target_pairs={{0,4},{2,6},{4,0},{6,2},{8,12},{10,14},{12,8},{14,10},{16,20},{18,... | collective-permute-start | bytes 786440 | tf_op jit(solution)/shard_map/ppermute | solution.py:262
  37.6 10.5 %collective-permute-start.9 = (bf16[128,1024]{1,0:T(8,128)(2,1)}, bf16[128,1024]{1,0:T(8,128)(2,1)S(1)}, u32[]{:S(2)}, u32[]{:S(2)}) collective-permute-start(bf16[128,1024]{1,0:T(8,128)(2,1)} %get-tuple-element.38), channel_id=1, source_target_pairs={{0,8},{2,10},{4,12},{6,14},{8,0},{10,2},{12,4},{14,6},{16,24},{18,... | collective-permute-start | bytes 786440 | tf_op jit(solution)/shard_map/ppermute | solution.py:262
  44.5 10.1 %collective-permute-start.10 = (bf16[128,1024]{1,0:T(8,128)(2,1)}, bf16[128,1024]{1,0:T(8,128)(2,1)S(1)}, u32[]{:S(2)}, u32[]{:S(2)}) collective-permute-start(bf16[128,1024]{1,0:T(8,128)(2,1)} %get-tuple-element.39), channel_id=1, source_target_pairs={{0,12},{2,14},{4,8},{6,10},{8,4},{10,6},{12,0},{14,2},{16,28},{18,... | collective-permute-start | bytes 786440 | tf_op jit(solution)/shard_map/ppermute | solution.py:262
  54.6 1.0 copy-start.33
  57.4 38.3 %collective-permute-start.11 = (bf16[4,128,1024]{2,1,0:T(8,128)(2,1)}, bf16[4,128,1024]{2,1,0:T(8,128)(2,1)S(1)}, u32[]{:S(2)}, u32[]{:S(2)}) collective-permute-start(bf16[4,128,1024]{2,1,0:T(8,128)(2,1)} %get-tuple-element.41), channel_id=1, source_target_pairs={{0,1},{1,0},{2,3},{3,2},{4,5},{5,4},{6,7},{7,6},{8,9},{9,8},{10,11... | collective-permute-start | bytes 3145736 | tf_op jit(solution)/shard_map/ppermute | solution.py:289
  59.0 37.7 %copy-start.38 = (s32[8,4]{0,1:T(4,128)S(1)}, s32[8,4]{0,1:T(4,128)}, u32[]{:S(2)}) copy-start(s32[8,4]{0,1:T(4,128)} %param.13) | copy-start | bytes 388
  59.0 40.6 %copy-start.2 = (bf16[8,128,1024]{2,1,0:T(8,128)(2,1)S(1)}, bf16[8,128,1024]{2,1,0:T(8,128)(2,1)}, u32[]{:S(2)}) copy-start(bf16[8,128,1024]{2,1,0:T(8,128)(2,1)} %get-tuple-element.40.refs_4_) | copy-start | bytes 6291460
  59.0 40.6 %collective-permute-start.15 = (bf16[8,128,1024]{2,1,0:T(8,128)(2,1)}, bf16[8,128,1024]{2,1,0:T(8,128)(2,1)}, u32[]{:S(2)}, u32[]{:S(2)}) collective-permute-start(bf16[8,128,1024]{2,1,0:T(8,128)(2,1)} %get-tuple-element.40.refs_4_), channel_id=1, source_target_pairs={{0,2},{2,0},{4,6},{6,4},{8,10},{10,8},{12,14},{14,12},{16,18},{18,... | collective-permute-start | bytes 6291464 | tf_op jit(solution)/shard_map/ppermute | solution.py:292
  61.5 18.2 %collective-permute-start = (bf16[128,512]{1,0:T(8,128)(2,1)}, bf16[128,512]{1,0:T(8,128)(2,1)S(1)}, u32[]{:S(2)}, u32[]{:S(2)}) collective-permute-start(bf16[128,512]{1,0:T(8,128)(2,1)} %get-tuple-element.28), channel_id=1, source_target_pairs={{0,16},{2,18},{4,20},{6,22},{8,24},{10,26},{12,28},{14,30},{16,0},... | collective-permute-start | bytes 393224 | tf_op jit(solution)/shard_map/ppermute | solution.py:262
  66.7 16.7 %collective-permute-start.1 = (bf16[128,512]{1,0:T(8,128)(2,1)}, bf16[128,512]{1,0:T(8,128)(2,1)S(1)}, u32[]{:S(2)}, u32[]{:S(2)}) collective-permute-start(bf16[128,512]{1,0:T(8,128)(2,1)} %get-tuple-element.29), channel_id=1, source_target_pairs={{0,20},{2,22},{4,16},{6,18},{8,28},{10,30},{12,24},{14,26},{16,4},... | collective-permute-start | bytes 393224 | tf_op jit(solution)/shard_map/ppermute | solution.py:262
  67.7 16.2 %collective-permute-start.2 = (bf16[128,512]{1,0:T(8,128)(2,1)}, bf16[128,512]{1,0:T(8,128)(2,1)S(1)}, u32[]{:S(2)}, u32[]{:S(2)}) collective-permute-start(bf16[128,512]{1,0:T(8,128)(2,1)} %get-tuple-element.30), channel_id=1, source_target_pairs={{0,24},{2,26},{4,28},{6,30},{8,16},{10,18},{12,20},{14,22},{16,8},... | collective-permute-start | bytes 393224 | tf_op jit(solution)/shard_map/ppermute | solution.py:262
  79.7 16.1 %copy-start.18 = (bf16[128,512]{1,0:T(8,128)(2,1)}, bf16[128,512]{1,0:T(8,128)(2,1)S(1)}, u32[]{:S(2)}) copy-start(bf16[128,512]{1,0:T(8,128)(2,1)S(1)} %collective-permute-done.refs_1_.refs_0_) | copy-start | bytes 393220
  79.7 9.0 %collective-permute-start.3 = (bf16[128,512]{1,0:T(8,128)(2,1)}, bf16[128,512]{1,0:T(8,128)(2,1)S(1)}, u32[]{:S(2)}, u32[]{:S(2)}) collective-permute-start(bf16[128,512]{1,0:T(8,128)(2,1)} %get-tuple-element.31), channel_id=1, source_target_pairs={{0,28},{2,30},{4,24},{6,26},{8,20},{10,22},{12,16},{14,18},{16,12}... | collective-permute-start | bytes 393224 | tf_op jit(solution)/shard_map/ppermute | solution.py:262
  83.4 12.3 %copy-start.20 = (bf16[128,512]{1,0:T(8,128)(2,1)}, bf16[128,512]{1,0:T(8,128)(2,1)S(1)}, u32[]{:S(2)}) copy-start(bf16[128,512]{1,0:T(8,128)(2,1)S(1)} %collective-permute-done.1.refs_2_.refs_1_) | copy-start | bytes 393220
  83.4 8.6 %collective-permute-start.12 = (bf16[128,512]{1,0:T(8,128)(2,1)}, bf16[128,512]{1,0:T(8,128)(2,1)S(1)}, u32[]{:S(2)}, u32[]{:S(2)}) collective-permute-start(bf16[128,512]{1,0:T(8,128)(2,1)} %get-tuple-element.43), channel_id=1, source_target_pairs={{0,4},{2,6},{4,0},{6,2},{8,12},{10,14},{12,8},{14,10},{16,20},{18,... | collective-permute-start | bytes 393224 | tf_op jit(solution)/shard_map/ppermute | solution.py:262
  83.9 11.8 %copy-start.22 = (bf16[128,512]{1,0:T(8,128)(2,1)}, bf16[128,512]{1,0:T(8,128)(2,1)S(1)}, u32[]{:S(2)}) copy-start(bf16[128,512]{1,0:T(8,128)(2,1)S(1)} %collective-permute-done.2.refs_3_.refs_2_) | copy-start | bytes 393220
  83.9 8.1 %collective-permute-start.13 = (bf16[128,512]{1,0:T(8,128)(2,1)}, bf16[128,512]{1,0:T(8,128)(2,1)S(1)}, u32[]{:S(2)}, u32[]{:S(2)}) collective-permute-start(bf16[128,512]{1,0:T(8,128)(2,1)} %get-tuple-element.44), channel_id=1, source_target_pairs={{0,8},{2,10},{4,12},{6,14},{8,0},{10,2},{12,4},{14,6},{16,24},{18,... | collective-permute-start | bytes 393224 | tf_op jit(solution)/shard_map/ppermute | solution.py:262
  88.7 7.1 %copy-start.24 = (bf16[128,512]{1,0:T(8,128)(2,1)}, bf16[128,512]{1,0:T(8,128)(2,1)S(1)}, u32[]{:S(2)}) copy-start(bf16[128,512]{1,0:T(8,128)(2,1)S(1)} %collective-permute-done.3.refs_4_.refs_3_) | copy-start | bytes 393220
  88.7 7.1 %collective-permute-start.14 = (bf16[128,512]{1,0:T(8,128)(2,1)}, bf16[128,512]{1,0:T(8,128)(2,1)S(1)}, u32[]{:S(2)}, u32[]{:S(2)}) collective-permute-start(bf16[128,512]{1,0:T(8,128)(2,1)} %get-tuple-element.45), channel_id=1, source_target_pairs={{0,12},{2,14},{4,8},{6,10},{8,4},{10,6},{12,0},{14,2},{16,28},{18,... | collective-permute-start | bytes 393224 | tf_op jit(solution)/shard_map/ppermute | solution.py:262
  92.0 3.7 %copy-start.12 = (bf16[128,512]{1,0:T(8,128)(2,1)}, bf16[128,512]{1,0:T(8,128)(2,1)S(1)}, u32[]{:S(2)}) copy-start(bf16[128,512]{1,0:T(8,128)(2,1)S(1)} %collective-permute-done.12.refs_6_.refs_1_) | copy-start | bytes 393220
  92.0 3.7 %copy-start.14 = (bf16[128,512]{1,0:T(8,128)(2,1)}, bf16[128,512]{1,0:T(8,128)(2,1)S(1)}, u32[]{:S(2)}) copy-start(bf16[128,512]{1,0:T(8,128)(2,1)S(1)} %collective-permute-done.13.refs_7_.refs_2_) | copy-start | bytes 393220
  95.7 0.6 copy-start.16
  95.8 1.0 copy-start
  96.8 2.9 %collective-permute-start.16 = (bf16[4,128,1024]{2,1,0:T(8,128)(2,1)}, bf16[4,128,1024]{2,1,0:T(8,128)(2,1)S(1)}, u32[]{:S(2)}, u32[]{:S(2)}) collective-permute-start(bf16[4,128,1024]{2,1,0:T(8,128)(2,1)} %shard_map.89.refs_5_), channel_id=1, source_target_pairs={{0,2},{2,0},{4,6},{6,4},{8,10},{10,8},{12,14},{14,12},{16,18},{18,... | collective-permute-start | bytes 3145736 | tf_op jit(solution)/shard_map/ppermute | solution.py:292
  99.6 1.2 copy-start.1
  100.9 0.9 copy-start.19
  101.8 0.9 copy-start.21
  102.7 0.9 copy-start.23
  103.6 0.9 copy-start.25
  104.5 7.2 %copy-start.11 = (bf16[128,512]{1,0:T(8,128)(2,1)S(1)}, bf16[128,512]{1,0:T(8,128)(2,1)}, u32[]{:S(2)}) copy-start(bf16[128,512]{1,0:T(8,128)(2,1)} %get-tuple-element.42.refs_5_.refs_0_) | copy-start | bytes 393220
  104.5 7.2 %copy-start.13 = (bf16[128,512]{1,0:T(8,128)(2,1)S(1)}, bf16[128,512]{1,0:T(8,128)(2,1)}, u32[]{:S(2)}) copy-start(bf16[128,512]{1,0:T(8,128)(2,1)} %copy-done.12) | copy-start | bytes 393220
  104.5 7.2 %copy-start.15 = (bf16[128,512]{1,0:T(8,128)(2,1)S(1)}, bf16[128,512]{1,0:T(8,128)(2,1)}, u32[]{:S(2)}) copy-start(bf16[128,512]{1,0:T(8,128)(2,1)} %copy-done.14) | copy-start | bytes 393220
  104.5 7.2 %copy-start.17 = (bf16[128,512]{1,0:T(8,128)(2,1)S(1)}, bf16[128,512]{1,0:T(8,128)(2,1)}, u32[]{:S(2)}) copy-start(bf16[128,512]{1,0:T(8,128)(2,1)} %copy-done.16) | copy-start | bytes 393220
  111.7 0.9 copy-start.34
  112.6 0.9 copy-start.35
  113.5 0.9 copy-start.36
  114.4 0.9 copy-start.37
  122.6 10.3 %collective-permute-start.23 = (bf16[128,512]{1,0:T(8,128)(2,1)}, bf16[128,512]{1,0:T(8,128)(2,1)S(1)}, u32[]{:S(2)}, u32[]{:S(2)}) collective-permute-start(bf16[128,512]{1,0:T(8,128)(2,1)} %get-tuple-element.53), channel_id=1, source_target_pairs={{0,12},{2,14},{4,8},{6,10},{8,4},{10,6},{12,0},{14,2},{16,28},{18,... | collective-permute-start | bytes 393224 | tf_op jit(solution)/shard_map/ppermute | solution.py:262
  125.2 18.5 %collective-permute-start.17 = (bf16[128,512]{1,0:T(8,128)(2,1)S(1)}, bf16[128,512]{1,0:T(8,128)(2,1)S(1)}, u32[]{:S(2)}, u32[]{:S(2)}) collective-permute-start(bf16[128,512]{1,0:T(8,128)(2,1)S(1)} %copy-done.37), channel_id=1, source_target_pairs={{0,16},{2,18},{4,20},{6,22},{8,24},{10,26},{12,28},{14,30},{16,0},... | collective-permute-start | bytes 393224 | tf_op jit(solution)/shard_map/ppermute | solution.py:262
  125.2 21.9 %collective-permute-start.18 = (bf16[128,512]{1,0:T(8,128)(2,1)S(1)}, bf16[128,512]{1,0:T(8,128)(2,1)S(1)}, u32[]{:S(2)}, u32[]{:S(2)}) collective-permute-start(bf16[128,512]{1,0:T(8,128)(2,1)S(1)} %copy-done.36), channel_id=1, source_target_pairs={{0,20},{2,22},{4,16},{6,18},{8,28},{10,30},{12,24},{14,26},{16,4},... | collective-permute-start | bytes 393224 | tf_op jit(solution)/shard_map/ppermute | solution.py:262
  129.1 18.1 %collective-permute-start.19 = (bf16[128,512]{1,0:T(8,128)(2,1)S(1)}, bf16[128,512]{1,0:T(8,128)(2,1)S(1)}, u32[]{:S(2)}, u32[]{:S(2)}) collective-permute-start(bf16[128,512]{1,0:T(8,128)(2,1)S(1)} %copy-done.35), channel_id=1, source_target_pairs={{0,24},{2,26},{4,28},{6,30},{8,16},{10,18},{12,20},{14,22},{16,8},... | collective-permute-start | bytes 393224 | tf_op jit(solution)/shard_map/ppermute | solution.py:262
  129.9 17.3 %collective-permute-start.20 = (bf16[128,512]{1,0:T(8,128)(2,1)S(1)}, bf16[128,512]{1,0:T(8,128)(2,1)S(1)}, u32[]{:S(2)}, u32[]{:S(2)}) collective-permute-start(bf16[128,512]{1,0:T(8,128)(2,1)S(1)} %copy-done.34), channel_id=1, source_target_pairs={{0,28},{2,30},{4,24},{6,26},{8,20},{10,22},{12,16},{14,18},{16,12}... | collective-permute-start | bytes 393224 | tf_op jit(solution)/shard_map/ppermute | solution.py:262
  132.9 14.3 %copy-start.27 = (bf16[128,512]{1,0:T(8,128)(2,1)}, bf16[128,512]{1,0:T(8,128)(2,1)S(1)}, u32[]{:S(2)}) copy-start(bf16[128,512]{1,0:T(8,128)(2,1)S(1)} %collective-permute-done.23.refs_0_) | copy-start | bytes 393220
  132.9 15.6 %collective-permute-start.22 = (bf16[128,512]{1,0:T(8,128)(2,1)}, bf16[128,512]{1,0:T(8,128)(2,1)S(1)}, u32[]{:S(2)}, u32[]{:S(2)}) collective-permute-start(bf16[128,512]{1,0:T(8,128)(2,1)} %get-tuple-element.52), channel_id=1, source_target_pairs={{0,8},{2,10},{4,12},{6,14},{8,0},{10,2},{12,4},{14,6},{16,24},{18,... | collective-permute-start | bytes 393224 | tf_op jit(solution)/shard_map/ppermute | solution.py:262
  143.7 3.5 %copy-start.3 = (bf16[128,512]{1,0:T(8,128)(2,1)}, bf16[128,512]{1,0:T(8,128)(2,1)S(1)}, u32[]{:S(2)}) copy-start(bf16[128,512]{1,0:T(8,128)(2,1)S(1)} %collective-permute-done.17.refs_1_.refs_0_) | copy-start | bytes 393220
  143.7 5.6 %collective-permute-start.21 = (bf16[128,512]{1,0:T(8,128)(2,1)}, bf16[128,512]{1,0:T(8,128)(2,1)S(1)}, u32[]{:S(2)}, u32[]{:S(2)}) collective-permute-start(bf16[128,512]{1,0:T(8,128)(2,1)} %get-tuple-element.51), channel_id=1, source_target_pairs={{0,4},{2,6},{4,0},{6,2},{8,12},{10,14},{12,8},{14,10},{16,20},{18,... | collective-permute-start | bytes 393224 | tf_op jit(solution)/shard_map/ppermute | solution.py:262
  147.2 0.7 copy-start.5
  147.2 0.7 copy-start.7
  147.9 0.6 copy-start.9
  148.5 1.4 copy-start.4
  148.5 1.4 copy-start.6
  148.5 1.4 copy-start.8
  148.5 1.4 copy-start.10
  148.5 1.4 copy-start.28
  148.5 0.6 copy-start.29
  149.3 0.6 copy-start.31
  150.0 0.9 copy-start.26
  150.9 0.9 copy-start.30
  151.8 0.9 copy-start.32

commit v5 on v1

v5 whole, which is shorter than its diff:
```python
import functools
import math

import jax
import jax.numpy as jnp
from jax import lax
from jax.experimental import pallas as pl
from jax.experimental.pallas import tpu as pltpu
from jax.sharding import PartitionSpec as P

BQ = 256
WK = 4
HB = 4
HALO = HB * BQ
PARAMS = pltpu.CompilerParams(vmem_limit_bytes=32 * 1024 * 1024)
ANY = pl.BlockSpec(memory_space=pl.ANY)
HBM = pl.BlockSpec(memory_space=pltpu.HBM)
VMEM = pl.BlockSpec(memory_space=pltpu.VMEM)
SMEM = pl.BlockSpec(memory_space=pltpu.SMEM)


def pin(*arrays):
    return [pltpu.with_memory_space_constraint(a, pltpu.HBM) for a in arrays]


def moves(size):
    return pl.CostEstimate(flops=0, bytes_accessed=size, transcendentals=0)


def hold_kernel(*refs):
    del refs


def hold(array, others):
    return pl.pallas_call(
        hold_kernel,
        in_specs=[ANY] * (1 + len(others)),
        out_specs=ANY,
        out_shape=jax.ShapeDtypeStruct(array.shape, array.dtype),
        input_output_aliases={0: 0},
    )(array, *others)


def pack_kernel(*refs, count, devices):
    arrays, out, held, sems = refs[:count], refs[count], refs[-2], refs[-1]
    hd = held.shape[2] // devices
    copies = [pltpu.make_async_copy(a, held.at[i], sems.at[i]) for i, a in enumerate(arrays)]
    for copy in copies:
        copy.start()
    for a, copy in enumerate(copies):
        copy.wait()
        for h in range(devices):
            out[h, :, a * hd : (a + 1) * hd] = held[a, :, h * hd : (h + 1) * hd]


def to_heads(arrays, devices):
    tokens, columns = arrays[0].shape
    count, hd = len(arrays), columns // devices
    return pl.pallas_call(
        functools.partial(pack_kernel, count=count, devices=devices),
        in_specs=[HBM] * count,
        out_specs=VMEM,
        out_shape=jax.ShapeDtypeStruct((devices, tokens, count * hd), jnp.bfloat16),
        scratch_shapes=[
            pltpu.VMEM((count, tokens, columns), jnp.bfloat16),
            pltpu.SemaphoreType.DMA((count,)),
        ],
        compiler_params=PARAMS,
        cost_estimate=moves(4 * count * tokens * columns),
    )(*pin(*arrays))


def unpack_kernel(piece, *arrays):
    devices, tokens, width = piece.shape
    hd = width // len(arrays)
    for h in range(devices):
        for a, array in enumerate(arrays):
            array[:, h * hd : (h + 1) * hd] = piece[h, :, a * hd : (a + 1) * hd]


def from_heads(pieces, count):
    devices, tokens, width = pieces.shape
    columns = devices * width // count
    return pl.pallas_call(
        unpack_kernel,
        in_specs=[VMEM],
        out_specs=[VMEM] * count,
        out_shape=[jax.ShapeDtypeStruct((tokens, columns), jnp.bfloat16)] * count,
        compiler_params=PARAMS,
        cost_estimate=moves(4 * pieces.size),
    )(pieces)


def exchange(pieces):
    got = lax.all_to_all(pieces, "heads", split_axis=0, concat_axis=0, tiled=True)
    return got.reshape(-1, got.shape[2])


def attend_kernel(table, q_ref, *refs, sources, hd):
    parts, out_ref, kv, sems = refs[:sources], refs[sources], refs[-2], refs[-1]
    copies, row = [], 0
    for i, ref in enumerate(parts):
        rows = ref.shape[0]
        copies.append(pltpu.make_async_copy(ref, kv.at[pl.ds(row, rows)], sems.at[i]))
        row += rows
    for copy in copies:
        copy.start()
    for copy in copies:
        copy.wait()

    scale = hd ** (-0.5)
    factor = scale * math.log2(math.e)
    trans = (((1,), (1,)), ((), ()))
    for block in range(q_ref.shape[0] // BQ):
        both = q_ref[block * BQ : (block + 1) * BQ]
        query = both[:, :hd]
        starts = [pl.multiple_of(table[block * WK + w] * BQ, BQ) for w in range(WK)]
        scores, tans = [], []
        for start in starts:
            keys = kv[pl.ds(start, BQ), : 2 * hd]
            scores.append(
                lax.dot_general(query, keys[:, hd:], trans, preferred_element_type=jnp.float32)
            )
            tans.append(lax.dot_general(both, keys, trans, preferred_element_type=jnp.float32))
        top = functools.reduce(jnp.maximum, scores)
        top = jnp.max(top, axis=1, keepdims=True) * factor
        probs = [jnp.exp2(s * factor - top) for s in scores]
        weighted = [p * t for p, t in zip(probs, tans)]
        total = jnp.sum(functools.reduce(jnp.add, probs), axis=1, keepdims=True)
        mean = jnp.sum(functools.reduce(jnp.add, weighted), axis=1, keepdims=True)
        main, side = 0.0, 0.0
        for start, p, w in zip(starts, probs, weighted):
            vals = kv[pl.ds(start, BQ), 2 * hd :]
            main += jnp.dot(p.astype(jnp.bfloat16), vals, preferred_element_type=jnp.float32)
            side += jnp.dot(
                w.astype(jnp.bfloat16), vals[:, :hd], preferred_element_type=jnp.float32
            )
        inverse = 1.0 / total
        out = main[:, :hd] * inverse
        tan = (main[:, hd:] + scale * side) * inverse - (scale * mean * inverse) * out
        rows = slice(block * BQ, (block + 1) * BQ)
        out_ref[rows, :hd] = out.astype(jnp.bfloat16)
        out_ref[rows, hd:] = tan.astype(jnp.bfloat16)


def attend(table, q_pair, parts):
    rows, width = q_pair.shape
    hd = width // 2
    total = sum(a.shape[0] for a in parts)
    elements = rows * WK * BQ
    return pl.pallas_call(
        functools.partial(attend_kernel, sources=len(parts), hd=hd),
        in_specs=[SMEM, VMEM] + [ANY] * len(parts),
        out_specs=VMEM,
        out_shape=jax.ShapeDtypeStruct((rows, width), jnp.bfloat16),
        scratch_shapes=[
            pltpu.VMEM((total, 4 * hd), jnp.bfloat16),
            pltpu.SemaphoreType.DMA((len(parts),)),
        ],
        compiler_params=PARAMS,
        cost_estimate=pl.CostEstimate(
            flops=12 * elements * hd,
            bytes_accessed=2 * (total * 4 * hd + 2 * rows * width),
            transcendentals=elements,
        ),
    )(table, q_pair, *parts)


def slots(neighbors, frame, blocks):
    local = neighbors - frame * blocks
    even = frame % 2 == 0
    before = blocks + jnp.where(even, HB, 0) + local + HB
    after = blocks + jnp.where(even, 0, HB) + local - blocks
    return jnp.where(local < 0, before, jnp.where(local >= blocks, after, local)).reshape(-1)


def per_device(query, keys, values, query_tan, keys_tan, values_tan, neighbors):
    devices, frames = lax.axis_size("heads"), lax.axis_size("frames")
    frame = lax.axis_index("frames")
    tokens = query.shape[0]
    kv_sent = to_heads([keys_tan, keys, values, values_tan], devices)
    q_sent = to_heads([query, query_tan], devices)
    kv = hold(exchange(kv_sent), [q_sent])
    rows = kv.shape[0]

    edges, parts = [], [kv]
    for first in (0, 1):
        pairs = [(i, i + 1) for i in range(first, frames - 1, 2)]
        if not pairs:
            continue
        start = jnp.where(frame % 2 == first, rows - HALO, 0)
        edges.append(lax.dynamic_slice_in_dim(kv, start, HALO, axis=0))
        parts.append(lax.ppermute(edges[-1], "frames", pairs + [(j, i) for i, j in pairs]))

    q_pair = exchange(hold(q_sent, edges))
    table = slots(neighbors, frame, neighbors.shape[0])
    pair = attend(table, q_pair, parts).reshape(devices, tokens, -1)
    back = lax.all_to_all(pair, "heads", split_axis=0, concat_axis=0, tiled=True)
    return from_heads(back, 2)


def solution(mesh):
    own = P(("frames", "heads"), None)
    return jax.shard_map(
        per_device,
        mesh=mesh,
        in_specs=(own,) * 6 + (P("frames", None),),
        out_specs=(own, own),
        check_vma=False,
    )
```

time: 137 us -> 134 us (0.978)
  other arithmetic: 2.75 us -> 0.01 us
  local copies, waits for them, and re-layouts: 8.17 us -> 6.1 us
  Pallas kernels: 11.2 us -> 13 us
    ppermute x1, waiting for transfers between devices: 3.81 us -> 24 us  [per_device(): lax.ppermute(edges[-1], 'frames', pairs + [(j, i) for i, j in pairs])]
    all_to_all x2, waiting for transfers between devices: 58.9 us -> 38.8 us  [exchange(): lax.all_to_all(pieces, 'heads', split_axis=0, concat_axis=0, tiled=True)]
    transpose x3 -> x0, local copies, waits for them, and re-layouts: 2.9 us -> none  [to_heads(): parts = [a.reshape(tokens, devices, hd).transpose(1, 0, 2) for a in arrays]]
    concatenate x2 -> x0, other arithmetic: 2.75 us -> none  [to_heads(): sent = jnp.concatenate(parts, axis=2)]
    pallas_call x1 -> x6, Pallas kernels: 11.2 us -> 13 us  [the longest x1 8.78 us: attend(): pl.pallas_call(functools.partial(attend_kernel, sources=len(parts), hd=hd...]
    unnamed x12 -> x10, local copies, waits for them, and re-layouts: 2.9 us -> 3.65 us
  transfers between devices with their start and end apart: 3 -> 3, of which waited for: 3 -> 2; matrix products, arithmetic and copies ran while one was open for 3% -> 0% of each run, Pallas kernels for 0% -> 1%
where the time goes in v5:
time: 134 us; the launch traced here: 133 us
  waiting for transfers between devices  62.8 us (47%)
  blocking collectives  30.4 us (23%)
  starting transfers between devices  20.3 us (15%)
  Pallas kernels  13 us (10%)
  local copies, waits for them, and re-layouts  6.1 us (5%)
    all_to_all x2, waiting for transfers between devices, exchange(): lax.all_to_all(pieces, 'heads', split_axis=0, concat_axis=0, tiled=True)  38.8 us
    all_to_all x1, blocking collectives, per_device(): lax.all_to_all(pair, 'heads', split_axis=0, concat_axis=0, tiled=True)  30.4 us
    ppermute x1, waiting for transfers between devices, per_device(): lax.ppermute(edges[-1], 'frames', pairs + [(j, i) for i, j in pairs])  24 us
    all_to_all x2, starting transfers between devices, exchange(): lax.all_to_all(pieces, 'heads', split_axis=0, concat_axis=0, tiled=True)  18.7 us
    pallas_call x1, Pallas kernels, attend(): pl.pallas_call(functools.partial(attend_kernel, sources=len(parts), hd=hd...  8.78 us
    unnamed x10, local copies, waits for them, and re-layouts  3.65 us
    pallas_call x2, Pallas kernels, to_heads(): pl.pallas_call(functools.partial(pack_kernel, count=count, devices=device...  2.96 us
  transfers between devices with their start and end apart: 3, of which 2 were waited for; matrix products, arithmetic and copies ran while one was open for 0% of the time, Pallas kernels for 1%

profile of v5, /device:TPU:0, one launch (start us, length us, event | category | flops | bytes accessed | tf_op | source)
XLA Modules:
  0.0 133.3 jit_solution(1700903129783145017)
XLA Ops:
  0.6 1.6 %shard_map.87 = bf16[16,128,512]{2,1,0:T(8,128)(2,1)S(1)} custom-call(bf16[128,2048]{1,0:T(8,128)(2,1)} %refs_0_.3, bf16[128,2048]{1,0:T(8,128)(2,1)} %refs_1_.3, bf16[128,2048]{1,0:T(8,128)(2,1)} %refs_2_.1, bf16[128,2048]{1,0:T(8,128)(2,1)} %refs_3_.1), custom_call_target="tpu_custom_call" | custom-call | bytes 4194304 | tf_op jit(solution)/shard_map/pallas_call | solution.py:59
  2.3 0.0 copy-start.3
  2.3 1.3 copy-done.3
  3.6 7.4 %all-to-all-start = ((bf16[16,128,512]{2,1,0:T(8,128)(2,1)}), bf16[16,128,512]{2,1,0:T(8,128)(2,1)S(1)}, u32[]{:S(2)}, u32[]{:S(2)}) async-start(bf16[16,128,512]{2,1,0:T(8,128)(2,1)} %copy-done.3), calls=%async_computation | async-start | bytes 4194304 | tf_op jit(solution)/shard_map/all_to_all | solution.py:95
  11.0 1.3 shard_map.86.refs_1_.refs_0_
  12.3 0.0 copy-start
  12.3 1.0 copy-done
  13.3 38.8 %all-to-all-done = bf16[16,128,512]{2,1,0:T(8,128)(2,1)S(1)} async-done(((bf16[16,128,512]{2,1,0:T(8,128)(2,1)}), bf16[16,128,512]{2,1,0:T(8,128)(2,1)S(1)}, u32[]{:S(2)}, u32[]{:S(2)}) %all-to-all-start) | async-done | bytes 2097184 | tf_op jit(solution)/shard_map/all_to_all | solution.py:95
  52.1 0.0 copy-start.1
  52.1 1.3 %copy-done.1 = bf16[16,128,512]{2,1,0:T(8,128)(2,1)} copy-done((bf16[16,128,512]{2,1,0:T(8,128)(2,1)}, bf16[16,128,512]{2,1,0:T(8,128)(2,1)S(1)}, u32[]{:S(2)}) %copy-start.1) | copy-done | bytes 2097176
  53.4 2.3 %constant_dynamic-slice_fusion.refs_1_ = bf16[1024,512]{1,0:T(8,128)(2,1)} fusion(bf16[2048,512]{1,0:T(8,128)(2,1)} %shard_map.88.refs_0_, s32[]{:T(128)S(6)} %select_n.32), kind=kLoop, calls=%fused_computation.2 | loop fusion | bytes 2097156 | tf_op jit(solution)/shard_map/dynamic_slice | solution.py:192
  55.7 0.0 copy-start.4
  55.7 0.0 copy-start.2
  55.7 11.3 %all-to-all-start.1 = ((bf16[16,128,256]{2,1,0:T(8,128)(2,1)}), bf16[16,128,256]{2,1,0:T(8,128)(2,1)S(1)}, u32[]{:S(2)}, u32[]{:S(2)}) async-start(bf16[16,128,256]{2,1,0:T(8,128)(2,1)} %shard_map.89), calls=%async_computation.1 | async-start | bytes 2097152 | tf_op jit(solution)/shard_map/all_to_all | solution.py:95
  67.1 1.6 %collective-permute-start = (bf16[1024,512]{1,0:T(8,128)(2,1)}, bf16[1024,512]{1,0:T(8,128)(2,1)}, u32[]{:S(2)}, u32[]{:S(2)}) collective-permute-start(bf16[1024,512]{1,0:T(8,128)(2,1)} %constant_dynamic-slice_fusion.refs_1_), channel_id=1, source_target_pairs={{0,1},{1,0},{2,3},{3,2},{4,5},{5,4},{6,7},{7,6},{8,9},{9,8},{10,11... | collective-permute-start | bytes 3145736 | tf_op jit(solution)/shard_map/ppermute | solution.py:193
  68.7 0.0 copy-done.4
  68.7 0.1 copy.12
  68.8 0.1 reshape.16.table
  68.8 24.0 %collective-permute-done.refs_1_ = bf16[1024,512]{1,0:T(8,128)(2,1)} collective-permute-done((bf16[1024,512]{1,0:T(8,128)(2,1)}, bf16[1024,512]{1,0:T(8,128)(2,1)}, u32[]{:S(2)}, u32[]{:S(2)}) %collective-permute-start) | collective-permute-done | bytes 1048608 | tf_op jit(solution)/shard_map/ppermute | solution.py:193
  92.9 0.0 all-to-all-done.1
  92.9 0.0 copy-done.2
  92.9 8.8 %shard_map.90 = bf16[2048,256]{1,0:T(8,128)(2,1)S(1)} custom-call(s32[32]{0:T(128)S(1)} %reshape.16.table, bf16[2048,256]{1,0:T(8,128)(2,1)S(1)} %bitcast.4, bf16[2048,512]{1,0:T(8,128)(2,1)S(1)} %copy-done.2, bf16[1024,512]{1,0:T(8,128)(2,1)} %collective-permute-done.refs_1_), custom_call_target="tpu_custom_call" | custom-call | flops 3221225472 | bytes 5242880 | tf_op jit(solution)/shard_map/pallas_call | solution.py:151
  101.7 30.4 %all_to_all.15.piece = bf16[16,128,256]{2,1,0:T(8,128)(2,1)S(1)} all-to-all(bf16[16,128,256]{2,1,0:T(8,128)(2,1)S(1)} %bitcast.5), channel_id=1, replica_groups=mesh['heads'=16,'frames'=2] {'heads'}, dimensions={0} | all-to-all | bytes 2097152 | tf_op jit(solution)/shard_map/all_to_all | solution.py:198
  132.1 1.3 shard_map.91
  (3 shorter events, 0.0 us)
Async XLA Ops:
  2.3 1.3 %copy-start.3 = (bf16[16,128,512]{2,1,0:T(8,128)(2,1)}, bf16[16,128,512]{2,1,0:T(8,128)(2,1)S(1)}, u32[]{:S(2)}) copy-start(bf16[16,128,512]{2,1,0:T(8,128)(2,1)S(1)} %shard_map.87) | copy-start | bytes 6291460
  3.6 48.5 %all-to-all-start = ((bf16[16,128,512]{2,1,0:T(8,128)(2,1)}), bf16[16,128,512]{2,1,0:T(8,128)(2,1)S(1)}, u32[]{:S(2)}, u32[]{:S(2)}) async-start(bf16[16,128,512]{2,1,0:T(8,128)(2,1)} %copy-done.3), calls=%async_computation | async-start | bytes 4194304 | tf_op jit(solution)/shard_map/all_to_all | solution.py:95
  12.3 1.0 copy-start
  52.1 1.3 %copy-start.1 = (bf16[16,128,512]{2,1,0:T(8,128)(2,1)}, bf16[16,128,512]{2,1,0:T(8,128)(2,1)S(1)}, u32[]{:S(2)}) copy-start(bf16[16,128,512]{2,1,0:T(8,128)(2,1)S(1)} %all-to-all-done) | copy-start | bytes 6291460
  55.7 12.9 %copy-start.4 = (s32[8,4]{0,1:T(4,128)S(1)}, s32[8,4]{0,1:T(4,128)}, u32[]{:S(2)}) copy-start(s32[8,4]{0,1:T(4,128)} %param.13) | copy-start | bytes 388
  55.7 37.2 %copy-start.2 = (bf16[2048,512]{1,0:T(8,128)(2,1)S(1)}, bf16[2048,512]{1,0:T(8,128)(2,1)}, u32[]{:S(2)}) copy-start(bf16[2048,512]{1,0:T(8,128)(2,1)} %shard_map.88.refs_0_) | copy-start | bytes 6291460
  55.7 37.1 %all-to-all-start.1 = ((bf16[16,128,256]{2,1,0:T(8,128)(2,1)}), bf16[16,128,256]{2,1,0:T(8,128)(2,1)S(1)}, u32[]{:S(2)}, u32[]{:S(2)}) async-start(bf16[16,128,256]{2,1,0:T(8,128)(2,1)} %shard_map.89), calls=%async_computation.1 | async-start | bytes 2097152 | tf_op jit(solution)/shard_map/all_to_all | solution.py:95
  67.1 25.8 %collective-permute-start = (bf16[1024,512]{1,0:T(8,128)(2,1)}, bf16[1024,512]{1,0:T(8,128)(2,1)}, u32[]{:S(2)}, u32[]{:S(2)}) collective-permute-start(bf16[1024,512]{1,0:T(8,128)(2,1)} %constant_dynamic-slice_fusion.refs_1_), channel_id=1, source_target_pairs={{0,1},{1,0},{2,3},{3,2},{4,5},{5,4},{6,7},{7,6},{8,9},{9,8},{10,11... | collective-permute-start | bytes 3145736 | tf_op jit(solution)/shard_map/ppermute | solution.py:193

commit v6 on v5

--- a/solution.py
+++ b/solution.py
@@ -27,43 +27,47 @@
     return pl.CostEstimate(flops=0, bytes_accessed=size, transcendentals=0)
 
 
-def hold_kernel(*refs):
-    del refs
-
-
-def hold(array, others):
-    return pl.pallas_call(
-        hold_kernel,
-        in_specs=[ANY] * (1 + len(others)),
-        out_specs=ANY,
-        out_shape=jax.ShapeDtypeStruct(array.shape, array.dtype),
-        input_output_aliases={0: 0},
-    )(array, *others)
-
-
-def pack_kernel(*refs, count, devices):
-    arrays, out, held, sems = refs[:count], refs[count], refs[-2], refs[-1]
-    hd = held.shape[2] // devices
-    copies = [pltpu.make_async_copy(a, held.at[i], sems.at[i]) for i, a in enumerate(arrays)]
-    for copy in copies:
-        copy.start()
-    for a, copy in enumerate(copies):
-        copy.wait()
-        for h in range(devices):
-            out[h, :, a * hd : (a + 1) * hd] = held[a, :, h * hd : (h + 1) * hd]
-
-
-def to_heads(arrays, devices):
+def pack_kernel(*refs, count, chunks):
+    arrays, out = refs[:count], refs[count]
+    held, staged, sems, out_sems = refs[-4:]
+    devices, columns = out.shape[0], held.shape[2]
+    hd, heads, step = columns // devices, devices // chunks, columns // chunks
+    copies = {}
+    for c in range(chunks):
+        lanes = pl.ds(c * step, step)
+        for a, array in enumerate(arrays):
+            copies[c, a] = pltpu.make_async_copy(
+                array.at[:, lanes], held.at[a, :, lanes], sems.at[c, a]
+            )
+            copies[c, a].start()
+    sends = []
+    for c in range(chunks):
+        for a in range(count):
+            copies[c, a].wait()
+        for h in range(c * heads, (c + 1) * heads):
+            for a in range(count):
+                staged[h, :, a * hd : (a + 1) * hd] = held[a, :, h * hd : (h + 1) * hd]
+        part = pl.ds(c * heads, heads)
+        sends.append(pltpu.make_async_copy(staged.at[part], out.at[part], out_sems.at[c]))
+        sends[-1].start()
+    for send in sends:
+        send.wait()
+
+
+def to_heads(arrays, devices, chunks=4):
     tokens, columns = arrays[0].shape
     count, hd = len(arrays), columns // devices
-    return pl.pallas_call(
-        functools.partial(pack_kernel, count=count, devices=devices),
+    shape = (devices, tokens, count * hd)
+    return pl.pallas_call(
+        functools.partial(pack_kernel, count=count, chunks=chunks),
         in_specs=[HBM] * count,
-        out_specs=VMEM,
-        out_shape=jax.ShapeDtypeStruct((devices, tokens, count * hd), jnp.bfloat16),
+        out_specs=HBM,
+        out_shape=pltpu.HBM(shape, jnp.bfloat16),
         scratch_shapes=[
             pltpu.VMEM((count, tokens, columns), jnp.bfloat16),
-            pltpu.SemaphoreType.DMA((count,)),
+            pltpu.VMEM(shape, jnp.bfloat16),
+            pltpu.SemaphoreType.DMA((chunks, count)),
+            pltpu.SemaphoreType.DMA((chunks,)),
         ],
         compiler_params=PARAMS,
         cost_estimate=moves(4 * count * tokens * columns),
@@ -96,18 +100,53 @@
     return got.reshape(-1, got.shape[2])
 
 
-def attend_kernel(table, q_ref, *refs, sources, hd):
-    parts, out_ref, kv, sems = refs[:sources], refs[sources], refs[-2], refs[-1]
+def edge_kernel(start, kv, q_sent, out, sem):
+    del q_sent
+    first = pl.multiple_of(start[0] * BQ, BQ)
+    copy = pltpu.make_async_copy(kv.at[pl.ds(first, HALO)], out, sem)
+    copy.start()
+    copy.wait()
+
+
+def edge(start, kv, q_sent):
+    shape = (HALO, kv.shape[1])
+    return pl.pallas_call(
+        edge_kernel,
+        in_specs=[SMEM, ANY, ANY],
+        out_specs=HBM,
+        out_shape=pltpu.HBM(shape, jnp.bfloat16),
+        scratch_shapes=[pltpu.SemaphoreType.DMA(())],
+        cost_estimate=moves(4 * HALO * kv.shape[1]),
+    )(start, kv, q_sent)
+
+
+def join_kernel(*refs, sources):
+    parts, out, sems = refs[:sources], refs[sources], refs[-1]
     copies, row = [], 0
     for i, ref in enumerate(parts):
         rows = ref.shape[0]
-        copies.append(pltpu.make_async_copy(ref, kv.at[pl.ds(row, rows)], sems.at[i]))
+        copies.append(pltpu.make_async_copy(ref, out.at[pl.ds(row, rows)], sems.at[i]))
         row += rows
     for copy in copies:
         copy.start()
     for copy in copies:
         copy.wait()
 
+
+def join(parts):
+    total, width = sum(a.shape[0] for a in parts), parts[0].shape[1]
+    return pl.pallas_call(
+        functools.partial(join_kernel, sources=len(parts)),
+        in_specs=[ANY] * len(parts),
+        out_specs=VMEM,
+        out_shape=jax.ShapeDtypeStruct((total, width), jnp.bfloat16),
+        scratch_shapes=[pltpu.SemaphoreType.DMA((len(parts),))],
+        compiler_params=PARAMS,
+        cost_estimate=moves(200_000_000),
+    )(*parts)
+
+
+def attend_kernel(table, q_ref, kv, out_ref, *, hd):
     scale = hd ** (-0.5)
     factor = scale * math.log2(math.e)
     trans = (((1,), (1,)), ((), ()))
@@ -143,27 +182,22 @@
         out_ref[rows, hd:] = tan.astype(jnp.bfloat16)
 
 
-def attend(table, q_pair, parts):
+def attend(table, q_pair, kv):
     rows, width = q_pair.shape
     hd = width // 2
-    total = sum(a.shape[0] for a in parts)
     elements = rows * WK * BQ
     return pl.pallas_call(
-        functools.partial(attend_kernel, sources=len(parts), hd=hd),
-        in_specs=[SMEM, VMEM] + [ANY] * len(parts),
+        functools.partial(attend_kernel, hd=hd),
+        in_specs=[SMEM, VMEM, VMEM],
         out_specs=VMEM,
         out_shape=jax.ShapeDtypeStruct((rows, width), jnp.bfloat16),
-        scratch_shapes=[
-            pltpu.VMEM((total, 4 * hd), jnp.bfloat16),
-            pltpu.SemaphoreType.DMA((len(parts),)),
-        ],
         compiler_params=PARAMS,
         cost_estimate=pl.CostEstimate(
             flops=12 * elements * hd,
-            bytes_accessed=2 * (total * 4 * hd + 2 * rows * width),
+            bytes_accessed=2 * (kv.size + 2 * rows * width),
             transcendentals=elements,
         ),
-    )(table, q_pair, *parts)
+    )(table, q_pair, kv)
 
 
 def slots(neighbors, frame, blocks):
@@ -178,23 +212,22 @@
     devices, frames = lax.axis_size("heads"), lax.axis_size("frames")
     frame = lax.axis_index("frames")
     tokens = query.shape[0]
-    kv_sent = to_heads([keys_tan, keys, values, values_tan], devices)
+    kv = exchange(to_heads([keys_tan, keys, values, values_tan], devices))
     q_sent = to_heads([query, query_tan], devices)
-    kv = hold(exchange(kv_sent), [q_sent])
-    rows = kv.shape[0]
-
-    edges, parts = [], [kv]
+    blocks = neighbors.shape[0]
+
+    parts = [kv]
     for first in (0, 1):
         pairs = [(i, i + 1) for i in range(first, frames - 1, 2)]
-        if not pairs:
-            continue
-        start = jnp.where(frame % 2 == first, rows - HALO, 0)
-        edges.append(lax.dynamic_slice_in_dim(kv, start, HALO, axis=0))
-        parts.append(lax.ppermute(edges[-1], "frames", pairs + [(j, i) for i, j in pairs]))
-
-    q_pair = exchange(hold(q_sent, edges))
-    table = slots(neighbors, frame, neighbors.shape[0])
-    pair = attend(table, q_pair, parts).reshape(devices, tokens, -1)
+        if pairs:
+            start = jnp.where(frame % 2 == first, blocks - HB, 0).reshape(1).astype(jnp.int32)
+            outer = edge(start, kv, q_sent)
+            parts.append(lax.ppermute(outer, "frames", pairs + [(j, i) for i, j in pairs]))
+    kv = join(parts)
+
+    q_pair = exchange(q_sent)
+    table = slots(neighbors, frame, blocks)
+    pair = attend(table, q_pair, kv).reshape(devices, tokens, -1)
     back = lax.all_to_all(pair, "heads", split_axis=0, concat_axis=0, tiled=True)
     return from_heads(back, 2)
 

time: 134 us -> 166 us (1.24)
  Pallas kernels: 13 us -> 47.3 us
  local copies, waits for them, and re-layouts: 6.1 us -> 3.95 us
    pallas_call x5, Pallas kernels: 11.7 us -> 46.1 us  [the longest x1 32.9 us: edge(): pl.pallas_call(edge_kernel, in_specs=[SMEM, ANY, ANY], out_specs=HBM, out...]
    dynamic_slice x1 -> x0, local copies, waits for them, and re-layouts: 2.29 us -> none  [per_device(): edges.append(lax.dynamic_slice_in_dim(kv, start, HALO, axis=0))]
  transfers between devices with their start and end apart: 3 -> 3, of which waited for: 2 -> 2; matrix products, arithmetic and copies ran while one was open for 0% -> 0% of each run, Pallas kernels for 1% -> 21%
where the time goes in v6:
time: 166 us
  waiting for transfers between devices  62.9 us (38%)
  Pallas kernels  47.3 us (28%)
  blocking collectives  30.4 us (18%)
  starting transfers between devices  20.2 us (12%)
  local copies, waits for them, and re-layouts  3.95 us (2%)
    all_to_all x2, waiting for transfers between devices, exchange(): lax.all_to_all(pieces, 'heads', split_axis=0, concat_axis=0, tiled=True)  38.9 us
    pallas_call x1, Pallas kernels, edge(): pl.pallas_call(edge_kernel, in_specs=[SMEM, ANY, ANY], out_specs=HBM, out...  32.9 us
    all_to_all x1, blocking collectives, per_device(): lax.all_to_all(pair, 'heads', split_axis=0, concat_axis=0, tiled=True)  30.4 us
    ppermute x1, waiting for transfers between devices, per_device(): lax.ppermute(outer, 'frames', pairs + [(j, i) for i, j in pairs])  23.9 us
    all_to_all x2, starting transfers between devices, exchange(): lax.all_to_all(pieces, 'heads', split_axis=0, concat_axis=0, tiled=True)  18.6 us
    pallas_call x1, Pallas kernels, attend(): pl.pallas_call(functools.partial(attend_kernel, hd=hd), in_specs=[SMEM, V...  8.07 us
    pallas_call x2, Pallas kernels, to_heads(): pl.pallas_call(functools.partial(pack_kernel, count=count, chunks=chunks)...  4.91 us
    unnamed x10, local copies, waits for them, and re-layouts  3.79 us
  transfers between devices with their start and end apart: 3, of which 2 were waited for; matrix products, arithmetic and copies ran while one was open for 0% of the time, Pallas kernels for 21%

profile of v6, /device:TPU:0, one launch (start us, length us, event | category | flops | bytes accessed | tf_op | source)
XLA Modules:
  0.0 165.5 jit_solution(15643246583585439842)
XLA Ops:
  0.6 2.7 %shard_map.87 = bf16[16,128,512]{2,1,0:T(8,128)(2,1)} custom-call(bf16[128,2048]{1,0:T(8,128)(2,1)} %refs_0_.3, bf16[128,2048]{1,0:T(8,128)(2,1)} %refs_1_.3, bf16[128,2048]{1,0:T(8,128)(2,1)} %refs_2_.1, bf16[128,2048]{1,0:T(8,128)(2,1)} %refs_3_.1), custom_call_target="tpu_custom_call" | custom-call | bytes 4194304 | tf_op jit(solution)/shard_map/pallas_call | solution.py:61
  3.4 7.4 %all-to-all-start.1 = ((bf16[16,128,512]{2,1,0:T(8,128)(2,1)}), bf16[16,128,512]{2,1,0:T(8,128)(2,1)S(1)}, u32[]{:S(2)}, u32[]{:S(2)}) async-start(bf16[16,128,512]{2,1,0:T(8,128)(2,1)} %shard_map.87), calls=%async_computation.1 | async-start | bytes 4194304 | tf_op jit(solution)/shard_map/all_to_all | solution.py:99
  10.8 2.2 %shard_map.86.q_sent = bf16[16,128,256]{2,1,0:T(8,128)(2,1)} custom-call(bf16[128,2048]{1,0:T(8,128)(2,1)} %refs_0_.2, bf16[128,2048]{1,0:T(8,128)(2,1)} %refs_1_.2), custom_call_target="tpu_custom_call" | custom-call | bytes 2097152 | tf_op jit(solution)/shard_map/pallas_call | solution.py:61
  12.9 38.9 %all-to-all-done.1 = bf16[16,128,512]{2,1,0:T(8,128)(2,1)S(1)} async-done(((bf16[16,128,512]{2,1,0:T(8,128)(2,1)}), bf16[16,128,512]{2,1,0:T(8,128)(2,1)S(1)}, u32[]{:S(2)}, u32[]{:S(2)}) %all-to-all-start.1) | async-done | bytes 2097184 | tf_op jit(solution)/shard_map/all_to_all | solution.py:99
  51.9 0.0 copy-start
  51.9 11.3 %all-to-all-start = ((bf16[16,128,256]{2,1,0:T(8,128)(2,1)}), bf16[16,128,256]{2,1,0:T(8,128)(2,1)}, u32[]{:S(2)}, u32[]{:S(2)}) async-start(bf16[16,128,256]{2,1,0:T(8,128)(2,1)} %shard_map.86.q_sent), calls=%async_computation | async-start | bytes 2097152 | tf_op jit(solution)/shard_map/all_to_all | solution.py:99
  63.2 0.0 copy-done
  63.2 0.0 copy-start.4
  63.2 32.9 %shard_map.88 = bf16[1024,512]{1,0:T(8,128)(2,1)} custom-call(s32[1]{0:T(128)} %bitcast.2.start, bf16[2048,512]{1,0:T(8,128)(2,1)} %bitcast.4, bf16[16,128,256]{2,1,0:T(8,128)(2,1)} %shard_map.86.q_sent), custom_call_target="tpu_custom_call" | custom-call | bytes 2097152 | tf_op jit(solution)/shard_map/pallas_call | solution.py:113
  96.1 1.6 collective-permute-start
  97.7 0.0 copy-done.4
  97.7 0.1 copy.10
  97.7 0.1 reshape.19.table
  97.8 23.9 %collective-permute-done.refs_1_ = bf16[1024,512]{1,0:T(8,128)(2,1)S(1)} collective-permute-done((bf16[1024,512]{1,0:T(8,128)(2,1)}, bf16[1024,512]{1,0:T(8,128)(2,1)S(1)}, u32[]{:S(2)}, u32[]{:S(2)}) %collective-permute-start) | collective-permute-done | bytes 1048608 | tf_op jit(solution)/shard_map/ppermute | solution.py:225
  121.7 0.0 copy-start.2
  121.7 1.0 copy-done.2
  122.7 0.0 copy-start.1
  122.7 1.6 copy-done.1
  124.3 0.0 copy-start.3
  124.3 1.2 copy-done.3
  125.5 0.2 shard_map.89.kv
  125.8 0.0 all-to-all-done
  125.8 8.1 %shard_map.90 = bf16[2048,256]{1,0:T(8,128)(2,1)S(1)} custom-call(s32[32]{0:T(128)S(1)} %reshape.19.table, bf16[2048,256]{1,0:T(8,128)(2,1)} %bitcast.q_ref, bf16[3072,512]{1,0:T(8,128)(2,1)S(1)} %shard_map.89.kv), custom_call_target="tpu_custom_call" | custom-call | flops 3221225472 | bytes 5242880 | tf_op jit(solution)/shard_map/pallas_call | solution.py:189
  133.8 30.4 %all_to_all.15.piece = bf16[16,128,256]{2,1,0:T(8,128)(2,1)S(1)} all-to-all(bf16[16,128,256]{2,1,0:T(8,128)(2,1)S(1)} %bitcast.6), channel_id=1, replica_groups=mesh['heads'=16,'frames'=2] {'heads'}, dimensions={0} | all-to-all | bytes 2097152 | tf_op jit(solution)/shard_map/all_to_all | solution.py:231
  164.2 1.3 shard_map.91
  (1 shorter events, 0.0 us)
Async XLA Ops:
  3.4 48.5 %all-to-all-start.1 = ((bf16[16,128,512]{2,1,0:T(8,128)(2,1)}), bf16[16,128,512]{2,1,0:T(8,128)(2,1)S(1)}, u32[]{:S(2)}, u32[]{:S(2)}) async-start(bf16[16,128,512]{2,1,0:T(8,128)(2,1)} %shard_map.87), calls=%async_computation.1 | async-start | bytes 4194304 | tf_op jit(solution)/shard_map/all_to_all | solution.py:99
  51.9 11.3 %copy-start = (bf16[16,128,512]{2,1,0:T(8,128)(2,1)}, bf16[16,128,512]{2,1,0:T(8,128)(2,1)S(1)}, u32[]{:S(2)}) copy-start(bf16[16,128,512]{2,1,0:T(8,128)(2,1)S(1)} %all-to-all-done.1) | copy-start | bytes 6291460
  51.9 73.9 %all-to-all-start = ((bf16[16,128,256]{2,1,0:T(8,128)(2,1)}), bf16[16,128,256]{2,1,0:T(8,128)(2,1)}, u32[]{:S(2)}, u32[]{:S(2)}) async-start(bf16[16,128,256]{2,1,0:T(8,128)(2,1)} %shard_map.86.q_sent), calls=%async_computation | async-start | bytes 2097152 | tf_op jit(solution)/shard_map/all_to_all | solution.py:99
  63.2 34.5 %copy-start.4 = (s32[8,4]{0,1:T(4,128)S(1)}, s32[8,4]{0,1:T(4,128)}, u32[]{:S(2)}) copy-start(s32[8,4]{0,1:T(4,128)} %param.13) | copy-start | bytes 388
  96.1 25.7 %collective-permute-start = (bf16[1024,512]{1,0:T(8,128)(2,1)}, bf16[1024,512]{1,0:T(8,128)(2,1)S(1)}, u32[]{:S(2)}, u32[]{:S(2)}) collective-permute-start(bf16[1024,512]{1,0:T(8,128)(2,1)} %shard_map.88), channel_id=1, source_target_pairs={{0,1},{1,0},{2,3},{3,2},{4,5},{5,4},{6,7},{7,6},{8,9},{9,8},{10,11... | collective-permute-start | bytes 3145736 | tf_op jit(solution)/shard_map/ppermute | solution.py:225
  121.7 1.0 copy-start.2
  122.7 1.6 copy-start.1
  124.3 1.2 copy-start.3

commit v7 on v6

--- a/solution.py
+++ b/solution.py
@@ -100,57 +100,23 @@
     return got.reshape(-1, got.shape[2])
 
 
-def edge_kernel(start, kv, q_sent, out, sem):
-    del q_sent
-    first = pl.multiple_of(start[0] * BQ, BQ)
-    copy = pltpu.make_async_copy(kv.at[pl.ds(first, HALO)], out, sem)
-    copy.start()
-    copy.wait()
-
-
-def edge(start, kv, q_sent):
-    shape = (HALO, kv.shape[1])
-    return pl.pallas_call(
-        edge_kernel,
-        in_specs=[SMEM, ANY, ANY],
-        out_specs=HBM,
-        out_shape=pltpu.HBM(shape, jnp.bfloat16),
-        scratch_shapes=[pltpu.SemaphoreType.DMA(())],
-        cost_estimate=moves(4 * HALO * kv.shape[1]),
-    )(start, kv, q_sent)
-
-
-def join_kernel(*refs, sources):
-    parts, out, sems = refs[:sources], refs[sources], refs[-1]
+def attend_kernel(table, q_ref, *refs, sources, hd):
+    parts, out_ref, kv, sems = refs[:sources], refs[sources], refs[-2], refs[-1]
     copies, row = [], 0
     for i, ref in enumerate(parts):
         rows = ref.shape[0]
-        copies.append(pltpu.make_async_copy(ref, out.at[pl.ds(row, rows)], sems.at[i]))
+        copies.append(pltpu.make_async_copy(ref, kv.at[pl.ds(row, rows)], sems.at[i]))
         row += rows
     for copy in copies:
         copy.start()
     for copy in copies:
         copy.wait()
 
-
-def join(parts):
-    total, width = sum(a.shape[0] for a in parts), parts[0].shape[1]
-    return pl.pallas_call(
-        functools.partial(join_kernel, sources=len(parts)),
-        in_specs=[ANY] * len(parts),
-        out_specs=VMEM,
-        out_shape=jax.ShapeDtypeStruct((total, width), jnp.bfloat16),
-        scratch_shapes=[pltpu.SemaphoreType.DMA((len(parts),))],
-        compiler_params=PARAMS,
-        cost_estimate=moves(200_000_000),
-    )(*parts)
-
-
-def attend_kernel(table, q_ref, kv, out_ref, *, hd):
     scale = hd ** (-0.5)
     factor = scale * math.log2(math.e)
     trans = (((1,), (1,)), ((), ()))
-    for block in range(q_ref.shape[0] // BQ):
+
+    def products(block):
         both = q_ref[block * BQ : (block + 1) * BQ]
         query = both[:, :hd]
         starts = [pl.multiple_of(table[block * WK + w] * BQ, BQ) for w in range(WK)]
@@ -161,6 +127,9 @@
                 lax.dot_general(query, keys[:, hd:], trans, preferred_element_type=jnp.float32)
             )
             tans.append(lax.dot_general(both, keys, trans, preferred_element_type=jnp.float32))
+        return starts, scores, tans
+
+    def finish(block, starts, scores, tans):
         top = functools.reduce(jnp.maximum, scores)
         top = jnp.max(top, axis=1, keepdims=True) * factor
         probs = [jnp.exp2(s * factor - top) for s in scores]
@@ -181,23 +150,36 @@
         out_ref[rows, :hd] = out.astype(jnp.bfloat16)
         out_ref[rows, hd:] = tan.astype(jnp.bfloat16)
 
-
-def attend(table, q_pair, kv):
+    blocks = q_ref.shape[0] // BQ
+    ahead = products(0)
+    for block in range(blocks):
+        current = ahead
+        if block + 1 < blocks:
+            ahead = products(block + 1)
+        finish(block, *current)
+
+
+def attend(table, q_pair, parts):
     rows, width = q_pair.shape
     hd = width // 2
+    total = sum(a.shape[0] for a in parts)
     elements = rows * WK * BQ
     return pl.pallas_call(
-        functools.partial(attend_kernel, hd=hd),
-        in_specs=[SMEM, VMEM, VMEM],
+        functools.partial(attend_kernel, sources=len(parts), hd=hd),
+        in_specs=[SMEM, VMEM] + [ANY] * len(parts),
         out_specs=VMEM,
         out_shape=jax.ShapeDtypeStruct((rows, width), jnp.bfloat16),
+        scratch_shapes=[
+            pltpu.VMEM((total, 4 * hd), jnp.bfloat16),
+            pltpu.SemaphoreType.DMA((len(parts),)),
+        ],
         compiler_params=PARAMS,
         cost_estimate=pl.CostEstimate(
             flops=12 * elements * hd,
-            bytes_accessed=2 * (kv.size + 2 * rows * width),
+            bytes_accessed=2 * (total * 4 * hd + 2 * rows * width),
             transcendentals=elements,
         ),
-    )(table, q_pair, kv)
+    )(table, q_pair, *parts)
 
 
 def slots(neighbors, frame, blocks):
@@ -213,21 +195,19 @@
     frame = lax.axis_index("frames")
     tokens = query.shape[0]
     kv = exchange(to_heads([keys_tan, keys, values, values_tan], devices))
-    q_sent = to_heads([query, query_tan], devices)
-    blocks = neighbors.shape[0]
+    rows = kv.shape[0]
 
     parts = [kv]
     for first in (0, 1):
         pairs = [(i, i + 1) for i in range(first, frames - 1, 2)]
         if pairs:
-            start = jnp.where(frame % 2 == first, blocks - HB, 0).reshape(1).astype(jnp.int32)
-            outer = edge(start, kv, q_sent)
-            parts.append(lax.ppermute(outer, "frames", pairs + [(j, i) for i, j in pairs]))
-    kv = join(parts)
-
-    q_pair = exchange(q_sent)
-    table = slots(neighbors, frame, blocks)
-    pair = attend(table, q_pair, kv).reshape(devices, tokens, -1)
+            start = jnp.where(frame % 2 == first, rows - HALO, 0)
+            edge = lax.dynamic_slice_in_dim(kv, start, HALO, axis=0)
+            parts.append(lax.ppermute(edge, "frames", pairs + [(j, i) for i, j in pairs]))
+
+    q_pair = exchange(to_heads([query, query_tan], devices))
+    table = slots(neighbors, frame, neighbors.shape[0])
+    pair = attend(table, q_pair, parts).reshape(devices, tokens, -1)
     back = lax.all_to_all(pair, "heads", split_axis=0, concat_axis=0, tiled=True)
     return from_heads(back, 2)
 

time: 166 us -> 130 us (0.78)
  Pallas kernels: 47.3 us -> 13.8 us
  local copies, waits for them, and re-layouts: 3.95 us -> 1.22 us
    pallas_call x3 -> x1, Pallas kernels: 41.2 us -> 7.68 us  [attend(): pl.pallas_call(functools.partial(attend_kernel, sources=len(parts), hd=hd...]
    all_to_all x2, waiting for transfers between devices: 38.9 us -> 59.1 us  [exchange(): lax.all_to_all(pieces, 'heads', split_axis=0, concat_axis=0, tiled=True)]
    ppermute x1, waiting for transfers between devices: 23.9 us -> 3.89 us  [per_device(): lax.ppermute(edge, 'frames', pairs + [(j, i) for i, j in pairs])]
    unnamed x10 -> x2, local copies, waits for them, and re-layouts: 3.79 us -> 0.01 us
  transfers between devices with their start and end apart: 3 -> 3, of which waited for: 2 -> 3; matrix products, arithmetic and copies ran while one was open for 0% -> 1% of each run, Pallas kernels for 21% -> 2%
where the time goes in v7:
time: 130 us; the launch traced here: 129 us
  waiting for transfers between devices  63 us (48%)
  blocking collectives  30.4 us (23%)
  starting transfers between devices  20.1 us (15%)
  Pallas kernels  13.8 us (11%)
    all_to_all x2, waiting for transfers between devices, exchange(): lax.all_to_all(pieces, 'heads', split_axis=0, concat_axis=0, tiled=True)  59.1 us
    all_to_all x1, blocking collectives, per_device(): lax.all_to_all(pair, 'heads', split_axis=0, concat_axis=0, tiled=True)  30.4 us
    all_to_all x2, starting transfers between devices, exchange(): lax.all_to_all(pieces, 'heads', split_axis=0, concat_axis=0, tiled=True)  18.6 us
    pallas_call x1, Pallas kernels, attend(): pl.pallas_call(functools.partial(attend_kernel, sources=len(parts), hd=hd...  7.68 us
    pallas_call x2, Pallas kernels, to_heads(): pl.pallas_call(functools.partial(pack_kernel, count=count, chunks=chunks)...  4.91 us
    ppermute x1, waiting for transfers between devices, per_device(): lax.ppermute(edge, 'frames', pairs + [(j, i) for i, j in pairs])  3.89 us
  transfers between devices with their start and end apart: 3, of which 3 were waited for; matrix products, arithmetic and copies ran while one was open for 1% of the time, Pallas kernels for 2%

profile of v7, /device:TPU:0, one launch (start us, length us, event | category | flops | bytes accessed | tf_op | source)
XLA Modules:
  0.0 129.3 jit_solution(17924476517885148096)
XLA Ops:
  0.6 2.7 %shard_map.87 = bf16[16,128,512]{2,1,0:T(8,128)(2,1)} custom-call(bf16[128,2048]{1,0:T(8,128)(2,1)} %refs_0_.3, bf16[128,2048]{1,0:T(8,128)(2,1)} %refs_1_.3, bf16[128,2048]{1,0:T(8,128)(2,1)} %refs_2_.1, bf16[128,2048]{1,0:T(8,128)(2,1)} %refs_3_.1), custom_call_target="tpu_custom_call" | custom-call | bytes 4194304 | tf_op jit(solution)/shard_map/pallas_call | solution.py:61
  3.4 7.4 %all-to-all-start.1 = ((bf16[16,128,512]{2,1,0:T(8,128)(2,1)}), bf16[16,128,512]{2,1,0:T(8,128)(2,1)S(1)}, u32[]{:S(2)}, u32[]{:S(2)}) async-start(bf16[16,128,512]{2,1,0:T(8,128)(2,1)} %shard_map.87), calls=%async_computation.1 | async-start | bytes 4194304 | tf_op jit(solution)/shard_map/all_to_all | solution.py:99
  10.8 2.2 %shard_map.86 = bf16[16,128,256]{2,1,0:T(8,128)(2,1)} custom-call(bf16[128,2048]{1,0:T(8,128)(2,1)} %refs_0_.2, bf16[128,2048]{1,0:T(8,128)(2,1)} %refs_1_.2), custom_call_target="tpu_custom_call" | custom-call | bytes 2097152 | tf_op jit(solution)/shard_map/pallas_call | solution.py:61
  12.9 0.0 copy-start
  12.9 38.9 %all-to-all-done.1 = bf16[16,128,512]{2,1,0:T(8,128)(2,1)S(1)} async-done(((bf16[16,128,512]{2,1,0:T(8,128)(2,1)}), bf16[16,128,512]{2,1,0:T(8,128)(2,1)S(1)}, u32[]{:S(2)}, u32[]{:S(2)}) %all-to-all-start.1) | async-done | bytes 2097184 | tf_op jit(solution)/shard_map/all_to_all | solution.py:99
  51.9 11.2 %all-to-all-start = ((bf16[16,128,256]{2,1,0:T(8,128)(2,1)}), bf16[16,128,256]{2,1,0:T(8,128)(2,1)S(1)}, u32[]{:S(2)}, u32[]{:S(2)}) async-start(bf16[16,128,256]{2,1,0:T(8,128)(2,1)} %shard_map.86), calls=%async_computation | async-start | bytes 2097152 | tf_op jit(solution)/shard_map/all_to_all | solution.py:99
  63.1 1.0 constant_dynamic-slice_fusion
  64.2 1.5 %collective-permute-start = (bf16[1024,512]{1,0:T(8,128)(2,1)}, bf16[1024,512]{1,0:T(8,128)(2,1)}, u32[]{:S(2)}, u32[]{:S(2)}) collective-permute-start(bf16[1024,512]{1,0:T(8,128)(2,1)} %constant_dynamic-slice_fusion), channel_id=1, source_target_pairs={{0,1},{1,0},{2,3},{3,2},{4,5},{5,4},{6,7},{7,6},{8,9},{9,8},{10,11... | collective-permute-start | bytes 3145736 | tf_op jit(solution)/shard_map/ppermute | solution.py:206
  65.7 0.0 copy-done
  65.7 0.1 copy.10
  65.8 0.1 reshape.16.table
  65.9 20.2 %all-to-all-done = bf16[16,128,256]{2,1,0:T(8,128)(2,1)S(1)} async-done(((bf16[16,128,256]{2,1,0:T(8,128)(2,1)}), bf16[16,128,256]{2,1,0:T(8,128)(2,1)S(1)}, u32[]{:S(2)}, u32[]{:S(2)}) %all-to-all-start) | async-done | bytes 1048608 | tf_op jit(solution)/shard_map/all_to_all | solution.py:99
  86.0 3.9 %collective-permute-done.refs_1_ = bf16[1024,512]{1,0:T(8,128)(2,1)} collective-permute-done((bf16[1024,512]{1,0:T(8,128)(2,1)}, bf16[1024,512]{1,0:T(8,128)(2,1)}, u32[]{:S(2)}, u32[]{:S(2)}) %collective-permute-start) | collective-permute-done | bytes 1048608 | tf_op jit(solution)/shard_map/ppermute | solution.py:206
  89.9 7.7 %shard_map.88 = bf16[2048,256]{1,0:T(8,128)(2,1)S(1)} custom-call(s32[32]{0:T(128)S(1)} %reshape.16.table, bf16[2048,256]{1,0:T(8,128)(2,1)S(1)} %bitcast.5, bf16[2048,512]{1,0:T(8,128)(2,1)S(1)} %bitcast.4, bf16[1024,512]{1,0:T(8,128)(2,1)} %collective-permute-done.refs_1_), custom_call_target="tpu_custom_call" | custom-call | flops 3221225472 | bytes 5242880 | tf_op jit(solution)/shard_map/pallas_call | solution.py:167
  97.6 30.4 %all_to_all.15.piece = bf16[16,128,256]{2,1,0:T(8,128)(2,1)S(1)} all-to-all(bf16[16,128,256]{2,1,0:T(8,128)(2,1)S(1)} %bitcast.6), channel_id=1, replica_groups=mesh['heads'=16,'frames'=2] {'heads'}, dimensions={0} | all-to-all | bytes 2097152 | tf_op jit(solution)/shard_map/all_to_all | solution.py:211
  128.0 1.3 shard_map.89
  (1 shorter events, 0.0 us)
Async XLA Ops:
  3.4 48.5 %all-to-all-start.1 = ((bf16[16,128,512]{2,1,0:T(8,128)(2,1)}), bf16[16,128,512]{2,1,0:T(8,128)(2,1)S(1)}, u32[]{:S(2)}, u32[]{:S(2)}) async-start(bf16[16,128,512]{2,1,0:T(8,128)(2,1)} %shard_map.87), calls=%async_computation.1 | async-start | bytes 4194304 | tf_op jit(solution)/shard_map/all_to_all | solution.py:99
  12.9 52.8 %copy-start = (s32[8,4]{0,1:T(4,128)S(1)}, s32[8,4]{0,1:T(4,128)}, u32[]{:S(2)}) copy-start(s32[8,4]{0,1:T(4,128)} %param.13) | copy-start | bytes 388
  51.9 34.2 %all-to-all-start = ((bf16[16,128,256]{2,1,0:T(8,128)(2,1)}), bf16[16,128,256]{2,1,0:T(8,128)(2,1)S(1)}, u32[]{:S(2)}, u32[]{:S(2)}) async-start(bf16[16,128,256]{2,1,0:T(8,128)(2,1)} %shard_map.86), calls=%async_computation | async-start | bytes 2097152 | tf_op jit(solution)/shard_map/all_to_all | solution.py:99
  64.2 25.8 %collective-permute-start = (bf16[1024,512]{1,0:T(8,128)(2,1)}, bf16[1024,512]{1,0:T(8,128)(2,1)}, u32[]{:S(2)}, u32[]{:S(2)}) collective-permute-start(bf16[1024,512]{1,0:T(8,128)(2,1)} %constant_dynamic-slice_fusion), channel_id=1, source_target_pairs={{0,1},{1,0},{2,3},{3,2},{4,5},{5,4},{6,7},{7,6},{8,9},{9,8},{10,11... | collective-permute-start | bytes 3145736 | tf_op jit(solution)/shard_map/ppermute | solution.py:206

commit v8 on v7

--- a/solution.py
+++ b/solution.py
@@ -74,25 +74,29 @@
     )(*pin(*arrays))
 
 
-def unpack_kernel(piece, *arrays):
-    devices, tokens, width = piece.shape
+def unpack_kernel(me, near, *refs):
+    half, _, width = near.shape
+    pieces, arrays = refs[:half], refs[half:]
     hd = width // len(arrays)
-    for h in range(devices):
+    heads = [((me[0] // half) * half + i, near.at[i]) for i in range(half)]
+    heads += [(me[0] ^ (half + i), pieces[i]) for i in range(half)]
+    for head, piece in heads:
+        columns = pl.ds(pl.multiple_of(head * hd, hd), hd)
         for a, array in enumerate(arrays):
-            array[:, h * hd : (h + 1) * hd] = piece[h, :, a * hd : (a + 1) * hd]
-
-
-def from_heads(pieces, count):
-    devices, tokens, width = pieces.shape
-    columns = devices * width // count
+            array[:, columns] = piece[:, a * hd : (a + 1) * hd]
+
+
+def from_heads(me, near, far, count):
+    half, tokens, width = near.shape
+    columns = 2 * half * width // count
     return pl.pallas_call(
         unpack_kernel,
-        in_specs=[VMEM],
+        in_specs=[SMEM] + [VMEM] * (1 + half),
         out_specs=[VMEM] * count,
         out_shape=[jax.ShapeDtypeStruct((tokens, columns), jnp.bfloat16)] * count,
         compiler_params=PARAMS,
-        cost_estimate=moves(4 * pieces.size),
-    )(pieces)
+        cost_estimate=moves(8 * near.size),
+    )(me, near, *far)
 
 
 def exchange(pieces):
@@ -100,8 +104,15 @@
     return got.reshape(-1, got.shape[2])
 
 
-def attend_kernel(table, q_ref, *refs, sources, hd):
-    parts, out_ref, kv, sems = refs[:sources], refs[sources], refs[-2], refs[-1]
+def attend_kernel(me, table, q_ref, *refs, sources, later, tokens, far, hd):
+    parts, outs = refs[:sources], refs[sources + later : -3]
+    kv, held, sems = refs[-3:]
+    count, per = q_ref.shape[0] // BQ // 2, BQ // tokens
+    chip, core = me[0] // per, me[0] % per
+    if far:
+        blocks = [chip ^ (count + i) for i in range(count)]
+    else:
+        blocks = [(chip // count) * count + i for i in range(count)]
     copies, row = [], 0
     for i, ref in enumerate(parts):
         rows = ref.shape[0]
@@ -117,7 +128,7 @@
     trans = (((1,), (1,)), ((), ()))
 
     def products(block):
-        both = q_ref[block * BQ : (block + 1) * BQ]
+        both = q_ref[pl.ds(pl.multiple_of(block * BQ, BQ), BQ)]
         query = both[:, :hd]
         starts = [pl.multiple_of(table[block * WK + w] * BQ, BQ) for w in range(WK)]
         scores, tans = [], []
@@ -129,7 +140,7 @@
             tans.append(lax.dot_general(both, keys, trans, preferred_element_type=jnp.float32))
         return starts, scores, tans
 
-    def finish(block, starts, scores, tans):
+    def finish(i, starts, scores, tans):
         top = functools.reduce(jnp.maximum, scores)
         top = jnp.max(top, axis=1, keepdims=True) * factor
         probs = [jnp.exp2(s * factor - top) for s in scores]
@@ -146,31 +157,38 @@
         inverse = 1.0 / total
         out = main[:, :hd] * inverse
         tan = (main[:, hd:] + scale * side) * inverse - (scale * mean * inverse) * out
-        rows = slice(block * BQ, (block + 1) * BQ)
-        out_ref[rows, :hd] = out.astype(jnp.bfloat16)
-        out_ref[rows, hd:] = tan.astype(jnp.bfloat16)
-
-    blocks = q_ref.shape[0] // BQ
-    ahead = products(0)
-    for block in range(blocks):
+        rows = held.at[i] if far else outs[0].at[i * BQ : (i + 1) * BQ]
+        rows[:, :hd] = out.astype(jnp.bfloat16)
+        rows[:, hd:] = tan.astype(jnp.bfloat16)
+        if far:
+            for p in range(per):
+                start = pl.multiple_of((core ^ p) * tokens, tokens)
+                outs[i * per + p][...] = held[i, pl.ds(start, tokens)]
+
+    ahead = products(blocks[0])
+    for i in range(count):
         current = ahead
-        if block + 1 < blocks:
-            ahead = products(block + 1)
-        finish(block, *current)
-
-
-def attend(table, q_pair, parts):
+        if i + 1 < count:
+            ahead = products(blocks[i + 1])
+        finish(i, *current)
+
+
+def attend(me, table, q_pair, parts, later, tokens, far):
     rows, width = q_pair.shape
-    hd = width // 2
+    hd, half = width // 2, rows // 2
     total = sum(a.shape[0] for a in parts)
-    elements = rows * WK * BQ
+    elements = half * WK * BQ
+    sizes = [tokens] * (half // tokens) if far else [half]
     return pl.pallas_call(
-        functools.partial(attend_kernel, sources=len(parts), hd=hd),
-        in_specs=[SMEM, VMEM] + [ANY] * len(parts),
-        out_specs=VMEM,
-        out_shape=jax.ShapeDtypeStruct((rows, width), jnp.bfloat16),
+        functools.partial(
+            attend_kernel, sources=len(parts), later=len(later), tokens=tokens, far=far, hd=hd
+        ),
+        in_specs=[SMEM, SMEM, VMEM] + [ANY] * (len(parts) + len(later)),
+        out_specs=[VMEM] * len(sizes),
+        out_shape=[jax.ShapeDtypeStruct((size, width), jnp.bfloat16) for size in sizes],
         scratch_shapes=[
             pltpu.VMEM((total, 4 * hd), jnp.bfloat16),
+            pltpu.VMEM((half // BQ, BQ, width), jnp.bfloat16),
             pltpu.SemaphoreType.DMA((len(parts),)),
         ],
         compiler_params=PARAMS,
@@ -179,7 +197,7 @@
             bytes_accessed=2 * (total * 4 * hd + 2 * rows * width),
             transcendentals=elements,
         ),
-    )(table, q_pair, *parts)
+    )(me, table, q_pair, *parts, *later)
 
 
 def slots(neighbors, frame, blocks):
@@ -207,9 +225,22 @@
 
     q_pair = exchange(to_heads([query, query_tan], devices))
     table = slots(neighbors, frame, neighbors.shape[0])
-    pair = attend(table, q_pair, parts).reshape(devices, tokens, -1)
-    back = lax.all_to_all(pair, "heads", split_axis=0, concat_axis=0, tiled=True)
-    return from_heads(back, 2)
+    me = lax.axis_index("heads").reshape(1).astype(jnp.int32)
+    half = devices // 2
+    pieces = attend(me, table, q_pair, parts, [], tokens, True)
+    far = []
+    for i, piece in enumerate(pieces):
+        far.append(lax.ppermute(piece, "heads", [(d, d ^ (half + i)) for d in range(devices)]))
+    (near,) = attend(me, table, q_pair, parts, far[:2], tokens, False)
+    near = lax.all_to_all(
+        near.reshape(half, tokens, -1),
+        "heads",
+        split_axis=0,
+        concat_axis=0,
+        axis_index_groups=[list(range(half)), list(range(half, devices))],
+        tiled=True,
+    )
+    return from_heads(me, near, far, 2)
 
 
 def solution(mesh):

time: 130 us -> 138 us (1.062)
  the two profiles are of different devices: /device:TPU:0 before, /device:TPU:9 now
where the time goes in v8:
time: 138 us; the launch traced here: 137 us
  waiting for transfers between devices  85.4 us (62%)
  starting transfers between devices  31.7 us (23%)
  Pallas kernels  16.2 us (12%)
  local copies, waits for them, and re-layouts  3.25 us (2%)
    all_to_all x2, waiting for transfers between devices, exchange(): lax.all_to_all(pieces, 'heads', split_axis=0, concat_axis=0, tiled=True)  66.2 us
    ppermute x8, waiting for transfers between devices, per_device(): lax.ppermute(piece, 'heads', [(d, d ^ half + i) for d in range(devices)])  18.3 us
    all_to_all x2, starting transfers between devices, exchange(): lax.all_to_all(pieces, 'heads', split_axis=0, concat_axis=0, tiled=True)  12.9 us
    ppermute x8, starting transfers between devices, per_device(): lax.ppermute(piece, 'heads', [(d, d ^ half + i) for d in range(devices)])  11.4 us
    pallas_call x2, Pallas kernels, attend(): pl.pallas_call(functools.partial(attend_kernel, sources=len(parts), later...  10 us
    all_to_all x1, starting transfers between devices, per_device(): lax.all_to_all(near.reshape(half, tokens, -1), 'heads', split_axis=0, con...  6.15 us
    pallas_call x2, Pallas kernels, to_heads(): pl.pallas_call(functools.partial(pack_kernel, count=count, chunks=chunks)...  4.89 us
  transfers between devices with their start and end apart: 12, of which 11 were waited for; matrix products, arithmetic and copies ran while one was open for 1% of the time, Pallas kernels for 2%

profile of v8, /device:TPU:9, one launch (start us, length us, event | category | flops | bytes accessed | tf_op | source)
XLA Modules:
  0.0 137.3 jit_solution(14592674981908956912)
XLA Ops:
  0.6 2.7 %shard_map.87 = bf16[16,128,512]{2,1,0:T(8,128)(2,1)} custom-call(bf16[128,2048]{1,0:T(8,128)(2,1)} %refs_0_.3, bf16[128,2048]{1,0:T(8,128)(2,1)} %refs_1_.3, bf16[128,2048]{1,0:T(8,128)(2,1)} %refs_2_.1, bf16[128,2048]{1,0:T(8,128)(2,1)} %refs_3_.1), custom_call_target="tpu_custom_call" | custom-call | bytes 4194304 | tf_op jit(solution)/shard_map/pallas_call | solution.py:61
  3.4 6.6 %all-to-all-start.1 = ((bf16[16,128,512]{2,1,0:T(8,128)(2,1)}), bf16[16,128,512]{2,1,0:T(8,128)(2,1)S(1)}, u32[]{:S(2)}, u32[]{:S(2)}) async-start(bf16[16,128,512]{2,1,0:T(8,128)(2,1)} %shard_map.87), calls=%async_computation.1 | async-start | bytes 4194304 | tf_op jit(solution)/shard_map/all_to_all | solution.py:103
  10.0 2.2 %shard_map.86 = bf16[16,128,256]{2,1,0:T(8,128)(2,1)} custom-call(bf16[128,2048]{1,0:T(8,128)(2,1)} %refs_0_.2, bf16[128,2048]{1,0:T(8,128)(2,1)} %refs_1_.2), custom_call_target="tpu_custom_call" | custom-call | bytes 2097152 | tf_op jit(solution)/shard_map/pallas_call | solution.py:61
  12.1 0.0 copy-start.3
  12.1 43.8 %all-to-all-done.1 = bf16[16,128,512]{2,1,0:T(8,128)(2,1)S(1)} async-done(((bf16[16,128,512]{2,1,0:T(8,128)(2,1)}), bf16[16,128,512]{2,1,0:T(8,128)(2,1)S(1)}, u32[]{:S(2)}, u32[]{:S(2)}) %all-to-all-start.1) | async-done | bytes 2097184 | tf_op jit(solution)/shard_map/all_to_all | solution.py:103
  56.0 6.3 %all-to-all-start = ((bf16[16,128,256]{2,1,0:T(8,128)(2,1)}), bf16[16,128,256]{2,1,0:T(8,128)(2,1)S(1)}, u32[]{:S(2)}, u32[]{:S(2)}) async-start(bf16[16,128,256]{2,1,0:T(8,128)(2,1)} %shard_map.86), calls=%async_computation | async-start | bytes 2097152 | tf_op jit(solution)/shard_map/all_to_all | solution.py:103
  62.3 1.1 constant_dynamic-slice_fusion
  63.4 1.2 collective-permute-start
  64.6 0.0 copy-done.3
  64.6 0.1 copy.10
  64.7 0.1 reshape.20.table
  64.8 22.4 %all-to-all-done = bf16[16,128,256]{2,1,0:T(8,128)(2,1)S(1)} async-done(((bf16[16,128,256]{2,1,0:T(8,128)(2,1)}), bf16[16,128,256]{2,1,0:T(8,128)(2,1)S(1)}, u32[]{:S(2)}, u32[]{:S(2)}) %all-to-all-start) | async-done | bytes 1048608 | tf_op jit(solution)/shard_map/all_to_all | solution.py:103
  87.1 0.9 collective-permute-done.refs_1_
  88.1 5.0 %shard_map.88 = (bf16[128,256]{1,0:T(8,128)(2,1)S(1)}, bf16[128,256]{1,0:T(8,128)(2,1)S(1)}, bf16[128,256]{1,0:T(8,128)(2,1)S(1)}, bf16[128,256]{1,0:T(8,128)(2,...) custom-call(s32[1]{0:T(128)} %bitcast.me, ...), custom_call_target="tpu_custom_call" | custom-call | flops 1610612736 | bytes 5242880 | tf_op jit(solution)/shard_map/pallas_call | solution.py:182
  93.1 0.0 copy-start.1
  93.1 0.6 copy-done.1
  93.7 0.0 copy-start.2
  93.7 0.6 copy-done.2
  94.4 2.1 %collective-permute-start.1 = (bf16[128,256]{1,0:T(8,128)(2,1)S(1)}, bf16[128,256]{1,0:T(8,128)(2,1)S(1)}, u32[]{:S(2)}, u32[]{:S(2)}) collective-permute-start(bf16[128,256]{1,0:T(8,128)(2,1)S(1)} %get-tuple-element.10), channel_id=1, source_target_pairs={{0,16},{2,18},{4,20},{6,22},{8,24},{10,26},{12,28},{14,30},{16,0},... | collective-permute-start | bytes 196616 | tf_op jit(solution)/shard_map/ppermute | solution.py:233
  96.4 1.6 %collective-permute-start.2 = (bf16[128,256]{1,0:T(8,128)(2,1)S(1)}, bf16[128,256]{1,0:T(8,128)(2,1)S(1)}, u32[]{:S(2)}, u32[]{:S(2)}) collective-permute-start(bf16[128,256]{1,0:T(8,128)(2,1)S(1)} %get-tuple-element.11), channel_id=1, source_target_pairs={{0,18},{2,16},{4,22},{6,20},{8,26},{10,24},{12,30},{14,28},{16,2},... | collective-permute-start | bytes 196616 | tf_op jit(solution)/shard_map/ppermute | solution.py:233
  98.1 0.3 collective-permute-done.1.refs_2_.refs_0_
  98.4 3.5 %collective-permute-done.2.refs_3_.refs_1_ = bf16[128,256]{1,0:T(8,128)(2,1)S(1)} collective-permute-done((bf16[128,256]{1,0:T(8,128)(2,1)S(1)}, bf16[128,256]{1,0:T(8,128)(2,1)S(1)}, u32[]{:S(2)}, u32[]{:S(2)}) %collective-permute-start.2) | collective-permute-done | bytes 65568 | tf_op jit(solution)/shard_map/ppermute | solution.py:233
  101.9 5.0 %shard_map.89 = bf16[1024,256]{1,0:T(8,128)(2,1)S(1)} custom-call(s32[1]{0:T(128)} %bitcast.me, s32[32]{0:T(128)S(1)} %reshape.20.table, bf16[2048,256]{1,0:T(8,128)(2,1)S(1)} %bitcast.8, bf16[2048,512]{1,0:T(8,128)(2,1)S(1)} %bitcast.6, bf16[1024,512]{1,0:T(8,128)(2,1)} %collective-permute-done.refs_1_, ...), custom_call_target="tpu_custom_call" | custom-call | flops 1610612736 | bytes 5242880 | tf_op jit(solution)/shard_map/pallas_call | solution.py:182
  106.9 0.0 copy-start
  106.9 0.8 copy-done
  107.7 6.1 %all-to-all-start.2 = ((bf16[8,128,256]{2,1,0:T(8,128)(2,1)}), bf16[8,128,256]{2,1,0:T(8,128)(2,1)S(1)}, u32[]{:S(2)}, u32[]{:S(2)}) async-start(bf16[8,128,256]{2,1,0:T(8,128)(2,1)} %bitcast.9), calls=%async_computation.2 | async-start | bytes 1048576 | tf_op jit(solution)/shard_map/all_to_all | solution.py:235
  113.8 2.4 %collective-permute-start.3 = (bf16[128,256]{1,0:T(8,128)(2,1)}, bf16[128,256]{1,0:T(8,128)(2,1)S(1)}, u32[]{:S(2)}, u32[]{:S(2)}) collective-permute-start(bf16[128,256]{1,0:T(8,128)(2,1)} %copy-done.2), channel_id=1, source_target_pairs={{0,20},{2,22},{4,16},{6,18},{8,28},{10,30},{12,24},{14,26},{16,4},... | collective-permute-start | bytes 196616 | tf_op jit(solution)/shard_map/ppermute | solution.py:233
  116.2 1.4 %collective-permute-start.4 = (bf16[128,256]{1,0:T(8,128)(2,1)}, bf16[128,256]{1,0:T(8,128)(2,1)S(1)}, u32[]{:S(2)}, u32[]{:S(2)}) collective-permute-start(bf16[128,256]{1,0:T(8,128)(2,1)} %copy-done.1), channel_id=1, source_target_pairs={{0,22},{2,20},{4,18},{6,16},{8,30},{10,28},{12,26},{14,24},{16,6},... | collective-permute-start | bytes 196616 | tf_op jit(solution)/shard_map/ppermute | solution.py:233
  117.6 0.1 collective-permute-start.5
  117.7 1.5 %collective-permute-start.6 = (bf16[128,256]{1,0:T(8,128)(2,1)S(1)}, bf16[128,256]{1,0:T(8,128)(2,1)S(1)}, u32[]{:S(2)}, u32[]{:S(2)}) collective-permute-start(bf16[128,256]{1,0:T(8,128)(2,1)S(1)} %get-tuple-element.15), channel_id=1, source_target_pairs={{0,26},{2,24},{4,30},{6,28},{8,18},{10,16},{12,22},{14,20},{16,10}... | collective-permute-start | bytes 196616 | tf_op jit(solution)/shard_map/ppermute | solution.py:233
  119.1 1.5 %collective-permute-start.7 = (bf16[128,256]{1,0:T(8,128)(2,1)S(1)}, bf16[128,256]{1,0:T(8,128)(2,1)S(1)}, u32[]{:S(2)}, u32[]{:S(2)}) collective-permute-start(bf16[128,256]{1,0:T(8,128)(2,1)S(1)} %get-tuple-element.16), channel_id=1, source_target_pairs={{0,28},{2,30},{4,24},{6,26},{8,20},{10,22},{12,16},{14,18},{16,12}... | collective-permute-start | bytes 196616 | tf_op jit(solution)/shard_map/ppermute | solution.py:233
  120.6 3.6 %collective-permute-done.3.refs_2_ = bf16[128,256]{1,0:T(8,128)(2,1)S(1)} collective-permute-done((bf16[128,256]{1,0:T(8,128)(2,1)}, bf16[128,256]{1,0:T(8,128)(2,1)S(1)}, u32[]{:S(2)}, u32[]{:S(2)}) %collective-permute-start.3) | collective-permute-done | bytes 65568 | tf_op jit(solution)/shard_map/ppermute | solution.py:233
  124.2 0.9 collective-permute-start.8
  125.1 1.3 collective-permute-done.4.refs_3_
  126.4 3.1 %collective-permute-done.5.refs_4_ = bf16[128,256]{1,0:T(8,128)(2,1)S(1)} collective-permute-done((bf16[128,256]{1,0:T(8,128)(2,1)S(1)}, bf16[128,256]{1,0:T(8,128)(2,1)S(1)}, u32[]{:S(2)}, u32[]{:S(2)}) %collective-permute-start.5) | collective-permute-done | bytes 65568 | tf_op jit(solution)/shard_map/ppermute | solution.py:233
  129.5 2.3 %collective-permute-done.6.refs_5_ = bf16[128,256]{1,0:T(8,128)(2,1)S(1)} collective-permute-done((bf16[128,256]{1,0:T(8,128)(2,1)S(1)}, bf16[128,256]{1,0:T(8,128)(2,1)S(1)}, u32[]{:S(2)}, u32[]{:S(2)}) %collective-permute-start.6) | collective-permute-done | bytes 65568 | tf_op jit(solution)/shard_map/ppermute | solution.py:233
  131.8 2.9 %collective-permute-done.7.refs_6_ = bf16[128,256]{1,0:T(8,128)(2,1)S(1)} collective-permute-done((bf16[128,256]{1,0:T(8,128)(2,1)S(1)}, bf16[128,256]{1,0:T(8,128)(2,1)S(1)}, u32[]{:S(2)}, u32[]{:S(2)}) %collective-permute-start.7) | collective-permute-done | bytes 65568 | tf_op jit(solution)/shard_map/ppermute | solution.py:233
  134.6 1.4 %collective-permute-done.8.refs_7_ = bf16[128,256]{1,0:T(8,128)(2,1)S(1)} collective-permute-done((bf16[128,256]{1,0:T(8,128)(2,1)S(1)}, bf16[128,256]{1,0:T(8,128)(2,1)S(1)}, u32[]{:S(2)}, u32[]{:S(2)}) %collective-permute-start.8) | collective-permute-done | bytes 65568 | tf_op jit(solution)/shard_map/ppermute | solution.py:233
  136.0 0.0 all-to-all-done.2.near
  136.0 1.3 shard_map.90
  (1 shorter events, 0.0 us)
Async XLA Ops:
  3.4 52.6 %all-to-all-start.1 = ((bf16[16,128,512]{2,1,0:T(8,128)(2,1)}), bf16[16,128,512]{2,1,0:T(8,128)(2,1)S(1)}, u32[]{:S(2)}, u32[]{:S(2)}) async-start(bf16[16,128,512]{2,1,0:T(8,128)(2,1)} %shard_map.87), calls=%async_computation.1 | async-start | bytes 4194304 | tf_op jit(solution)/shard_map/all_to_all | solution.py:103
  12.1 52.5 %copy-start.3 = (s32[8,4]{0,1:T(4,128)S(1)}, s32[8,4]{0,1:T(4,128)}, u32[]{:S(2)}) copy-start(s32[8,4]{0,1:T(4,128)} %param.13) | copy-start | bytes 388
  56.0 31.2 %all-to-all-start = ((bf16[16,128,256]{2,1,0:T(8,128)(2,1)}), bf16[16,128,256]{2,1,0:T(8,128)(2,1)S(1)}, u32[]{:S(2)}, u32[]{:S(2)}) async-start(bf16[16,128,256]{2,1,0:T(8,128)(2,1)} %shard_map.86), calls=%async_computation | async-start | bytes 2097152 | tf_op jit(solution)/shard_map/all_to_all | solution.py:103
  63.4 24.7 %collective-permute-start = (bf16[1024,512]{1,0:T(8,128)(2,1)}, bf16[1024,512]{1,0:T(8,128)(2,1)}, u32[]{:S(2)}, u32[]{:S(2)}) collective-permute-start(bf16[1024,512]{1,0:T(8,128)(2,1)} %constant_dynamic-slice_fusion), channel_id=1, source_target_pairs={{0,1},{1,0},{2,3},{3,2},{4,5},{5,4},{6,7},{7,6},{8,9},{9,8},{10,11... | collective-permute-start | bytes 3145736 | tf_op jit(solution)/shard_map/ppermute | solution.py:224
  93.1 0.6 copy-start.1
  93.7 0.6 copy-start.2
  94.4 4.0 %collective-permute-start.1 = (bf16[128,256]{1,0:T(8,128)(2,1)S(1)}, bf16[128,256]{1,0:T(8,128)(2,1)S(1)}, u32[]{:S(2)}, u32[]{:S(2)}) collective-permute-start(bf16[128,256]{1,0:T(8,128)(2,1)S(1)} %get-tuple-element.10), channel_id=1, source_target_pairs={{0,16},{2,18},{4,20},{6,22},{8,24},{10,26},{12,28},{14,30},{16,0},... | collective-permute-start | bytes 196616 | tf_op jit(solution)/shard_map/ppermute | solution.py:233
  96.4 5.4 %collective-permute-start.2 = (bf16[128,256]{1,0:T(8,128)(2,1)S(1)}, bf16[128,256]{1,0:T(8,128)(2,1)S(1)}, u32[]{:S(2)}, u32[]{:S(2)}) collective-permute-start(bf16[128,256]{1,0:T(8,128)(2,1)S(1)} %get-tuple-element.11), channel_id=1, source_target_pairs={{0,18},{2,16},{4,22},{6,20},{8,26},{10,24},{12,30},{14,28},{16,2},... | collective-permute-start | bytes 196616 | tf_op jit(solution)/shard_map/ppermute | solution.py:233
  106.9 0.8 copy-start
  107.7 28.4 %all-to-all-start.2 = ((bf16[8,128,256]{2,1,0:T(8,128)(2,1)}), bf16[8,128,256]{2,1,0:T(8,128)(2,1)S(1)}, u32[]{:S(2)}, u32[]{:S(2)}) async-start(bf16[8,128,256]{2,1,0:T(8,128)(2,1)} %bitcast.9), calls=%async_computation.2 | async-start | bytes 1048576 | tf_op jit(solution)/shard_map/all_to_all | solution.py:235
  113.8 10.4 %collective-permute-start.3 = (bf16[128,256]{1,0:T(8,128)(2,1)}, bf16[128,256]{1,0:T(8,128)(2,1)S(1)}, u32[]{:S(2)}, u32[]{:S(2)}) collective-permute-start(bf16[128,256]{1,0:T(8,128)(2,1)} %copy-done.2), channel_id=1, source_target_pairs={{0,20},{2,22},{4,16},{6,18},{8,28},{10,30},{12,24},{14,26},{16,4},... | collective-permute-start | bytes 196616 | tf_op jit(solution)/shard_map/ppermute | solution.py:233
  116.2 10.2 %collective-permute-start.4 = (bf16[128,256]{1,0:T(8,128)(2,1)}, bf16[128,256]{1,0:T(8,128)(2,1)S(1)}, u32[]{:S(2)}, u32[]{:S(2)}) collective-permute-start(bf16[128,256]{1,0:T(8,128)(2,1)} %copy-done.1), channel_id=1, source_target_pairs={{0,22},{2,20},{4,18},{6,16},{8,30},{10,28},{12,26},{14,24},{16,6},... | collective-permute-start | bytes 196616 | tf_op jit(solution)/shard_map/ppermute | solution.py:233
  117.6 11.9 %collective-permute-start.5 = (bf16[128,256]{1,0:T(8,128)(2,1)S(1)}, bf16[128,256]{1,0:T(8,128)(2,1)S(1)}, u32[]{:S(2)}, u32[]{:S(2)}) collective-permute-start(bf16[128,256]{1,0:T(8,128)(2,1)S(1)} %get-tuple-element.14), channel_id=1, source_target_pairs={{0,24},{2,26},{4,28},{6,30},{8,16},{10,18},{12,20},{14,22},{16,8},... | collective-permute-start | bytes 196616 | tf_op jit(solution)/shard_map/ppermute | solution.py:233
  117.7 14.1 %collective-permute-start.6 = (bf16[128,256]{1,0:T(8,128)(2,1)S(1)}, bf16[128,256]{1,0:T(8,128)(2,1)S(1)}, u32[]{:S(2)}, u32[]{:S(2)}) collective-permute-start(bf16[128,256]{1,0:T(8,128)(2,1)S(1)} %get-tuple-element.15), channel_id=1, source_target_pairs={{0,26},{2,24},{4,30},{6,28},{8,18},{10,16},{12,22},{14,20},{16,10}... | collective-permute-start | bytes 196616 | tf_op jit(solution)/shard_map/ppermute | solution.py:233
  119.1 15.5 %collective-permute-start.7 = (bf16[128,256]{1,0:T(8,128)(2,1)S(1)}, bf16[128,256]{1,0:T(8,128)(2,1)S(1)}, u32[]{:S(2)}, u32[]{:S(2)}) collective-permute-start(bf16[128,256]{1,0:T(8,128)(2,1)S(1)} %get-tuple-element.16), channel_id=1, source_target_pairs={{0,28},{2,30},{4,24},{6,26},{8,20},{10,22},{12,16},{14,18},{16,12}... | collective-permute-start | bytes 196616 | tf_op jit(solution)/shard_map/ppermute | solution.py:233
  124.2 11.8 %collective-permute-start.8 = (bf16[128,256]{1,0:T(8,128)(2,1)S(1)}, bf16[128,256]{1,0:T(8,128)(2,1)S(1)}, u32[]{:S(2)}, u32[]{:S(2)}) collective-permute-start(bf16[128,256]{1,0:T(8,128)(2,1)S(1)} %get-tuple-element.17), channel_id=1, source_target_pairs={{0,30},{2,28},{4,26},{6,24},{8,22},{10,20},{12,18},{14,16},{16,14}... | collective-permute-start | bytes 196616 | tf_op jit(solution)/shard_map/ppermute | solution.py:233

commit v9 on v7

--- a/solution.py
+++ b/solution.py
@@ -74,25 +74,26 @@
     )(*pin(*arrays))
 
 
-def unpack_kernel(piece, *arrays):
-    devices, tokens, width = piece.shape
-    hd = width // len(arrays)
-    for h in range(devices):
+def unpack_kernel(me, *refs, order):
+    pieces, arrays = refs[: len(order)], refs[len(order) :]
+    hd = pieces[0].shape[1] // len(arrays)
+    for k, piece in zip(order, pieces):
+        columns = pl.ds(pl.multiple_of((me[0] ^ k) * hd, hd), hd)
         for a, array in enumerate(arrays):
-            array[:, h * hd : (h + 1) * hd] = piece[h, :, a * hd : (a + 1) * hd]
-
-
-def from_heads(pieces, count):
-    devices, tokens, width = pieces.shape
-    columns = devices * width // count
+            array[:, columns] = piece[:, a * hd : (a + 1) * hd]
+
+
+def from_heads(me, pieces, count):
+    tokens, width = pieces[0].shape
+    columns = len(pieces) * width // count
     return pl.pallas_call(
-        unpack_kernel,
-        in_specs=[VMEM],
+        functools.partial(unpack_kernel, order=list(pieces)),
+        in_specs=[SMEM] + [VMEM] * len(pieces),
         out_specs=[VMEM] * count,
         out_shape=[jax.ShapeDtypeStruct((tokens, columns), jnp.bfloat16)] * count,
         compiler_params=PARAMS,
-        cost_estimate=moves(4 * pieces.size),
-    )(pieces)
+        cost_estimate=moves(4 * len(pieces) * tokens * width),
+    )(me, *pieces.values())
 
 
 def exchange(pieces):
@@ -100,8 +101,12 @@
     return got.reshape(-1, got.shape[2])
 
 
-def attend_kernel(table, q_ref, *refs, sources, hd):
-    parts, out_ref, kv, sems = refs[:sources], refs[sources], refs[-2], refs[-1]
+def attend_kernel(me, table, q_ref, *refs, sources, later, tokens, first, hd):
+    parts, outs = refs[:sources], refs[sources + later : -3]
+    kv, held, sems = refs[-3:]
+    count, per = held.shape[0], BQ // tokens
+    chip, core = me[0] // per, me[0] % per
+    blocks = [chip ^ (first + i) for i in range(count)]
     copies, row = [], 0
     for i, ref in enumerate(parts):
         rows = ref.shape[0]
@@ -117,7 +122,7 @@
     trans = (((1,), (1,)), ((), ()))
 
     def products(block):
-        both = q_ref[block * BQ : (block + 1) * BQ]
+        both = q_ref[pl.ds(pl.multiple_of(block * BQ, BQ), BQ)]
         query = both[:, :hd]
         starts = [pl.multiple_of(table[block * WK + w] * BQ, BQ) for w in range(WK)]
         scores, tans = [], []
@@ -129,7 +134,7 @@
             tans.append(lax.dot_general(both, keys, trans, preferred_element_type=jnp.float32))
         return starts, scores, tans
 
-    def finish(block, starts, scores, tans):
+    def finish(i, starts, scores, tans):
         top = functools.reduce(jnp.maximum, scores)
         top = jnp.max(top, axis=1, keepdims=True) * factor
         probs = [jnp.exp2(s * factor - top) for s in scores]
@@ -146,31 +151,36 @@
         inverse = 1.0 / total
         out = main[:, :hd] * inverse
         tan = (main[:, hd:] + scale * side) * inverse - (scale * mean * inverse) * out
-        rows = slice(block * BQ, (block + 1) * BQ)
-        out_ref[rows, :hd] = out.astype(jnp.bfloat16)
-        out_ref[rows, hd:] = tan.astype(jnp.bfloat16)
-
-    blocks = q_ref.shape[0] // BQ
-    ahead = products(0)
-    for block in range(blocks):
+        held[i, :, :hd] = out.astype(jnp.bfloat16)
+        held[i, :, hd:] = tan.astype(jnp.bfloat16)
+        for p in range(per):
+            start = pl.multiple_of((core ^ p) * tokens, tokens)
+            outs[i * per + p][...] = held[i, pl.ds(start, tokens)]
+
+    ahead = products(blocks[0])
+    for i in range(count):
         current = ahead
-        if block + 1 < blocks:
-            ahead = products(block + 1)
-        finish(block, *current)
-
-
-def attend(table, q_pair, parts):
+        if i + 1 < count:
+            ahead = products(blocks[i + 1])
+        finish(i, *current)
+
+
+def attend(me, table, q_pair, parts, later, tokens, first, count):
     rows, width = q_pair.shape
     hd = width // 2
     total = sum(a.shape[0] for a in parts)
-    elements = rows * WK * BQ
+    elements = count * BQ * WK * BQ
+    pieces = count * BQ // tokens
     return pl.pallas_call(
-        functools.partial(attend_kernel, sources=len(parts), hd=hd),
-        in_specs=[SMEM, VMEM] + [ANY] * len(parts),
-        out_specs=VMEM,
-        out_shape=jax.ShapeDtypeStruct((rows, width), jnp.bfloat16),
+        functools.partial(
+            attend_kernel, sources=len(parts), later=len(later), tokens=tokens, first=first, hd=hd
+        ),
+        in_specs=[SMEM, SMEM, VMEM] + [ANY] * (len(parts) + len(later)),
+        out_specs=[VMEM] * pieces,
+        out_shape=[jax.ShapeDtypeStruct((tokens, width), jnp.bfloat16)] * pieces,
         scratch_shapes=[
             pltpu.VMEM((total, 4 * hd), jnp.bfloat16),
+            pltpu.VMEM((count, BQ, width), jnp.bfloat16),
             pltpu.SemaphoreType.DMA((len(parts),)),
         ],
         compiler_params=PARAMS,
@@ -179,7 +189,7 @@
             bytes_accessed=2 * (total * 4 * hd + 2 * rows * width),
             transcendentals=elements,
         ),
-    )(table, q_pair, *parts)
+    )(me, table, q_pair, *parts, *later)
 
 
 def slots(neighbors, frame, blocks):
@@ -207,9 +217,16 @@
 
     q_pair = exchange(to_heads([query, query_tan], devices))
     table = slots(neighbors, frame, neighbors.shape[0])
-    pair = attend(table, q_pair, parts).reshape(devices, tokens, -1)
-    back = lax.all_to_all(pair, "heads", split_axis=0, concat_axis=0, tiled=True)
-    return from_heads(back, 2)
+    me = lax.axis_index("heads").reshape(1).astype(jnp.int32)
+    half, middle = devices // 2, neighbors.shape[0] // 2
+    back, later = {}, []
+    for slot, first in ((half, middle), (0, 0)):
+        pieces = attend(me, table, q_pair, parts, later, tokens, first, middle)
+        for k, piece in enumerate(pieces, slot):
+            pairs = [(d, d ^ k) for d in range(devices)]
+            back[k] = lax.ppermute(piece, "heads", pairs) if k else piece
+        later = [back[half], back[half + 1]]
+    return from_heads(me, back, 2)
 
 
 def solution(mesh):

time: 130 us -> 132 us (1.015)
  blocking collectives: 30.4 us -> 0 us
  starting transfers between devices: 20.1 us -> 43.7 us
  waiting for transfers between devices: 63 us -> 70.1 us
  Pallas kernels: 13.8 us -> 16.2 us
    all_to_all x1 -> x0, blocking collectives: 30.4 us -> none  [per_device(): lax.all_to_all(pair, 'heads', split_axis=0, concat_axis=0, tiled=True)]
    ppermute x0 -> x15, starting transfers between devices: none -> 23.6 us  [per_device(): back[k] = lax.ppermute(piece, 'heads', pairs) if k else piece]
    ppermute x0 -> x15, waiting for transfers between devices: none -> 7.13 us  [per_device(): back[k] = lax.ppermute(piece, 'heads', pairs) if k else piece]
    pallas_call x2 -> x3, Pallas kernels: 8.94 us -> 11.3 us  [the longest x2 10.1 us: attend(): pl.pallas_call(functools.partial(attend_kernel, sources=len(parts), later...]
  transfers between devices with their start and end apart: 3 -> 18, of which waited for: 3 -> 6; matrix products, arithmetic and copies ran while one was open for 1% -> 1% of each run, Pallas kernels for 2% -> 5%
where the time goes in v9:
time: 132 us
  waiting for transfers between devices  70.1 us (53%)
  starting transfers between devices  43.7 us (33%)
  Pallas kernels  16.2 us (12%)
    all_to_all x2, waiting for transfers between devices, exchange(): lax.all_to_all(pieces, 'heads', split_axis=0, concat_axis=0, tiled=True)  59.1 us
    ppermute x15, starting transfers between devices, per_device(): back[k] = lax.ppermute(piece, 'heads', pairs) if k else piece  23.6 us
    all_to_all x2, starting transfers between devices, exchange(): lax.all_to_all(pieces, 'heads', split_axis=0, concat_axis=0, tiled=True)  18.6 us
    pallas_call x2, Pallas kernels, attend(): pl.pallas_call(functools.partial(attend_kernel, sources=len(parts), later...  10.1 us
    ppermute x15, waiting for transfers between devices, per_device(): back[k] = lax.ppermute(piece, 'heads', pairs) if k else piece  7.13 us
    pallas_call x2, Pallas kernels, to_heads(): pl.pallas_call(functools.partial(pack_kernel, count=count, chunks=chunks)...  4.89 us
    ppermute x1, waiting for transfers between devices, per_device(): lax.ppermute(edge, 'frames', pairs + [(j, i) for i, j in pairs])  3.92 us
  transfers between devices with their start and end apart: 18, of which 6 were waited for; matrix products, arithmetic and copies ran while one was open for 1% of the time, Pallas kernels for 5%

profile of v9, /device:TPU:0, one launch (start us, length us, event | category | flops | bytes accessed | tf_op | source)
XLA Modules:
  0.0 132.1 jit_solution(16614669033091906650)
XLA Ops:
  0.6 2.7 %shard_map.87 = bf16[16,128,512]{2,1,0:T(8,128)(2,1)} custom-call(bf16[128,2048]{1,0:T(8,128)(2,1)} %refs_0_.3, bf16[128,2048]{1,0:T(8,128)(2,1)} %refs_1_.3, bf16[128,2048]{1,0:T(8,128)(2,1)} %refs_2_.1, bf16[128,2048]{1,0:T(8,128)(2,1)} %refs_3_.1), custom_call_target="tpu_custom_call" | custom-call | bytes 4194304 | tf_op jit(solution)/shard_map/pallas_call | solution.py:61
  3.4 7.4 %all-to-all-start.1 = ((bf16[16,128,512]{2,1,0:T(8,128)(2,1)}), bf16[16,128,512]{2,1,0:T(8,128)(2,1)S(1)}, u32[]{:S(2)}, u32[]{:S(2)}) async-start(bf16[16,128,512]{2,1,0:T(8,128)(2,1)} %shard_map.87), calls=%async_computation.1 | async-start | bytes 4194304 | tf_op jit(solution)/shard_map/all_to_all | solution.py:100
  10.7 2.2 %shard_map.86 = bf16[16,128,256]{2,1,0:T(8,128)(2,1)} custom-call(bf16[128,2048]{1,0:T(8,128)(2,1)} %refs_0_.2, bf16[128,2048]{1,0:T(8,128)(2,1)} %refs_1_.2), custom_call_target="tpu_custom_call" | custom-call | bytes 2097152 | tf_op jit(solution)/shard_map/pallas_call | solution.py:61
  12.9 0.0 copy-start
  12.9 38.9 %all-to-all-done.1 = bf16[16,128,512]{2,1,0:T(8,128)(2,1)S(1)} async-done(((bf16[16,128,512]{2,1,0:T(8,128)(2,1)}), bf16[16,128,512]{2,1,0:T(8,128)(2,1)S(1)}, u32[]{:S(2)}, u32[]{:S(2)}) %all-to-all-start.1) | async-done | bytes 2097184 | tf_op jit(solution)/shard_map/all_to_all | solution.py:100
  51.8 11.2 %all-to-all-start = ((bf16[16,128,256]{2,1,0:T(8,128)(2,1)}), bf16[16,128,256]{2,1,0:T(8,128)(2,1)S(1)}, u32[]{:S(2)}, u32[]{:S(2)}) async-start(bf16[16,128,256]{2,1,0:T(8,128)(2,1)} %shard_map.86), calls=%async_computation | async-start | bytes 2097152 | tf_op jit(solution)/shard_map/all_to_all | solution.py:100
  63.1 1.1 constant_dynamic-slice_fusion
  64.2 1.5 %collective-permute-start = (bf16[1024,512]{1,0:T(8,128)(2,1)}, bf16[1024,512]{1,0:T(8,128)(2,1)}, u32[]{:S(2)}, u32[]{:S(2)}) collective-permute-start(bf16[1024,512]{1,0:T(8,128)(2,1)} %constant_dynamic-slice_fusion), channel_id=1, source_target_pairs={{0,1},{1,0},{2,3},{3,2},{4,5},{5,4},{6,7},{7,6},{8,9},{9,8},{10,11... | collective-permute-start | bytes 3145736 | tf_op jit(solution)/shard_map/ppermute | solution.py:216
  65.7 0.0 copy-done
  65.7 0.1 copy.10
  65.8 0.1 reshape.17.table
  65.9 20.1 %all-to-all-done = bf16[16,128,256]{2,1,0:T(8,128)(2,1)S(1)} async-done(((bf16[16,128,256]{2,1,0:T(8,128)(2,1)}), bf16[16,128,256]{2,1,0:T(8,128)(2,1)S(1)}, u32[]{:S(2)}, u32[]{:S(2)}) %all-to-all-start) | async-done | bytes 1048608 | tf_op jit(solution)/shard_map/all_to_all | solution.py:100
  86.0 3.9 %collective-permute-done.refs_1_ = bf16[1024,512]{1,0:T(8,128)(2,1)} collective-permute-done((bf16[1024,512]{1,0:T(8,128)(2,1)}, bf16[1024,512]{1,0:T(8,128)(2,1)}, u32[]{:S(2)}, u32[]{:S(2)}) %collective-permute-start) | collective-permute-done | bytes 1048608 | tf_op jit(solution)/shard_map/ppermute | solution.py:216
  89.9 5.0 %shard_map.88 = (bf16[128,256]{1,0:T(8,128)(2,1)S(1)}, bf16[128,256]{1,0:T(8,128)(2,1)S(1)}, bf16[128,256]{1,0:T(8,128)(2,1)S(1)}, bf16[128,256]{1,0:T(8,128)(2,...) custom-call(s32[1]{0:T(128)} %bitcast.me, ...), custom_call_target="tpu_custom_call" | custom-call | flops 1610612736 | bytes 5242880 | tf_op jit(solution)/shard_map/pallas_call | solution.py:174
  95.0 2.6 %collective-permute-start.1 = (bf16[128,256]{1,0:T(8,128)(2,1)S(1)}, bf16[128,256]{1,0:T(8,128)(2,1)S(1)}, u32[]{:S(2)}, u32[]{:S(2)}) collective-permute-start(bf16[128,256]{1,0:T(8,128)(2,1)S(1)} %get-tuple-element.18), channel_id=1, source_target_pairs={{0,16},{2,18},{4,20},{6,22},{8,24},{10,26},{12,28},{14,30},{16,0},... | collective-permute-start | bytes 196616 | tf_op jit(solution)/shard_map/ppermute | solution.py:227
  97.6 0.0 collective-permute-start.2
  97.6 2.5 %collective-permute-start.3 = (bf16[128,256]{1,0:T(8,128)(2,1)S(1)}, bf16[128,256]{1,0:T(8,128)(2,1)S(1)}, u32[]{:S(2)}, u32[]{:S(2)}) collective-permute-start(bf16[128,256]{1,0:T(8,128)(2,1)S(1)} %get-tuple-element.20), channel_id=1, source_target_pairs={{0,20},{2,22},{4,16},{6,18},{8,28},{10,30},{12,24},{14,26},{16,4},... | collective-permute-start | bytes 196616 | tf_op jit(solution)/shard_map/ppermute | solution.py:227
  100.1 1.1 collective-permute-start.4
  101.2 3.5 %collective-permute-start.5 = (bf16[128,256]{1,0:T(8,128)(2,1)S(1)}, bf16[128,256]{1,0:T(8,128)(2,1)S(1)}, u32[]{:S(2)}, u32[]{:S(2)}) collective-permute-start(bf16[128,256]{1,0:T(8,128)(2,1)S(1)} %get-tuple-element.22), channel_id=1, source_target_pairs={{0,24},{2,26},{4,28},{6,30},{8,16},{10,18},{12,20},{14,22},{16,8},... | collective-permute-start | bytes 196616 | tf_op jit(solution)/shard_map/ppermute | solution.py:227
  104.7 0.0 collective-permute-done.1.refs_2_.refs_0_
  104.7 0.0 collective-permute-start.6
  104.7 3.8 %collective-permute-done.2.refs_3_.refs_1_ = bf16[128,256]{1,0:T(8,128)(2,1)S(1)} collective-permute-done((bf16[128,256]{1,0:T(8,128)(2,1)S(1)}, bf16[128,256]{1,0:T(8,128)(2,1)S(1)}, u32[]{:S(2)}, u32[]{:S(2)}) %collective-permute-start.2) | collective-permute-done | bytes 65568 | tf_op jit(solution)/shard_map/ppermute | solution.py:227
  108.5 2.4 %collective-permute-start.7 = (bf16[128,256]{1,0:T(8,128)(2,1)S(1)}, bf16[128,256]{1,0:T(8,128)(2,1)S(1)}, u32[]{:S(2)}, u32[]{:S(2)}) collective-permute-start(bf16[128,256]{1,0:T(8,128)(2,1)S(1)} %get-tuple-element.24), channel_id=1, source_target_pairs={{0,28},{2,30},{4,24},{6,26},{8,20},{10,22},{12,16},{14,18},{16,12}... | collective-permute-start | bytes 196616 | tf_op jit(solution)/shard_map/ppermute | solution.py:227
  110.9 5.0 %shard_map.89 = (bf16[128,256]{1,0:T(8,128)(2,1)S(1)}, bf16[128,256]{1,0:T(8,128)(2,1)S(1)}, bf16[128,256]{1,0:T(8,128)(2,1)S(1)}, bf16[128,256]{1,0:T(8,128)(2,...) custom-call(s32[1]{0:T(128)} %bitcast.me, ...), custom_call_target="tpu_custom_call" | custom-call | flops 1610612736 | bytes 5242880 | tf_op jit(solution)/shard_map/pallas_call | solution.py:174
  115.9 0.0 collective-permute-done.3.refs_2_
  115.9 3.1 %collective-permute-start.8 = (bf16[128,256]{1,0:T(8,128)(2,1)S(1)}, bf16[128,256]{1,0:T(8,128)(2,1)S(1)}, u32[]{:S(2)}, u32[]{:S(2)}) collective-permute-start(bf16[128,256]{1,0:T(8,128)(2,1)S(1)} %get-tuple-element.25), channel_id=1, source_target_pairs={{0,30},{2,28},{4,26},{6,24},{8,22},{10,20},{12,18},{14,16},{16,14}... | collective-permute-start | bytes 196616 | tf_op jit(solution)/shard_map/ppermute | solution.py:227
  119.1 0.0 collective-permute-done.4.refs_3_
  119.1 1.7 %collective-permute-start.10 = (bf16[128,256]{1,0:T(8,128)(2,1)S(1)}, bf16[128,256]{1,0:T(8,128)(2,1)S(1)}, u32[]{:S(2)}, u32[]{:S(2)}) collective-permute-start(bf16[128,256]{1,0:T(8,128)(2,1)S(1)} %get-tuple-element.28), channel_id=1, source_target_pairs={{0,4},{2,6},{4,0},{6,2},{8,12},{10,14},{12,8},{14,10},{16,20},{18,... | collective-permute-start | bytes 196616 | tf_op jit(solution)/shard_map/ppermute | solution.py:227
  120.7 0.0 collective-permute-done.5.refs_4_
  120.7 0.0 collective-permute-start.11
  120.7 0.0 collective-permute-done.6.refs_5_
  120.7 0.1 collective-permute-start.12
  120.8 0.0 collective-permute-done.7.refs_6_
  120.8 1.8 %collective-permute-start.13 = (bf16[128,256]{1,0:T(8,128)(2,1)S(1)}, bf16[128,256]{1,0:T(8,128)(2,1)S(1)}, u32[]{:S(2)}, u32[]{:S(2)}) collective-permute-start(bf16[128,256]{1,0:T(8,128)(2,1)S(1)} %get-tuple-element.31), channel_id=1, source_target_pairs={{0,10},{2,8},{4,14},{6,12},{8,2},{10,0},{12,6},{14,4},{16,26},{18,... | collective-permute-start | bytes 196616 | tf_op jit(solution)/shard_map/ppermute | solution.py:227
  122.6 0.0 collective-permute-done.8.refs_7_
  122.6 1.4 %collective-permute-start.14 = (bf16[128,256]{1,0:T(8,128)(2,1)S(1)}, bf16[128,256]{1,0:T(8,128)(2,1)S(1)}, u32[]{:S(2)}, u32[]{:S(2)}) collective-permute-start(bf16[128,256]{1,0:T(8,128)(2,1)S(1)} %get-tuple-element.32), channel_id=1, source_target_pairs={{0,12},{2,14},{4,8},{6,10},{8,4},{10,6},{12,0},{14,2},{16,28},{18,... | collective-permute-start | bytes 196616 | tf_op jit(solution)/shard_map/ppermute | solution.py:227
  124.0 0.0 collective-permute-done.10.refs_10_
  124.0 3.4 %collective-permute-start.15 = (bf16[128,256]{1,0:T(8,128)(2,1)S(1)}, bf16[128,256]{1,0:T(8,128)(2,1)S(1)}, u32[]{:S(2)}, u32[]{:S(2)}) collective-permute-start(bf16[128,256]{1,0:T(8,128)(2,1)S(1)} %get-tuple-element.33), channel_id=1, source_target_pairs={{0,14},{2,12},{4,10},{6,8},{8,6},{10,4},{12,2},{14,0},{16,30},{18,... | collective-permute-start | bytes 196616 | tf_op jit(solution)/shard_map/ppermute | solution.py:227
  127.4 0.0 collective-permute-done.11.refs_11_
  127.4 0.0 collective-permute-start.9
  127.4 0.0 collective-permute-done.12.refs_12_
  127.5 0.0 collective-permute-done.13.refs_13_
  127.5 1.1 collective-permute-done.14.refs_14_
  128.5 2.3 %collective-permute-done.15.refs_15_ = bf16[128,256]{1,0:T(8,128)(2,1)S(1)} collective-permute-done((bf16[128,256]{1,0:T(8,128)(2,1)S(1)}, bf16[128,256]{1,0:T(8,128)(2,1)S(1)}, u32[]{:S(2)}, u32[]{:S(2)}) %collective-permute-start.15) | collective-permute-done | bytes 65568 | tf_op jit(solution)/shard_map/ppermute | solution.py:227
  130.8 0.0 collective-permute-done.9.refs_9_
  130.8 1.3 shard_map.90
  (1 shorter events, 0.0 us)
Async XLA Ops:
  3.4 48.5 %all-to-all-start.1 = ((bf16[16,128,512]{2,1,0:T(8,128)(2,1)}), bf16[16,128,512]{2,1,0:T(8,128)(2,1)S(1)}, u32[]{:S(2)}, u32[]{:S(2)}) async-start(bf16[16,128,512]{2,1,0:T(8,128)(2,1)} %shard_map.87), calls=%async_computation.1 | async-start | bytes 4194304 | tf_op jit(solution)/shard_map/all_to_all | solution.py:100
  12.9 52.8 %copy-start = (s32[8,4]{0,1:T(4,128)S(1)}, s32[8,4]{0,1:T(4,128)}, u32[]{:S(2)}) copy-start(s32[8,4]{0,1:T(4,128)} %param.13) | copy-start | bytes 388
  51.8 34.2 %all-to-all-start = ((bf16[16,128,256]{2,1,0:T(8,128)(2,1)}), bf16[16,128,256]{2,1,0:T(8,128)(2,1)S(1)}, u32[]{:S(2)}, u32[]{:S(2)}) async-start(bf16[16,128,256]{2,1,0:T(8,128)(2,1)} %shard_map.86), calls=%async_computation | async-start | bytes 2097152 | tf_op jit(solution)/shard_map/all_to_all | solution.py:100
  64.2 25.8 %collective-permute-start = (bf16[1024,512]{1,0:T(8,128)(2,1)}, bf16[1024,512]{1,0:T(8,128)(2,1)}, u32[]{:S(2)}, u32[]{:S(2)}) collective-permute-start(bf16[1024,512]{1,0:T(8,128)(2,1)} %constant_dynamic-slice_fusion), channel_id=1, source_target_pairs={{0,1},{1,0},{2,3},{3,2},{4,5},{5,4},{6,7},{7,6},{8,9},{9,8},{10,11... | collective-permute-start | bytes 3145736 | tf_op jit(solution)/shard_map/ppermute | solution.py:216
  95.0 9.7 %collective-permute-start.1 = (bf16[128,256]{1,0:T(8,128)(2,1)S(1)}, bf16[128,256]{1,0:T(8,128)(2,1)S(1)}, u32[]{:S(2)}, u32[]{:S(2)}) collective-permute-start(bf16[128,256]{1,0:T(8,128)(2,1)S(1)} %get-tuple-element.18), channel_id=1, source_target_pairs={{0,16},{2,18},{4,20},{6,22},{8,24},{10,26},{12,28},{14,30},{16,0},... | collective-permute-start | bytes 196616 | tf_op jit(solution)/shard_map/ppermute | solution.py:227
  97.6 10.9 %collective-permute-start.2 = (bf16[128,256]{1,0:T(8,128)(2,1)S(1)}, bf16[128,256]{1,0:T(8,128)(2,1)S(1)}, u32[]{:S(2)}, u32[]{:S(2)}) collective-permute-start(bf16[128,256]{1,0:T(8,128)(2,1)S(1)} %get-tuple-element.19), channel_id=1, source_target_pairs={{0,18},{2,16},{4,22},{6,20},{8,26},{10,24},{12,30},{14,28},{16,2},... | collective-permute-start | bytes 196616 | tf_op jit(solution)/shard_map/ppermute | solution.py:227
  97.6 18.3 %collective-permute-start.3 = (bf16[128,256]{1,0:T(8,128)(2,1)S(1)}, bf16[128,256]{1,0:T(8,128)(2,1)S(1)}, u32[]{:S(2)}, u32[]{:S(2)}) collective-permute-start(bf16[128,256]{1,0:T(8,128)(2,1)S(1)} %get-tuple-element.20), channel_id=1, source_target_pairs={{0,20},{2,22},{4,16},{6,18},{8,28},{10,30},{12,24},{14,26},{16,4},... | collective-permute-start | bytes 196616 | tf_op jit(solution)/shard_map/ppermute | solution.py:227
  100.1 19.0 %collective-permute-start.4 = (bf16[128,256]{1,0:T(8,128)(2,1)S(1)}, bf16[128,256]{1,0:T(8,128)(2,1)S(1)}, u32[]{:S(2)}, u32[]{:S(2)}) collective-permute-start(bf16[128,256]{1,0:T(8,128)(2,1)S(1)} %get-tuple-element.21), channel_id=1, source_target_pairs={{0,22},{2,20},{4,18},{6,16},{8,30},{10,28},{12,26},{14,24},{16,6},... | collective-permute-start | bytes 196616 | tf_op jit(solution)/shard_map/ppermute | solution.py:227
  101.2 19.5 %collective-permute-start.5 = (bf16[128,256]{1,0:T(8,128)(2,1)S(1)}, bf16[128,256]{1,0:T(8,128)(2,1)S(1)}, u32[]{:S(2)}, u32[]{:S(2)}) collective-permute-start(bf16[128,256]{1,0:T(8,128)(2,1)S(1)} %get-tuple-element.22), channel_id=1, source_target_pairs={{0,24},{2,26},{4,28},{6,30},{8,16},{10,18},{12,20},{14,22},{16,8},... | collective-permute-start | bytes 196616 | tf_op jit(solution)/shard_map/ppermute | solution.py:227
  104.7 16.0 %collective-permute-start.6 = (bf16[128,256]{1,0:T(8,128)(2,1)S(1)}, bf16[128,256]{1,0:T(8,128)(2,1)S(1)}, u32[]{:S(2)}, u32[]{:S(2)}) collective-permute-start(bf16[128,256]{1,0:T(8,128)(2,1)S(1)} %get-tuple-element.23), channel_id=1, source_target_pairs={{0,26},{2,24},{4,30},{6,28},{8,18},{10,16},{12,22},{14,20},{16,10}... | collective-permute-start | bytes 196616 | tf_op jit(solution)/shard_map/ppermute | solution.py:227
  108.5 12.3 %collective-permute-start.7 = (bf16[128,256]{1,0:T(8,128)(2,1)S(1)}, bf16[128,256]{1,0:T(8,128)(2,1)S(1)}, u32[]{:S(2)}, u32[]{:S(2)}) collective-permute-start(bf16[128,256]{1,0:T(8,128)(2,1)S(1)} %get-tuple-element.24), channel_id=1, source_target_pairs={{0,28},{2,30},{4,24},{6,26},{8,20},{10,22},{12,16},{14,18},{16,12}... | collective-permute-start | bytes 196616 | tf_op jit(solution)/shard_map/ppermute | solution.py:227
  115.9 6.7 %collective-permute-start.8 = (bf16[128,256]{1,0:T(8,128)(2,1)S(1)}, bf16[128,256]{1,0:T(8,128)(2,1)S(1)}, u32[]{:S(2)}, u32[]{:S(2)}) collective-permute-start(bf16[128,256]{1,0:T(8,128)(2,1)S(1)} %get-tuple-element.25), channel_id=1, source_target_pairs={{0,30},{2,28},{4,26},{6,24},{8,22},{10,20},{12,18},{14,16},{16,14}... | collective-permute-start | bytes 196616 | tf_op jit(solution)/shard_map/ppermute | solution.py:227
  119.1 5.0 %collective-permute-start.10 = (bf16[128,256]{1,0:T(8,128)(2,1)S(1)}, bf16[128,256]{1,0:T(8,128)(2,1)S(1)}, u32[]{:S(2)}, u32[]{:S(2)}) collective-permute-start(bf16[128,256]{1,0:T(8,128)(2,1)S(1)} %get-tuple-element.28), channel_id=1, source_target_pairs={{0,4},{2,6},{4,0},{6,2},{8,12},{10,14},{12,8},{14,10},{16,20},{18,... | collective-permute-start | bytes 196616 | tf_op jit(solution)/shard_map/ppermute | solution.py:227
  120.7 6.7 %collective-permute-start.11 = (bf16[128,256]{1,0:T(8,128)(2,1)S(1)}, bf16[128,256]{1,0:T(8,128)(2,1)S(1)}, u32[]{:S(2)}, u32[]{:S(2)}) collective-permute-start(bf16[128,256]{1,0:T(8,128)(2,1)S(1)} %get-tuple-element.29), channel_id=1, source_target_pairs={{0,6},{2,4},{4,2},{6,0},{8,14},{10,12},{12,10},{14,8},{16,22},{18,... | collective-permute-start | bytes 196616 | tf_op jit(solution)/shard_map/ppermute | solution.py:227
  120.7 6.7 %collective-permute-start.12 = (bf16[128,256]{1,0:T(8,128)(2,1)S(1)}, bf16[128,256]{1,0:T(8,128)(2,1)S(1)}, u32[]{:S(2)}, u32[]{:S(2)}) collective-permute-start(bf16[128,256]{1,0:T(8,128)(2,1)S(1)} %get-tuple-element.30), channel_id=1, source_target_pairs={{0,8},{2,10},{4,12},{6,14},{8,0},{10,2},{12,4},{14,6},{16,24},{18,... | collective-permute-start | bytes 196616 | tf_op jit(solution)/shard_map/ppermute | solution.py:227
  120.8 6.6 %collective-permute-start.13 = (bf16[128,256]{1,0:T(8,128)(2,1)S(1)}, bf16[128,256]{1,0:T(8,128)(2,1)S(1)}, u32[]{:S(2)}, u32[]{:S(2)}) collective-permute-start(bf16[128,256]{1,0:T(8,128)(2,1)S(1)} %get-tuple-element.31), channel_id=1, source_target_pairs={{0,10},{2,8},{4,14},{6,12},{8,2},{10,0},{12,6},{14,4},{16,26},{18,... | collective-permute-start | bytes 196616 | tf_op jit(solution)/shard_map/ppermute | solution.py:227
  122.6 5.9 %collective-permute-start.14 = (bf16[128,256]{1,0:T(8,128)(2,1)S(1)}, bf16[128,256]{1,0:T(8,128)(2,1)S(1)}, u32[]{:S(2)}, u32[]{:S(2)}) collective-permute-start(bf16[128,256]{1,0:T(8,128)(2,1)S(1)} %get-tuple-element.32), channel_id=1, source_target_pairs={{0,12},{2,14},{4,8},{6,10},{8,4},{10,6},{12,0},{14,2},{16,28},{18,... | collective-permute-start | bytes 196616 | tf_op jit(solution)/shard_map/ppermute | solution.py:227
  124.0 6.8 %collective-permute-start.15 = (bf16[128,256]{1,0:T(8,128)(2,1)S(1)}, bf16[128,256]{1,0:T(8,128)(2,1)S(1)}, u32[]{:S(2)}, u32[]{:S(2)}) collective-permute-start(bf16[128,256]{1,0:T(8,128)(2,1)S(1)} %get-tuple-element.33), channel_id=1, source_target_pairs={{0,14},{2,12},{4,10},{6,8},{8,6},{10,4},{12,2},{14,0},{16,30},{18,... | collective-permute-start | bytes 196616 | tf_op jit(solution)/shard_map/ppermute | solution.py:227
  127.4 3.3 %collective-permute-start.9 = (bf16[128,256]{1,0:T(8,128)(2,1)S(1)}, bf16[128,256]{1,0:T(8,128)(2,1)S(1)}, u32[]{:S(2)}, u32[]{:S(2)}) collective-permute-start(bf16[128,256]{1,0:T(8,128)(2,1)S(1)} %get-tuple-element.27), channel_id=1, source_target_pairs={{0,2},{2,0},{4,6},{6,4},{8,10},{10,8},{12,14},{14,12},{16,18},{18,... | collective-permute-start | bytes 196616 | tf_op jit(solution)/shard_map/ppermute | solution.py:227

commit v10 on v9

v10 whole, which is shorter than its diff:
```python
import functools
import math

import jax
import jax.numpy as jnp
from jax import lax
from jax.experimental import pallas as pl
from jax.experimental.pallas import tpu as pltpu
from jax.sharding import PartitionSpec as P

BQ = 256
WK = 4
HB = 4
PAIR = 2
PARAMS = pltpu.CompilerParams(vmem_limit_bytes=40 * 1024 * 1024)
ANY = pl.BlockSpec(memory_space=pl.ANY)
HBM = pl.BlockSpec(memory_space=pltpu.HBM)
VMEM = pl.BlockSpec(memory_space=pltpu.VMEM)
SMEM = pl.BlockSpec(memory_space=pltpu.SMEM)


def pin(*arrays):
    return [pltpu.with_memory_space_constraint(a, pltpu.HBM) for a in arrays]


def moves(size):
    return pl.CostEstimate(flops=0, bytes_accessed=size, transcendentals=0)


def pack_kernel(*refs, count, chunks):
    arrays, out = refs[:count], refs[count]
    held, staged, sems, out_sems = refs[-4:]
    chips, columns = out.shape[0], held.shape[2]
    hd, some, step = columns // chips // PAIR, chips // chunks, columns // chunks
    copies = {}
    for c in range(chunks):
        lanes = pl.ds(c * step, step)
        for a, array in enumerate(arrays):
            copies[c, a] = pltpu.make_async_copy(
                array.at[:, lanes], held.at[a, :, lanes], sems.at[c, a]
            )
            copies[c, a].start()
    sends = []
    for c in range(chunks):
        for a in range(count):
            copies[c, a].wait()
        for chip in range(c * some, (c + 1) * some):
            for h in range(PAIR):
                source = (chip * PAIR + h) * hd
                for a in range(count):
                    target = (h * count + a) * hd
                    staged[chip, :, target : target + hd] = held[a, :, source : source + hd]
        part = pl.ds(c * some, some)
        sends.append(pltpu.make_async_copy(staged.at[part], out.at[part], out_sems.at[c]))
        sends[-1].start()
    for send in sends:
        send.wait()


def to_chips(arrays, devices, chunks=4):
    tokens, columns = arrays[0].shape
    count, chips = len(arrays), devices // PAIR
    shape = (chips, tokens, count * columns // chips)
    return pl.pallas_call(
        functools.partial(pack_kernel, count=count, chunks=chunks),
        in_specs=[HBM] * count,
        out_specs=HBM,
        out_shape=pltpu.HBM(shape, jnp.bfloat16),
        scratch_shapes=[
            pltpu.VMEM((count, tokens, columns), jnp.bfloat16),
            pltpu.VMEM(shape, jnp.bfloat16),
            pltpu.SemaphoreType.DMA((chunks, count)),
            pltpu.SemaphoreType.DMA((chunks,)),
        ],
        compiler_params=PARAMS,
        cost_estimate=moves(4 * count * tokens * columns),
    )(*pin(*arrays))


def exchange(pieces, devices):
    groups = [list(range(core, devices, PAIR)) for core in range(PAIR)]
    return lax.all_to_all(
        pieces, "heads", split_axis=0, concat_axis=0, axis_index_groups=groups, tiled=True
    )


def unpack_kernel(chip, *refs, order):
    pieces, arrays = refs[: len(order)], refs[len(order) :]
    hd = pieces[0].shape[1] // len(arrays) // PAIR
    for k, piece in zip(order, pieces):
        for h in range(PAIR):
            columns = pl.ds(pl.multiple_of(((chip[0] ^ k) * PAIR + h) * hd, hd), hd)
            for a, array in enumerate(arrays):
                source = (h * len(arrays) + a) * hd
                array[:, columns] = piece[:, source : source + hd]


def unpack(chip, pieces, count):
    tokens, width = pieces[0].shape
    columns = len(pieces) * width // count
    return pl.pallas_call(
        functools.partial(unpack_kernel, order=list(pieces)),
        in_specs=[SMEM] + [VMEM] * len(pieces),
        out_specs=[VMEM] * count,
        out_shape=[jax.ShapeDtypeStruct((tokens, columns), jnp.bfloat16)] * count,
        compiler_params=PARAMS,
        cost_estimate=moves(4 * len(pieces) * tokens * width),
    )(chip, *pieces.values())


def attend_kernel(chip, table, q_ref, *refs, sources, later, first, hd):
    parts, outs = refs[: PAIR * sources], refs[PAIR * sources + later : -2]
    kv, sems = refs[-2:]
    tokens = q_ref.shape[1]
    copies = []
    for core in range(PAIR):
        row = 0
        for i in range(sources):
            ref = parts[core * sources + i]
            target = kv.at[pl.ds(row, ref.shape[0]), core]
            copies.append(pltpu.make_async_copy(ref, target, sems.at[core * sources + i]))
            row += ref.shape[0]
    for copy in copies:
        copy.start()
    for copy in copies:
        copy.wait()

    scale = hd ** (-0.5)
    factor = scale * math.log2(math.e)
    trans = (((1,), (1,)), ((), ()))

    def products(i, h):
        block = chip[0] ^ (first + i)
        both = q_ref[block, :, 2 * h * hd : 2 * (h + 1) * hd]
        query = both[:, :hd]
        left = jnp.concatenate([jnp.zeros_like(query), query], axis=1)
        left = jnp.concatenate([left, both], axis=0)
        window = [table[block * WK + w] for w in range(WK)]
        low = 4 * h * hd
        scores, tans = [], []
        for index in window:
            keys = kv[index, :, :, low : low + 2 * hd].reshape(BQ, 2 * hd)
            product = lax.dot_general(left, keys, trans, preferred_element_type=jnp.float32)
            scores.append(product[:tokens])
            tans.append(product[tokens:])
        return window, scores, tans

    def finish(i, h, window, scores, tans):
        top = functools.reduce(jnp.maximum, scores)
        top = jnp.max(top, axis=1, keepdims=True) * factor
        probs = [jnp.exp2(s * factor - top) for s in scores]
        weighted = [p * t for p, t in zip(probs, tans)]
        total = jnp.sum(functools.reduce(jnp.add, probs), axis=1, keepdims=True)
        mean = jnp.sum(functools.reduce(jnp.add, weighted), axis=1, keepdims=True)
        low = (4 * h + 2) * hd
        mixed = jnp.zeros((2 * tokens, 2 * hd), jnp.float32)
        for index, p, w in zip(window, probs, weighted):
            vals = kv[index, :, :, low : low + 2 * hd].reshape(BQ, 2 * hd)
            right = jnp.concatenate([p.astype(jnp.bfloat16), w.astype(jnp.bfloat16)], axis=0)
            mixed += jnp.dot(right, vals, preferred_element_type=jnp.float32)
        inverse = 1.0 / total
        out = mixed[:tokens, :hd] * inverse
        tan = (mixed[:tokens, hd:] + scale * mixed[tokens:, :hd]) * inverse
        tan = tan - (scale * mean * inverse) * out
        outs[i][:, 2 * h * hd : (2 * h + 1) * hd] = out.astype(jnp.bfloat16)
        outs[i][:, (2 * h + 1) * hd : 2 * (h + 1) * hd] = tan.astype(jnp.bfloat16)

    units = [(i, h) for i in range(len(outs)) for h in range(PAIR)]
    ahead = products(*units[0])
    for unit, following in zip(units, units[1:] + [None]):
        current = ahead
        if following is not None:
            ahead = products(*following)
        finish(*unit, *current)


def attend(chip, table, queries, mine, other, later, first, count):
    _, tokens, width = queries.shape
    hd, sources = width // (2 * PAIR), len(mine)
    total = sum(a.shape[0] for a in mine)
    elements = count * BQ * WK * BQ
    return pl.pallas_call(
        functools.partial(
            attend_kernel, sources=sources, later=len(later), first=first, hd=hd
        ),
        in_specs=[SMEM, SMEM, VMEM] + [ANY] * (PAIR * sources + len(later)),
        out_specs=[VMEM] * count,
        out_shape=[jax.ShapeDtypeStruct((tokens, width), jnp.bfloat16)] * count,
        scratch_shapes=[
            pltpu.VMEM((total, PAIR, tokens, 2 * width), jnp.bfloat16),
            pltpu.SemaphoreType.DMA((PAIR * sources,)),
        ],
        compiler_params=PARAMS,
        cost_estimate=pl.CostEstimate(
            flops=12 * elements * hd,
            bytes_accessed=8 * total * tokens * width,
            transcendentals=elements,
        ),
    )(chip, table, queries, *mine, *other, *later)


def slots(neighbors, frame, blocks):
    local = neighbors - frame * blocks
    even = frame % 2 == 0
    before = blocks + jnp.where(even, HB, 0) + local + HB
    after = blocks + jnp.where(even, 0, HB) + local - blocks
    return jnp.where(local < 0, before, jnp.where(local >= blocks, after, local)).reshape(-1)


def per_device(query, keys, values, query_tan, keys_tan, values_tan, neighbors):
    devices, frames = lax.axis_size("heads"), lax.axis_size("frames")
    frame = lax.axis_index("frames")
    chip = (lax.axis_index("heads") // PAIR).reshape(1).astype(jnp.int32)
    blocks = neighbors.shape[0]
    swap = [(d, d ^ 1) for d in range(devices)]
    kv = exchange(to_chips([keys_tan, keys, values, values_tan], devices), devices)

    mine = [kv]
    for first in (0, 1):
        pairs = [(i, i + 1) for i in range(first, frames - 1, 2)]
        if pairs:
            start = jnp.where(frame % 2 == first, blocks - HB, 0)
            edge = lax.dynamic_slice_in_dim(kv, start, HB, axis=0)
            mine.append(lax.ppermute(edge, "frames", pairs + [(j, i) for i, j in pairs]))
    other = [lax.ppermute(a, "heads", swap) for a in mine]

    queries = exchange(to_chips([query, query_tan], devices), devices)
    table = slots(neighbors, frame, blocks)
    half = blocks // 2
    back, later = {}, []
    for first in (half, 0):
        pieces = attend(chip, table, queries, mine, other, later, first, half)
        for k, piece in enumerate(pieces, first):
            pairs = [(d, d ^ (k * PAIR)) for d in range(devices)]
            back[k] = lax.ppermute(piece, "heads", pairs) if k else piece
        later = [back[half]]
    return unpack(chip, back, 2)


def solution(mesh):
    own = P(("frames", "heads"), None)
    return jax.shard_map(
        per_device,
        mesh=mesh,
        in_specs=(own,) * 6 + (P("frames", None),),
        out_specs=(own, own),
        check_vma=False,
    )
```

time: 132 us -> 134 us (1.015)
  starting transfers between devices: 43.7 us -> 23.7 us
  waiting for transfers between devices: 70.1 us -> 89.8 us
  Pallas kernels: 16.2 us -> 17.9 us
    ppermute x1, waiting for transfers between devices: 3.92 us -> 16.7 us  [per_device(): lax.ppermute(edge, 'frames', pairs + [(j, i) for i, j in pairs])]
    ppermute x15 -> x7, starting transfers between devices: 23.6 us -> 11.3 us  [per_device(): back[k] = lax.ppermute(piece, 'heads', pairs) if k else piece]
    ppermute x15 -> x7, waiting for transfers between devices: 7.13 us -> 15.2 us  [per_device(): back[k] = lax.ppermute(piece, 'heads', pairs) if k else piece]
    all_to_all x2, starting transfers between devices: 18.6 us -> 10.9 us  [exchange(): lax.all_to_all(pieces, 'heads', split_axis=0, concat_axis=0, axis_index_g...]
    pallas_call x5, Pallas kernels: 16.2 us -> 17.9 us  [the longest x2 11.8 us: attend(): pl.pallas_call(functools.partial(attend_kernel, sources=sources, later=le...]
  transfers between devices with their start and end apart: 18 -> 12, of which waited for: 6 -> 7; matrix products, arithmetic and copies ran while one was open for 1% -> 0% of each run, Pallas kernels for 5% -> 6%
where the time goes in v10:
time: 134 us; the launch traced here: 133 us
  waiting for transfers between devices  89.8 us (67%)
  starting transfers between devices  23.7 us (18%)
  Pallas kernels  17.9 us (13%)
    all_to_all x2, waiting for transfers between devices, exchange(): lax.all_to_all(pieces, 'heads', split_axis=0, concat_axis=0, axis_index_g...  57.9 us
    ppermute x1, waiting for transfers between devices, per_device(): lax.ppermute(edge, 'frames', pairs + [(j, i) for i, j in pairs])  16.7 us
    ppermute x7, waiting for transfers between devices, per_device(): back[k] = lax.ppermute(piece, 'heads', pairs) if k else piece  15.2 us
    pallas_call x2, Pallas kernels, attend(): pl.pallas_call(functools.partial(attend_kernel, sources=sources, later=le...  11.8 us
    ppermute x7, starting transfers between devices, per_device(): back[k] = lax.ppermute(piece, 'heads', pairs) if k else piece  11.3 us
    all_to_all x2, starting transfers between devices, exchange(): lax.all_to_all(pieces, 'heads', split_axis=0, concat_axis=0, axis_index_g...  10.9 us
    pallas_call x2, Pallas kernels, to_chips(): pl.pallas_call(functools.partial(pack_kernel, count=count, chunks=chunks)...  4.9 us
  transfers between devices with their start and end apart: 12, of which 7 were waited for; matrix products, arithmetic and copies ran while one was open for 0% of the time, Pallas kernels for 6%

profile of v10, /device:TPU:0, one launch (start us, length us, event | category | flops | bytes accessed | tf_op | source)
XLA Modules:
  0.0 133.4 jit_solution(3968159683115244998)
XLA Ops:
  0.6 2.7 %shard_map.87 = bf16[8,128,1024]{2,1,0:T(8,128)(2,1)} custom-call(bf16[128,2048]{1,0:T(8,128)(2,1)} %refs_0_.3, bf16[128,2048]{1,0:T(8,128)(2,1)} %refs_1_.3, bf16[128,2048]{1,0:T(8,128)(2,1)} %refs_2_.1, bf16[128,2048]{1,0:T(8,128)(2,1)} %refs_3_.1), custom_call_target="tpu_custom_call" | custom-call | bytes 4194304 | tf_op jit(solution)/shard_map/pallas_call | solution.py:64
  3.4 7.3 %all-to-all-start.1 = ((bf16[8,128,1024]{2,1,0:T(8,128)(2,1)}), bf16[8,128,1024]{2,1,0:T(8,128)(2,1)S(1)}, u32[]{:S(2)}, u32[]{:S(2)}) async-start(bf16[8,128,1024]{2,1,0:T(8,128)(2,1)} %shard_map.87), calls=%async_computation.1 | async-start | bytes 4194304 | tf_op jit(solution)/shard_map/all_to_all | solution.py:82
  10.6 48.2 %all-to-all-done.1.refs_0_ = bf16[8,128,1024]{2,1,0:T(8,128)(2,1)S(1)} async-done(((bf16[8,128,1024]{2,1,0:T(8,128)(2,1)}), bf16[8,128,1024]{2,1,0:T(8,128)(2,1)S(1)}, u32[]{:S(2)}, u32[]{:S(2)}) %all-to-all-start.1) | async-done | bytes 2097184 | tf_op jit(solution)/shard_map/all_to_all | solution.py:82
  58.9 1.1 constant_dynamic-slice_fusion
  60.0 0.0 copy-start
  60.0 1.5 %collective-permute-start = (bf16[4,128,1024]{2,1,0:T(8,128)(2,1)}, bf16[4,128,1024]{2,1,0:T(8,128)(2,1)}, u32[]{:S(2)}, u32[]{:S(2)}) collective-permute-start(bf16[4,128,1024]{2,1,0:T(8,128)(2,1)} %constant_dynamic-slice_fusion), channel_id=1, source_target_pairs={{0,1},{1,0},{2,3},{3,2},{4,5},{5,4},{6,7},{7,6},{8,9},{9,8},{10,11... | collective-permute-start | bytes 3145736 | tf_op jit(solution)/shard_map/ppermute | solution.py:224
  61.5 0.0 collective-permute-start.1
  61.5 2.2 %shard_map.86 = bf16[8,128,512]{2,1,0:T(8,128)(2,1)} custom-call(bf16[128,2048]{1,0:T(8,128)(2,1)} %refs_0_.2, bf16[128,2048]{1,0:T(8,128)(2,1)} %refs_1_.2), custom_call_target="tpu_custom_call" | custom-call | bytes 2097152 | tf_op jit(solution)/shard_map/pallas_call | solution.py:64
  63.7 3.6 %all-to-all-start = ((bf16[8,128,512]{2,1,0:T(8,128)(2,1)}), bf16[8,128,512]{2,1,0:T(8,128)(2,1)S(1)}, u32[]{:S(2)}, u32[]{:S(2)}) async-start(bf16[8,128,512]{2,1,0:T(8,128)(2,1)} %shard_map.86), calls=%async_computation | async-start | bytes 2097152 | tf_op jit(solution)/shard_map/all_to_all | solution.py:82
  67.3 16.7 %collective-permute-done.refs_1_ = bf16[4,128,1024]{2,1,0:T(8,128)(2,1)} collective-permute-done((bf16[4,128,1024]{2,1,0:T(8,128)(2,1)}, bf16[4,128,1024]{2,1,0:T(8,128)(2,1)}, u32[]{:S(2)}, u32[]{:S(2)}) %collective-permute-start) | collective-permute-done | bytes 1048608 | tf_op jit(solution)/shard_map/ppermute | solution.py:224
  84.0 0.0 collective-permute-start.2
  84.0 0.0 copy-done
  84.0 0.1 copy.10
  84.1 0.1 reshape.11.table
  84.2 9.7 %all-to-all-done.q_ref = bf16[8,128,512]{2,1,0:T(8,128)(2,1)S(1)} async-done(((bf16[8,128,512]{2,1,0:T(8,128)(2,1)}), bf16[8,128,512]{2,1,0:T(8,128)(2,1)S(1)}, u32[]{:S(2)}, u32[]{:S(2)}) %all-to-all-start) | async-done | bytes 1048608 | tf_op jit(solution)/shard_map/all_to_all | solution.py:82
  93.9 0.0 collective-permute-done.2.refs_3_
  93.9 0.0 collective-permute-done.1.refs_2_
  93.9 5.9 %shard_map.88 = (bf16[128,512]{1,0:T(8,128)(2,1)S(1)}, bf16[128,512]{1,0:T(8,128)(2,1)S(1)}, bf16[128,512]{1,0:T(8,128)(2,1)S(1)}, bf16[128,512]{1,0:T(8,128)(2,1)S(1)}) custom-call(s32[1]{0:T(128)} %bitcast.chip, s32[32]{0:T(128)S(1)} %reshape.11.table, bf16[8,128,512]{2,1,0:T(8,128)(2,1)S(1)} %all-to-all-done.q_ref, ...), custom_call_target="tpu_custom_call" | custom-call | flops 1610612736 | bytes 6291456 | tf_op jit(solution)/shard_map/pallas_call | solution.py:182
  99.8 0.1 collective-permute-start.3
  99.8 3.8 %collective-permute-start.4 = (bf16[128,512]{1,0:T(8,128)(2,1)S(1)}, bf16[128,512]{1,0:T(8,128)(2,1)S(1)}, u32[]{:S(2)}, u32[]{:S(2)}) collective-permute-start(bf16[128,512]{1,0:T(8,128)(2,1)S(1)} %get-tuple-element.11), channel_id=1, source_target_pairs={{0,20},{2,22},{4,16},{6,18},{8,28},{10,30},{12,24},{14,26},{16,4},... | collective-permute-start | bytes 393224 | tf_op jit(solution)/shard_map/ppermute | solution.py:235
  103.6 1.5 %collective-permute-start.5 = (bf16[128,512]{1,0:T(8,128)(2,1)S(1)}, bf16[128,512]{1,0:T(8,128)(2,1)S(1)}, u32[]{:S(2)}, u32[]{:S(2)}) collective-permute-start(bf16[128,512]{1,0:T(8,128)(2,1)S(1)} %get-tuple-element.12), channel_id=1, source_target_pairs={{0,24},{2,26},{4,28},{6,30},{8,16},{10,18},{12,20},{14,22},{16,8},... | collective-permute-start | bytes 393224 | tf_op jit(solution)/shard_map/ppermute | solution.py:235
  105.1 2.4 %collective-permute-start.6 = (bf16[128,512]{1,0:T(8,128)(2,1)S(1)}, bf16[128,512]{1,0:T(8,128)(2,1)S(1)}, u32[]{:S(2)}, u32[]{:S(2)}) collective-permute-start(bf16[128,512]{1,0:T(8,128)(2,1)S(1)} %get-tuple-element.13), channel_id=1, source_target_pairs={{0,28},{2,30},{4,24},{6,26},{8,20},{10,22},{12,16},{14,18},{16,12}... | collective-permute-start | bytes 393224 | tf_op jit(solution)/shard_map/ppermute | solution.py:235
  107.5 9.7 %collective-permute-done.3.refs_4_.refs_0_ = bf16[128,512]{1,0:T(8,128)(2,1)S(1)} collective-permute-done((bf16[128,512]{1,0:T(8,128)(2,1)S(1)}, bf16[128,512]{1,0:T(8,128)(2,1)S(1)}, u32[]{:S(2)}, u32[]{:S(2)}) %collective-permute-start.3) | collective-permute-done | bytes 131104 | tf_op jit(solution)/shard_map/ppermute | solution.py:235
  117.2 5.9 %shard_map.89 = (bf16[128,512]{1,0:T(8,128)(2,1)S(1)}, bf16[128,512]{1,0:T(8,128)(2,1)S(1)}, bf16[128,512]{1,0:T(8,128)(2,1)S(1)}, bf16[128,512]{1,0:T(8,128)(2,1)S(1)}) custom-call(s32[1]{0:T(128)} %bitcast.chip, s32[32]{0:T(128)S(1)} %reshape.11.table, bf16[8,128,512]{2,1,0:T(8,128)(2,1)S(1)} %all-to-all-done.q_ref, ...), custom_call_target="tpu_custom_call" | custom-call | flops 1610612736 | bytes 6291456 | tf_op jit(solution)/shard_map/pallas_call | solution.py:182
  123.1 0.7 collective-permute-start.7
  123.7 0.0 collective-permute-start.8
  123.7 0.0 collective-permute-done.4.refs_1_
  123.7 2.9 %collective-permute-start.9 = (bf16[128,512]{1,0:T(8,128)(2,1)S(1)}, bf16[128,512]{1,0:T(8,128)(2,1)S(1)}, u32[]{:S(2)}, u32[]{:S(2)}) collective-permute-start(bf16[128,512]{1,0:T(8,128)(2,1)S(1)} %get-tuple-element.17), channel_id=1, source_target_pairs={{0,12},{2,14},{4,8},{6,10},{8,4},{10,6},{12,0},{14,2},{16,28},{18,... | collective-permute-start | bytes 393224 | tf_op jit(solution)/shard_map/ppermute | solution.py:235
  126.6 0.0 collective-permute-done.5.refs_2_
  126.6 0.0 collective-permute-done.6.refs_3_
  126.6 2.0 %collective-permute-done.7.refs_5_ = bf16[128,512]{1,0:T(8,128)(2,1)S(1)} collective-permute-done((bf16[128,512]{1,0:T(8,128)(2,1)S(1)}, bf16[128,512]{1,0:T(8,128)(2,1)S(1)}, u32[]{:S(2)}, u32[]{:S(2)}) %collective-permute-start.7) | collective-permute-done | bytes 131104 | tf_op jit(solution)/shard_map/ppermute | solution.py:235
  128.7 1.5 %collective-permute-done.8.refs_6_ = bf16[128,512]{1,0:T(8,128)(2,1)S(1)} collective-permute-done((bf16[128,512]{1,0:T(8,128)(2,1)S(1)}, bf16[128,512]{1,0:T(8,128)(2,1)S(1)}, u32[]{:S(2)}, u32[]{:S(2)}) %collective-permute-start.8) | collective-permute-done | bytes 131104 | tf_op jit(solution)/shard_map/ppermute | solution.py:235
  130.2 2.0 %collective-permute-done.9.refs_7_ = bf16[128,512]{1,0:T(8,128)(2,1)S(1)} collective-permute-done((bf16[128,512]{1,0:T(8,128)(2,1)S(1)}, bf16[128,512]{1,0:T(8,128)(2,1)S(1)}, u32[]{:S(2)}, u32[]{:S(2)}) %collective-permute-start.9) | collective-permute-done | bytes 131104 | tf_op jit(solution)/shard_map/ppermute | solution.py:235
  132.1 1.3 shard_map.90
  (1 shorter events, 0.0 us)
Async XLA Ops:
  3.4 55.5 %all-to-all-start.1 = ((bf16[8,128,1024]{2,1,0:T(8,128)(2,1)}), bf16[8,128,1024]{2,1,0:T(8,128)(2,1)S(1)}, u32[]{:S(2)}, u32[]{:S(2)}) async-start(bf16[8,128,1024]{2,1,0:T(8,128)(2,1)} %shard_map.87), calls=%async_computation.1 | async-start | bytes 4194304 | tf_op jit(solution)/shard_map/all_to_all | solution.py:82
  60.0 24.1 %copy-start = (s32[8,4]{0,1:T(4,128)S(1)}, s32[8,4]{0,1:T(4,128)}, u32[]{:S(2)}) copy-start(s32[8,4]{0,1:T(4,128)} %param.13) | copy-start | bytes 388
  60.0 24.1 %collective-permute-start = (bf16[4,128,1024]{2,1,0:T(8,128)(2,1)}, bf16[4,128,1024]{2,1,0:T(8,128)(2,1)}, u32[]{:S(2)}, u32[]{:S(2)}) collective-permute-start(bf16[4,128,1024]{2,1,0:T(8,128)(2,1)} %constant_dynamic-slice_fusion), channel_id=1, source_target_pairs={{0,1},{1,0},{2,3},{3,2},{4,5},{5,4},{6,7},{7,6},{8,9},{9,8},{10,11... | collective-permute-start | bytes 3145736 | tf_op jit(solution)/shard_map/ppermute | solution.py:224
  61.5 32.4 %collective-permute-start.1 = (bf16[8,128,1024]{2,1,0:T(8,128)(2,1)S(1)}, bf16[8,128,1024]{2,1,0:T(8,128)(2,1)}, u32[]{:S(2)}, u32[]{:S(2)}) collective-permute-start(bf16[8,128,1024]{2,1,0:T(8,128)(2,1)S(1)} %all-to-all-done.1.refs_0_), channel_id=1, source_target_pairs={{0,2},{2,0},{4,6},{6,4},{8,10},{10,8},{12,14},{14,12},{16,18},{18,... | collective-permute-start | bytes 6291464 | tf_op jit(solution)/shard_map/ppermute | solution.py:225
  63.7 30.2 %all-to-all-start = ((bf16[8,128,512]{2,1,0:T(8,128)(2,1)}), bf16[8,128,512]{2,1,0:T(8,128)(2,1)S(1)}, u32[]{:S(2)}, u32[]{:S(2)}) async-start(bf16[8,128,512]{2,1,0:T(8,128)(2,1)} %shard_map.86), calls=%async_computation | async-start | bytes 2097152 | tf_op jit(solution)/shard_map/all_to_all | solution.py:82
  84.0 9.8 %collective-permute-start.2 = (bf16[4,128,1024]{2,1,0:T(8,128)(2,1)}, bf16[4,128,1024]{2,1,0:T(8,128)(2,1)}, u32[]{:S(2)}, u32[]{:S(2)}) collective-permute-start(bf16[4,128,1024]{2,1,0:T(8,128)(2,1)} %collective-permute-done.refs_1_), channel_id=1, source_target_pairs={{0,2},{2,0},{4,6},{6,4},{8,10},{10,8},{12,14},{14,12},{16,18},{18,... | collective-permute-start | bytes 3145736 | tf_op jit(solution)/shard_map/ppermute | solution.py:225
  99.8 17.4 %collective-permute-start.3 = (bf16[128,512]{1,0:T(8,128)(2,1)S(1)}, bf16[128,512]{1,0:T(8,128)(2,1)S(1)}, u32[]{:S(2)}, u32[]{:S(2)}) collective-permute-start(bf16[128,512]{1,0:T(8,128)(2,1)S(1)} %get-tuple-element.10), channel_id=1, source_target_pairs={{0,16},{2,18},{4,20},{6,22},{8,24},{10,26},{12,28},{14,30},{16,0},... | collective-permute-start | bytes 393224 | tf_op jit(solution)/shard_map/ppermute | solution.py:235
  99.8 23.9 %collective-permute-start.4 = (bf16[128,512]{1,0:T(8,128)(2,1)S(1)}, bf16[128,512]{1,0:T(8,128)(2,1)S(1)}, u32[]{:S(2)}, u32[]{:S(2)}) collective-permute-start(bf16[128,512]{1,0:T(8,128)(2,1)S(1)} %get-tuple-element.11), channel_id=1, source_target_pairs={{0,20},{2,22},{4,16},{6,18},{8,28},{10,30},{12,24},{14,26},{16,4},... | collective-permute-start | bytes 393224 | tf_op jit(solution)/shard_map/ppermute | solution.py:235
  103.6 23.0 %collective-permute-start.5 = (bf16[128,512]{1,0:T(8,128)(2,1)S(1)}, bf16[128,512]{1,0:T(8,128)(2,1)S(1)}, u32[]{:S(2)}, u32[]{:S(2)}) collective-permute-start(bf16[128,512]{1,0:T(8,128)(2,1)S(1)} %get-tuple-element.12), channel_id=1, source_target_pairs={{0,24},{2,26},{4,28},{6,30},{8,16},{10,18},{12,20},{14,22},{16,8},... | collective-permute-start | bytes 393224 | tf_op jit(solution)/shard_map/ppermute | solution.py:235
  105.1 21.5 %collective-permute-start.6 = (bf16[128,512]{1,0:T(8,128)(2,1)S(1)}, bf16[128,512]{1,0:T(8,128)(2,1)S(1)}, u32[]{:S(2)}, u32[]{:S(2)}) collective-permute-start(bf16[128,512]{1,0:T(8,128)(2,1)S(1)} %get-tuple-element.13), channel_id=1, source_target_pairs={{0,28},{2,30},{4,24},{6,26},{8,20},{10,22},{12,16},{14,18},{16,12}... | collective-permute-start | bytes 393224 | tf_op jit(solution)/shard_map/ppermute | solution.py:235
  123.1 5.6 %collective-permute-start.7 = (bf16[128,512]{1,0:T(8,128)(2,1)S(1)}, bf16[128,512]{1,0:T(8,128)(2,1)S(1)}, u32[]{:S(2)}, u32[]{:S(2)}) collective-permute-start(bf16[128,512]{1,0:T(8,128)(2,1)S(1)} %get-tuple-element.15), channel_id=1, source_target_pairs={{0,4},{2,6},{4,0},{6,2},{8,12},{10,14},{12,8},{14,10},{16,20},{18,... | collective-permute-start | bytes 393224 | tf_op jit(solution)/shard_map/ppermute | solution.py:235
  123.7 6.4 %collective-permute-start.8 = (bf16[128,512]{1,0:T(8,128)(2,1)S(1)}, bf16[128,512]{1,0:T(8,128)(2,1)S(1)}, u32[]{:S(2)}, u32[]{:S(2)}) collective-permute-start(bf16[128,512]{1,0:T(8,128)(2,1)S(1)} %get-tuple-element.16), channel_id=1, source_target_pairs={{0,8},{2,10},{4,12},{6,14},{8,0},{10,2},{12,4},{14,6},{16,24},{18,... | collective-permute-start | bytes 393224 | tf_op jit(solution)/shard_map/ppermute | solution.py:235
  123.7 8.4 %collective-permute-start.9 = (bf16[128,512]{1,0:T(8,128)(2,1)S(1)}, bf16[128,512]{1,0:T(8,128)(2,1)S(1)}, u32[]{:S(2)}, u32[]{:S(2)}) collective-permute-start(bf16[128,512]{1,0:T(8,128)(2,1)S(1)} %get-tuple-element.17), channel_id=1, source_target_pairs={{0,12},{2,14},{4,8},{6,10},{8,4},{10,6},{12,0},{14,2},{16,28},{18,... | collective-permute-start | bytes 393224 | tf_op jit(solution)/shard_map/ppermute | solution.py:235

commit v11 on v10

--- a/solution.py
+++ b/solution.py
@@ -12,6 +12,7 @@
 WK = 4
 HB = 4
 PAIR = 2
+LEAD = 16
 PARAMS = pltpu.CompilerParams(vmem_limit_bytes=40 * 1024 * 1024)
 ANY = pl.BlockSpec(memory_space=pl.ANY)
 HBM = pl.BlockSpec(memory_space=pltpu.HBM)
@@ -27,9 +28,10 @@
     return pl.CostEstimate(flops=0, bytes_accessed=size, transcendentals=0)
 
 
-def pack_kernel(*refs, count, chunks):
-    arrays, out = refs[:count], refs[count]
+def pack_kernel(before, *refs, count, chunks):
+    arrays, out, zero = refs[:count], refs[count], refs[count + 1]
     held, staged, sems, out_sems = refs[-4:]
+    zero[0] = before[0]
     chips, columns = out.shape[0], held.shape[2]
     hd, some, step = columns // chips // PAIR, chips // chunks, columns // chunks
     copies = {}
@@ -57,15 +59,15 @@
         send.wait()
 
 
-def to_chips(arrays, devices, chunks=4):
+def to_chips(before, arrays, devices, chunks=4):
     tokens, columns = arrays[0].shape
     count, chips = len(arrays), devices // PAIR
     shape = (chips, tokens, count * columns // chips)
     return pl.pallas_call(
         functools.partial(pack_kernel, count=count, chunks=chunks),
-        in_specs=[HBM] * count,
-        out_specs=HBM,
-        out_shape=pltpu.HBM(shape, jnp.bfloat16),
+        in_specs=[SMEM] + [HBM] * count,
+        out_specs=[HBM, SMEM],
+        out_shape=[pltpu.HBM(shape, jnp.bfloat16), jax.ShapeDtypeStruct((1,), jnp.int32)],
         scratch_shapes=[
             pltpu.VMEM((count, tokens, columns), jnp.bfloat16),
             pltpu.VMEM(shape, jnp.bfloat16),
@@ -74,7 +76,7 @@
         ],
         compiler_params=PARAMS,
         cost_estimate=moves(4 * count * tokens * columns),
-    )(*pin(*arrays))
+    )(before, *pin(*arrays))
 
 
 def exchange(pieces, devices):
@@ -84,31 +86,30 @@
     )
 
 
-def unpack_kernel(chip, *refs, order):
-    pieces, arrays = refs[: len(order)], refs[len(order) :]
+def unpack_kernel(chip, *refs, places):
+    pieces, arrays = refs[: len(places)], refs[len(places) :]
     hd = pieces[0].shape[1] // len(arrays) // PAIR
-    for k, piece in zip(order, pieces):
+    for (k, row), piece in zip(places, pieces):
+        rows = slice(row, row + piece.shape[0])
         for h in range(PAIR):
             columns = pl.ds(pl.multiple_of(((chip[0] ^ k) * PAIR + h) * hd, hd), hd)
             for a, array in enumerate(arrays):
                 source = (h * len(arrays) + a) * hd
-                array[:, columns] = piece[:, source : source + hd]
-
-
-def unpack(chip, pieces, count):
-    tokens, width = pieces[0].shape
-    columns = len(pieces) * width // count
+                array[rows, columns] = piece[:, source : source + hd]
+
+
+def unpack(chip, pieces, tokens, columns, count):
     return pl.pallas_call(
-        functools.partial(unpack_kernel, order=list(pieces)),
+        functools.partial(unpack_kernel, places=list(pieces)),
         in_specs=[SMEM] + [VMEM] * len(pieces),
         out_specs=[VMEM] * count,
         out_shape=[jax.ShapeDtypeStruct((tokens, columns), jnp.bfloat16)] * count,
         compiler_params=PARAMS,
-        cost_estimate=moves(4 * len(pieces) * tokens * width),
+        cost_estimate=moves(4 * count * tokens * columns),
     )(chip, *pieces.values())
 
 
-def attend_kernel(chip, table, q_ref, *refs, sources, later, first, hd):
+def attend_kernel(chip, table, q_ref, *refs, sources, later, places, hd):
     parts, outs = refs[: PAIR * sources], refs[PAIR * sources + later : -2]
     kv, sems = refs[-2:]
     tokens = q_ref.shape[1]
@@ -129,8 +130,8 @@
     factor = scale * math.log2(math.e)
     trans = (((1,), (1,)), ((), ()))
 
-    def products(i, h):
-        block = chip[0] ^ (first + i)
+    def products(k, h):
+        block = chip[0] ^ k
         both = q_ref[block, :, 2 * h * hd : 2 * (h + 1) * hd]
         query = both[:, :hd]
         left = jnp.concatenate([jnp.zeros_like(query), query], axis=1)
@@ -145,7 +146,7 @@
             tans.append(product[tokens:])
         return window, scores, tans
 
-    def finish(i, h, window, scores, tans):
+    def finish(k, h, window, scores, tans):
         top = functools.reduce(jnp.maximum, scores)
         top = jnp.max(top, axis=1, keepdims=True) * factor
         probs = [jnp.exp2(s * factor - top) for s in scores]
@@ -162,10 +163,13 @@
         out = mixed[:tokens, :hd] * inverse
         tan = (mixed[:tokens, hd:] + scale * mixed[tokens:, :hd]) * inverse
         tan = tan - (scale * mean * inverse) * out
-        outs[i][:, 2 * h * hd : (2 * h + 1) * hd] = out.astype(jnp.bfloat16)
-        outs[i][:, (2 * h + 1) * hd : 2 * (h + 1) * hd] = tan.astype(jnp.bfloat16)
-
-    units = [(i, h) for i in range(len(outs)) for h in range(PAIR)]
+        for (slot, row), ref in zip(places, outs):
+            if slot == k:
+                rows = slice(row, row + ref.shape[0])
+                ref[:, 2 * h * hd : (2 * h + 1) * hd] = out[rows].astype(jnp.bfloat16)
+                ref[:, (2 * h + 1) * hd : 2 * (h + 1) * hd] = tan[rows].astype(jnp.bfloat16)
+
+    units = [(k, h) for k in dict(places) for h in range(PAIR)]
     ahead = products(*units[0])
     for unit, following in zip(units, units[1:] + [None]):
         current = ahead
@@ -174,18 +178,20 @@
         finish(*unit, *current)
 
 
-def attend(chip, table, queries, mine, other, later, first, count):
+def attend(chip, table, queries, mine, other, later, places):
     _, tokens, width = queries.shape
     hd, sources = width // (2 * PAIR), len(mine)
     total = sum(a.shape[0] for a in mine)
-    elements = count * BQ * WK * BQ
+    elements = len(dict(places)) * BQ * WK * BQ
+    ends = [following[1] or tokens for following in places[1:]] + [tokens]
+    sizes = [end - row for (_, row), end in zip(places, ends)]
     return pl.pallas_call(
         functools.partial(
-            attend_kernel, sources=sources, later=len(later), first=first, hd=hd
+            attend_kernel, sources=sources, later=len(later), places=places, hd=hd
         ),
         in_specs=[SMEM, SMEM, VMEM] + [ANY] * (PAIR * sources + len(later)),
-        out_specs=[VMEM] * count,
-        out_shape=[jax.ShapeDtypeStruct((tokens, width), jnp.bfloat16)] * count,
+        out_specs=[VMEM] * len(places),
+        out_shape=[jax.ShapeDtypeStruct((size, width), jnp.bfloat16) for size in sizes],
         scratch_shapes=[
             pltpu.VMEM((total, PAIR, tokens, 2 * width), jnp.bfloat16),
             pltpu.SemaphoreType.DMA((PAIR * sources,)),
@@ -213,28 +219,33 @@
     chip = (lax.axis_index("heads") // PAIR).reshape(1).astype(jnp.int32)
     blocks = neighbors.shape[0]
     swap = [(d, d ^ 1) for d in range(devices)]
-    kv = exchange(to_chips([keys_tan, keys, values, values_tan], devices), devices)
+    zero = jnp.zeros((1,), jnp.int32)
+    kv_sent, zero = to_chips(zero, [keys_tan, keys, values, values_tan], devices)
+    q_sent, zero = to_chips(zero, [query, query_tan], devices)
+    kv = exchange(kv_sent, devices)
 
     mine = [kv]
     for first in (0, 1):
         pairs = [(i, i + 1) for i in range(first, frames - 1, 2)]
         if pairs:
-            start = jnp.where(frame % 2 == first, blocks - HB, 0)
+            start = jnp.where(frame % 2 == first, blocks - HB, 0) + zero[0]
             edge = lax.dynamic_slice_in_dim(kv, start, HB, axis=0)
             mine.append(lax.ppermute(edge, "frames", pairs + [(j, i) for i, j in pairs]))
     other = [lax.ppermute(a, "heads", swap) for a in mine]
 
-    queries = exchange(to_chips([query, query_tan], devices), devices)
+    queries = exchange(q_sent, devices)
     table = slots(neighbors, frame, blocks)
     half = blocks // 2
+    far, near = [(k, 0) for k in range(half, blocks)], [(k, 0) for k in range(half)]
+    far.insert(1, (half, LEAD))
     back, later = {}, []
-    for first in (half, 0):
-        pieces = attend(chip, table, queries, mine, other, later, first, half)
-        for k, piece in enumerate(pieces, first):
-            pairs = [(d, d ^ (k * PAIR)) for d in range(devices)]
-            back[k] = lax.ppermute(piece, "heads", pairs) if k else piece
-        later = [back[half]]
-    return unpack(chip, back, 2)
+    for places in (far, near):
+        pieces = attend(chip, table, queries, mine, other, later, places)
+        for place, piece in zip(places, pieces):
+            pairs = [(d, d ^ (place[0] * PAIR)) for d in range(devices)]
+            back[place] = lax.ppermute(piece, "heads", pairs) if place[0] else piece
+        later = [back[far[0]]]
+    return unpack(chip, back, *query.shape, 2)
 
 
 def solution(mesh):

time: 134 us -> 127 us (0.948)
  waiting for transfers between devices: 89.8 us -> 83.2 us
  starting transfers between devices: 23.7 us -> 21.7 us
  Pallas kernels: 17.9 us -> 19.6 us
    all_to_all x2, waiting for transfers between devices: 57.9 us -> 51.7 us  [exchange(): lax.all_to_all(pieces, 'heads', split_axis=0, concat_axis=0, axis_index_g...]
    ppermute x7 -> x8, waiting for transfers between devices: 15.2 us -> 12.6 us  [per_device(): back[place] = lax.ppermute(piece, 'heads', pairs) if place[0] else piece]
    ppermute x1, waiting for transfers between devices: 16.7 us -> 18.9 us  [per_device(): lax.ppermute(edge, 'frames', pairs + [(j, i) for i, j in pairs])]
    ppermute x7 -> x8, starting transfers between devices: 11.3 us -> 9.28 us  [per_device(): back[place] = lax.ppermute(piece, 'heads', pairs) if place[0] else piece]
    pallas_call x2, Pallas kernels: 4.9 us -> 6.57 us  [to_chips(): pl.pallas_call(functools.partial(pack_kernel, count=count, chunks=chunks)...]
  transfers between devices with their start and end apart: 12 -> 13, of which waited for: 7 -> 8; matrix products, arithmetic and copies ran while one was open for 0% -> 0% of each run, Pallas kernels for 6% -> 7%
where the time goes in v11:
time: 127 us
  waiting for transfers between devices  83.2 us (66%)
  starting transfers between devices  21.7 us (17%)
  Pallas kernels  19.6 us (15%)
  between operations  1.35 us (1%)
    all_to_all x2, waiting for transfers between devices, exchange(): lax.all_to_all(pieces, 'heads', split_axis=0, concat_axis=0, axis_index_g...  51.7 us
    ppermute x1, waiting for transfers between devices, per_device(): lax.ppermute(edge, 'frames', pairs + [(j, i) for i, j in pairs])  18.9 us
    ppermute x8, waiting for transfers between devices, per_device(): back[place] = lax.ppermute(piece, 'heads', pairs) if place[0] else piece  12.6 us
    pallas_call x2, Pallas kernels, attend(): pl.pallas_call(functools.partial(attend_kernel, sources=sources, later=le...  11.8 us
    all_to_all x2, starting transfers between devices, exchange(): lax.all_to_all(pieces, 'heads', split_axis=0, concat_axis=0, axis_index_g...  10.9 us
    ppermute x8, starting transfers between devices, per_device(): back[place] = lax.ppermute(piece, 'heads', pairs) if place[0] else piece  9.28 us
    pallas_call x2, Pallas kernels, to_chips(): pl.pallas_call(functools.partial(pack_kernel, count=count, chunks=chunks)...  6.57 us
  transfers between devices with their start and end apart: 13, of which 8 were waited for; matrix products, arithmetic and copies ran while one was open for 0% of the time, Pallas kernels for 7%

profile of v11, /device:TPU:0, one launch (start us, length us, event | category | flops | bytes accessed | tf_op | source)
XLA Modules:
  0.0 127.1 jit_solution(8852881717640198812)
XLA Ops:
  0.6 3.3 %shard_map.86 = (bf16[8,128,1024]{2,1,0:T(8,128)(2,1)}, s32[1]{0:T(128)}) custom-call(s32[1]{0:T(128)} %constant.45.clone.1.before, bf16[128,2048]{1,0:T(8,128)(2,1)} %refs_0_.2, bf16[128,2048]{1,0:T(8,128)(2,1)} %refs_1_.2, bf16[128,2048]{1,0:T(8,128)(2,1)} %refs_2_.1, bf16[128,2048]{1,0:T(8,128)(2,1)} %refs_3_.1), custom_call_target="tpu_custom_call" | custom-call | bytes 4194304 | tf_op jit(solution)/shard_map/pallas_call | solution.py:66
  3.9 7.3 %all-to-all-start.1 = ((bf16[8,128,1024]{2,1,0:T(8,128)(2,1)}), bf16[8,128,1024]{2,1,0:T(8,128)(2,1)S(1)}, u32[]{:S(2)}, u32[]{:S(2)}) async-start(bf16[8,128,1024]{2,1,0:T(8,128)(2,1)} %get-tuple-element.17), calls=%async_computation.1 | async-start | bytes 4194304 | tf_op jit(solution)/shard_map/all_to_all | solution.py:84
  11.2 3.3 %shard_map.87 = (bf16[8,128,512]{2,1,0:T(8,128)(2,1)}, s32[1]{0:T(128)}) custom-call(s32[1]{0:T(128)} %get-tuple-element.15.before, bf16[128,2048]{1,0:T(8,128)(2,1)} %refs_0_.3, bf16[128,2048]{1,0:T(8,128)(2,1)} %refs_1_.3), custom_call_target="tpu_custom_call" | custom-call | bytes 2097152 | tf_op jit(solution)/shard_map/pallas_call | solution.py:66
  15.1 0.0 copy-start
  15.1 44.3 %all-to-all-done.1.refs_0_ = bf16[8,128,1024]{2,1,0:T(8,128)(2,1)S(1)} async-done(((bf16[8,128,1024]{2,1,0:T(8,128)(2,1)}), bf16[8,128,1024]{2,1,0:T(8,128)(2,1)S(1)}, u32[]{:S(2)}, u32[]{:S(2)}) %all-to-all-start.1) | async-done | bytes 2097184 | tf_op jit(solution)/shard_map/all_to_all | solution.py:84
  59.4 1.0 constant_dynamic-slice_fusion
  60.4 1.5 %collective-permute-start = (bf16[4,128,1024]{2,1,0:T(8,128)(2,1)}, bf16[4,128,1024]{2,1,0:T(8,128)(2,1)}, u32[]{:S(2)}, u32[]{:S(2)}) collective-permute-start(bf16[4,128,1024]{2,1,0:T(8,128)(2,1)} %constant_dynamic-slice_fusion), channel_id=1, source_target_pairs={{0,1},{1,0},{2,3},{3,2},{4,5},{5,4},{6,7},{7,6},{8,9},{9,8},{10,11... | collective-permute-start | bytes 3145736 | tf_op jit(solution)/shard_map/ppermute | solution.py:233
  62.0 0.0 collective-permute-start.1
  62.0 3.6 %all-to-all-start = ((bf16[8,128,512]{2,1,0:T(8,128)(2,1)}), bf16[8,128,512]{2,1,0:T(8,128)(2,1)S(1)}, u32[]{:S(2)}, u32[]{:S(2)}) async-start(bf16[8,128,512]{2,1,0:T(8,128)(2,1)} %get-tuple-element.16), calls=%async_computation | async-start | bytes 2097152 | tf_op jit(solution)/shard_map/all_to_all | solution.py:84
  65.6 18.9 %collective-permute-done.refs_1_ = bf16[4,128,1024]{2,1,0:T(8,128)(2,1)} collective-permute-done((bf16[4,128,1024]{2,1,0:T(8,128)(2,1)}, bf16[4,128,1024]{2,1,0:T(8,128)(2,1)}, u32[]{:S(2)}, u32[]{:S(2)}) %collective-permute-start) | collective-permute-done | bytes 1048608 | tf_op jit(solution)/shard_map/ppermute | solution.py:233
  84.5 0.0 collective-permute-start.2
  84.5 0.0 copy-done
  84.5 0.1 copy.10
  84.6 0.1 reshape.11.table
  84.7 7.5 %all-to-all-done.q_ref = bf16[8,128,512]{2,1,0:T(8,128)(2,1)S(1)} async-done(((bf16[8,128,512]{2,1,0:T(8,128)(2,1)}), bf16[8,128,512]{2,1,0:T(8,128)(2,1)S(1)}, u32[]{:S(2)}, u32[]{:S(2)}) %all-to-all-start) | async-done | bytes 1048608 | tf_op jit(solution)/shard_map/all_to_all | solution.py:84
  92.2 0.0 collective-permute-done.2.refs_3_
  92.2 0.0 collective-permute-done.1.refs_2_
  92.2 5.9 %shard_map.88 = (bf16[16,512]{1,0:T(8,128)(2,1)S(1)}, bf16[112,512]{1,0:T(8,128)(2,1)S(1)}, bf16[128,512]{1,0:T(8,128)(2,1)S(1)}, bf16[128,512]{1,0:T(8,128)(2,1)S(1)}, bf16[128,512]{1,0:T(8,128)(2,1)S(1)}) custom-call(s32[1]{0:T(128)} %bitcast.chip, s32[32]{0:T(128)S(1)} %reshape.11.table, bf16[8,128,512]{2,1,0:T(8,128)(2,1)S(1)} %all-to-all-done.q_ref, ...), custom_call_target="tpu_custom_call" | custom-call | flops 1610612736 | bytes 6291456 | tf_op jit(solution)/shard_map/pallas_call | solution.py:188
  98.0 0.1 collective-permute-start.3
  98.1 2.9 %collective-permute-start.4 = (bf16[112,512]{1,0:T(8,128)(2,1)S(1)}, bf16[112,512]{1,0:T(8,128)(2,1)S(1)}, u32[]{:S(2)}, u32[]{:S(2)}) collective-permute-start(bf16[112,512]{1,0:T(8,128)(2,1)S(1)} %get-tuple-element.20), channel_id=1, source_target_pairs={{0,16},{2,18},{4,20},{6,22},{8,24},{10,26},{12,28},{14,30},{16,0},... | collective-permute-start | bytes 344072 | tf_op jit(solution)/shard_map/ppermute | solution.py:246
  101.0 0.9 collective-permute-start.5
  102.0 1.5 %collective-permute-start.6 = (bf16[128,512]{1,0:T(8,128)(2,1)S(1)}, bf16[128,512]{1,0:T(8,128)(2,1)S(1)}, u32[]{:S(2)}, u32[]{:S(2)}) collective-permute-start(bf16[128,512]{1,0:T(8,128)(2,1)S(1)} %get-tuple-element.22), channel_id=1, source_target_pairs={{0,24},{2,26},{4,28},{6,30},{8,16},{10,18},{12,20},{14,22},{16,8},... | collective-permute-start | bytes 393224 | tf_op jit(solution)/shard_map/ppermute | solution.py:246
  103.5 2.4 %collective-permute-start.7 = (bf16[128,512]{1,0:T(8,128)(2,1)S(1)}, bf16[128,512]{1,0:T(8,128)(2,1)S(1)}, u32[]{:S(2)}, u32[]{:S(2)}) collective-permute-start(bf16[128,512]{1,0:T(8,128)(2,1)S(1)} %get-tuple-element.23), channel_id=1, source_target_pairs={{0,28},{2,30},{4,24},{6,26},{8,20},{10,22},{12,16},{14,18},{16,12}... | collective-permute-start | bytes 393224 | tf_op jit(solution)/shard_map/ppermute | solution.py:246
  105.8 0.0 collective-permute-done.3.refs_4_.refs_0_
  105.8 5.9 %shard_map.89 = (bf16[128,512]{1,0:T(8,128)(2,1)S(1)}, bf16[128,512]{1,0:T(8,128)(2,1)S(1)}, bf16[128,512]{1,0:T(8,128)(2,1)S(1)}, bf16[128,512]{1,0:T(8,128)(2,1)S(1)}) custom-call(s32[1]{0:T(128)} %bitcast.chip, s32[32]{0:T(128)S(1)} %reshape.11.table, bf16[8,128,512]{2,1,0:T(8,128)(2,1)S(1)} %all-to-all-done.q_ref, ...), custom_call_target="tpu_custom_call" | custom-call | flops 1610612736 | bytes 6291456 | tf_op jit(solution)/shard_map/pallas_call | solution.py:188
  111.7 1.5 %collective-permute-start.8 = (bf16[128,512]{1,0:T(8,128)(2,1)S(1)}, bf16[128,512]{1,0:T(8,128)(2,1)S(1)}, u32[]{:S(2)}, u32[]{:S(2)}) collective-permute-start(bf16[128,512]{1,0:T(8,128)(2,1)S(1)} %get-tuple-element.25), channel_id=1, source_target_pairs={{0,4},{2,6},{4,0},{6,2},{8,12},{10,14},{12,8},{14,10},{16,20},{18,... | collective-permute-start | bytes 393224 | tf_op jit(solution)/shard_map/ppermute | solution.py:246
  113.2 2.6 %collective-permute-done.4.refs_1_ = bf16[112,512]{1,0:T(8,128)(2,1)S(1)} collective-permute-done((bf16[112,512]{1,0:T(8,128)(2,1)S(1)}, bf16[112,512]{1,0:T(8,128)(2,1)S(1)}, u32[]{:S(2)}, u32[]{:S(2)}) %collective-permute-start.4) | collective-permute-done | bytes 114720 | tf_op jit(solution)/shard_map/ppermute | solution.py:246
  115.8 0.0 collective-permute-start.9
  115.8 4.1 %collective-permute-done.5.refs_2_ = bf16[128,512]{1,0:T(8,128)(2,1)S(1)} collective-permute-done((bf16[128,512]{1,0:T(8,128)(2,1)S(1)}, bf16[128,512]{1,0:T(8,128)(2,1)S(1)}, u32[]{:S(2)}, u32[]{:S(2)}) %collective-permute-start.5) | collective-permute-done | bytes 131104 | tf_op jit(solution)/shard_map/ppermute | solution.py:246
  119.9 0.0 collective-permute-start.10
  119.9 0.0 collective-permute-done.6.refs_3_
  119.9 0.0 collective-permute-done.7.refs_4_
  119.9 0.3 collective-permute-done.8.refs_6_
  120.2 0.7 collective-permute-done.9.refs_7_
  120.9 4.9 %collective-permute-done.10.refs_8_ = bf16[128,512]{1,0:T(8,128)(2,1)S(1)} collective-permute-done((bf16[128,512]{1,0:T(8,128)(2,1)S(1)}, bf16[128,512]{1,0:T(8,128)(2,1)S(1)}, u32[]{:S(2)}, u32[]{:S(2)}) %collective-permute-start.10) | collective-permute-done | bytes 131104 | tf_op jit(solution)/shard_map/ppermute | solution.py:246
  125.8 1.3 shard_map.90
  (1 shorter events, 0.0 us)
Async XLA Ops:
  3.9 55.5 %all-to-all-start.1 = ((bf16[8,128,1024]{2,1,0:T(8,128)(2,1)}), bf16[8,128,1024]{2,1,0:T(8,128)(2,1)S(1)}, u32[]{:S(2)}, u32[]{:S(2)}) async-start(bf16[8,128,1024]{2,1,0:T(8,128)(2,1)} %get-tuple-element.17), calls=%async_computation.1 | async-start | bytes 4194304 | tf_op jit(solution)/shard_map/all_to_all | solution.py:84
  15.1 69.4 %copy-start = (s32[8,4]{0,1:T(4,128)S(1)}, s32[8,4]{0,1:T(4,128)}, u32[]{:S(2)}) copy-start(s32[8,4]{0,1:T(4,128)} %param.13) | copy-start | bytes 388
  60.4 24.1 %collective-permute-start = (bf16[4,128,1024]{2,1,0:T(8,128)(2,1)}, bf16[4,128,1024]{2,1,0:T(8,128)(2,1)}, u32[]{:S(2)}, u32[]{:S(2)}) collective-permute-start(bf16[4,128,1024]{2,1,0:T(8,128)(2,1)} %constant_dynamic-slice_fusion), channel_id=1, source_target_pairs={{0,1},{1,0},{2,3},{3,2},{4,5},{5,4},{6,7},{7,6},{8,9},{9,8},{10,11... | collective-permute-start | bytes 3145736 | tf_op jit(solution)/shard_map/ppermute | solution.py:233
  62.0 30.2 %collective-permute-start.1 = (bf16[8,128,1024]{2,1,0:T(8,128)(2,1)S(1)}, bf16[8,128,1024]{2,1,0:T(8,128)(2,1)}, u32[]{:S(2)}, u32[]{:S(2)}) collective-permute-start(bf16[8,128,1024]{2,1,0:T(8,128)(2,1)S(1)} %all-to-all-done.1.refs_0_), channel_id=1, source_target_pairs={{0,2},{2,0},{4,6},{6,4},{8,10},{10,8},{12,14},{14,12},{16,18},{18,... | collective-permute-start | bytes 6291464 | tf_op jit(solution)/shard_map/ppermute | solution.py:234
  62.0 30.2 %all-to-all-start = ((bf16[8,128,512]{2,1,0:T(8,128)(2,1)}), bf16[8,128,512]{2,1,0:T(8,128)(2,1)S(1)}, u32[]{:S(2)}, u32[]{:S(2)}) async-start(bf16[8,128,512]{2,1,0:T(8,128)(2,1)} %get-tuple-element.16), calls=%async_computation | async-start | bytes 2097152 | tf_op jit(solution)/shard_map/all_to_all | solution.py:84
  84.5 7.7 %collective-permute-start.2 = (bf16[4,128,1024]{2,1,0:T(8,128)(2,1)}, bf16[4,128,1024]{2,1,0:T(8,128)(2,1)}, u32[]{:S(2)}, u32[]{:S(2)}) collective-permute-start(bf16[4,128,1024]{2,1,0:T(8,128)(2,1)} %collective-permute-done.refs_1_), channel_id=1, source_target_pairs={{0,2},{2,0},{4,6},{6,4},{8,10},{10,8},{12,14},{14,12},{16,18},{18,... | collective-permute-start | bytes 3145736 | tf_op jit(solution)/shard_map/ppermute | solution.py:234
  98.0 7.8 %collective-permute-start.3 = (bf16[16,512]{1,0:T(8,128)(2,1)S(1)}, bf16[16,512]{1,0:T(8,128)(2,1)S(1)}, u32[]{:S(2)}, u32[]{:S(2)}) collective-permute-start(bf16[16,512]{1,0:T(8,128)(2,1)S(1)} %get-tuple-element.19), channel_id=1, source_target_pairs={{0,16},{2,18},{4,20},{6,22},{8,24},{10,26},{12,28},{14,30},{16,0},... | collective-permute-start | bytes 49160 | tf_op jit(solution)/shard_map/ppermute | solution.py:246
  98.1 17.7 %collective-permute-start.4 = (bf16[112,512]{1,0:T(8,128)(2,1)S(1)}, bf16[112,512]{1,0:T(8,128)(2,1)S(1)}, u32[]{:S(2)}, u32[]{:S(2)}) collective-permute-start(bf16[112,512]{1,0:T(8,128)(2,1)S(1)} %get-tuple-element.20), channel_id=1, source_target_pairs={{0,16},{2,18},{4,20},{6,22},{8,24},{10,26},{12,28},{14,30},{16,0},... | collective-permute-start | bytes 344072 | tf_op jit(solution)/shard_map/ppermute | solution.py:246
  101.0 18.9 %collective-permute-start.5 = (bf16[128,512]{1,0:T(8,128)(2,1)S(1)}, bf16[128,512]{1,0:T(8,128)(2,1)S(1)}, u32[]{:S(2)}, u32[]{:S(2)}) collective-permute-start(bf16[128,512]{1,0:T(8,128)(2,1)S(1)} %get-tuple-element.21), channel_id=1, source_target_pairs={{0,20},{2,22},{4,16},{6,18},{8,28},{10,30},{12,24},{14,26},{16,4},... | collective-permute-start | bytes 393224 | tf_op jit(solution)/shard_map/ppermute | solution.py:246
  102.0 17.9 %collective-permute-start.6 = (bf16[128,512]{1,0:T(8,128)(2,1)S(1)}, bf16[128,512]{1,0:T(8,128)(2,1)S(1)}, u32[]{:S(2)}, u32[]{:S(2)}) collective-permute-start(bf16[128,512]{1,0:T(8,128)(2,1)S(1)} %get-tuple-element.22), channel_id=1, source_target_pairs={{0,24},{2,26},{4,28},{6,30},{8,16},{10,18},{12,20},{14,22},{16,8},... | collective-permute-start | bytes 393224 | tf_op jit(solution)/shard_map/ppermute | solution.py:246
  103.5 16.5 %collective-permute-start.7 = (bf16[128,512]{1,0:T(8,128)(2,1)S(1)}, bf16[128,512]{1,0:T(8,128)(2,1)S(1)}, u32[]{:S(2)}, u32[]{:S(2)}) collective-permute-start(bf16[128,512]{1,0:T(8,128)(2,1)S(1)} %get-tuple-element.23), channel_id=1, source_target_pairs={{0,28},{2,30},{4,24},{6,26},{8,20},{10,22},{12,16},{14,18},{16,12}... | collective-permute-start | bytes 393224 | tf_op jit(solution)/shard_map/ppermute | solution.py:246
  111.7 8.5 %collective-permute-start.8 = (bf16[128,512]{1,0:T(8,128)(2,1)S(1)}, bf16[128,512]{1,0:T(8,128)(2,1)S(1)}, u32[]{:S(2)}, u32[]{:S(2)}) collective-permute-start(bf16[128,512]{1,0:T(8,128)(2,1)S(1)} %get-tuple-element.25), channel_id=1, source_target_pairs={{0,4},{2,6},{4,0},{6,2},{8,12},{10,14},{12,8},{14,10},{16,20},{18,... | collective-permute-start | bytes 393224 | tf_op jit(solution)/shard_map/ppermute | solution.py:246
  115.8 5.1 %collective-permute-start.9 = (bf16[128,512]{1,0:T(8,128)(2,1)S(1)}, bf16[128,512]{1,0:T(8,128)(2,1)S(1)}, u32[]{:S(2)}, u32[]{:S(2)}) collective-permute-start(bf16[128,512]{1,0:T(8,128)(2,1)S(1)} %get-tuple-element.26), channel_id=1, source_target_pairs={{0,8},{2,10},{4,12},{6,14},{8,0},{10,2},{12,4},{14,6},{16,24},{18,... | collective-permute-start | bytes 393224 | tf_op jit(solution)/shard_map/ppermute | solution.py:246
  119.9 5.9 %collective-permute-start.10 = (bf16[128,512]{1,0:T(8,128)(2,1)S(1)}, bf16[128,512]{1,0:T(8,128)(2,1)S(1)}, u32[]{:S(2)}, u32[]{:S(2)}) collective-permute-start(bf16[128,512]{1,0:T(8,128)(2,1)S(1)} %get-tuple-element.27), channel_id=1, source_target_pairs={{0,12},{2,14},{4,8},{6,10},{8,4},{10,6},{12,0},{14,2},{16,28},{18,... | collective-permute-start | bytes 393224 | tf_op jit(solution)/shard_map/ppermute | solution.py:246

commit v12 on v10

--- a/solution.py
+++ b/solution.py
@@ -27,9 +27,11 @@
     return pl.CostEstimate(flops=0, bytes_accessed=size, transcendentals=0)
 
 
-def pack_kernel(*refs, count, chunks):
-    arrays, out = refs[:count], refs[count]
+def pack_kernel(*refs, count, before, chunks):
+    arrays, out = refs[:count], refs[count + before]
     held, staged, sems, out_sems = refs[-4:]
+    if before:
+        refs[count + before + 1][0] = 0
     chips, columns = out.shape[0], held.shape[2]
     hd, some, step = columns // chips // PAIR, chips // chunks, columns // chunks
     copies = {}
@@ -57,15 +59,17 @@
         send.wait()
 
 
-def to_chips(arrays, devices, chunks=4):
+def to_chips(arrays, devices, before=(), chunks=4):
     tokens, columns = arrays[0].shape
     count, chips = len(arrays), devices // PAIR
     shape = (chips, tokens, count * columns // chips)
+    more = min(len(before), 1)
     return pl.pallas_call(
-        functools.partial(pack_kernel, count=count, chunks=chunks),
-        in_specs=[HBM] * count,
-        out_specs=HBM,
-        out_shape=pltpu.HBM(shape, jnp.bfloat16),
+        functools.partial(pack_kernel, count=count, before=len(before), chunks=chunks),
+        in_specs=[HBM] * (count + len(before)),
+        out_specs=[HBM] + [SMEM] * more,
+        out_shape=[pltpu.HBM(shape, jnp.bfloat16)]
+        + [jax.ShapeDtypeStruct((1,), jnp.int32)] * more,
         scratch_shapes=[
             pltpu.VMEM((count, tokens, columns), jnp.bfloat16),
             pltpu.VMEM(shape, jnp.bfloat16),
@@ -74,7 +78,7 @@
         ],
         compiler_params=PARAMS,
         cost_estimate=moves(4 * count * tokens * columns),
-    )(*pin(*arrays))
+    )(*pin(*arrays, *before))
 
 
 def exchange(pieces, devices):
@@ -108,29 +112,39 @@
     )(chip, *pieces.values())
 
 
-def attend_kernel(chip, table, q_ref, *refs, sources, later, first, hd):
+def attend_kernel(chip, table, q_ref, *refs, sources, later, slots, hd):
     parts, outs = refs[: PAIR * sources], refs[PAIR * sources + later : -2]
     kv, sems = refs[-2:]
     tokens = q_ref.shape[1]
+    groups = 2 * PAIR
     copies = []
-    for core in range(PAIR):
-        row = 0
-        for i in range(sources):
-            ref = parts[core * sources + i]
-            target = kv.at[pl.ds(row, ref.shape[0]), core]
-            copies.append(pltpu.make_async_copy(ref, target, sems.at[core * sources + i]))
-            row += ref.shape[0]
+    for g in range(groups):
+        lanes = pl.ds(g * 2 * hd, 2 * hd)
+        for core in range(PAIR):
+            row = 0
+            for i in range(sources):
+                ref, n = parts[core * sources + i], core * sources + i
+                rows = pl.ds(row, ref.shape[0])
+                copies.append(
+                    pltpu.make_async_copy(
+                        ref.at[:, :, lanes], kv.at[rows, core, :, lanes], sems.at[g, n]
+                    )
+                )
+                row += ref.shape[0]
     for copy in copies:
         copy.start()
-    for copy in copies:
-        copy.wait()
+
+    def arrive(group):
+        size = len(copies) // groups
+        for copy in copies[group * size : (group + 1) * size]:
+            copy.wait()
 
     scale = hd ** (-0.5)
     factor = scale * math.log2(math.e)
     trans = (((1,), (1,)), ((), ()))
 
-    def products(i, h):
-        block = chip[0] ^ (first + i)
+    def products(k, h):
+        block = chip[0] ^ k
         both = q_ref[block, :, 2 * h * hd : 2 * (h + 1) * hd]
         query = both[:, :hd]
         left = jnp.concatenate([jnp.zeros_like(query), query], axis=1)
@@ -145,7 +159,7 @@
             tans.append(product[tokens:])
         return window, scores, tans
 
-    def finish(i, h, window, scores, tans):
+    def finish(k, h, window, scores, tans):
         top = functools.reduce(jnp.maximum, scores)
         top = jnp.max(top, axis=1, keepdims=True) * factor
         probs = [jnp.exp2(s * factor - top) for s in scores]
@@ -162,33 +176,39 @@
         out = mixed[:tokens, :hd] * inverse
         tan = (mixed[:tokens, hd:] + scale * mixed[tokens:, :hd]) * inverse
         tan = tan - (scale * mean * inverse) * out
-        outs[i][:, 2 * h * hd : (2 * h + 1) * hd] = out.astype(jnp.bfloat16)
-        outs[i][:, (2 * h + 1) * hd : 2 * (h + 1) * hd] = tan.astype(jnp.bfloat16)
-
-    units = [(i, h) for i in range(len(outs)) for h in range(PAIR)]
+        ref = outs[slots.index(k)]
+        ref[:, 2 * h * hd : (2 * h + 1) * hd] = out.astype(jnp.bfloat16)
+        ref[:, (2 * h + 1) * hd : 2 * (h + 1) * hd] = tan.astype(jnp.bfloat16)
+
+    units = [(k, h) for h in range(PAIR) for k in slots]
+    arrive(0)
     ahead = products(*units[0])
+    arrive(1)
     for unit, following in zip(units, units[1:] + [None]):
         current = ahead
         if following is not None:
+            if following[1] > unit[1]:
+                arrive(2)
+                arrive(3)
             ahead = products(*following)
         finish(*unit, *current)
 
 
-def attend(chip, table, queries, mine, other, later, first, count):
+def attend(chip, table, queries, mine, other, later, slots):
     _, tokens, width = queries.shape
     hd, sources = width // (2 * PAIR), len(mine)
     total = sum(a.shape[0] for a in mine)
-    elements = count * BQ * WK * BQ
+    elements = len(slots) * BQ * WK * BQ
     return pl.pallas_call(
         functools.partial(
-            attend_kernel, sources=sources, later=len(later), first=first, hd=hd
+            attend_kernel, sources=sources, later=len(later), slots=slots, hd=hd
         ),
         in_specs=[SMEM, SMEM, VMEM] + [ANY] * (PAIR * sources + len(later)),
-        out_specs=[VMEM] * count,
-        out_shape=[jax.ShapeDtypeStruct((tokens, width), jnp.bfloat16)] * count,
+        out_specs=[VMEM] * len(slots),
+        out_shape=[jax.ShapeDtypeStruct((tokens, width), jnp.bfloat16)] * len(slots),
         scratch_shapes=[
             pltpu.VMEM((total, PAIR, tokens, 2 * width), jnp.bfloat16),
-            pltpu.SemaphoreType.DMA((PAIR * sources,)),
+            pltpu.SemaphoreType.DMA((2 * PAIR, PAIR * sources)),
         ],
         compiler_params=PARAMS,
         cost_estimate=pl.CostEstimate(
@@ -199,7 +219,7 @@
     )(chip, table, queries, *mine, *other, *later)
 
 
-def slots(neighbors, frame, blocks):
+def places(neighbors, frame, blocks):
     local = neighbors - frame * blocks
     even = frame % 2 == 0
     before = blocks + jnp.where(even, HB, 0) + local + HB
@@ -213,27 +233,29 @@
     chip = (lax.axis_index("heads") // PAIR).reshape(1).astype(jnp.int32)
     blocks = neighbors.shape[0]
     swap = [(d, d ^ 1) for d in range(devices)]
-    kv = exchange(to_chips([keys_tan, keys, values, values_tan], devices), devices)
+    (kv_sent,) = to_chips([keys_tan, keys, values, values_tan], devices)
+    q_sent, zero = to_chips([query, query_tan], devices, [kv_sent])
+    kv = exchange(kv_sent, devices)
 
     mine = [kv]
     for first in (0, 1):
         pairs = [(i, i + 1) for i in range(first, frames - 1, 2)]
         if pairs:
-            start = jnp.where(frame % 2 == first, blocks - HB, 0)
+            start = jnp.where(frame % 2 == first, blocks - HB, 0) + zero[0]
             edge = lax.dynamic_slice_in_dim(kv, start, HB, axis=0)
             mine.append(lax.ppermute(edge, "frames", pairs + [(j, i) for i, j in pairs]))
     other = [lax.ppermute(a, "heads", swap) for a in mine]
 
-    queries = exchange(to_chips([query, query_tan], devices), devices)
-    table = slots(neighbors, frame, blocks)
+    queries = exchange(q_sent, devices)
+    table = places(neighbors, frame, blocks)
     half = blocks // 2
     back, later = {}, []
-    for first in (half, 0):
-        pieces = attend(chip, table, queries, mine, other, later, first, half)
-        for k, piece in enumerate(pieces, first):
+    for part in ([1, *range(half, blocks)], [*range(2, half), 0]):
+        pieces = attend(chip, table, queries, mine, other, later, part)
+        for k, piece in zip(part, pieces):
             pairs = [(d, d ^ (k * PAIR)) for d in range(devices)]
             back[k] = lax.ppermute(piece, "heads", pairs) if k else piece
-        later = [back[half]]
+        later = [back[1]]
     return unpack(chip, back, 2)
 
 

time: 134 us -> 127 us (0.948)
  waiting for transfers between devices: 89.8 us -> 83.8 us
  starting transfers between devices: 23.7 us -> 21.6 us
    all_to_all x2, waiting for transfers between devices: 57.9 us -> 52.4 us  [exchange(): lax.all_to_all(pieces, 'heads', split_axis=0, concat_axis=0, axis_index_g...]
    ppermute x7, waiting for transfers between devices: 15.2 us -> 12.5 us  [per_device(): back[k] = lax.ppermute(piece, 'heads', pairs) if k else piece]
    ppermute x1, waiting for transfers between devices: 16.7 us -> 18.9 us  [per_device(): lax.ppermute(edge, 'frames', pairs + [(j, i) for i, j in pairs])]
    ppermute x7, starting transfers between devices: 11.3 us -> 9.22 us  [per_device(): back[k] = lax.ppermute(piece, 'heads', pairs) if k else piece]
where the time goes in v12:
time: 127 us; the launch traced here: 126 us
  waiting for transfers between devices  83.8 us (66%)
  starting transfers between devices  21.6 us (17%)
  Pallas kernels  18.2 us (14%)
  between operations  1.35 us (1%)
    all_to_all x2, waiting for transfers between devices, exchange(): lax.all_to_all(pieces, 'heads', split_axis=0, concat_axis=0, axis_index_g...  52.4 us
    ppermute x1, waiting for transfers between devices, per_device(): lax.ppermute(edge, 'frames', pairs + [(j, i) for i, j in pairs])  18.9 us
    ppermute x7, waiting for transfers between devices, per_device(): back[k] = lax.ppermute(piece, 'heads', pairs) if k else piece  12.5 us
    pallas_call x2, Pallas kernels, attend(): pl.pallas_call(functools.partial(attend_kernel, sources=sources, later=le...  11.5 us
    all_to_all x2, starting transfers between devices, exchange(): lax.all_to_all(pieces, 'heads', split_axis=0, concat_axis=0, axis_index_g...  10.9 us
    ppermute x7, starting transfers between devices, per_device(): back[k] = lax.ppermute(piece, 'heads', pairs) if k else piece  9.22 us
    pallas_call x2, Pallas kernels, to_chips(): pl.pallas_call(functools.partial(pack_kernel, count=count, before=len(bef...  5.43 us
  transfers between devices with their start and end apart: 12, of which 7 were waited for; matrix products, arithmetic and copies ran while one was open for 0% of the time, Pallas kernels for 6%

profile of v12, /device:TPU:0, one launch (start us, length us, event | category | flops | bytes accessed | tf_op | source)
XLA Modules:
  0.0 126.2 jit_solution(1908937311358774254)
XLA Ops:
  0.6 2.8 %shard_map.86.refs_2_ = bf16[8,128,1024]{2,1,0:T(8,128)(2,1)} custom-call(bf16[128,2048]{1,0:T(8,128)(2,1)} %refs_0_.2, bf16[128,2048]{1,0:T(8,128)(2,1)} %refs_1_.2, bf16[128,2048]{1,0:T(8,128)(2,1)} %refs_2_.1, bf16[128,2048]{1,0:T(8,128)(2,1)} %refs_3_.1), custom_call_target="tpu_custom_call" | custom-call | bytes 4194304 | tf_op jit(solution)/shard_map/pallas_call | solution.py:67
  3.4 7.3 %all-to-all-start.1 = ((bf16[8,128,1024]{2,1,0:T(8,128)(2,1)}), bf16[8,128,1024]{2,1,0:T(8,128)(2,1)S(1)}, u32[]{:S(2)}, u32[]{:S(2)}) async-start(bf16[8,128,1024]{2,1,0:T(8,128)(2,1)} %shard_map.86.refs_2_), calls=%async_computation.1 | async-start | bytes 4194304 | tf_op jit(solution)/shard_map/all_to_all | solution.py:86
  10.7 2.7 %shard_map.87 = (bf16[8,128,512]{2,1,0:T(8,128)(2,1)}, s32[1]{0:T(128)}) custom-call(bf16[128,2048]{1,0:T(8,128)(2,1)} %refs_0_.3, bf16[128,2048]{1,0:T(8,128)(2,1)} %refs_1_.3, bf16[8,128,1024]{2,1,0:T(8,128)(2,1)} %shard_map.86.refs_2_), custom_call_target="tpu_custom_call" | custom-call | bytes 2097152 | tf_op jit(solution)/shard_map/pallas_call | solution.py:67
  14.0 0.0 copy-start
  14.0 44.9 %all-to-all-done.1.refs_0_ = bf16[8,128,1024]{2,1,0:T(8,128)(2,1)S(1)} async-done(((bf16[8,128,1024]{2,1,0:T(8,128)(2,1)}), bf16[8,128,1024]{2,1,0:T(8,128)(2,1)S(1)}, u32[]{:S(2)}, u32[]{:S(2)}) %all-to-all-start.1) | async-done | bytes 2097184 | tf_op jit(solution)/shard_map/all_to_all | solution.py:86
  58.9 1.0 constant_dynamic-slice_fusion
  59.9 1.5 %collective-permute-start = (bf16[4,128,1024]{2,1,0:T(8,128)(2,1)}, bf16[4,128,1024]{2,1,0:T(8,128)(2,1)}, u32[]{:S(2)}, u32[]{:S(2)}) collective-permute-start(bf16[4,128,1024]{2,1,0:T(8,128)(2,1)} %constant_dynamic-slice_fusion), channel_id=1, source_target_pairs={{0,1},{1,0},{2,3},{3,2},{4,5},{5,4},{6,7},{7,6},{8,9},{9,8},{10,11... | collective-permute-start | bytes 3145736 | tf_op jit(solution)/shard_map/ppermute | solution.py:246
  61.5 0.0 collective-permute-start.1
  61.5 3.6 %all-to-all-start = ((bf16[8,128,512]{2,1,0:T(8,128)(2,1)}), bf16[8,128,512]{2,1,0:T(8,128)(2,1)S(1)}, u32[]{:S(2)}, u32[]{:S(2)}) async-start(bf16[8,128,512]{2,1,0:T(8,128)(2,1)} %get-tuple-element.12), calls=%async_computation | async-start | bytes 2097152 | tf_op jit(solution)/shard_map/all_to_all | solution.py:86
  65.1 18.9 %collective-permute-done.refs_1_ = bf16[4,128,1024]{2,1,0:T(8,128)(2,1)} collective-permute-done((bf16[4,128,1024]{2,1,0:T(8,128)(2,1)}, bf16[4,128,1024]{2,1,0:T(8,128)(2,1)}, u32[]{:S(2)}, u32[]{:S(2)}) %collective-permute-start) | collective-permute-done | bytes 1048608 | tf_op jit(solution)/shard_map/ppermute | solution.py:246
  84.0 0.0 collective-permute-start.2
  84.0 0.0 copy-done
  84.0 0.1 copy.10
  84.1 0.1 reshape.11.table
  84.2 7.5 %all-to-all-done.q_ref = bf16[8,128,512]{2,1,0:T(8,128)(2,1)S(1)} async-done(((bf16[8,128,512]{2,1,0:T(8,128)(2,1)}), bf16[8,128,512]{2,1,0:T(8,128)(2,1)S(1)}, u32[]{:S(2)}, u32[]{:S(2)}) %all-to-all-start) | async-done | bytes 1048608 | tf_op jit(solution)/shard_map/all_to_all | solution.py:86
  91.7 0.0 collective-permute-done.2.refs_3_
  91.7 0.0 collective-permute-done.1.refs_2_
  91.7 6.5 %shard_map.88 = (bf16[128,512]{1,0:T(8,128)(2,1)S(1)}, bf16[128,512]{1,0:T(8,128)(2,1)S(1)}, bf16[128,512]{1,0:T(8,128)(2,1)S(1)}, bf16[128,512]{1,0:T(8,128)(2,1)S(1)}, bf16[128,512]{1,0:T(8,128)(2,1)S(1)}) custom-call(s32[1]{0:T(128)} %bitcast.chip, s32[32]{0:T(128)S(1)} %reshape.11.table, bf16[8,128,512]{2,1,0:T(8,128)(2,1)S(1)} %all-to-all-done.q_ref, ...), custom_call_target="tpu_custom_call" | custom-call | flops 2013265920 | bytes 6291456 | tf_op jit(solution)/shard_map/pallas_call | solution.py:202
  98.2 1.5 %collective-permute-start.3 = (bf16[128,512]{1,0:T(8,128)(2,1)S(1)}, bf16[128,512]{1,0:T(8,128)(2,1)S(1)}, u32[]{:S(2)}, u32[]{:S(2)}) collective-permute-start(bf16[128,512]{1,0:T(8,128)(2,1)S(1)} %get-tuple-element.14), channel_id=1, source_target_pairs={{0,4},{2,6},{4,0},{6,2},{8,12},{10,14},{12,8},{14,10},{16,20},{18,... | collective-permute-start | bytes 393224 | tf_op jit(solution)/shard_map/ppermute | solution.py:257
  99.7 0.0 collective-permute-start.4
  99.7 3.0 %collective-permute-start.5 = (bf16[128,512]{1,0:T(8,128)(2,1)S(1)}, bf16[128,512]{1,0:T(8,128)(2,1)S(1)}, u32[]{:S(2)}, u32[]{:S(2)}) collective-permute-start(bf16[128,512]{1,0:T(8,128)(2,1)S(1)} %get-tuple-element.16), channel_id=1, source_target_pairs={{0,20},{2,22},{4,16},{6,18},{8,28},{10,30},{12,24},{14,26},{16,4},... | collective-permute-start | bytes 393224 | tf_op jit(solution)/shard_map/ppermute | solution.py:257
  102.6 2.3 %collective-permute-start.6 = (bf16[128,512]{1,0:T(8,128)(2,1)S(1)}, bf16[128,512]{1,0:T(8,128)(2,1)S(1)}, u32[]{:S(2)}, u32[]{:S(2)}) collective-permute-start(bf16[128,512]{1,0:T(8,128)(2,1)S(1)} %get-tuple-element.17), channel_id=1, source_target_pairs={{0,24},{2,26},{4,28},{6,30},{8,16},{10,18},{12,20},{14,22},{16,8},... | collective-permute-start | bytes 393224 | tf_op jit(solution)/shard_map/ppermute | solution.py:257
  104.9 2.4 %collective-permute-start.7 = (bf16[128,512]{1,0:T(8,128)(2,1)S(1)}, bf16[128,512]{1,0:T(8,128)(2,1)S(1)}, u32[]{:S(2)}, u32[]{:S(2)}) collective-permute-start(bf16[128,512]{1,0:T(8,128)(2,1)S(1)} %get-tuple-element.18), channel_id=1, source_target_pairs={{0,28},{2,30},{4,24},{6,26},{8,20},{10,22},{12,16},{14,18},{16,12}... | collective-permute-start | bytes 393224 | tf_op jit(solution)/shard_map/ppermute | solution.py:257
  107.3 0.0 collective-permute-done.3.refs_4_.refs_0_
  107.3 5.0 %shard_map.89 = (bf16[128,512]{1,0:T(8,128)(2,1)S(1)}, bf16[128,512]{1,0:T(8,128)(2,1)S(1)}, bf16[128,512]{1,0:T(8,128)(2,1)S(1)}) custom-call(s32[1]{0:T(128)} %bitcast.chip, s32[32]{0:T(128)S(1)} %reshape.11.table, bf16[8,128,512]{2,1,0:T(8,128)(2,1)S(1)} %all-to-all-done.q_ref, bf16[8,128,1024]{2,1,0:T(8,128)(2,1)S(1)} %all-to-all-done.1.refs_0_, ...), custom_call_target="tpu_custom_call" | custom-call | flops 1207959552 | bytes 6291456 | tf_op jit(solution)/shard_map/pallas_call | solution.py:202
  112.3 0.1 collective-permute-start.8
  112.4 3.6 %collective-permute-done.4.refs_1_ = bf16[128,512]{1,0:T(8,128)(2,1)S(1)} collective-permute-done((bf16[128,512]{1,0:T(8,128)(2,1)S(1)}, bf16[128,512]{1,0:T(8,128)(2,1)S(1)}, u32[]{:S(2)}, u32[]{:S(2)}) %collective-permute-start.4) | collective-permute-done | bytes 131104 | tf_op jit(solution)/shard_map/ppermute | solution.py:257
  116.0 0.0 collective-permute-start.9
  116.0 3.6 %collective-permute-done.5.refs_2_ = bf16[128,512]{1,0:T(8,128)(2,1)S(1)} collective-permute-done((bf16[128,512]{1,0:T(8,128)(2,1)S(1)}, bf16[128,512]{1,0:T(8,128)(2,1)S(1)}, u32[]{:S(2)}, u32[]{:S(2)}) %collective-permute-start.5) | collective-permute-done | bytes 131104 | tf_op jit(solution)/shard_map/ppermute | solution.py:257
  119.6 0.0 collective-permute-done.6.refs_3_
  119.6 0.0 collective-permute-done.7.refs_4_
  119.6 1.9 %collective-permute-done.8.refs_5_ = bf16[128,512]{1,0:T(8,128)(2,1)S(1)} collective-permute-done((bf16[128,512]{1,0:T(8,128)(2,1)S(1)}, bf16[128,512]{1,0:T(8,128)(2,1)S(1)}, u32[]{:S(2)}, u32[]{:S(2)}) %collective-permute-start.8) | collective-permute-done | bytes 131104 | tf_op jit(solution)/shard_map/ppermute | solution.py:257
  121.5 3.4 %collective-permute-done.9.refs_6_ = bf16[128,512]{1,0:T(8,128)(2,1)S(1)} collective-permute-done((bf16[128,512]{1,0:T(8,128)(2,1)S(1)}, bf16[128,512]{1,0:T(8,128)(2,1)S(1)}, u32[]{:S(2)}, u32[]{:S(2)}) %collective-permute-start.9) | collective-permute-done | bytes 131104 | tf_op jit(solution)/shard_map/ppermute | solution.py:257
  124.9 1.3 %shard_map.90 = (bf16[128,2048]{1,0:T(8,128)(2,1)}, bf16[128,2048]{1,0:T(8,128)(2,1)}) custom-call(s32[1]{0:T(128)} %bitcast.chip, bf16[128,512]{1,0:T(8,128)(2,1)S(1)} %collective-permute-done.3.refs_4_.refs_0_, bf16[128,512]{1,0:T(8,128)(2,1)S(1)} %collective-permute-done.4.refs_1_, bf16[128,512]{1,0:T(8,128)(2,1)S(1)} %collective-permute-done.5.refs_2_, ...), custom_call_target="tpu_custom_call" | custom-call | bytes 2097152 | tf_op jit(solution)/shard_map/pallas_call | solution.py:105
  (1 shorter events, 0.0 us)
Async XLA Ops:
  3.4 55.5 %all-to-all-start.1 = ((bf16[8,128,1024]{2,1,0:T(8,128)(2,1)}), bf16[8,128,1024]{2,1,0:T(8,128)(2,1)S(1)}, u32[]{:S(2)}, u32[]{:S(2)}) async-start(bf16[8,128,1024]{2,1,0:T(8,128)(2,1)} %shard_map.86.refs_2_), calls=%async_computation.1 | async-start | bytes 4194304 | tf_op jit(solution)/shard_map/all_to_all | solution.py:86
  14.0 70.0 %copy-start = (s32[8,4]{0,1:T(4,128)S(1)}, s32[8,4]{0,1:T(4,128)}, u32[]{:S(2)}) copy-start(s32[8,4]{0,1:T(4,128)} %param.13) | copy-start | bytes 388
  59.9 24.1 %collective-permute-start = (bf16[4,128,1024]{2,1,0:T(8,128)(2,1)}, bf16[4,128,1024]{2,1,0:T(8,128)(2,1)}, u32[]{:S(2)}, u32[]{:S(2)}) collective-permute-start(bf16[4,128,1024]{2,1,0:T(8,128)(2,1)} %constant_dynamic-slice_fusion), channel_id=1, source_target_pairs={{0,1},{1,0},{2,3},{3,2},{4,5},{5,4},{6,7},{7,6},{8,9},{9,8},{10,11... | collective-permute-start | bytes 3145736 | tf_op jit(solution)/shard_map/ppermute | solution.py:246
  61.5 30.2 %collective-permute-start.1 = (bf16[8,128,1024]{2,1,0:T(8,128)(2,1)S(1)}, bf16[8,128,1024]{2,1,0:T(8,128)(2,1)}, u32[]{:S(2)}, u32[]{:S(2)}) collective-permute-start(bf16[8,128,1024]{2,1,0:T(8,128)(2,1)S(1)} %all-to-all-done.1.refs_0_), channel_id=1, source_target_pairs={{0,2},{2,0},{4,6},{6,4},{8,10},{10,8},{12,14},{14,12},{16,18},{18,... | collective-permute-start | bytes 6291464 | tf_op jit(solution)/shard_map/ppermute | solution.py:247
  61.5 30.2 %all-to-all-start = ((bf16[8,128,512]{2,1,0:T(8,128)(2,1)}), bf16[8,128,512]{2,1,0:T(8,128)(2,1)S(1)}, u32[]{:S(2)}, u32[]{:S(2)}) async-start(bf16[8,128,512]{2,1,0:T(8,128)(2,1)} %get-tuple-element.12), calls=%async_computation | async-start | bytes 2097152 | tf_op jit(solution)/shard_map/all_to_all | solution.py:86
  84.0 7.7 %collective-permute-start.2 = (bf16[4,128,1024]{2,1,0:T(8,128)(2,1)}, bf16[4,128,1024]{2,1,0:T(8,128)(2,1)}, u32[]{:S(2)}, u32[]{:S(2)}) collective-permute-start(bf16[4,128,1024]{2,1,0:T(8,128)(2,1)} %collective-permute-done.refs_1_), channel_id=1, source_target_pairs={{0,2},{2,0},{4,6},{6,4},{8,10},{10,8},{12,14},{14,12},{16,18},{18,... | collective-permute-start | bytes 3145736 | tf_op jit(solution)/shard_map/ppermute | solution.py:247
  98.2 9.1 %collective-permute-start.3 = (bf16[128,512]{1,0:T(8,128)(2,1)S(1)}, bf16[128,512]{1,0:T(8,128)(2,1)S(1)}, u32[]{:S(2)}, u32[]{:S(2)}) collective-permute-start(bf16[128,512]{1,0:T(8,128)(2,1)S(1)} %get-tuple-element.14), channel_id=1, source_target_pairs={{0,4},{2,6},{4,0},{6,2},{8,12},{10,14},{12,8},{14,10},{16,20},{18,... | collective-permute-start | bytes 393224 | tf_op jit(solution)/shard_map/ppermute | solution.py:257
  99.7 16.3 %collective-permute-start.4 = (bf16[128,512]{1,0:T(8,128)(2,1)S(1)}, bf16[128,512]{1,0:T(8,128)(2,1)S(1)}, u32[]{:S(2)}, u32[]{:S(2)}) collective-permute-start(bf16[128,512]{1,0:T(8,128)(2,1)S(1)} %get-tuple-element.15), channel_id=1, source_target_pairs={{0,16},{2,18},{4,20},{6,22},{8,24},{10,26},{12,28},{14,30},{16,0},... | collective-permute-start | bytes 393224 | tf_op jit(solution)/shard_map/ppermute | solution.py:257
  99.7 19.9 %collective-permute-start.5 = (bf16[128,512]{1,0:T(8,128)(2,1)S(1)}, bf16[128,512]{1,0:T(8,128)(2,1)S(1)}, u32[]{:S(2)}, u32[]{:S(2)}) collective-permute-start(bf16[128,512]{1,0:T(8,128)(2,1)S(1)} %get-tuple-element.16), channel_id=1, source_target_pairs={{0,20},{2,22},{4,16},{6,18},{8,28},{10,30},{12,24},{14,26},{16,4},... | collective-permute-start | bytes 393224 | tf_op jit(solution)/shard_map/ppermute | solution.py:257
  102.6 17.0 %collective-permute-start.6 = (bf16[128,512]{1,0:T(8,128)(2,1)S(1)}, bf16[128,512]{1,0:T(8,128)(2,1)S(1)}, u32[]{:S(2)}, u32[]{:S(2)}) collective-permute-start(bf16[128,512]{1,0:T(8,128)(2,1)S(1)} %get-tuple-element.17), channel_id=1, source_target_pairs={{0,24},{2,26},{4,28},{6,30},{8,16},{10,18},{12,20},{14,22},{16,8},... | collective-permute-start | bytes 393224 | tf_op jit(solution)/shard_map/ppermute | solution.py:257
  104.9 14.7 %collective-permute-start.7 = (bf16[128,512]{1,0:T(8,128)(2,1)S(1)}, bf16[128,512]{1,0:T(8,128)(2,1)S(1)}, u32[]{:S(2)}, u32[]{:S(2)}) collective-permute-start(bf16[128,512]{1,0:T(8,128)(2,1)S(1)} %get-tuple-element.18), channel_id=1, source_target_pairs={{0,28},{2,30},{4,24},{6,26},{8,20},{10,22},{12,16},{14,18},{16,12}... | collective-permute-start | bytes 393224 | tf_op jit(solution)/shard_map/ppermute | solution.py:257
  112.3 9.2 %collective-permute-start.8 = (bf16[128,512]{1,0:T(8,128)(2,1)S(1)}, bf16[128,512]{1,0:T(8,128)(2,1)S(1)}, u32[]{:S(2)}, u32[]{:S(2)}) collective-permute-start(bf16[128,512]{1,0:T(8,128)(2,1)S(1)} %get-tuple-element.19), channel_id=1, source_target_pairs={{0,8},{2,10},{4,12},{6,14},{8,0},{10,2},{12,4},{14,6},{16,24},{18,... | collective-permute-start | bytes 393224 | tf_op jit(solution)/shard_map/ppermute | solution.py:257
  116.0 8.9 %collective-permute-start.9 = (bf16[128,512]{1,0:T(8,128)(2,1)S(1)}, bf16[128,512]{1,0:T(8,128)(2,1)S(1)}, u32[]{:S(2)}, u32[]{:S(2)}) collective-permute-start(bf16[128,512]{1,0:T(8,128)(2,1)S(1)} %get-tuple-element.20), channel_id=1, source_target_pairs={{0,12},{2,14},{4,8},{6,10},{8,4},{10,6},{12,0},{14,2},{16,28},{18,... | collective-permute-start | bytes 393224 | tf_op jit(solution)/shard_map/ppermute | solution.py:257

commit v13 on v12

--- a/solution.py
+++ b/solution.py
@@ -12,6 +12,7 @@
 WK = 4
 HB = 4
 PAIR = 2
+LEAD = 16
 PARAMS = pltpu.CompilerParams(vmem_limit_bytes=40 * 1024 * 1024)
 ANY = pl.BlockSpec(memory_space=pl.ANY)
 HBM = pl.BlockSpec(memory_space=pltpu.HBM)
@@ -88,31 +89,30 @@
     )
 
 
-def unpack_kernel(chip, *refs, order):
-    pieces, arrays = refs[: len(order)], refs[len(order) :]
+def unpack_kernel(chip, *refs, places):
+    pieces, arrays = refs[: len(places)], refs[len(places) :]
     hd = pieces[0].shape[1] // len(arrays) // PAIR
-    for k, piece in zip(order, pieces):
+    for (k, row), piece in zip(places, pieces):
+        rows = slice(row, row + piece.shape[0])
         for h in range(PAIR):
             columns = pl.ds(pl.multiple_of(((chip[0] ^ k) * PAIR + h) * hd, hd), hd)
             for a, array in enumerate(arrays):
                 source = (h * len(arrays) + a) * hd
-                array[:, columns] = piece[:, source : source + hd]
-
-
-def unpack(chip, pieces, count):
-    tokens, width = pieces[0].shape
-    columns = len(pieces) * width // count
+                array[rows, columns] = piece[:, source : source + hd]
+
+
+def unpack(chip, pieces, tokens, columns, count):
     return pl.pallas_call(
-        functools.partial(unpack_kernel, order=list(pieces)),
+        functools.partial(unpack_kernel, places=list(pieces)),
         in_specs=[SMEM] + [VMEM] * len(pieces),
         out_specs=[VMEM] * count,
         out_shape=[jax.ShapeDtypeStruct((tokens, columns), jnp.bfloat16)] * count,
         compiler_params=PARAMS,
-        cost_estimate=moves(4 * len(pieces) * tokens * width),
+        cost_estimate=moves(4 * count * tokens * columns),
     )(chip, *pieces.values())
 
 
-def attend_kernel(chip, table, q_ref, *refs, sources, later, slots, hd):
+def attend_kernel(chip, table, q_ref, *refs, sources, later, places, hd):
     parts, outs = refs[: PAIR * sources], refs[PAIR * sources + later : -2]
     kv, sems = refs[-2:]
     tokens = q_ref.shape[1]
@@ -176,11 +176,13 @@
         out = mixed[:tokens, :hd] * inverse
         tan = (mixed[:tokens, hd:] + scale * mixed[tokens:, :hd]) * inverse
         tan = tan - (scale * mean * inverse) * out
-        ref = outs[slots.index(k)]
-        ref[:, 2 * h * hd : (2 * h + 1) * hd] = out.astype(jnp.bfloat16)
-        ref[:, (2 * h + 1) * hd : 2 * (h + 1) * hd] = tan.astype(jnp.bfloat16)
-
-    units = [(k, h) for h in range(PAIR) for k in slots]
+        for (slot, row), ref in zip(places, outs):
+            if slot == k:
+                rows = slice(row, row + ref.shape[0])
+                ref[:, 2 * h * hd : (2 * h + 1) * hd] = out[rows].astype(jnp.bfloat16)
+                ref[:, (2 * h + 1) * hd : 2 * (h + 1) * hd] = tan[rows].astype(jnp.bfloat16)
+
+    units = [(k, h) for h in range(PAIR) for k in dict(places)]
     arrive(0)
     ahead = products(*units[0])
     arrive(1)
@@ -194,18 +196,20 @@
         finish(*unit, *current)
 
 
-def attend(chip, table, queries, mine, other, later, slots):
+def attend(chip, table, queries, mine, other, later, places):
     _, tokens, width = queries.shape
     hd, sources = width // (2 * PAIR), len(mine)
     total = sum(a.shape[0] for a in mine)
-    elements = len(slots) * BQ * WK * BQ
+    elements = len(dict(places)) * BQ * WK * BQ
+    ends = [following[1] or tokens for following in places[1:]] + [tokens]
+    sizes = [end - row for (_, row), end in zip(places, ends)]
     return pl.pallas_call(
         functools.partial(
-            attend_kernel, sources=sources, later=len(later), slots=slots, hd=hd
+            attend_kernel, sources=sources, later=len(later), places=places, hd=hd
         ),
         in_specs=[SMEM, SMEM, VMEM] + [ANY] * (PAIR * sources + len(later)),
-        out_specs=[VMEM] * len(slots),
-        out_shape=[jax.ShapeDtypeStruct((tokens, width), jnp.bfloat16)] * len(slots),
+        out_specs=[VMEM] * len(places),
+        out_shape=[jax.ShapeDtypeStruct((size, width), jnp.bfloat16) for size in sizes],
         scratch_shapes=[
             pltpu.VMEM((total, PAIR, tokens, 2 * width), jnp.bfloat16),
             pltpu.SemaphoreType.DMA((2 * PAIR, PAIR * sources)),
@@ -219,7 +223,7 @@
     )(chip, table, queries, *mine, *other, *later)
 
 
-def places(neighbors, frame, blocks):
+def locate(neighbors, frame, blocks):
     local = neighbors - frame * blocks
     even = frame % 2 == 0
     before = blocks + jnp.where(even, HB, 0) + local + HB
@@ -247,16 +251,20 @@
     other = [lax.ppermute(a, "heads", swap) for a in mine]
 
     queries = exchange(q_sent, devices)
-    table = places(neighbors, frame, blocks)
-    half = blocks // 2
+    table = locate(neighbors, frame, blocks)
+    half, middle = blocks // 2, blocks // 2 + blocks // 4
+    calls = [
+        [(half, 0), (half, LEAD), *((k, 0) for k in range(half + 1, middle))],
+        [(k, 0) for k in (*range(middle, blocks), *range(1, half), 0)],
+    ]
     back, later = {}, []
-    for part in ([1, *range(half, blocks)], [*range(2, half), 0]):
-        pieces = attend(chip, table, queries, mine, other, later, part)
-        for k, piece in zip(part, pieces):
-            pairs = [(d, d ^ (k * PAIR)) for d in range(devices)]
-            back[k] = lax.ppermute(piece, "heads", pairs) if k else piece
-        later = [back[1]]
-    return unpack(chip, back, 2)
+    for places in calls:
+        pieces = attend(chip, table, queries, mine, other, later, places)
+        for place, piece in zip(places, pieces):
+            pairs = [(d, d ^ (place[0] * PAIR)) for d in range(devices)]
+            back[place] = lax.ppermute(piece, "heads", pairs) if place[0] else piece
+        later = [back[places[0]]]
+    return unpack(chip, back, *query.shape, 2)
 
 
 def solution(mesh):

time: 127 us -> 126 us (level)
  waiting for transfers between devices: 83.8 us -> 78 us
  starting transfers between devices: 21.6 us -> 27.3 us
    ppermute x7 -> x8, waiting for transfers between devices: 12.5 us -> 6.75 us  [per_device(): back[place] = lax.ppermute(piece, 'heads', pairs) if place[0] else piece]
    ppermute x7 -> x8, starting transfers between devices: 9.22 us -> 14.9 us  [per_device(): back[place] = lax.ppermute(piece, 'heads', pairs) if place[0] else piece]
  transfers between devices with their start and end apart: 12 -> 13, of which waited for: 7 -> 6; matrix products, arithmetic and copies ran while one was open for 0% -> 0% of each run, Pallas kernels for 6% -> 8%
where the time goes in v13:
time: 126 us
  waiting for transfers between devices  78 us (62%)
  starting transfers between devices  27.3 us (22%)
  Pallas kernels  18.2 us (14%)
  between operations  1.35 us (1%)
    all_to_all x2, waiting for transfers between devices, exchange(): lax.all_to_all(pieces, 'heads', split_axis=0, concat_axis=0, axis_index_g...  52.4 us
    ppermute x1, waiting for transfers between devices, per_device(): lax.ppermute(edge, 'frames', pairs + [(j, i) for i, j in pairs])  18.9 us
    ppermute x8, starting transfers between devices, per_device(): back[place] = lax.ppermute(piece, 'heads', pairs) if place[0] else piece  14.9 us
    pallas_call x2, Pallas kernels, attend(): pl.pallas_call(functools.partial(attend_kernel, sources=sources, later=le...  11.5 us
    all_to_all x2, starting transfers between devices, exchange(): lax.all_to_all(pieces, 'heads', split_axis=0, concat_axis=0, axis_index_g...  10.9 us
    ppermute x8, waiting for transfers between devices, per_device(): back[place] = lax.ppermute(piece, 'heads', pairs) if place[0] else piece  6.75 us
    pallas_call x2, Pallas kernels, to_chips(): pl.pallas_call(functools.partial(pack_kernel, count=count, before=len(bef...  5.42 us
  transfers between devices with their start and end apart: 13, of which 6 were waited for; matrix products, arithmetic and copies ran while one was open for 0% of the time, Pallas kernels for 8%

profile of v13, /device:TPU:0, one launch (start us, length us, event | category | flops | bytes accessed | tf_op | source)
XLA Modules:
  0.0 126.1 jit_solution(17089280787185565558)
XLA Ops:
  0.6 2.7 %shard_map.86.refs_2_ = bf16[8,128,1024]{2,1,0:T(8,128)(2,1)} custom-call(bf16[128,2048]{1,0:T(8,128)(2,1)} %refs_0_.2, bf16[128,2048]{1,0:T(8,128)(2,1)} %refs_1_.2, bf16[128,2048]{1,0:T(8,128)(2,1)} %refs_2_.1, bf16[128,2048]{1,0:T(8,128)(2,1)} %refs_3_.1), custom_call_target="tpu_custom_call" | custom-call | bytes 4194304 | tf_op jit(solution)/shard_map/pallas_call | solution.py:68
  3.4 7.3 %all-to-all-start.1 = ((bf16[8,128,1024]{2,1,0:T(8,128)(2,1)}), bf16[8,128,1024]{2,1,0:T(8,128)(2,1)S(1)}, u32[]{:S(2)}, u32[]{:S(2)}) async-start(bf16[8,128,1024]{2,1,0:T(8,128)(2,1)} %shard_map.86.refs_2_), calls=%async_computation.1 | async-start | bytes 4194304 | tf_op jit(solution)/shard_map/all_to_all | solution.py:87
  10.7 2.7 %shard_map.87 = (bf16[8,128,512]{2,1,0:T(8,128)(2,1)}, s32[1]{0:T(128)}) custom-call(bf16[128,2048]{1,0:T(8,128)(2,1)} %refs_0_.3, bf16[128,2048]{1,0:T(8,128)(2,1)} %refs_1_.3, bf16[8,128,1024]{2,1,0:T(8,128)(2,1)} %shard_map.86.refs_2_), custom_call_target="tpu_custom_call" | custom-call | bytes 2097152 | tf_op jit(solution)/shard_map/pallas_call | solution.py:68
  14.0 0.0 copy-start
  14.0 44.9 %all-to-all-done.1.refs_0_ = bf16[8,128,1024]{2,1,0:T(8,128)(2,1)S(1)} async-done(((bf16[8,128,1024]{2,1,0:T(8,128)(2,1)}), bf16[8,128,1024]{2,1,0:T(8,128)(2,1)S(1)}, u32[]{:S(2)}, u32[]{:S(2)}) %all-to-all-start.1) | async-done | bytes 2097184 | tf_op jit(solution)/shard_map/all_to_all | solution.py:87
  58.9 1.0 constant_dynamic-slice_fusion
  59.9 1.5 %collective-permute-start = (bf16[4,128,1024]{2,1,0:T(8,128)(2,1)}, bf16[4,128,1024]{2,1,0:T(8,128)(2,1)}, u32[]{:S(2)}, u32[]{:S(2)}) collective-permute-start(bf16[4,128,1024]{2,1,0:T(8,128)(2,1)} %constant_dynamic-slice_fusion), channel_id=1, source_target_pairs={{0,1},{1,0},{2,3},{3,2},{4,5},{5,4},{6,7},{7,6},{8,9},{9,8},{10,11... | collective-permute-start | bytes 3145736 | tf_op jit(solution)/shard_map/ppermute | solution.py:250
  61.5 0.0 collective-permute-start.1
  61.5 3.6 %all-to-all-start = ((bf16[8,128,512]{2,1,0:T(8,128)(2,1)}), bf16[8,128,512]{2,1,0:T(8,128)(2,1)S(1)}, u32[]{:S(2)}, u32[]{:S(2)}) async-start(bf16[8,128,512]{2,1,0:T(8,128)(2,1)} %get-tuple-element.13), calls=%async_computation | async-start | bytes 2097152 | tf_op jit(solution)/shard_map/all_to_all | solution.py:87
  65.1 18.9 %collective-permute-done.refs_1_ = bf16[4,128,1024]{2,1,0:T(8,128)(2,1)} collective-permute-done((bf16[4,128,1024]{2,1,0:T(8,128)(2,1)}, bf16[4,128,1024]{2,1,0:T(8,128)(2,1)}, u32[]{:S(2)}, u32[]{:S(2)}) %collective-permute-start) | collective-permute-done | bytes 1048608 | tf_op jit(solution)/shard_map/ppermute | solution.py:250
  84.0 0.0 collective-permute-start.2
  84.0 0.0 copy-done
  84.0 0.1 copy.10
  84.1 0.1 reshape.11.table
  84.2 7.5 %all-to-all-done.q_ref = bf16[8,128,512]{2,1,0:T(8,128)(2,1)S(1)} async-done(((bf16[8,128,512]{2,1,0:T(8,128)(2,1)}), bf16[8,128,512]{2,1,0:T(8,128)(2,1)S(1)}, u32[]{:S(2)}, u32[]{:S(2)}) %all-to-all-start) | async-done | bytes 1048608 | tf_op jit(solution)/shard_map/all_to_all | solution.py:87
  91.7 0.0 collective-permute-done.2.refs_3_
  91.7 0.0 collective-permute-done.1.refs_2_
  91.7 4.4 %shard_map.88 = (bf16[16,512]{1,0:T(8,128)(2,1)S(1)}, bf16[112,512]{1,0:T(8,128)(2,1)S(1)}, bf16[128,512]{1,0:T(8,128)(2,1)S(1)}) custom-call(s32[1]{0:T(128)} %bitcast.chip, s32[32]{0:T(128)S(1)} %reshape.11.table, bf16[8,128,512]{2,1,0:T(8,128)(2,1)S(1)} %all-to-all-done.q_ref, bf16[8,128,1024]{2,1,0:T(8,128)(2,1)S(1)} %all-to-all-done.1.refs_0_, ...), custom_call_target="tpu_custom_call" | custom-call | flops 805306368 | bytes 6291456 | tf_op jit(solution)/shard_map/pallas_call | solution.py:206
  96.0 0.1 collective-permute-start.3
  96.1 2.9 %collective-permute-start.4 = (bf16[112,512]{1,0:T(8,128)(2,1)S(1)}, bf16[112,512]{1,0:T(8,128)(2,1)S(1)}, u32[]{:S(2)}, u32[]{:S(2)}) collective-permute-start(bf16[112,512]{1,0:T(8,128)(2,1)S(1)} %get-tuple-element.16), channel_id=1, source_target_pairs={{0,16},{2,18},{4,20},{6,22},{8,24},{10,26},{12,28},{14,30},{16,0},... | collective-permute-start | bytes 344072 | tf_op jit(solution)/shard_map/ppermute | solution.py:265
  99.0 0.9 collective-permute-start.5
  100.0 1.0 collective-permute-done.3.refs_4_.refs_0_
  101.0 7.1 %shard_map.89 = (bf16[128,512]{1,0:T(8,128)(2,1)S(1)}, bf16[128,512]{1,0:T(8,128)(2,1)S(1)}, bf16[128,512]{1,0:T(8,128)(2,1)S(1)}, bf16[128,512]{1,0:T(8,128)(2,...) custom-call(s32[1]{0:T(128)} %bitcast.chip, s32[32]{0:T(128)S(1)} %reshape.11.table, ...), custom_call_target="tpu_custom_call" | custom-call | flops 2415919104 | bytes 6291456 | tf_op jit(solution)/shard_map/pallas_call | solution.py:206
  108.1 7.5 %collective-permute-start.6 = (bf16[128,512]{1,0:T(8,128)(2,1)S(1)}, bf16[128,512]{1,0:T(8,128)(2,1)S(1)}, u32[]{:S(2)}, u32[]{:S(2)}) collective-permute-start(bf16[128,512]{1,0:T(8,128)(2,1)S(1)} %get-tuple-element.18), channel_id=1, source_target_pairs={{0,24},{2,26},{4,28},{6,30},{8,16},{10,18},{12,20},{14,22},{16,8},... | collective-permute-start | bytes 393224 | tf_op jit(solution)/shard_map/ppermute | solution.py:265
  115.6 0.0 collective-permute-start.7
  115.6 1.5 %collective-permute-start.8 = (bf16[128,512]{1,0:T(8,128)(2,1)S(1)}, bf16[128,512]{1,0:T(8,128)(2,1)S(1)}, u32[]{:S(2)}, u32[]{:S(2)}) collective-permute-start(bf16[128,512]{1,0:T(8,128)(2,1)S(1)} %get-tuple-element.20), channel_id=1, source_target_pairs={{0,4},{2,6},{4,0},{6,2},{8,12},{10,14},{12,8},{14,10},{16,20},{18,... | collective-permute-start | bytes 393224 | tf_op jit(solution)/shard_map/ppermute | solution.py:265
  117.1 0.0 collective-permute-done.4.refs_1_
  117.1 0.0 collective-permute-start.9
  117.1 0.0 collective-permute-done.5.refs_2_
  117.1 1.9 %collective-permute-start.10 = (bf16[128,512]{1,0:T(8,128)(2,1)S(1)}, bf16[128,512]{1,0:T(8,128)(2,1)S(1)}, u32[]{:S(2)}, u32[]{:S(2)}) collective-permute-start(bf16[128,512]{1,0:T(8,128)(2,1)S(1)} %get-tuple-element.22), channel_id=1, source_target_pairs={{0,12},{2,14},{4,8},{6,10},{8,4},{10,6},{12,0},{14,2},{16,28},{18,... | collective-permute-start | bytes 393224 | tf_op jit(solution)/shard_map/ppermute | solution.py:265
  119.1 0.0 collective-permute-done.6.refs_3_
  119.1 4.3 %collective-permute-done.7.refs_4_ = bf16[128,512]{1,0:T(8,128)(2,1)S(1)} collective-permute-done((bf16[128,512]{1,0:T(8,128)(2,1)S(1)}, bf16[128,512]{1,0:T(8,128)(2,1)S(1)}, u32[]{:S(2)}, u32[]{:S(2)}) %collective-permute-start.7) | collective-permute-done | bytes 131104 | tf_op jit(solution)/shard_map/ppermute | solution.py:265
  123.3 0.0 collective-permute-done.8.refs_5_
  123.4 0.0 collective-permute-done.9.refs_6_
  123.4 1.5 %collective-permute-done.10.refs_7_ = bf16[128,512]{1,0:T(8,128)(2,1)S(1)} collective-permute-done((bf16[128,512]{1,0:T(8,128)(2,1)S(1)}, bf16[128,512]{1,0:T(8,128)(2,1)S(1)}, u32[]{:S(2)}, u32[]{:S(2)}) %collective-permute-start.10) | collective-permute-done | bytes 131104 | tf_op jit(solution)/shard_map/ppermute | solution.py:265
  124.8 1.3 %shard_map.90 = (bf16[128,2048]{1,0:T(8,128)(2,1)}, bf16[128,2048]{1,0:T(8,128)(2,1)}) custom-call(s32[1]{0:T(128)} %bitcast.chip, bf16[16,512]{1,0:T(8,128)(2,1)S(1)} %collective-permute-done.3.refs_4_.refs_0_, bf16[112,512]{1,0:T(8,128)(2,1)S(1)} %collective-permute-done.4.refs_1_, bf16[128,512]{1,0:T(8,128)(2,1)S(1)} %collective-permute-done.5.refs_2_, ...), custom_call_target="tpu_custom_call" | custom-call | bytes 2097152 | tf_op jit(solution)/shard_map/pallas_call | solution.py:105
  (1 shorter events, 0.0 us)
Async XLA Ops:
  3.4 55.5 %all-to-all-start.1 = ((bf16[8,128,1024]{2,1,0:T(8,128)(2,1)}), bf16[8,128,1024]{2,1,0:T(8,128)(2,1)S(1)}, u32[]{:S(2)}, u32[]{:S(2)}) async-start(bf16[8,128,1024]{2,1,0:T(8,128)(2,1)} %shard_map.86.refs_2_), calls=%async_computation.1 | async-start | bytes 4194304 | tf_op jit(solution)/shard_map/all_to_all | solution.py:87
  14.0 70.0 %copy-start = (s32[8,4]{0,1:T(4,128)S(1)}, s32[8,4]{0,1:T(4,128)}, u32[]{:S(2)}) copy-start(s32[8,4]{0,1:T(4,128)} %param.13) | copy-start | bytes 388
  59.9 24.1 %collective-permute-start = (bf16[4,128,1024]{2,1,0:T(8,128)(2,1)}, bf16[4,128,1024]{2,1,0:T(8,128)(2,1)}, u32[]{:S(2)}, u32[]{:S(2)}) collective-permute-start(bf16[4,128,1024]{2,1,0:T(8,128)(2,1)} %constant_dynamic-slice_fusion), channel_id=1, source_target_pairs={{0,1},{1,0},{2,3},{3,2},{4,5},{5,4},{6,7},{7,6},{8,9},{9,8},{10,11... | collective-permute-start | bytes 3145736 | tf_op jit(solution)/shard_map/ppermute | solution.py:250
  61.5 30.2 %collective-permute-start.1 = (bf16[8,128,1024]{2,1,0:T(8,128)(2,1)S(1)}, bf16[8,128,1024]{2,1,0:T(8,128)(2,1)}, u32[]{:S(2)}, u32[]{:S(2)}) collective-permute-start(bf16[8,128,1024]{2,1,0:T(8,128)(2,1)S(1)} %all-to-all-done.1.refs_0_), channel_id=1, source_target_pairs={{0,2},{2,0},{4,6},{6,4},{8,10},{10,8},{12,14},{14,12},{16,18},{18,... | collective-permute-start | bytes 6291464 | tf_op jit(solution)/shard_map/ppermute | solution.py:251
  61.5 30.2 %all-to-all-start = ((bf16[8,128,512]{2,1,0:T(8,128)(2,1)}), bf16[8,128,512]{2,1,0:T(8,128)(2,1)S(1)}, u32[]{:S(2)}, u32[]{:S(2)}) async-start(bf16[8,128,512]{2,1,0:T(8,128)(2,1)} %get-tuple-element.13), calls=%async_computation | async-start | bytes 2097152 | tf_op jit(solution)/shard_map/all_to_all | solution.py:87
  84.0 7.7 %collective-permute-start.2 = (bf16[4,128,1024]{2,1,0:T(8,128)(2,1)}, bf16[4,128,1024]{2,1,0:T(8,128)(2,1)}, u32[]{:S(2)}, u32[]{:S(2)}) collective-permute-start(bf16[4,128,1024]{2,1,0:T(8,128)(2,1)} %collective-permute-done.refs_1_), channel_id=1, source_target_pairs={{0,2},{2,0},{4,6},{6,4},{8,10},{10,8},{12,14},{14,12},{16,18},{18,... | collective-permute-start | bytes 3145736 | tf_op jit(solution)/shard_map/ppermute | solution.py:251
  96.0 4.9 %collective-permute-start.3 = (bf16[16,512]{1,0:T(8,128)(2,1)S(1)}, bf16[16,512]{1,0:T(8,128)(2,1)S(1)}, u32[]{:S(2)}, u32[]{:S(2)}) collective-permute-start(bf16[16,512]{1,0:T(8,128)(2,1)S(1)} %get-tuple-element.15), channel_id=1, source_target_pairs={{0,16},{2,18},{4,20},{6,22},{8,24},{10,26},{12,28},{14,30},{16,0},... | collective-permute-start | bytes 49160 | tf_op jit(solution)/shard_map/ppermute | solution.py:265
  96.1 21.0 %collective-permute-start.4 = (bf16[112,512]{1,0:T(8,128)(2,1)S(1)}, bf16[112,512]{1,0:T(8,128)(2,1)S(1)}, u32[]{:S(2)}, u32[]{:S(2)}) collective-permute-start(bf16[112,512]{1,0:T(8,128)(2,1)S(1)} %get-tuple-element.16), channel_id=1, source_target_pairs={{0,16},{2,18},{4,20},{6,22},{8,24},{10,26},{12,28},{14,30},{16,0},... | collective-permute-start | bytes 344072 | tf_op jit(solution)/shard_map/ppermute | solution.py:265
  99.0 18.1 %collective-permute-start.5 = (bf16[128,512]{1,0:T(8,128)(2,1)S(1)}, bf16[128,512]{1,0:T(8,128)(2,1)S(1)}, u32[]{:S(2)}, u32[]{:S(2)}) collective-permute-start(bf16[128,512]{1,0:T(8,128)(2,1)S(1)} %get-tuple-element.17), channel_id=1, source_target_pairs={{0,20},{2,22},{4,16},{6,18},{8,28},{10,30},{12,24},{14,26},{16,4},... | collective-permute-start | bytes 393224 | tf_op jit(solution)/shard_map/ppermute | solution.py:265
  108.1 11.0 %collective-permute-start.6 = (bf16[128,512]{1,0:T(8,128)(2,1)S(1)}, bf16[128,512]{1,0:T(8,128)(2,1)S(1)}, u32[]{:S(2)}, u32[]{:S(2)}) collective-permute-start(bf16[128,512]{1,0:T(8,128)(2,1)S(1)} %get-tuple-element.18), channel_id=1, source_target_pairs={{0,24},{2,26},{4,28},{6,30},{8,16},{10,18},{12,20},{14,22},{16,8},... | collective-permute-start | bytes 393224 | tf_op jit(solution)/shard_map/ppermute | solution.py:265
  115.6 7.8 %collective-permute-start.7 = (bf16[128,512]{1,0:T(8,128)(2,1)S(1)}, bf16[128,512]{1,0:T(8,128)(2,1)S(1)}, u32[]{:S(2)}, u32[]{:S(2)}) collective-permute-start(bf16[128,512]{1,0:T(8,128)(2,1)S(1)} %get-tuple-element.19), channel_id=1, source_target_pairs={{0,28},{2,30},{4,24},{6,26},{8,20},{10,22},{12,16},{14,18},{16,12}... | collective-permute-start | bytes 393224 | tf_op jit(solution)/shard_map/ppermute | solution.py:265
  115.6 7.8 %collective-permute-start.8 = (bf16[128,512]{1,0:T(8,128)(2,1)S(1)}, bf16[128,512]{1,0:T(8,128)(2,1)S(1)}, u32[]{:S(2)}, u32[]{:S(2)}) collective-permute-start(bf16[128,512]{1,0:T(8,128)(2,1)S(1)} %get-tuple-element.20), channel_id=1, source_target_pairs={{0,4},{2,6},{4,0},{6,2},{8,12},{10,14},{12,8},{14,10},{16,20},{18,... | collective-permute-start | bytes 393224 | tf_op jit(solution)/shard_map/ppermute | solution.py:265
  117.1 6.2 %collective-permute-start.9 = (bf16[128,512]{1,0:T(8,128)(2,1)S(1)}, bf16[128,512]{1,0:T(8,128)(2,1)S(1)}, u32[]{:S(2)}, u32[]{:S(2)}) collective-permute-start(bf16[128,512]{1,0:T(8,128)(2,1)S(1)} %get-tuple-element.21), channel_id=1, source_target_pairs={{0,8},{2,10},{4,12},{6,14},{8,0},{10,2},{12,4},{14,6},{16,24},{18,... | collective-permute-start | bytes 393224 | tf_op jit(solution)/shard_map/ppermute | solution.py:265
  117.1 7.7 %collective-permute-start.10 = (bf16[128,512]{1,0:T(8,128)(2,1)S(1)}, bf16[128,512]{1,0:T(8,128)(2,1)S(1)}, u32[]{:S(2)}, u32[]{:S(2)}) collective-permute-start(bf16[128,512]{1,0:T(8,128)(2,1)S(1)} %get-tuple-element.22), channel_id=1, source_target_pairs={{0,12},{2,14},{4,8},{6,10},{8,4},{10,6},{12,0},{14,2},{16,28},{18,... | collective-permute-start | bytes 393224 | tf_op jit(solution)/shard_map/ppermute | solution.py:265

commit v14 on v12

--- a/solution.py
+++ b/solution.py
@@ -12,7 +12,8 @@
 WK = 4
 HB = 4
 PAIR = 2
-PARAMS = pltpu.CompilerParams(vmem_limit_bytes=40 * 1024 * 1024)
+LEAD = 16
+PARAMS = pltpu.CompilerParams(vmem_limit_bytes=32 * 1024 * 1024)
 ANY = pl.BlockSpec(memory_space=pl.ANY)
 HBM = pl.BlockSpec(memory_space=pltpu.HBM)
 VMEM = pl.BlockSpec(memory_space=pltpu.VMEM)
@@ -112,33 +113,39 @@
     )(chip, *pieces.values())
 
 
-def attend_kernel(chip, table, q_ref, *refs, sources, later, slots, hd):
-    parts, outs = refs[: PAIR * sources], refs[PAIR * sources + later : -2]
-    kv, sems = refs[-2:]
-    tokens = q_ref.shape[1]
-    groups = 2 * PAIR
+def join_kernel(*refs, sources):
+    parts, kv, sems = refs[: PAIR * sources], refs[-2], refs[-1]
     copies = []
-    for g in range(groups):
-        lanes = pl.ds(g * 2 * hd, 2 * hd)
-        for core in range(PAIR):
-            row = 0
-            for i in range(sources):
-                ref, n = parts[core * sources + i], core * sources + i
-                rows = pl.ds(row, ref.shape[0])
-                copies.append(
-                    pltpu.make_async_copy(
-                        ref.at[:, :, lanes], kv.at[rows, core, :, lanes], sems.at[g, n]
-                    )
-                )
-                row += ref.shape[0]
+    for core in range(PAIR):
+        row = 0
+        for i in range(sources):
+            n = core * sources + i
+            target = kv.at[pl.ds(row, parts[n].shape[0]), core]
+            copies.append(pltpu.make_async_copy(parts[n], target, sems.at[n]))
+            row += parts[n].shape[0]
     for copy in copies:
         copy.start()
-
-    def arrive(group):
-        size = len(copies) // groups
-        for copy in copies[group * size : (group + 1) * size]:
-            copy.wait()
-
+    for copy in copies:
+        copy.wait()
+
+
+def join(mine, other):
+    _, tokens, width = mine[0].shape
+    shape = (sum(a.shape[0] for a in mine), PAIR, tokens, width)
+    return pl.pallas_call(
+        functools.partial(join_kernel, sources=len(mine)),
+        in_specs=[ANY] * (PAIR * len(mine)),
+        out_specs=VMEM,
+        out_shape=jax.ShapeDtypeStruct(shape, jnp.bfloat16),
+        scratch_shapes=[pltpu.SemaphoreType.DMA((PAIR * len(mine),))],
+        compiler_params=PARAMS,
+        cost_estimate=moves(8 * shape[0] * PAIR * tokens * width),
+    )(*mine, *other)
+
+
+def attend_kernel(chip, table, q_ref, kv, *refs, later, places, token, hd):
+    outs = refs[later:]
+    tokens = q_ref.shape[1]
     scale = hd ** (-0.5)
     factor = scale * math.log2(math.e)
     trans = (((1,), (1,)), ((), ()))
@@ -176,50 +183,43 @@
         out = mixed[:tokens, :hd] * inverse
         tan = (mixed[:tokens, hd:] + scale * mixed[tokens:, :hd]) * inverse
         tan = tan - (scale * mean * inverse) * out
-        ref = outs[slots.index(k)]
+        ref = outs[places.index(k)]
         ref[:, 2 * h * hd : (2 * h + 1) * hd] = out.astype(jnp.bfloat16)
         ref[:, (2 * h + 1) * hd : 2 * (h + 1) * hd] = tan.astype(jnp.bfloat16)
 
-    units = [(k, h) for h in range(PAIR) for k in slots]
-    arrive(0)
+    units = [(k, h) for k in places for h in range(PAIR)]
     ahead = products(*units[0])
-    arrive(1)
     for unit, following in zip(units, units[1:] + [None]):
         current = ahead
         if following is not None:
-            if following[1] > unit[1]:
-                arrive(2)
-                arrive(3)
             ahead = products(*following)
         finish(*unit, *current)
-
-
-def attend(chip, table, queries, mine, other, later, slots):
+    if token:
+        outs[-1][...] = outs[0][:LEAD]
+
+
+def attend(chip, table, queries, kv, later, places, token):
     _, tokens, width = queries.shape
-    hd, sources = width // (2 * PAIR), len(mine)
-    total = sum(a.shape[0] for a in mine)
-    elements = len(slots) * BQ * WK * BQ
+    hd = width // (2 * PAIR)
+    elements = len(places) * BQ * WK * BQ
+    sizes = [tokens] * len(places) + [LEAD] * token
     return pl.pallas_call(
         functools.partial(
-            attend_kernel, sources=sources, later=len(later), slots=slots, hd=hd
+            attend_kernel, later=len(later), places=places, token=token, hd=hd
         ),
-        in_specs=[SMEM, SMEM, VMEM] + [ANY] * (PAIR * sources + len(later)),
-        out_specs=[VMEM] * len(slots),
-        out_shape=[jax.ShapeDtypeStruct((tokens, width), jnp.bfloat16)] * len(slots),
-        scratch_shapes=[
-            pltpu.VMEM((total, PAIR, tokens, 2 * width), jnp.bfloat16),
-            pltpu.SemaphoreType.DMA((2 * PAIR, PAIR * sources)),
-        ],
+        in_specs=[SMEM, SMEM, VMEM, VMEM] + [ANY] * len(later),
+        out_specs=[VMEM] * len(sizes),
+        out_shape=[jax.ShapeDtypeStruct((size, width), jnp.bfloat16) for size in sizes],
         compiler_params=PARAMS,
         cost_estimate=pl.CostEstimate(
             flops=12 * elements * hd,
-            bytes_accessed=8 * total * tokens * width,
+            bytes_accessed=2 * kv.size,
             transcendentals=elements,
         ),
-    )(chip, table, queries, *mine, *other, *later)
-
-
-def places(neighbors, frame, blocks):
+    )(chip, table, queries, kv, *later)
+
+
+def locate(neighbors, frame, blocks):
     local = neighbors - frame * blocks
     even = frame % 2 == 0
     before = blocks + jnp.where(even, HB, 0) + local + HB
@@ -247,15 +247,16 @@
     other = [lax.ppermute(a, "heads", swap) for a in mine]
 
     queries = exchange(q_sent, devices)
-    table = places(neighbors, frame, blocks)
-    half = blocks // 2
+    table = locate(neighbors, frame, blocks)
+    half, middle = blocks // 2, blocks // 2 + blocks // 4
+    kv = join(mine, other)
     back, later = {}, []
-    for part in ([1, *range(half, blocks)], [*range(2, half), 0]):
-        pieces = attend(chip, table, queries, mine, other, later, part)
+    for part in (range(half, middle), [*range(middle, blocks), *range(1, half), 0]):
+        pieces = attend(chip, table, queries, kv, later, list(part), not later)
         for k, piece in zip(part, pieces):
             pairs = [(d, d ^ (k * PAIR)) for d in range(devices)]
             back[k] = lax.ppermute(piece, "heads", pairs) if k else piece
-        later = [back[1]]
+        later = [lax.ppermute(pieces[-1], "heads", swap)] if not later else later
     return unpack(chip, back, 2)
 
 

time: 127 us -> 127 us (level)
  local copies, waits for them, and re-layouts: 1.22 us -> 6.68 us
  waiting for transfers between devices: 83.8 us -> 80.5 us
  Pallas kernels: 18.2 us -> 16.2 us
    all_to_all x2, waiting for transfers between devices: 52.4 us -> 44.9 us  [exchange(): lax.all_to_all(pieces, 'heads', split_axis=0, concat_axis=0, axis_index_g...]
    unnamed x2 -> x6, local copies, waits for them, and re-layouts: 0.01 us -> 5.45 us
    ppermute x2, waiting for transfers between devices: 0.01 us -> 2.83 us  [per_device(): other = [lax.ppermute(a, 'heads', swap) for a in mine]]
    pallas_call x2 -> x3, Pallas kernels: 11.5 us -> 9.49 us  [the longest x2 7.14 us: attend(): pl.pallas_call(functools.partial(attend_kernel, later=len(later), places=...]
    ppermute x7, waiting for transfers between devices: 12.5 us -> 13.9 us  [per_device(): back[k] = lax.ppermute(piece, 'heads', pairs) if k else piece]
  transfers between devices with their start and end apart: 12 -> 13, of which waited for: 7 -> 7; matrix products, arithmetic and copies ran while one was open for 0% -> 0% of each run, Pallas kernels for 6% -> 8%
where the time goes in v14:
time: 127 us
  waiting for transfers between devices  80.5 us (63%)
  starting transfers between devices  22.2 us (17%)
  Pallas kernels  16.2 us (13%)
  local copies, waits for them, and re-layouts  6.68 us (5%)
  between operations  1.36 us (1%)
    all_to_all x2, waiting for transfers between devices, exchange(): lax.all_to_all(pieces, 'heads', split_axis=0, concat_axis=0, axis_index_g...  44.9 us
    ppermute x1, waiting for transfers between devices, per_device(): lax.ppermute(edge, 'frames', pairs + [(j, i) for i, j in pairs])  18.9 us
    ppermute x7, waiting for transfers between devices, per_device(): back[k] = lax.ppermute(piece, 'heads', pairs) if k else piece  13.9 us
    all_to_all x2, starting transfers between devices, exchange(): lax.all_to_all(pieces, 'heads', split_axis=0, concat_axis=0, axis_index_g...  10.9 us
    ppermute x7, starting transfers between devices, per_device(): back[k] = lax.ppermute(piece, 'heads', pairs) if k else piece  9.57 us
    pallas_call x2, Pallas kernels, attend(): pl.pallas_call(functools.partial(attend_kernel, later=len(later), places=...  7.14 us
    unnamed x6, local copies, waits for them, and re-layouts  5.45 us
    pallas_call x2, Pallas kernels, to_chips(): pl.pallas_call(functools.partial(pack_kernel, count=count, before=len(bef...  5.42 us
  transfers between devices with their start and end apart: 13, of which 7 were waited for; matrix products, arithmetic and copies ran while one was open for 0% of the time, Pallas kernels for 8%

profile of v14, /device:TPU:0, one launch (start us, length us, event | category | flops | bytes accessed | tf_op | source)
XLA Modules:
  0.0 126.9 jit_solution(12157984558215856357)
XLA Ops:
  0.6 2.7 %shard_map.86.refs_2_ = bf16[8,128,1024]{2,1,0:T(8,128)(2,1)} custom-call(bf16[128,2048]{1,0:T(8,128)(2,1)} %refs_0_.2, bf16[128,2048]{1,0:T(8,128)(2,1)} %refs_1_.2, bf16[128,2048]{1,0:T(8,128)(2,1)} %refs_2_.1, bf16[128,2048]{1,0:T(8,128)(2,1)} %refs_3_.1), custom_call_target="tpu_custom_call" | custom-call | bytes 4194304 | tf_op jit(solution)/shard_map/pallas_call | solution.py:68
  3.4 7.3 %all-to-all-start.1 = ((bf16[8,128,1024]{2,1,0:T(8,128)(2,1)}), bf16[8,128,1024]{2,1,0:T(8,128)(2,1)S(1)}, u32[]{:S(2)}, u32[]{:S(2)}) async-start(bf16[8,128,1024]{2,1,0:T(8,128)(2,1)} %shard_map.86.refs_2_), calls=%async_computation.1 | async-start | bytes 4194304 | tf_op jit(solution)/shard_map/all_to_all | solution.py:87
  10.6 2.7 %shard_map.87 = (bf16[8,128,512]{2,1,0:T(8,128)(2,1)}, s32[1]{0:T(128)}) custom-call(bf16[128,2048]{1,0:T(8,128)(2,1)} %refs_0_.3, bf16[128,2048]{1,0:T(8,128)(2,1)} %refs_1_.3, bf16[8,128,1024]{2,1,0:T(8,128)(2,1)} %shard_map.86.refs_2_), custom_call_target="tpu_custom_call" | custom-call | bytes 2097152 | tf_op jit(solution)/shard_map/pallas_call | solution.py:68
  14.0 0.0 copy-start.2
  14.0 44.9 %all-to-all-done.1.refs_0_ = bf16[8,128,1024]{2,1,0:T(8,128)(2,1)S(1)} async-done(((bf16[8,128,1024]{2,1,0:T(8,128)(2,1)}), bf16[8,128,1024]{2,1,0:T(8,128)(2,1)S(1)}, u32[]{:S(2)}, u32[]{:S(2)}) %all-to-all-start.1) | async-done | bytes 2097184 | tf_op jit(solution)/shard_map/all_to_all | solution.py:87
  58.9 1.1 constant_dynamic-slice_fusion
  59.9 1.5 %collective-permute-start = (bf16[4,128,1024]{2,1,0:T(8,128)(2,1)}, bf16[4,128,1024]{2,1,0:T(8,128)(2,1)}, u32[]{:S(2)}, u32[]{:S(2)}) collective-permute-start(bf16[4,128,1024]{2,1,0:T(8,128)(2,1)} %constant_dynamic-slice_fusion), channel_id=1, source_target_pairs={{0,1},{1,0},{2,3},{3,2},{4,5},{5,4},{6,7},{7,6},{8,9},{9,8},{10,11... | collective-permute-start | bytes 3145736 | tf_op jit(solution)/shard_map/ppermute | solution.py:246
  61.5 0.0 collective-permute-start.1
  61.5 3.6 %all-to-all-start = ((bf16[8,128,512]{2,1,0:T(8,128)(2,1)}), bf16[8,128,512]{2,1,0:T(8,128)(2,1)S(1)}, u32[]{:S(2)}, u32[]{:S(2)}) async-start(bf16[8,128,512]{2,1,0:T(8,128)(2,1)} %get-tuple-element.13), calls=%async_computation | async-start | bytes 2097152 | tf_op jit(solution)/shard_map/all_to_all | solution.py:87
  65.1 18.9 %collective-permute-done.refs_1_ = bf16[4,128,1024]{2,1,0:T(8,128)(2,1)} collective-permute-done((bf16[4,128,1024]{2,1,0:T(8,128)(2,1)}, bf16[4,128,1024]{2,1,0:T(8,128)(2,1)}, u32[]{:S(2)}, u32[]{:S(2)}) %collective-permute-start) | collective-permute-done | bytes 1048608 | tf_op jit(solution)/shard_map/ppermute | solution.py:246
  84.0 0.0 collective-permute-start.2
  84.0 0.0 copy-done.2
  84.0 0.1 copy.10
  84.1 0.1 reshape.11.table
  84.2 2.8 %collective-permute-done.2.refs_3_ = bf16[4,128,1024]{2,1,0:T(8,128)(2,1)} collective-permute-done((bf16[4,128,1024]{2,1,0:T(8,128)(2,1)}, bf16[4,128,1024]{2,1,0:T(8,128)(2,1)}, u32[]{:S(2)}, u32[]{:S(2)}) %collective-permute-start.2) | collective-permute-done | bytes 1048608 | tf_op jit(solution)/shard_map/ppermute | solution.py:247
  87.0 0.0 collective-permute-done.1.refs_2_
  87.0 2.3 %shard_map.88.kv = bf16[12,2,128,1024]{3,2,1,0:T(8,128)(2,1)S(1)} custom-call(bf16[8,128,1024]{2,1,0:T(8,128)(2,1)S(1)} %all-to-all-done.1.refs_0_, bf16[4,128,1024]{2,1,0:T(8,128)(2,1)} %collective-permute-done.refs_1_, bf16[8,128,1024]{2,1,0:T(8,128)(2,1)} %collective-permute-done.1.refs_2_, bf16[4,128,1024]{2,1,0:T(8,128)(2,1)} %collective-permute-done.2.refs_3_), custom_call_target="tpu_custom_call" | custom-call | bytes 25165824 | tf_op jit(solution)/shard_map/pallas_call | solution.py:135
  89.4 0.0 copy-start
  89.4 2.7 %copy-done = bf16[12,2,128,1024]{3,2,1,0:T(8,128)(2,1)} copy-done((bf16[12,2,128,1024]{3,2,1,0:T(8,128)(2,1)}, bf16[12,2,128,1024]{3,2,1,0:T(8,128)(2,1)S(1)}, u32[]{:S(2)}) %copy-start) | copy-done | bytes 6291480
  92.0 0.0 all-to-all-done.q_ref
  92.0 0.0 copy-start.1
  92.0 2.8 %copy-done.1 = bf16[12,2,128,1024]{3,2,1,0:T(8,128)(2,1)S(1)} copy-done((bf16[12,2,128,1024]{3,2,1,0:T(8,128)(2,1)S(1)}, bf16[12,2,128,1024]{3,2,1,0:T(8,128)(2,1)}, u32[]{:S(2)}) %copy-start.1) | copy-done | bytes 6291480
  94.8 2.4 %shard_map.89 = (bf16[128,512]{1,0:T(8,128)(2,1)S(1)}, bf16[128,512]{1,0:T(8,128)(2,1)S(1)}, bf16[16,512]{1,0:T(8,128)(2,1)S(1)}) custom-call(s32[1]{0:T(128)} %bitcast.chip, s32[32]{0:T(128)S(1)} %reshape.11.table, bf16[8,128,512]{2,1,0:T(8,128)(2,1)S(1)} %all-to-all-done.q_ref, bf16[12,2,128,1024]{3,2,1,0:T(8,128)(2,1)S(1)} %copy-done.1), custom_call_target="tpu_custom_call" | custom-call | flops 805306368 | bytes 6291456 | tf_op jit(solution)/shard_map/pallas_call | solution.py:206
  97.2 0.2 collective-permute-start.5
  97.4 0.0 collective-permute-start.3
  97.4 4.2 %collective-permute-start.4 = (bf16[128,512]{1,0:T(8,128)(2,1)S(1)}, bf16[128,512]{1,0:T(8,128)(2,1)S(1)}, u32[]{:S(2)}, u32[]{:S(2)}) collective-permute-start(bf16[128,512]{1,0:T(8,128)(2,1)S(1)} %get-tuple-element.16), channel_id=1, source_target_pairs={{0,20},{2,22},{4,16},{6,18},{8,28},{10,30},{12,24},{14,26},{16,4},... | collective-permute-start | bytes 393224 | tf_op jit(solution)/shard_map/ppermute | solution.py:258
  101.6 0.0 collective-permute-done.5.refs_0_
  101.6 4.8 %shard_map.90 = (bf16[128,512]{1,0:T(8,128)(2,1)S(1)}, bf16[128,512]{1,0:T(8,128)(2,1)S(1)}, bf16[128,512]{1,0:T(8,128)(2,1)S(1)}, bf16[128,512]{1,0:T(8,128)(2,...) custom-call(s32[1]{0:T(128)} %bitcast.chip, s32[32]{0:T(128)S(1)} %reshape.11.table, ...), custom_call_target="tpu_custom_call" | custom-call | flops 2415919104 | bytes 6291456 | tf_op jit(solution)/shard_map/pallas_call | solution.py:206
  106.4 2.5 %collective-permute-start.6 = (bf16[128,512]{1,0:T(8,128)(2,1)S(1)}, bf16[128,512]{1,0:T(8,128)(2,1)S(1)}, u32[]{:S(2)}, u32[]{:S(2)}) collective-permute-start(bf16[128,512]{1,0:T(8,128)(2,1)S(1)} %get-tuple-element.18), channel_id=1, source_target_pairs={{0,24},{2,26},{4,28},{6,30},{8,16},{10,18},{12,20},{14,22},{16,8},... | collective-permute-start | bytes 393224 | tf_op jit(solution)/shard_map/ppermute | solution.py:258
  108.9 1.0 collective-permute-start.7
  109.9 1.8 %collective-permute-start.8 = (bf16[128,512]{1,0:T(8,128)(2,1)S(1)}, bf16[128,512]{1,0:T(8,128)(2,1)S(1)}, u32[]{:S(2)}, u32[]{:S(2)}) collective-permute-start(bf16[128,512]{1,0:T(8,128)(2,1)S(1)} %get-tuple-element.20), channel_id=1, source_target_pairs={{0,4},{2,6},{4,0},{6,2},{8,12},{10,14},{12,8},{14,10},{16,20},{18,... | collective-permute-start | bytes 393224 | tf_op jit(solution)/shard_map/ppermute | solution.py:258
  111.7 0.0 collective-permute-done.3.refs_0_
  111.7 0.0 collective-permute-start.9
  111.7 7.6 %collective-permute-done.4.refs_1_ = bf16[128,512]{1,0:T(8,128)(2,1)S(1)} collective-permute-done((bf16[128,512]{1,0:T(8,128)(2,1)S(1)}, bf16[128,512]{1,0:T(8,128)(2,1)S(1)}, u32[]{:S(2)}, u32[]{:S(2)}) %collective-permute-start.4) | collective-permute-done | bytes 131104 | tf_op jit(solution)/shard_map/ppermute | solution.py:258
  119.4 0.0 collective-permute-start.10
  119.4 0.0 collective-permute-done.6.refs_2_
  119.4 0.0 collective-permute-done.7.refs_3_
  119.4 1.1 collective-permute-done.8.refs_4_
  120.5 0.5 collective-permute-done.9.refs_5_
  121.0 4.7 %collective-permute-done.10.refs_6_ = bf16[128,512]{1,0:T(8,128)(2,1)S(1)} collective-permute-done((bf16[128,512]{1,0:T(8,128)(2,1)S(1)}, bf16[128,512]{1,0:T(8,128)(2,1)S(1)}, u32[]{:S(2)}, u32[]{:S(2)}) %collective-permute-start.10) | collective-permute-done | bytes 131104 | tf_op jit(solution)/shard_map/ppermute | solution.py:258
  125.6 1.3 shard_map.91
  (1 shorter events, 0.0 us)
Async XLA Ops:
  3.4 55.5 %all-to-all-start.1 = ((bf16[8,128,1024]{2,1,0:T(8,128)(2,1)}), bf16[8,128,1024]{2,1,0:T(8,128)(2,1)S(1)}, u32[]{:S(2)}, u32[]{:S(2)}) async-start(bf16[8,128,1024]{2,1,0:T(8,128)(2,1)} %shard_map.86.refs_2_), calls=%async_computation.1 | async-start | bytes 4194304 | tf_op jit(solution)/shard_map/all_to_all | solution.py:87
  14.0 70.0 %copy-start.2 = (s32[8,4]{0,1:T(4,128)S(1)}, s32[8,4]{0,1:T(4,128)}, u32[]{:S(2)}) copy-start(s32[8,4]{0,1:T(4,128)} %param.13) | copy-start | bytes 388
  59.9 24.1 %collective-permute-start = (bf16[4,128,1024]{2,1,0:T(8,128)(2,1)}, bf16[4,128,1024]{2,1,0:T(8,128)(2,1)}, u32[]{:S(2)}, u32[]{:S(2)}) collective-permute-start(bf16[4,128,1024]{2,1,0:T(8,128)(2,1)} %constant_dynamic-slice_fusion), channel_id=1, source_target_pairs={{0,1},{1,0},{2,3},{3,2},{4,5},{5,4},{6,7},{7,6},{8,9},{9,8},{10,11... | collective-permute-start | bytes 3145736 | tf_op jit(solution)/shard_map/ppermute | solution.py:246
  61.5 25.6 %collective-permute-start.1 = (bf16[8,128,1024]{2,1,0:T(8,128)(2,1)S(1)}, bf16[8,128,1024]{2,1,0:T(8,128)(2,1)}, u32[]{:S(2)}, u32[]{:S(2)}) collective-permute-start(bf16[8,128,1024]{2,1,0:T(8,128)(2,1)S(1)} %all-to-all-done.1.refs_0_), channel_id=1, source_target_pairs={{0,2},{2,0},{4,6},{6,4},{8,10},{10,8},{12,14},{14,12},{16,18},{18,... | collective-permute-start | bytes 6291464 | tf_op jit(solution)/shard_map/ppermute | solution.py:247
  61.5 30.6 %all-to-all-start = ((bf16[8,128,512]{2,1,0:T(8,128)(2,1)}), bf16[8,128,512]{2,1,0:T(8,128)(2,1)S(1)}, u32[]{:S(2)}, u32[]{:S(2)}) async-start(bf16[8,128,512]{2,1,0:T(8,128)(2,1)} %get-tuple-element.13), calls=%async_computation | async-start | bytes 2097152 | tf_op jit(solution)/shard_map/all_to_all | solution.py:87
  84.0 3.0 %collective-permute-start.2 = (bf16[4,128,1024]{2,1,0:T(8,128)(2,1)}, bf16[4,128,1024]{2,1,0:T(8,128)(2,1)}, u32[]{:S(2)}, u32[]{:S(2)}) collective-permute-start(bf16[4,128,1024]{2,1,0:T(8,128)(2,1)} %collective-permute-done.refs_1_), channel_id=1, source_target_pairs={{0,2},{2,0},{4,6},{6,4},{8,10},{10,8},{12,14},{14,12},{16,18},{18,... | collective-permute-start | bytes 3145736 | tf_op jit(solution)/shard_map/ppermute | solution.py:247
  89.4 2.7 %copy-start = (bf16[12,2,128,1024]{3,2,1,0:T(8,128)(2,1)}, bf16[12,2,128,1024]{3,2,1,0:T(8,128)(2,1)S(1)}, u32[]{:S(2)}) copy-start(bf16[12,2,128,1024]{3,2,1,0:T(8,128)(2,1)S(1)} %shard_map.88.kv) | copy-start | bytes 18874372
  92.0 2.8 %copy-start.1 = (bf16[12,2,128,1024]{3,2,1,0:T(8,128)(2,1)S(1)}, bf16[12,2,128,1024]{3,2,1,0:T(8,128)(2,1)}, u32[]{:S(2)}) copy-start(bf16[12,2,128,1024]{3,2,1,0:T(8,128)(2,1)} %copy-done) | copy-start | bytes 18874372
  97.2 4.4 %collective-permute-start.5 = (bf16[16,512]{1,0:T(8,128)(2,1)S(1)}, bf16[16,512]{1,0:T(8,128)(2,1)S(1)}, u32[]{:S(2)}, u32[]{:S(2)}) collective-permute-start(bf16[16,512]{1,0:T(8,128)(2,1)S(1)} %get-tuple-element.17), channel_id=1, source_target_pairs={{0,2},{2,0},{4,6},{6,4},{8,10},{10,8},{12,14},{14,12},{16,18},{18,... | collective-permute-start | bytes 49160 | tf_op jit(solution)/shard_map/ppermute | solution.py:259
  97.4 14.3 %collective-permute-start.3 = (bf16[128,512]{1,0:T(8,128)(2,1)S(1)}, bf16[128,512]{1,0:T(8,128)(2,1)S(1)}, u32[]{:S(2)}, u32[]{:S(2)}) collective-permute-start(bf16[128,512]{1,0:T(8,128)(2,1)S(1)} %get-tuple-element.15), channel_id=1, source_target_pairs={{0,16},{2,18},{4,20},{6,22},{8,24},{10,26},{12,28},{14,30},{16,0},... | collective-permute-start | bytes 393224 | tf_op jit(solution)/shard_map/ppermute | solution.py:258
  97.4 22.0 %collective-permute-start.4 = (bf16[128,512]{1,0:T(8,128)(2,1)S(1)}, bf16[128,512]{1,0:T(8,128)(2,1)S(1)}, u32[]{:S(2)}, u32[]{:S(2)}) collective-permute-start(bf16[128,512]{1,0:T(8,128)(2,1)S(1)} %get-tuple-element.16), channel_id=1, source_target_pairs={{0,20},{2,22},{4,16},{6,18},{8,28},{10,30},{12,24},{14,26},{16,4},... | collective-permute-start | bytes 393224 | tf_op jit(solution)/shard_map/ppermute | solution.py:258
  106.4 13.0 %collective-permute-start.6 = (bf16[128,512]{1,0:T(8,128)(2,1)S(1)}, bf16[128,512]{1,0:T(8,128)(2,1)S(1)}, u32[]{:S(2)}, u32[]{:S(2)}) collective-permute-start(bf16[128,512]{1,0:T(8,128)(2,1)S(1)} %get-tuple-element.18), channel_id=1, source_target_pairs={{0,24},{2,26},{4,28},{6,30},{8,16},{10,18},{12,20},{14,22},{16,8},... | collective-permute-start | bytes 393224 | tf_op jit(solution)/shard_map/ppermute | solution.py:258
  108.9 10.5 %collective-permute-start.7 = (bf16[128,512]{1,0:T(8,128)(2,1)S(1)}, bf16[128,512]{1,0:T(8,128)(2,1)S(1)}, u32[]{:S(2)}, u32[]{:S(2)}) collective-permute-start(bf16[128,512]{1,0:T(8,128)(2,1)S(1)} %get-tuple-element.19), channel_id=1, source_target_pairs={{0,28},{2,30},{4,24},{6,26},{8,20},{10,22},{12,16},{14,18},{16,12}... | collective-permute-start | bytes 393224 | tf_op jit(solution)/shard_map/ppermute | solution.py:258
  109.9 10.6 %collective-permute-start.8 = (bf16[128,512]{1,0:T(8,128)(2,1)S(1)}, bf16[128,512]{1,0:T(8,128)(2,1)S(1)}, u32[]{:S(2)}, u32[]{:S(2)}) collective-permute-start(bf16[128,512]{1,0:T(8,128)(2,1)S(1)} %get-tuple-element.20), channel_id=1, source_target_pairs={{0,4},{2,6},{4,0},{6,2},{8,12},{10,14},{12,8},{14,10},{16,20},{18,... | collective-permute-start | bytes 393224 | tf_op jit(solution)/shard_map/ppermute | solution.py:258
  111.7 9.2 %collective-permute-start.9 = (bf16[128,512]{1,0:T(8,128)(2,1)S(1)}, bf16[128,512]{1,0:T(8,128)(2,1)S(1)}, u32[]{:S(2)}, u32[]{:S(2)}) collective-permute-start(bf16[128,512]{1,0:T(8,128)(2,1)S(1)} %get-tuple-element.21), channel_id=1, source_target_pairs={{0,8},{2,10},{4,12},{6,14},{8,0},{10,2},{12,4},{14,6},{16,24},{18,... | collective-permute-start | bytes 393224 | tf_op jit(solution)/shard_map/ppermute | solution.py:258
  119.4 6.2 %collective-permute-start.10 = (bf16[128,512]{1,0:T(8,128)(2,1)S(1)}, bf16[128,512]{1,0:T(8,128)(2,1)S(1)}, u32[]{:S(2)}, u32[]{:S(2)}) collective-permute-start(bf16[128,512]{1,0:T(8,128)(2,1)S(1)} %get-tuple-element.22), channel_id=1, source_target_pairs={{0,12},{2,14},{4,8},{6,10},{8,4},{10,6},{12,0},{14,2},{16,28},{18,... | collective-permute-start | bytes 393224 | tf_op jit(solution)/shard_map/ppermute | solution.py:258

commit v15 on v14

--- a/solution.py
+++ b/solution.py
@@ -12,7 +12,6 @@
 WK = 4
 HB = 4
 PAIR = 2
-LEAD = 16
 PARAMS = pltpu.CompilerParams(vmem_limit_bytes=32 * 1024 * 1024)
 ANY = pl.BlockSpec(memory_space=pl.ANY)
 HBM = pl.BlockSpec(memory_space=pltpu.HBM)
@@ -113,39 +112,33 @@
     )(chip, *pieces.values())
 
 
-def join_kernel(*refs, sources):
-    parts, kv, sems = refs[: PAIR * sources], refs[-2], refs[-1]
-    copies = []
-    for core in range(PAIR):
-        row = 0
-        for i in range(sources):
-            n = core * sources + i
-            target = kv.at[pl.ds(row, parts[n].shape[0]), core]
-            copies.append(pltpu.make_async_copy(parts[n], target, sems.at[n]))
-            row += parts[n].shape[0]
-    for copy in copies:
-        copy.start()
-    for copy in copies:
-        copy.wait()
-
-
-def join(mine, other):
-    _, tokens, width = mine[0].shape
-    shape = (sum(a.shape[0] for a in mine), PAIR, tokens, width)
-    return pl.pallas_call(
-        functools.partial(join_kernel, sources=len(mine)),
-        in_specs=[ANY] * (PAIR * len(mine)),
-        out_specs=VMEM,
-        out_shape=jax.ShapeDtypeStruct(shape, jnp.bfloat16),
-        scratch_shapes=[pltpu.SemaphoreType.DMA((PAIR * len(mine),))],
-        compiler_params=PARAMS,
-        cost_estimate=moves(8 * shape[0] * PAIR * tokens * width),
-    )(*mine, *other)
-
-
-def attend_kernel(chip, table, q_ref, kv, *refs, later, places, token, hd):
-    outs = refs[later:]
+def attend_kernel(chip, table, q_ref, *refs, sources, later, places, hd):
     tokens = q_ref.shape[1]
+    if sources:
+        parts, sems, kv = refs[: PAIR * sources], refs[-1], refs[-2]
+        outs = refs[PAIR * sources + later : -2]
+    else:
+        kv, outs = refs[0], refs[1 + later :]
+    groups = []
+    for g in range(2 * PAIR if sources else 0):
+        lanes, copies = pl.ds(g * 2 * hd, 2 * hd), []
+        for n, ref in enumerate(parts):
+            core, row = n // sources, 0 if n % sources == 0 else parts[0].shape[0]
+            row += max(n % sources - 1, 0) * HB
+            target = kv.at[pl.ds(row, ref.shape[0]), core, :, lanes]
+            copies.append(pltpu.make_async_copy(ref.at[:, :, lanes], target, sems.at[g, n]))
+        groups.append(copies)
+
+    def start(*group):
+        for g in group:
+            for copy in groups[g] if sources else []:
+                copy.start()
+
+    def wait(*group):
+        for g in group:
+            for copy in groups[g] if sources else []:
+                copy.wait()
+
     scale = hd ** (-0.5)
     factor = scale * math.log2(math.e)
     trans = (((1,), (1,)), ((), ()))
@@ -187,36 +180,52 @@
         ref[:, 2 * h * hd : (2 * h + 1) * hd] = out.astype(jnp.bfloat16)
         ref[:, (2 * h + 1) * hd : 2 * (h + 1) * hd] = tan.astype(jnp.bfloat16)
 
-    units = [(k, h) for k in places for h in range(PAIR)]
+    units = [(k, h) for h in range(PAIR) for k in places]
+    start(0)
+    wait(0)
+    start(1, 2, 3)
     ahead = products(*units[0])
+    wait(1)
     for unit, following in zip(units, units[1:] + [None]):
         current = ahead
         if following is not None:
+            if following[1] > unit[1]:
+                wait(2, 3)
             ahead = products(*following)
         finish(*unit, *current)
-    if token:
-        outs[-1][...] = outs[0][:LEAD]
-
-
-def attend(chip, table, queries, kv, later, places, token):
+
+
+def attend(chip, table, queries, sources, later, places):
     _, tokens, width = queries.shape
-    hd = width // (2 * PAIR)
+    hd, joins = width // (2 * PAIR), len(sources) > 1
     elements = len(places) * BQ * WK * BQ
-    sizes = [tokens] * len(places) + [LEAD] * token
+    outs = [jax.ShapeDtypeStruct((tokens, width), jnp.bfloat16)] * len(places)
+    scratch, total = [], 0
+    if joins:
+        total = sum(a.shape[0] for a in sources) // PAIR
+        outs.append(jax.ShapeDtypeStruct((total, PAIR, tokens, 2 * width), jnp.bfloat16))
+        scratch.append(pltpu.SemaphoreType.DMA((2 * PAIR, len(sources))))
     return pl.pallas_call(
         functools.partial(
-            attend_kernel, later=len(later), places=places, token=token, hd=hd
+            attend_kernel,
+            sources=len(sources) // PAIR if joins else 0,
+            later=len(later),
+            places=places,
+            hd=hd,
         ),
-        in_specs=[SMEM, SMEM, VMEM, VMEM] + [ANY] * len(later),
-        out_specs=[VMEM] * len(sizes),
-        out_shape=[jax.ShapeDtypeStruct((size, width), jnp.bfloat16) for size in sizes],
+        in_specs=[SMEM, SMEM, VMEM]
+        + [ANY if joins else VMEM] * len(sources)
+        + [ANY] * len(later),
+        out_specs=[VMEM] * len(outs),
+        out_shape=outs,
+        scratch_shapes=scratch,
         compiler_params=PARAMS,
         cost_estimate=pl.CostEstimate(
             flops=12 * elements * hd,
-            bytes_accessed=2 * kv.size,
+            bytes_accessed=8 * total * tokens * width,
             transcendentals=elements,
         ),
-    )(chip, table, queries, kv, *later)
+    )(chip, table, queries, *sources, *later)
 
 
 def locate(neighbors, frame, blocks):
@@ -249,14 +258,13 @@
     queries = exchange(q_sent, devices)
     table = locate(neighbors, frame, blocks)
     half, middle = blocks // 2, blocks // 2 + blocks // 4
-    kv = join(mine, other)
-    back, later = {}, []
-    for part in (range(half, middle), [*range(middle, blocks), *range(1, half), 0]):
-        pieces = attend(chip, table, queries, kv, later, list(part), not later)
+    back, later, sources = {}, [], mine + other
+    for part in ([*range(half, middle), 1], [*range(middle, blocks), *range(2, half), 0]):
+        pieces = attend(chip, table, queries, sources, later, part)
         for k, piece in zip(part, pieces):
             pairs = [(d, d ^ (k * PAIR)) for d in range(devices)]
             back[k] = lax.ppermute(piece, "heads", pairs) if k else piece
-        later = [lax.ppermute(pieces[-1], "heads", swap)] if not later else later
+        later, sources = [back[1]], pieces[len(part) :]
     return unpack(chip, back, 2)
 
 

time: 127 us -> 126 us (level)
  local copies, waits for them, and re-layouts: 6.68 us -> 1.22 us
  waiting for transfers between devices: 80.5 us -> 82.6 us
  starting transfers between devices: 22.2 us -> 23.7 us
    all_to_all x2, waiting for transfers between devices: 44.9 us -> 52.4 us  [exchange(): lax.all_to_all(pieces, 'heads', split_axis=0, concat_axis=0, axis_index_g...]
    unnamed x6 -> x2, local copies, waits for them, and re-layouts: 5.45 us -> 0.01 us
    ppermute x2, waiting for transfers between devices: 2.83 us -> 0.01 us  [per_device(): other = [lax.ppermute(a, 'heads', swap) for a in mine]]
    ppermute x7, waiting for transfers between devices: 13.9 us -> 11.3 us  [per_device(): back[k] = lax.ppermute(piece, 'heads', pairs) if k else piece]
    ppermute x7, starting transfers between devices: 9.57 us -> 11.3 us  [per_device(): back[k] = lax.ppermute(piece, 'heads', pairs) if k else piece]
    pallas_call x3 -> x2, Pallas kernels: 9.49 us -> 10.1 us  [attend(): pl.pallas_call(functools.partial(attend_kernel, sources=len(sources) // P...]
  transfers between devices with their start and end apart: 13 -> 12, of which waited for: 7 -> 7; matrix products, arithmetic and copies ran while one was open for 0% -> 0% of each run, Pallas kernels for 8% -> 5%
where the time goes in v15:
time: 126 us
  waiting for transfers between devices  82.6 us (66%)
  starting transfers between devices  23.7 us (19%)
  Pallas kernels  16.8 us (13%)
  between operations  1.34 us (1%)
    all_to_all x2, waiting for transfers between devices, exchange(): lax.all_to_all(pieces, 'heads', split_axis=0, concat_axis=0, axis_index_g...  52.4 us
    ppermute x1, waiting for transfers between devices, per_device(): lax.ppermute(edge, 'frames', pairs + [(j, i) for i, j in pairs])  18.9 us
    ppermute x7, waiting for transfers between devices, per_device(): back[k] = lax.ppermute(piece, 'heads', pairs) if k else piece  11.3 us
    ppermute x7, starting transfers between devices, per_device(): back[k] = lax.ppermute(piece, 'heads', pairs) if k else piece  11.3 us
    all_to_all x2, starting transfers between devices, exchange(): lax.all_to_all(pieces, 'heads', split_axis=0, concat_axis=0, axis_index_g...  10.9 us
    pallas_call x2, Pallas kernels, attend(): pl.pallas_call(functools.partial(attend_kernel, sources=len(sources) // P...  10.1 us
    pallas_call x2, Pallas kernels, to_chips(): pl.pallas_call(functools.partial(pack_kernel, count=count, before=len(bef...  5.43 us
  transfers between devices with their start and end apart: 12, of which 7 were waited for; matrix products, arithmetic and copies ran while one was open for 0% of the time, Pallas kernels for 5%

profile of v15, /device:TPU:0, one launch (start us, length us, event | category | flops | bytes accessed | tf_op | source)
XLA Modules:
  0.0 125.7 jit_solution(18186561294456412195)
XLA Ops:
  0.6 2.8 %shard_map.86.refs_2_ = bf16[8,128,1024]{2,1,0:T(8,128)(2,1)} custom-call(bf16[128,2048]{1,0:T(8,128)(2,1)} %refs_0_.2, bf16[128,2048]{1,0:T(8,128)(2,1)} %refs_1_.2, bf16[128,2048]{1,0:T(8,128)(2,1)} %refs_2_.1, bf16[128,2048]{1,0:T(8,128)(2,1)} %refs_3_.1), custom_call_target="tpu_custom_call" | custom-call | bytes 4194304 | tf_op jit(solution)/shard_map/pallas_call | solution.py:67
  3.4 7.3 %all-to-all-start.1 = ((bf16[8,128,1024]{2,1,0:T(8,128)(2,1)}), bf16[8,128,1024]{2,1,0:T(8,128)(2,1)S(1)}, u32[]{:S(2)}, u32[]{:S(2)}) async-start(bf16[8,128,1024]{2,1,0:T(8,128)(2,1)} %shard_map.86.refs_2_), calls=%async_computation.1 | async-start | bytes 4194304 | tf_op jit(solution)/shard_map/all_to_all | solution.py:86
  10.7 2.7 %shard_map.87 = (bf16[8,128,512]{2,1,0:T(8,128)(2,1)}, s32[1]{0:T(128)}) custom-call(bf16[128,2048]{1,0:T(8,128)(2,1)} %refs_0_.3, bf16[128,2048]{1,0:T(8,128)(2,1)} %refs_1_.3, bf16[8,128,1024]{2,1,0:T(8,128)(2,1)} %shard_map.86.refs_2_), custom_call_target="tpu_custom_call" | custom-call | bytes 2097152 | tf_op jit(solution)/shard_map/pallas_call | solution.py:67
  14.0 0.0 copy-start
  14.0 44.9 %all-to-all-done.1.refs_0_ = bf16[8,128,1024]{2,1,0:T(8,128)(2,1)S(1)} async-done(((bf16[8,128,1024]{2,1,0:T(8,128)(2,1)}), bf16[8,128,1024]{2,1,0:T(8,128)(2,1)S(1)}, u32[]{:S(2)}, u32[]{:S(2)}) %all-to-all-start.1) | async-done | bytes 2097184 | tf_op jit(solution)/shard_map/all_to_all | solution.py:86
  58.9 1.0 constant_dynamic-slice_fusion
  59.9 1.5 %collective-permute-start = (bf16[4,128,1024]{2,1,0:T(8,128)(2,1)}, bf16[4,128,1024]{2,1,0:T(8,128)(2,1)}, u32[]{:S(2)}, u32[]{:S(2)}) collective-permute-start(bf16[4,128,1024]{2,1,0:T(8,128)(2,1)} %constant_dynamic-slice_fusion), channel_id=1, source_target_pairs={{0,1},{1,0},{2,3},{3,2},{4,5},{5,4},{6,7},{7,6},{8,9},{9,8},{10,11... | collective-permute-start | bytes 3145736 | tf_op jit(solution)/shard_map/ppermute | solution.py:255
  61.5 0.0 collective-permute-start.1
  61.5 3.6 %all-to-all-start = ((bf16[8,128,512]{2,1,0:T(8,128)(2,1)}), bf16[8,128,512]{2,1,0:T(8,128)(2,1)S(1)}, u32[]{:S(2)}, u32[]{:S(2)}) async-start(bf16[8,128,512]{2,1,0:T(8,128)(2,1)} %get-tuple-element.13), calls=%async_computation | async-start | bytes 2097152 | tf_op jit(solution)/shard_map/all_to_all | solution.py:86
  65.1 18.9 %collective-permute-done.refs_1_ = bf16[4,128,1024]{2,1,0:T(8,128)(2,1)} collective-permute-done((bf16[4,128,1024]{2,1,0:T(8,128)(2,1)}, bf16[4,128,1024]{2,1,0:T(8,128)(2,1)}, u32[]{:S(2)}, u32[]{:S(2)}) %collective-permute-start) | collective-permute-done | bytes 1048608 | tf_op jit(solution)/shard_map/ppermute | solution.py:255
  84.0 0.0 collective-permute-start.2
  84.0 0.0 copy-done
  84.0 0.1 copy.10
  84.1 0.1 reshape.11.table
  84.2 7.5 %all-to-all-done.q_ref = bf16[8,128,512]{2,1,0:T(8,128)(2,1)S(1)} async-done(((bf16[8,128,512]{2,1,0:T(8,128)(2,1)}), bf16[8,128,512]{2,1,0:T(8,128)(2,1)S(1)}, u32[]{:S(2)}, u32[]{:S(2)}) %all-to-all-start) | async-done | bytes 1048608 | tf_op jit(solution)/shard_map/all_to_all | solution.py:86
  91.7 0.0 collective-permute-done.2.refs_3_
  91.7 0.0 collective-permute-done.1.refs_2_
  91.7 5.9 %shard_map.88 = (bf16[128,512]{1,0:T(8,128)(2,1)S(1)}, bf16[128,512]{1,0:T(8,128)(2,1)S(1)}, bf16[128,512]{1,0:T(8,128)(2,1)S(1)}, bf16[12,2,128,1024]{3,2,1,0:T(8,128)(2,1)S(1)}) custom-call(s32[1]{0:T(128)} %bitcast.chip, s32[32]{0:T(128)S(1)} %reshape.11.table, bf16[8,128,512]{2,1,0:T(8,128)(2,1)S(1)} %all-to-all-done.q_ref, ...), custom_call_target="tpu_custom_call" | custom-call | flops 1207959552 | bytes 6291456 | tf_op jit(solution)/shard_map/pallas_call | solution.py:208
  97.6 1.5 %collective-permute-start.5 = (bf16[128,512]{1,0:T(8,128)(2,1)S(1)}, bf16[128,512]{1,0:T(8,128)(2,1)S(1)}, u32[]{:S(2)}, u32[]{:S(2)}) collective-permute-start(bf16[128,512]{1,0:T(8,128)(2,1)S(1)} %get-tuple-element.17), channel_id=1, source_target_pairs={{0,4},{2,6},{4,0},{6,2},{8,12},{10,14},{12,8},{14,10},{16,20},{18,... | collective-permute-start | bytes 393224 | tf_op jit(solution)/shard_map/ppermute | solution.py:266
  99.1 0.0 collective-permute-start.3
  99.1 3.0 %collective-permute-start.4 = (bf16[128,512]{1,0:T(8,128)(2,1)S(1)}, bf16[128,512]{1,0:T(8,128)(2,1)S(1)}, u32[]{:S(2)}, u32[]{:S(2)}) collective-permute-start(bf16[128,512]{1,0:T(8,128)(2,1)S(1)} %get-tuple-element.16), channel_id=1, source_target_pairs={{0,20},{2,22},{4,16},{6,18},{8,28},{10,30},{12,24},{14,26},{16,4},... | collective-permute-start | bytes 393224 | tf_op jit(solution)/shard_map/ppermute | solution.py:266
  102.1 0.6 collective-permute-done.5.refs_1_.refs_2_
  102.7 4.2 %shard_map.89 = (bf16[128,512]{1,0:T(8,128)(2,1)S(1)}, bf16[128,512]{1,0:T(8,128)(2,1)S(1)}, bf16[128,512]{1,0:T(8,128)(2,1)S(1)}, bf16[128,512]{1,0:T(8,128)(2,1)S(1)}, bf16[128,512]{1,0:T(8,128)(2,1)S(1)}) custom-call(s32[1]{0:T(128)} %bitcast.chip, s32[32]{0:T(128)S(1)} %reshape.11.table, bf16[8,128,512]{2,1,0:T(8,128)(2,1)S(1)} %all-to-all-done.q_ref, ...), custom_call_target="tpu_custom_call" | custom-call | flops 2013265920 | tf_op jit(solution)/shard_map/pallas_call | solution.py:208
  106.8 2.8 %collective-permute-start.6 = (bf16[128,512]{1,0:T(8,128)(2,1)S(1)}, bf16[128,512]{1,0:T(8,128)(2,1)S(1)}, u32[]{:S(2)}, u32[]{:S(2)}) collective-permute-start(bf16[128,512]{1,0:T(8,128)(2,1)S(1)} %get-tuple-element.19), channel_id=1, source_target_pairs={{0,24},{2,26},{4,28},{6,30},{8,16},{10,18},{12,20},{14,22},{16,8},... | collective-permute-start | bytes 393224 | tf_op jit(solution)/shard_map/ppermute | solution.py:266
  109.7 1.9 %collective-permute-start.7 = (bf16[128,512]{1,0:T(8,128)(2,1)S(1)}, bf16[128,512]{1,0:T(8,128)(2,1)S(1)}, u32[]{:S(2)}, u32[]{:S(2)}) collective-permute-start(bf16[128,512]{1,0:T(8,128)(2,1)S(1)} %get-tuple-element.20), channel_id=1, source_target_pairs={{0,28},{2,30},{4,24},{6,26},{8,20},{10,22},{12,16},{14,18},{16,12}... | collective-permute-start | bytes 393224 | tf_op jit(solution)/shard_map/ppermute | solution.py:266
  111.6 0.0 collective-permute-start.8
  111.6 0.0 collective-permute-done.3.refs_0_
  111.6 2.1 %collective-permute-start.9 = (bf16[128,512]{1,0:T(8,128)(2,1)S(1)}, bf16[128,512]{1,0:T(8,128)(2,1)S(1)}, u32[]{:S(2)}, u32[]{:S(2)}) collective-permute-start(bf16[128,512]{1,0:T(8,128)(2,1)S(1)} %get-tuple-element.22), channel_id=1, source_target_pairs={{0,12},{2,14},{4,8},{6,10},{8,4},{10,6},{12,0},{14,2},{16,28},{18,... | collective-permute-start | bytes 393224 | tf_op jit(solution)/shard_map/ppermute | solution.py:266
  113.7 5.4 %collective-permute-done.4.refs_1_ = bf16[128,512]{1,0:T(8,128)(2,1)S(1)} collective-permute-done((bf16[128,512]{1,0:T(8,128)(2,1)S(1)}, bf16[128,512]{1,0:T(8,128)(2,1)S(1)}, u32[]{:S(2)}, u32[]{:S(2)}) %collective-permute-start.4) | collective-permute-done | bytes 131104 | tf_op jit(solution)/shard_map/ppermute | solution.py:266
  119.1 0.0 collective-permute-done.6.refs_3_
  119.1 0.0 collective-permute-done.7.refs_4_
  119.1 1.9 %collective-permute-done.8.refs_5_ = bf16[128,512]{1,0:T(8,128)(2,1)S(1)} collective-permute-done((bf16[128,512]{1,0:T(8,128)(2,1)S(1)}, bf16[128,512]{1,0:T(8,128)(2,1)S(1)}, u32[]{:S(2)}, u32[]{:S(2)}) %collective-permute-start.8) | collective-permute-done | bytes 131104 | tf_op jit(solution)/shard_map/ppermute | solution.py:266
  121.0 3.4 %collective-permute-done.9.refs_6_ = bf16[128,512]{1,0:T(8,128)(2,1)S(1)} collective-permute-done((bf16[128,512]{1,0:T(8,128)(2,1)S(1)}, bf16[128,512]{1,0:T(8,128)(2,1)S(1)}, u32[]{:S(2)}, u32[]{:S(2)}) %collective-permute-start.9) | collective-permute-done | bytes 131104 | tf_op jit(solution)/shard_map/ppermute | solution.py:266
  124.4 1.3 %shard_map.90 = (bf16[128,2048]{1,0:T(8,128)(2,1)}, bf16[128,2048]{1,0:T(8,128)(2,1)}) custom-call(s32[1]{0:T(128)} %bitcast.chip, bf16[128,512]{1,0:T(8,128)(2,1)S(1)} %collective-permute-done.3.refs_0_, bf16[128,512]{1,0:T(8,128)(2,1)S(1)} %collective-permute-done.4.refs_1_, bf16[128,512]{1,0:T(8,128)(2,1)S(1)} %collective-permute-done.5.refs_1_.refs_2_, ...), custom_call_target="tpu_custom_call" | custom-call | bytes 2097152 | tf_op jit(solution)/shard_map/pallas_call | solution.py:105
  (1 shorter events, 0.0 us)
Async XLA Ops:
  3.4 55.5 %all-to-all-start.1 = ((bf16[8,128,1024]{2,1,0:T(8,128)(2,1)}), bf16[8,128,1024]{2,1,0:T(8,128)(2,1)S(1)}, u32[]{:S(2)}, u32[]{:S(2)}) async-start(bf16[8,128,1024]{2,1,0:T(8,128)(2,1)} %shard_map.86.refs_2_), calls=%async_computation.1 | async-start | bytes 4194304 | tf_op jit(solution)/shard_map/all_to_all | solution.py:86
  14.0 70.0 %copy-start = (s32[8,4]{0,1:T(4,128)S(1)}, s32[8,4]{0,1:T(4,128)}, u32[]{:S(2)}) copy-start(s32[8,4]{0,1:T(4,128)} %param.13) | copy-start | bytes 388
  59.9 24.1 %collective-permute-start = (bf16[4,128,1024]{2,1,0:T(8,128)(2,1)}, bf16[4,128,1024]{2,1,0:T(8,128)(2,1)}, u32[]{:S(2)}, u32[]{:S(2)}) collective-permute-start(bf16[4,128,1024]{2,1,0:T(8,128)(2,1)} %constant_dynamic-slice_fusion), channel_id=1, source_target_pairs={{0,1},{1,0},{2,3},{3,2},{4,5},{5,4},{6,7},{7,6},{8,9},{9,8},{10,11... | collective-permute-start | bytes 3145736 | tf_op jit(solution)/shard_map/ppermute | solution.py:255
  61.5 30.2 %collective-permute-start.1 = (bf16[8,128,1024]{2,1,0:T(8,128)(2,1)S(1)}, bf16[8,128,1024]{2,1,0:T(8,128)(2,1)}, u32[]{:S(2)}, u32[]{:S(2)}) collective-permute-start(bf16[8,128,1024]{2,1,0:T(8,128)(2,1)S(1)} %all-to-all-done.1.refs_0_), channel_id=1, source_target_pairs={{0,2},{2,0},{4,6},{6,4},{8,10},{10,8},{12,14},{14,12},{16,18},{18,... | collective-permute-start | bytes 6291464 | tf_op jit(solution)/shard_map/ppermute | solution.py:256
  61.5 30.2 %all-to-all-start = ((bf16[8,128,512]{2,1,0:T(8,128)(2,1)}), bf16[8,128,512]{2,1,0:T(8,128)(2,1)S(1)}, u32[]{:S(2)}, u32[]{:S(2)}) async-start(bf16[8,128,512]{2,1,0:T(8,128)(2,1)} %get-tuple-element.13), calls=%async_computation | async-start | bytes 2097152 | tf_op jit(solution)/shard_map/all_to_all | solution.py:86
  84.0 7.7 %collective-permute-start.2 = (bf16[4,128,1024]{2,1,0:T(8,128)(2,1)}, bf16[4,128,1024]{2,1,0:T(8,128)(2,1)}, u32[]{:S(2)}, u32[]{:S(2)}) collective-permute-start(bf16[4,128,1024]{2,1,0:T(8,128)(2,1)} %collective-permute-done.refs_1_), channel_id=1, source_target_pairs={{0,2},{2,0},{4,6},{6,4},{8,10},{10,8},{12,14},{14,12},{16,18},{18,... | collective-permute-start | bytes 3145736 | tf_op jit(solution)/shard_map/ppermute | solution.py:256
  97.6 5.0 %collective-permute-start.5 = (bf16[128,512]{1,0:T(8,128)(2,1)S(1)}, bf16[128,512]{1,0:T(8,128)(2,1)S(1)}, u32[]{:S(2)}, u32[]{:S(2)}) collective-permute-start(bf16[128,512]{1,0:T(8,128)(2,1)S(1)} %get-tuple-element.17), channel_id=1, source_target_pairs={{0,4},{2,6},{4,0},{6,2},{8,12},{10,14},{12,8},{14,10},{16,20},{18,... | collective-permute-start | bytes 393224 | tf_op jit(solution)/shard_map/ppermute | solution.py:266
  99.1 12.5 %collective-permute-start.3 = (bf16[128,512]{1,0:T(8,128)(2,1)S(1)}, bf16[128,512]{1,0:T(8,128)(2,1)S(1)}, u32[]{:S(2)}, u32[]{:S(2)}) collective-permute-start(bf16[128,512]{1,0:T(8,128)(2,1)S(1)} %get-tuple-element.15), channel_id=1, source_target_pairs={{0,16},{2,18},{4,20},{6,22},{8,24},{10,26},{12,28},{14,30},{16,0},... | collective-permute-start | bytes 393224 | tf_op jit(solution)/shard_map/ppermute | solution.py:266
  99.1 19.9 %collective-permute-start.4 = (bf16[128,512]{1,0:T(8,128)(2,1)S(1)}, bf16[128,512]{1,0:T(8,128)(2,1)S(1)}, u32[]{:S(2)}, u32[]{:S(2)}) collective-permute-start(bf16[128,512]{1,0:T(8,128)(2,1)S(1)} %get-tuple-element.16), channel_id=1, source_target_pairs={{0,20},{2,22},{4,16},{6,18},{8,28},{10,30},{12,24},{14,26},{16,4},... | collective-permute-start | bytes 393224 | tf_op jit(solution)/shard_map/ppermute | solution.py:266
  106.8 12.2 %collective-permute-start.6 = (bf16[128,512]{1,0:T(8,128)(2,1)S(1)}, bf16[128,512]{1,0:T(8,128)(2,1)S(1)}, u32[]{:S(2)}, u32[]{:S(2)}) collective-permute-start(bf16[128,512]{1,0:T(8,128)(2,1)S(1)} %get-tuple-element.19), channel_id=1, source_target_pairs={{0,24},{2,26},{4,28},{6,30},{8,16},{10,18},{12,20},{14,22},{16,8},... | collective-permute-start | bytes 393224 | tf_op jit(solution)/shard_map/ppermute | solution.py:266
  109.7 9.4 %collective-permute-start.7 = (bf16[128,512]{1,0:T(8,128)(2,1)S(1)}, bf16[128,512]{1,0:T(8,128)(2,1)S(1)}, u32[]{:S(2)}, u32[]{:S(2)}) collective-permute-start(bf16[128,512]{1,0:T(8,128)(2,1)S(1)} %get-tuple-element.20), channel_id=1, source_target_pairs={{0,28},{2,30},{4,24},{6,26},{8,20},{10,22},{12,16},{14,18},{16,12}... | collective-permute-start | bytes 393224 | tf_op jit(solution)/shard_map/ppermute | solution.py:266
  111.6 9.4 %collective-permute-start.8 = (bf16[128,512]{1,0:T(8,128)(2,1)S(1)}, bf16[128,512]{1,0:T(8,128)(2,1)S(1)}, u32[]{:S(2)}, u32[]{:S(2)}) collective-permute-start(bf16[128,512]{1,0:T(8,128)(2,1)S(1)} %get-tuple-element.21), channel_id=1, source_target_pairs={{0,8},{2,10},{4,12},{6,14},{8,0},{10,2},{12,4},{14,6},{16,24},{18,... | collective-permute-start | bytes 393224 | tf_op jit(solution)/shard_map/ppermute | solution.py:266
  111.6 12.8 %collective-permute-start.9 = (bf16[128,512]{1,0:T(8,128)(2,1)S(1)}, bf16[128,512]{1,0:T(8,128)(2,1)S(1)}, u32[]{:S(2)}, u32[]{:S(2)}) collective-permute-start(bf16[128,512]{1,0:T(8,128)(2,1)S(1)} %get-tuple-element.22), channel_id=1, source_target_pairs={{0,12},{2,14},{4,8},{6,10},{8,4},{10,6},{12,0},{14,2},{16,28},{18,... | collective-permute-start | bytes 393224 | tf_op jit(solution)/shard_map/ppermute | solution.py:266

commit v16 on v15

--- a/solution.py
+++ b/solution.py
@@ -50,8 +50,10 @@
             for h in range(PAIR):
                 source = (chip * PAIR + h) * hd
                 for a in range(count):
-                    target = (h * count + a) * hd
-                    staged[chip, :, target : target + hd] = held[a, :, source : source + hd]
+                    group, target = h * (count // 2) + a // 2, a % 2 * hd
+                    staged[chip, group, :, target : target + hd] = held[
+                        a, :, source : source + hd
+                    ]
         part = pl.ds(c * some, some)
         sends.append(pltpu.make_async_copy(staged.at[part], out.at[part], out_sems.at[c]))
         sends[-1].start()
@@ -61,8 +63,8 @@
 
 def to_chips(arrays, devices, before=(), chunks=4):
     tokens, columns = arrays[0].shape
-    count, chips = len(arrays), devices // PAIR
-    shape = (chips, tokens, count * columns // chips)
+    count, chips, hd = len(arrays), devices // PAIR, columns // devices
+    shape = (chips, PAIR * count // 2, tokens, 2 * hd)
     more = min(len(before), 1)
     return pl.pallas_call(
         functools.partial(pack_kernel, count=count, before=len(before), chunks=chunks),
@@ -113,7 +115,7 @@
 
 
 def attend_kernel(chip, table, q_ref, *refs, sources, later, places, hd):
-    tokens = q_ref.shape[1]
+    tokens = q_ref.shape[2]
     if sources:
         parts, sems, kv = refs[: PAIR * sources], refs[-1], refs[-2]
         outs = refs[PAIR * sources + later : -2]
@@ -121,12 +123,12 @@
         kv, outs = refs[0], refs[1 + later :]
     groups = []
     for g in range(2 * PAIR if sources else 0):
-        lanes, copies = pl.ds(g * 2 * hd, 2 * hd), []
+        copies = []
         for n, ref in enumerate(parts):
             core, row = n // sources, 0 if n % sources == 0 else parts[0].shape[0]
             row += max(n % sources - 1, 0) * HB
-            target = kv.at[pl.ds(row, ref.shape[0]), core, :, lanes]
-            copies.append(pltpu.make_async_copy(ref.at[:, :, lanes], target, sems.at[g, n]))
+            target = kv.at[pl.ds(row, ref.shape[0]), core, g]
+            copies.append(pltpu.make_async_copy(ref.at[:, g], target, sems.at[g, n]))
         groups.append(copies)
 
     def start(*group):
@@ -145,15 +147,14 @@
 
     def products(k, h):
         block = chip[0] ^ k
-        both = q_ref[block, :, 2 * h * hd : 2 * (h + 1) * hd]
+        both = q_ref[block, h]
         query = both[:, :hd]
         left = jnp.concatenate([jnp.zeros_like(query), query], axis=1)
         left = jnp.concatenate([left, both], axis=0)
         window = [table[block * WK + w] for w in range(WK)]
-        low = 4 * h * hd
         scores, tans = [], []
         for index in window:
-            keys = kv[index, :, :, low : low + 2 * hd].reshape(BQ, 2 * hd)
+            keys = kv[index, :, 2 * h].reshape(BQ, 2 * hd)
             product = lax.dot_general(left, keys, trans, preferred_element_type=jnp.float32)
             scores.append(product[:tokens])
             tans.append(product[tokens:])
@@ -166,10 +167,9 @@
         weighted = [p * t for p, t in zip(probs, tans)]
         total = jnp.sum(functools.reduce(jnp.add, probs), axis=1, keepdims=True)
         mean = jnp.sum(functools.reduce(jnp.add, weighted), axis=1, keepdims=True)
-        low = (4 * h + 2) * hd
         mixed = jnp.zeros((2 * tokens, 2 * hd), jnp.float32)
         for index, p, w in zip(window, probs, weighted):
-            vals = kv[index, :, :, low : low + 2 * hd].reshape(BQ, 2 * hd)
+            vals = kv[index, :, 2 * h + 1].reshape(BQ, 2 * hd)
             right = jnp.concatenate([p.astype(jnp.bfloat16), w.astype(jnp.bfloat16)], axis=0)
             mixed += jnp.dot(right, vals, preferred_element_type=jnp.float32)
         inverse = 1.0 / total
@@ -196,14 +196,14 @@
 
 
 def attend(chip, table, queries, sources, later, places):
-    _, tokens, width = queries.shape
-    hd, joins = width // (2 * PAIR), len(sources) > 1
+    _, _, tokens, pair = queries.shape
+    hd, joins, width = pair // 2, len(sources) > 1, PAIR * pair
     elements = len(places) * BQ * WK * BQ
     outs = [jax.ShapeDtypeStruct((tokens, width), jnp.bfloat16)] * len(places)
     scratch, total = [], 0
     if joins:
         total = sum(a.shape[0] for a in sources) // PAIR
-        outs.append(jax.ShapeDtypeStruct((total, PAIR, tokens, 2 * width), jnp.bfloat16))
+        outs.append(jax.ShapeDtypeStruct((total, PAIR, 2 * PAIR, tokens, pair), jnp.bfloat16))
         scratch.append(pltpu.SemaphoreType.DMA((2 * PAIR, len(sources))))
     return pl.pallas_call(
         functools.partial(

time: 126 us -> 126 us (level)
  transfers between devices with their start and end apart: 12 -> 12, of which waited for: 7 -> 7; matrix products, arithmetic and copies ran while one was open for 0% -> 0% of each run, Pallas kernels for 5% -> 6%
where the time goes in v16:
time: 126 us
  waiting for transfers between devices  82.4 us (65%)
  starting transfers between devices  23.7 us (19%)
  Pallas kernels  16.8 us (13%)
  between operations  1.34 us (1%)
    all_to_all x2, waiting for transfers between devices, exchange(): lax.all_to_all(pieces, 'heads', split_axis=0, concat_axis=0, axis_index_g...  52.4 us
    ppermute x1, waiting for transfers between devices, per_device(): lax.ppermute(edge, 'frames', pairs + [(j, i) for i, j in pairs])  18.9 us
    ppermute x7, starting transfers between devices, per_device(): back[k] = lax.ppermute(piece, 'heads', pairs) if k else piece  11.3 us
    ppermute x7, waiting for transfers between devices, per_device(): back[k] = lax.ppermute(piece, 'heads', pairs) if k else piece  11.1 us
    all_to_all x2, starting transfers between devices, exchange(): lax.all_to_all(pieces, 'heads', split_axis=0, concat_axis=0, axis_index_g...  10.9 us
    pallas_call x2, Pallas kernels, attend(): pl.pallas_call(functools.partial(attend_kernel, sources=len(sources) // P...  10.1 us
    pallas_call x2, Pallas kernels, to_chips(): pl.pallas_call(functools.partial(pack_kernel, count=count, before=len(bef...  5.43 us
  transfers between devices with their start and end apart: 12, of which 7 were waited for; matrix products, arithmetic and copies ran while one was open for 0% of the time, Pallas kernels for 6%

profile of v16, /device:TPU:0, one launch (start us, length us, event | category | flops | bytes accessed | tf_op | source)
XLA Modules:
  0.0 125.5 jit_solution(14668723492058906689)
XLA Ops:
  0.6 2.8 %shard_map.86.refs_2_ = bf16[8,4,128,256]{3,2,1,0:T(8,128)(2,1)} custom-call(bf16[128,2048]{1,0:T(8,128)(2,1)} %refs_0_.2, bf16[128,2048]{1,0:T(8,128)(2,1)} %refs_1_.2, bf16[128,2048]{1,0:T(8,128)(2,1)} %refs_2_.1, bf16[128,2048]{1,0:T(8,128)(2,1)} %refs_3_.1), custom_call_target="tpu_custom_call" | custom-call | bytes 4194304 | tf_op jit(solution)/shard_map/pallas_call | solution.py:69
  3.4 7.3 %all-to-all-start.1 = ((bf16[8,4,128,256]{3,2,1,0:T(8,128)(2,1)}), bf16[8,4,128,256]{3,2,1,0:T(8,128)(2,1)S(1)}, u32[]{:S(2)}, u32[]{:S(2)}) async-start(bf16[8,4,128,256]{3,2,1,0:T(8,128)(2,1)} %shard_map.86.refs_2_), calls=%async_computation.1 | async-start | bytes 4194304 | tf_op jit(solution)/shard_map/all_to_all | solution.py:88
  10.7 2.7 %shard_map.87 = (bf16[8,2,128,256]{3,2,1,0:T(8,128)(2,1)}, s32[1]{0:T(128)}) custom-call(bf16[128,2048]{1,0:T(8,128)(2,1)} %refs_0_.3, bf16[128,2048]{1,0:T(8,128)(2,1)} %refs_1_.3, bf16[8,4,128,256]{3,2,1,0:T(8,128)(2,1)} %shard_map.86.refs_2_), custom_call_target="tpu_custom_call" | custom-call | bytes 2097152 | tf_op jit(solution)/shard_map/pallas_call | solution.py:69
  14.0 0.0 copy-start
  14.0 44.9 %all-to-all-done.1.refs_0_ = bf16[8,4,128,256]{3,2,1,0:T(8,128)(2,1)S(1)} async-done(((bf16[8,4,128,256]{3,2,1,0:T(8,128)(2,1)}), bf16[8,4,128,256]{3,2,1,0:T(8,128)(2,1)S(1)}, u32[]{:S(2)}, u32[]{:S(2)}) %all-to-all-start.1) | async-done | bytes 2097184 | tf_op jit(solution)/shard_map/all_to_all | solution.py:88
  58.9 1.1 constant_dynamic-slice_fusion
  60.0 1.5 %collective-permute-start = (bf16[4,4,128,256]{3,2,1,0:T(8,128)(2,1)}, bf16[4,4,128,256]{3,2,1,0:T(8,128)(2,1)}, u32[]{:S(2)}, u32[]{:S(2)}) collective-permute-start(bf16[4,4,128,256]{3,2,1,0:T(8,128)(2,1)} %constant_dynamic-slice_fusion), channel_id=1, source_target_pairs={{0,1},{1,0},{2,3},{3,2},{4,5},{5,4},{6,7},{7,6},{8,9},{9,8},{10,11... | collective-permute-start | bytes 3145736 | tf_op jit(solution)/shard_map/ppermute | solution.py:255
  61.5 0.0 collective-permute-start.1
  61.5 3.6 %all-to-all-start = ((bf16[8,2,128,256]{3,2,1,0:T(8,128)(2,1)}), bf16[8,2,128,256]{3,2,1,0:T(8,128)(2,1)S(1)}, u32[]{:S(2)}, u32[]{:S(2)}) async-start(bf16[8,2,128,256]{3,2,1,0:T(8,128)(2,1)} %get-tuple-element.13), calls=%async_computation | async-start | bytes 2097152 | tf_op jit(solution)/shard_map/all_to_all | solution.py:88
  65.1 18.9 %collective-permute-done.refs_1_ = bf16[4,4,128,256]{3,2,1,0:T(8,128)(2,1)} collective-permute-done((bf16[4,4,128,256]{3,2,1,0:T(8,128)(2,1)}, bf16[4,4,128,256]{3,2,1,0:T(8,128)(2,1)}, u32[]{:S(2)}, u32[]{:S(2)}) %collective-permute-start) | collective-permute-done | bytes 1048608 | tf_op jit(solution)/shard_map/ppermute | solution.py:255
  84.0 0.0 collective-permute-start.2
  84.0 0.0 copy-done
  84.1 0.1 copy.10
  84.1 0.1 reshape.11.table
  84.2 7.5 %all-to-all-done.q_ref = bf16[8,2,128,256]{3,2,1,0:T(8,128)(2,1)S(1)} async-done(((bf16[8,2,128,256]{3,2,1,0:T(8,128)(2,1)}), bf16[8,2,128,256]{3,2,1,0:T(8,128)(2,1)S(1)}, u32[]{:S(2)}, u32[]{:S(2)}) %all-to-all-start) | async-done | bytes 1048608 | tf_op jit(solution)/shard_map/all_to_all | solution.py:88
  91.7 0.0 collective-permute-done.2.refs_3_
  91.7 0.0 collective-permute-done.1.refs_2_
  91.7 5.8 %shard_map.88 = (bf16[128,512]{1,0:T(8,128)(2,1)S(1)}, bf16[128,512]{1,0:T(8,128)(2,1)S(1)}, bf16[128,512]{1,0:T(8,128)(2,1)S(1)}, bf16[12,2,4,128,256]{4,3,2,1,0:T(8,128)(2,1)S(1)}) custom-call(s32[1]{0:T(128)} %bitcast.chip, s32[32]{0:T(128)S(1)} %reshape.11.table, bf16[8,2,128,256]{3,2,1,0:T(8,128)(2,1)S(1)} %all-to-all-done.q_ref, ...), custom_call_target="tpu_custom_call" | custom-call | flops 1207959552 | bytes 6291456 | tf_op jit(solution)/shard_map/pallas_call | solution.py:208
  97.5 1.5 %collective-permute-start.5 = (bf16[128,512]{1,0:T(8,128)(2,1)S(1)}, bf16[128,512]{1,0:T(8,128)(2,1)S(1)}, u32[]{:S(2)}, u32[]{:S(2)}) collective-permute-start(bf16[128,512]{1,0:T(8,128)(2,1)S(1)} %get-tuple-element.17), channel_id=1, source_target_pairs={{0,4},{2,6},{4,0},{6,2},{8,12},{10,14},{12,8},{14,10},{16,20},{18,... | collective-permute-start | bytes 393224 | tf_op jit(solution)/shard_map/ppermute | solution.py:266
  99.0 0.0 collective-permute-start.3
  99.0 3.0 %collective-permute-start.4 = (bf16[128,512]{1,0:T(8,128)(2,1)S(1)}, bf16[128,512]{1,0:T(8,128)(2,1)S(1)}, u32[]{:S(2)}, u32[]{:S(2)}) collective-permute-start(bf16[128,512]{1,0:T(8,128)(2,1)S(1)} %get-tuple-element.16), channel_id=1, source_target_pairs={{0,20},{2,22},{4,16},{6,18},{8,28},{10,30},{12,24},{14,26},{16,4},... | collective-permute-start | bytes 393224 | tf_op jit(solution)/shard_map/ppermute | solution.py:266
  102.0 0.6 collective-permute-done.5.refs_1_.refs_2_
  102.5 4.3 %shard_map.89 = (bf16[128,512]{1,0:T(8,128)(2,1)S(1)}, bf16[128,512]{1,0:T(8,128)(2,1)S(1)}, bf16[128,512]{1,0:T(8,128)(2,1)S(1)}, bf16[128,512]{1,0:T(8,128)(2,1)S(1)}, bf16[128,512]{1,0:T(8,128)(2,1)S(1)}) custom-call(s32[1]{0:T(128)} %bitcast.chip, s32[32]{0:T(128)S(1)} %reshape.11.table, bf16[8,2,128,256]{3,2,1,0:T(8,128)(2,1)S(1)} %all-to-all-done.q_ref, ...), custom_call_target="tpu_custom_call" | custom-call | flops 2013265920 | tf_op jit(solution)/shard_map/pallas_call | solution.py:208
  106.9 2.8 %collective-permute-start.6 = (bf16[128,512]{1,0:T(8,128)(2,1)S(1)}, bf16[128,512]{1,0:T(8,128)(2,1)S(1)}, u32[]{:S(2)}, u32[]{:S(2)}) collective-permute-start(bf16[128,512]{1,0:T(8,128)(2,1)S(1)} %get-tuple-element.19), channel_id=1, source_target_pairs={{0,24},{2,26},{4,28},{6,30},{8,16},{10,18},{12,20},{14,22},{16,8},... | collective-permute-start | bytes 393224 | tf_op jit(solution)/shard_map/ppermute | solution.py:266
  109.7 1.9 %collective-permute-start.7 = (bf16[128,512]{1,0:T(8,128)(2,1)S(1)}, bf16[128,512]{1,0:T(8,128)(2,1)S(1)}, u32[]{:S(2)}, u32[]{:S(2)}) collective-permute-start(bf16[128,512]{1,0:T(8,128)(2,1)S(1)} %get-tuple-element.20), channel_id=1, source_target_pairs={{0,28},{2,30},{4,24},{6,26},{8,20},{10,22},{12,16},{14,18},{16,12}... | collective-permute-start | bytes 393224 | tf_op jit(solution)/shard_map/ppermute | solution.py:266
  111.6 0.0 collective-permute-start.8
  111.6 0.0 collective-permute-done.3.refs_0_
  111.7 2.1 %collective-permute-start.9 = (bf16[128,512]{1,0:T(8,128)(2,1)S(1)}, bf16[128,512]{1,0:T(8,128)(2,1)S(1)}, u32[]{:S(2)}, u32[]{:S(2)}) collective-permute-start(bf16[128,512]{1,0:T(8,128)(2,1)S(1)} %get-tuple-element.22), channel_id=1, source_target_pairs={{0,12},{2,14},{4,8},{6,10},{8,4},{10,6},{12,0},{14,2},{16,28},{18,... | collective-permute-start | bytes 393224 | tf_op jit(solution)/shard_map/ppermute | solution.py:266
  113.7 5.2 %collective-permute-done.4.refs_1_ = bf16[128,512]{1,0:T(8,128)(2,1)S(1)} collective-permute-done((bf16[128,512]{1,0:T(8,128)(2,1)S(1)}, bf16[128,512]{1,0:T(8,128)(2,1)S(1)}, u32[]{:S(2)}, u32[]{:S(2)}) %collective-permute-start.4) | collective-permute-done | bytes 131104 | tf_op jit(solution)/shard_map/ppermute | solution.py:266
  118.9 0.0 collective-permute-done.6.refs_3_
  118.9 0.0 collective-permute-done.7.refs_4_
  118.9 1.9 %collective-permute-done.8.refs_5_ = bf16[128,512]{1,0:T(8,128)(2,1)S(1)} collective-permute-done((bf16[128,512]{1,0:T(8,128)(2,1)S(1)}, bf16[128,512]{1,0:T(8,128)(2,1)S(1)}, u32[]{:S(2)}, u32[]{:S(2)}) %collective-permute-start.8) | collective-permute-done | bytes 131104 | tf_op jit(solution)/shard_map/ppermute | solution.py:266
  120.9 3.4 %collective-permute-done.9.refs_6_ = bf16[128,512]{1,0:T(8,128)(2,1)S(1)} collective-permute-done((bf16[128,512]{1,0:T(8,128)(2,1)S(1)}, bf16[128,512]{1,0:T(8,128)(2,1)S(1)}, u32[]{:S(2)}, u32[]{:S(2)}) %collective-permute-start.9) | collective-permute-done | bytes 131104 | tf_op jit(solution)/shard_map/ppermute | solution.py:266
  124.3 1.3 %shard_map.90 = (bf16[128,2048]{1,0:T(8,128)(2,1)}, bf16[128,2048]{1,0:T(8,128)(2,1)}) custom-call(s32[1]{0:T(128)} %bitcast.chip, bf16[128,512]{1,0:T(8,128)(2,1)S(1)} %collective-permute-done.3.refs_0_, bf16[128,512]{1,0:T(8,128)(2,1)S(1)} %collective-permute-done.4.refs_1_, bf16[128,512]{1,0:T(8,128)(2,1)S(1)} %collective-permute-done.5.refs_1_.refs_2_, ...), custom_call_target="tpu_custom_call" | custom-call | bytes 2097152 | tf_op jit(solution)/shard_map/pallas_call | solution.py:107
  (1 shorter events, 0.0 us)
Async XLA Ops:
  3.4 55.5 %all-to-all-start.1 = ((bf16[8,4,128,256]{3,2,1,0:T(8,128)(2,1)}), bf16[8,4,128,256]{3,2,1,0:T(8,128)(2,1)S(1)}, u32[]{:S(2)}, u32[]{:S(2)}) async-start(bf16[8,4,128,256]{3,2,1,0:T(8,128)(2,1)} %shard_map.86.refs_2_), calls=%async_computation.1 | async-start | bytes 4194304 | tf_op jit(solution)/shard_map/all_to_all | solution.py:88
  14.0 70.1 %copy-start = (s32[8,4]{0,1:T(4,128)S(1)}, s32[8,4]{0,1:T(4,128)}, u32[]{:S(2)}) copy-start(s32[8,4]{0,1:T(4,128)} %param.13) | copy-start | bytes 388
  60.0 24.1 %collective-permute-start = (bf16[4,4,128,256]{3,2,1,0:T(8,128)(2,1)}, bf16[4,4,128,256]{3,2,1,0:T(8,128)(2,1)}, u32[]{:S(2)}, u32[]{:S(2)}) collective-permute-start(bf16[4,4,128,256]{3,2,1,0:T(8,128)(2,1)} %constant_dynamic-slice_fusion), channel_id=1, source_target_pairs={{0,1},{1,0},{2,3},{3,2},{4,5},{5,4},{6,7},{7,6},{8,9},{9,8},{10,11... | collective-permute-start | bytes 3145736 | tf_op jit(solution)/shard_map/ppermute | solution.py:255
  61.5 30.2 %collective-permute-start.1 = (bf16[8,4,128,256]{3,2,1,0:T(8,128)(2,1)S(1)}, bf16[8,4,128,256]{3,2,1,0:T(8,128)(2,1)}, u32[]{:S(2)}, u32[]{:S(2)}) collective-permute-start(bf16[8,4,128,256]{3,2,1,0:T(8,128)(2,1)S(1)} %all-to-all-done.1.refs_0_), channel_id=1, source_target_pairs={{0,2},{2,0},{4,6},{6,4},{8,10},{10,8},{12,14},{14,12},{16,18},{18,... | collective-permute-start | bytes 6291464 | tf_op jit(solution)/shard_map/ppermute | solution.py:256
  61.5 30.2 %all-to-all-start = ((bf16[8,2,128,256]{3,2,1,0:T(8,128)(2,1)}), bf16[8,2,128,256]{3,2,1,0:T(8,128)(2,1)S(1)}, u32[]{:S(2)}, u32[]{:S(2)}) async-start(bf16[8,2,128,256]{3,2,1,0:T(8,128)(2,1)} %get-tuple-element.13), calls=%async_computation | async-start | bytes 2097152 | tf_op jit(solution)/shard_map/all_to_all | solution.py:88
  84.0 7.7 %collective-permute-start.2 = (bf16[4,4,128,256]{3,2,1,0:T(8,128)(2,1)}, bf16[4,4,128,256]{3,2,1,0:T(8,128)(2,1)}, u32[]{:S(2)}, u32[]{:S(2)}) collective-permute-start(bf16[4,4,128,256]{3,2,1,0:T(8,128)(2,1)} %collective-permute-done.refs_1_), channel_id=1, source_target_pairs={{0,2},{2,0},{4,6},{6,4},{8,10},{10,8},{12,14},{14,12},{16,18},{18,... | collective-permute-start | bytes 3145736 | tf_op jit(solution)/shard_map/ppermute | solution.py:256
  97.5 5.0 %collective-permute-start.5 = (bf16[128,512]{1,0:T(8,128)(2,1)S(1)}, bf16[128,512]{1,0:T(8,128)(2,1)S(1)}, u32[]{:S(2)}, u32[]{:S(2)}) collective-permute-start(bf16[128,512]{1,0:T(8,128)(2,1)S(1)} %get-tuple-element.17), channel_id=1, source_target_pairs={{0,4},{2,6},{4,0},{6,2},{8,12},{10,14},{12,8},{14,10},{16,20},{18,... | collective-permute-start | bytes 393224 | tf_op jit(solution)/shard_map/ppermute | solution.py:266
  99.0 12.7 %collective-permute-start.3 = (bf16[128,512]{1,0:T(8,128)(2,1)S(1)}, bf16[128,512]{1,0:T(8,128)(2,1)S(1)}, u32[]{:S(2)}, u32[]{:S(2)}) collective-permute-start(bf16[128,512]{1,0:T(8,128)(2,1)S(1)} %get-tuple-element.15), channel_id=1, source_target_pairs={{0,16},{2,18},{4,20},{6,22},{8,24},{10,26},{12,28},{14,30},{16,0},... | collective-permute-start | bytes 393224 | tf_op jit(solution)/shard_map/ppermute | solution.py:266
  99.0 19.9 %collective-permute-start.4 = (bf16[128,512]{1,0:T(8,128)(2,1)S(1)}, bf16[128,512]{1,0:T(8,128)(2,1)S(1)}, u32[]{:S(2)}, u32[]{:S(2)}) collective-permute-start(bf16[128,512]{1,0:T(8,128)(2,1)S(1)} %get-tuple-element.16), channel_id=1, source_target_pairs={{0,20},{2,22},{4,16},{6,18},{8,28},{10,30},{12,24},{14,26},{16,4},... | collective-permute-start | bytes 393224 | tf_op jit(solution)/shard_map/ppermute | solution.py:266
  106.9 12.0 %collective-permute-start.6 = (bf16[128,512]{1,0:T(8,128)(2,1)S(1)}, bf16[128,512]{1,0:T(8,128)(2,1)S(1)}, u32[]{:S(2)}, u32[]{:S(2)}) collective-permute-start(bf16[128,512]{1,0:T(8,128)(2,1)S(1)} %get-tuple-element.19), channel_id=1, source_target_pairs={{0,24},{2,26},{4,28},{6,30},{8,16},{10,18},{12,20},{14,22},{16,8},... | collective-permute-start | bytes 393224 | tf_op jit(solution)/shard_map/ppermute | solution.py:266
  109.7 9.2 %collective-permute-start.7 = (bf16[128,512]{1,0:T(8,128)(2,1)S(1)}, bf16[128,512]{1,0:T(8,128)(2,1)S(1)}, u32[]{:S(2)}, u32[]{:S(2)}) collective-permute-start(bf16[128,512]{1,0:T(8,128)(2,1)S(1)} %get-tuple-element.20), channel_id=1, source_target_pairs={{0,28},{2,30},{4,24},{6,26},{8,20},{10,22},{12,16},{14,18},{16,12}... | collective-permute-start | bytes 393224 | tf_op jit(solution)/shard_map/ppermute | solution.py:266
  111.6 9.2 %collective-permute-start.8 = (bf16[128,512]{1,0:T(8,128)(2,1)S(1)}, bf16[128,512]{1,0:T(8,128)(2,1)S(1)}, u32[]{:S(2)}, u32[]{:S(2)}) collective-permute-start(bf16[128,512]{1,0:T(8,128)(2,1)S(1)} %get-tuple-element.21), channel_id=1, source_target_pairs={{0,8},{2,10},{4,12},{6,14},{8,0},{10,2},{12,4},{14,6},{16,24},{18,... | collective-permute-start | bytes 393224 | tf_op jit(solution)/shard_map/ppermute | solution.py:266
  111.7 12.6 %collective-permute-start.9 = (bf16[128,512]{1,0:T(8,128)(2,1)S(1)}, bf16[128,512]{1,0:T(8,128)(2,1)S(1)}, u32[]{:S(2)}, u32[]{:S(2)}) collective-permute-start(bf16[128,512]{1,0:T(8,128)(2,1)S(1)} %get-tuple-element.22), channel_id=1, source_target_pairs={{0,12},{2,14},{4,8},{6,10},{8,4},{10,6},{12,0},{14,2},{16,28},{18,... | collective-permute-start | bytes 393224 | tf_op jit(solution)/shard_map/ppermute | solution.py:266

commit v17 on v16

--- a/solution.py
+++ b/solution.py
@@ -61,7 +61,7 @@
         send.wait()
 
 
-def to_chips(arrays, devices, before=(), chunks=4):
+def to_chips(arrays, devices, before=(), chunks=8):
     tokens, columns = arrays[0].shape
     count, chips, hd = len(arrays), devices // PAIR, columns // devices
     shape = (chips, PAIR * count // 2, tokens, 2 * hd)
@@ -181,11 +181,11 @@
         ref[:, (2 * h + 1) * hd : 2 * (h + 1) * hd] = tan.astype(jnp.bfloat16)
 
     units = [(k, h) for h in range(PAIR) for k in places]
-    start(0)
+    start(0, 1)
     wait(0)
-    start(1, 2, 3)
     ahead = products(*units[0])
     wait(1)
+    start(2, 3)
     for unit, following in zip(units, units[1:] + [None]):
         current = ahead
         if following is not None:

time: 126 us -> 126 us (level)
  no operation moved by 1% of the time
where the time goes in v17:
time: 126 us; the launch traced here: 125 us
  waiting for transfers between devices  82.4 us (65%)
  starting transfers between devices  23.7 us (19%)
  Pallas kernels  16.6 us (13%)
  between operations  1.34 us (1%)
    all_to_all x2, waiting for transfers between devices, exchange(): lax.all_to_all(pieces, 'heads', split_axis=0, concat_axis=0, axis_index_g...  52.4 us
    ppermute x1, waiting for transfers between devices, per_device(): lax.ppermute(edge, 'frames', pairs + [(j, i) for i, j in pairs])  18.9 us
    ppermute x7, starting transfers between devices, per_device(): back[k] = lax.ppermute(piece, 'heads', pairs) if k else piece  11.3 us
    ppermute x7, waiting for transfers between devices, per_device(): back[k] = lax.ppermute(piece, 'heads', pairs) if k else piece  11.1 us
    all_to_all x2, starting transfers between devices, exchange(): lax.all_to_all(pieces, 'heads', split_axis=0, concat_axis=0, axis_index_g...  10.9 us
    pallas_call x2, Pallas kernels, attend(): pl.pallas_call(functools.partial(attend_kernel, sources=len(sources) // P...  9.85 us
    pallas_call x2, Pallas kernels, to_chips(): pl.pallas_call(functools.partial(pack_kernel, count=count, before=len(bef...  5.44 us
  transfers between devices with their start and end apart: 12, of which 7 were waited for; matrix products, arithmetic and copies ran while one was open for 0% of the time, Pallas kernels for 6%

profile of v17, /device:TPU:0, one launch (start us, length us, event | category | flops | bytes accessed | tf_op | source)
XLA Modules:
  0.0 125.2 jit_solution(3257224917485529143)
XLA Ops:
  0.6 2.8 %shard_map.86.refs_2_ = bf16[8,4,128,256]{3,2,1,0:T(8,128)(2,1)} custom-call(bf16[128,2048]{1,0:T(8,128)(2,1)} %refs_0_.2, bf16[128,2048]{1,0:T(8,128)(2,1)} %refs_1_.2, bf16[128,2048]{1,0:T(8,128)(2,1)} %refs_2_.1, bf16[128,2048]{1,0:T(8,128)(2,1)} %refs_3_.1), custom_call_target="tpu_custom_call" | custom-call | bytes 4194304 | tf_op jit(solution)/shard_map/pallas_call | solution.py:69
  3.4 7.3 %all-to-all-start.1 = ((bf16[8,4,128,256]{3,2,1,0:T(8,128)(2,1)}), bf16[8,4,128,256]{3,2,1,0:T(8,128)(2,1)S(1)}, u32[]{:S(2)}, u32[]{:S(2)}) async-start(bf16[8,4,128,256]{3,2,1,0:T(8,128)(2,1)} %shard_map.86.refs_2_), calls=%async_computation.1 | async-start | bytes 4194304 | tf_op jit(solution)/shard_map/all_to_all | solution.py:88
  10.7 2.7 %shard_map.87 = (bf16[8,2,128,256]{3,2,1,0:T(8,128)(2,1)}, s32[1]{0:T(128)}) custom-call(bf16[128,2048]{1,0:T(8,128)(2,1)} %refs_0_.3, bf16[128,2048]{1,0:T(8,128)(2,1)} %refs_1_.3, bf16[8,4,128,256]{3,2,1,0:T(8,128)(2,1)} %shard_map.86.refs_2_), custom_call_target="tpu_custom_call" | custom-call | bytes 2097152 | tf_op jit(solution)/shard_map/pallas_call | solution.py:69
  14.0 0.0 copy-start
  14.0 44.9 %all-to-all-done.1.refs_0_ = bf16[8,4,128,256]{3,2,1,0:T(8,128)(2,1)S(1)} async-done(((bf16[8,4,128,256]{3,2,1,0:T(8,128)(2,1)}), bf16[8,4,128,256]{3,2,1,0:T(8,128)(2,1)S(1)}, u32[]{:S(2)}, u32[]{:S(2)}) %all-to-all-start.1) | async-done | bytes 2097184 | tf_op jit(solution)/shard_map/all_to_all | solution.py:88
  58.9 1.1 constant_dynamic-slice_fusion
  60.0 1.5 %collective-permute-start = (bf16[4,4,128,256]{3,2,1,0:T(8,128)(2,1)}, bf16[4,4,128,256]{3,2,1,0:T(8,128)(2,1)}, u32[]{:S(2)}, u32[]{:S(2)}) collective-permute-start(bf16[4,4,128,256]{3,2,1,0:T(8,128)(2,1)} %constant_dynamic-slice_fusion), channel_id=1, source_target_pairs={{0,1},{1,0},{2,3},{3,2},{4,5},{5,4},{6,7},{7,6},{8,9},{9,8},{10,11... | collective-permute-start | bytes 3145736 | tf_op jit(solution)/shard_map/ppermute | solution.py:255
  61.5 0.0 collective-permute-start.1
  61.5 3.6 %all-to-all-start = ((bf16[8,2,128,256]{3,2,1,0:T(8,128)(2,1)}), bf16[8,2,128,256]{3,2,1,0:T(8,128)(2,1)S(1)}, u32[]{:S(2)}, u32[]{:S(2)}) async-start(bf16[8,2,128,256]{3,2,1,0:T(8,128)(2,1)} %get-tuple-element.13), calls=%async_computation | async-start | bytes 2097152 | tf_op jit(solution)/shard_map/all_to_all | solution.py:88
  65.1 18.9 %collective-permute-done.refs_1_ = bf16[4,4,128,256]{3,2,1,0:T(8,128)(2,1)} collective-permute-done((bf16[4,4,128,256]{3,2,1,0:T(8,128)(2,1)}, bf16[4,4,128,256]{3,2,1,0:T(8,128)(2,1)}, u32[]{:S(2)}, u32[]{:S(2)}) %collective-permute-start) | collective-permute-done | bytes 1048608 | tf_op jit(solution)/shard_map/ppermute | solution.py:255
  84.0 0.0 collective-permute-start.2
  84.1 0.0 copy-done
  84.1 0.1 copy.10
  84.1 0.1 reshape.11.table
  84.2 7.5 %all-to-all-done.q_ref = bf16[8,2,128,256]{3,2,1,0:T(8,128)(2,1)S(1)} async-done(((bf16[8,2,128,256]{3,2,1,0:T(8,128)(2,1)}), bf16[8,2,128,256]{3,2,1,0:T(8,128)(2,1)S(1)}, u32[]{:S(2)}, u32[]{:S(2)}) %all-to-all-start) | async-done | bytes 1048608 | tf_op jit(solution)/shard_map/all_to_all | solution.py:88
  91.7 0.0 collective-permute-done.2.refs_3_
  91.7 0.0 collective-permute-done.1.refs_2_
  91.7 5.5 %shard_map.88 = (bf16[128,512]{1,0:T(8,128)(2,1)S(1)}, bf16[128,512]{1,0:T(8,128)(2,1)S(1)}, bf16[128,512]{1,0:T(8,128)(2,1)S(1)}, bf16[12,2,4,128,256]{4,3,2,1,0:T(8,128)(2,1)S(1)}) custom-call(s32[1]{0:T(128)} %bitcast.chip, s32[32]{0:T(128)S(1)} %reshape.11.table, bf16[8,2,128,256]{3,2,1,0:T(8,128)(2,1)S(1)} %all-to-all-done.q_ref, ...), custom_call_target="tpu_custom_call" | custom-call | flops 1207959552 | bytes 6291456 | tf_op jit(solution)/shard_map/pallas_call | solution.py:208
  97.2 1.5 %collective-permute-start.5 = (bf16[128,512]{1,0:T(8,128)(2,1)S(1)}, bf16[128,512]{1,0:T(8,128)(2,1)S(1)}, u32[]{:S(2)}, u32[]{:S(2)}) collective-permute-start(bf16[128,512]{1,0:T(8,128)(2,1)S(1)} %get-tuple-element.17), channel_id=1, source_target_pairs={{0,4},{2,6},{4,0},{6,2},{8,12},{10,14},{12,8},{14,10},{16,20},{18,... | collective-permute-start | bytes 393224 | tf_op jit(solution)/shard_map/ppermute | solution.py:266
  98.7 0.0 collective-permute-start.3
  98.7 3.0 %collective-permute-start.4 = (bf16[128,512]{1,0:T(8,128)(2,1)S(1)}, bf16[128,512]{1,0:T(8,128)(2,1)S(1)}, u32[]{:S(2)}, u32[]{:S(2)}) collective-permute-start(bf16[128,512]{1,0:T(8,128)(2,1)S(1)} %get-tuple-element.16), channel_id=1, source_target_pairs={{0,20},{2,22},{4,16},{6,18},{8,28},{10,30},{12,24},{14,26},{16,4},... | collective-permute-start | bytes 393224 | tf_op jit(solution)/shard_map/ppermute | solution.py:266
  101.7 0.6 collective-permute-done.5.refs_1_.refs_2_
  102.3 4.3 %shard_map.89 = (bf16[128,512]{1,0:T(8,128)(2,1)S(1)}, bf16[128,512]{1,0:T(8,128)(2,1)S(1)}, bf16[128,512]{1,0:T(8,128)(2,1)S(1)}, bf16[128,512]{1,0:T(8,128)(2,1)S(1)}, bf16[128,512]{1,0:T(8,128)(2,1)S(1)}) custom-call(s32[1]{0:T(128)} %bitcast.chip, s32[32]{0:T(128)S(1)} %reshape.11.table, bf16[8,2,128,256]{3,2,1,0:T(8,128)(2,1)S(1)} %all-to-all-done.q_ref, ...), custom_call_target="tpu_custom_call" | custom-call | flops 2013265920 | tf_op jit(solution)/shard_map/pallas_call | solution.py:208
  106.6 2.8 %collective-permute-start.6 = (bf16[128,512]{1,0:T(8,128)(2,1)S(1)}, bf16[128,512]{1,0:T(8,128)(2,1)S(1)}, u32[]{:S(2)}, u32[]{:S(2)}) collective-permute-start(bf16[128,512]{1,0:T(8,128)(2,1)S(1)} %get-tuple-element.19), channel_id=1, source_target_pairs={{0,24},{2,26},{4,28},{6,30},{8,16},{10,18},{12,20},{14,22},{16,8},... | collective-permute-start | bytes 393224 | tf_op jit(solution)/shard_map/ppermute | solution.py:266
  109.4 1.9 %collective-permute-start.7 = (bf16[128,512]{1,0:T(8,128)(2,1)S(1)}, bf16[128,512]{1,0:T(8,128)(2,1)S(1)}, u32[]{:S(2)}, u32[]{:S(2)}) collective-permute-start(bf16[128,512]{1,0:T(8,128)(2,1)S(1)} %get-tuple-element.20), channel_id=1, source_target_pairs={{0,28},{2,30},{4,24},{6,26},{8,20},{10,22},{12,16},{14,18},{16,12}... | collective-permute-start | bytes 393224 | tf_op jit(solution)/shard_map/ppermute | solution.py:266
  111.4 0.0 collective-permute-start.8
  111.4 0.0 collective-permute-done.3.refs_0_
  111.4 2.1 %collective-permute-start.9 = (bf16[128,512]{1,0:T(8,128)(2,1)S(1)}, bf16[128,512]{1,0:T(8,128)(2,1)S(1)}, u32[]{:S(2)}, u32[]{:S(2)}) collective-permute-start(bf16[128,512]{1,0:T(8,128)(2,1)S(1)} %get-tuple-element.22), channel_id=1, source_target_pairs={{0,12},{2,14},{4,8},{6,10},{8,4},{10,6},{12,0},{14,2},{16,28},{18,... | collective-permute-start | bytes 393224 | tf_op jit(solution)/shard_map/ppermute | solution.py:266
  113.4 5.2 %collective-permute-done.4.refs_1_ = bf16[128,512]{1,0:T(8,128)(2,1)S(1)} collective-permute-done((bf16[128,512]{1,0:T(8,128)(2,1)S(1)}, bf16[128,512]{1,0:T(8,128)(2,1)S(1)}, u32[]{:S(2)}, u32[]{:S(2)}) %collective-permute-start.4) | collective-permute-done | bytes 131104 | tf_op jit(solution)/shard_map/ppermute | solution.py:266
  118.7 0.0 collective-permute-done.6.refs_3_
  118.7 0.0 collective-permute-done.7.refs_4_
  118.7 1.9 %collective-permute-done.8.refs_5_ = bf16[128,512]{1,0:T(8,128)(2,1)S(1)} collective-permute-done((bf16[128,512]{1,0:T(8,128)(2,1)S(1)}, bf16[128,512]{1,0:T(8,128)(2,1)S(1)}, u32[]{:S(2)}, u32[]{:S(2)}) %collective-permute-start.8) | collective-permute-done | bytes 131104 | tf_op jit(solution)/shard_map/ppermute | solution.py:266
  120.6 3.4 %collective-permute-done.9.refs_6_ = bf16[128,512]{1,0:T(8,128)(2,1)S(1)} collective-permute-done((bf16[128,512]{1,0:T(8,128)(2,1)S(1)}, bf16[128,512]{1,0:T(8,128)(2,1)S(1)}, u32[]{:S(2)}, u32[]{:S(2)}) %collective-permute-start.9) | collective-permute-done | bytes 131104 | tf_op jit(solution)/shard_map/ppermute | solution.py:266
  124.0 1.3 %shard_map.90 = (bf16[128,2048]{1,0:T(8,128)(2,1)}, bf16[128,2048]{1,0:T(8,128)(2,1)}) custom-call(s32[1]{0:T(128)} %bitcast.chip, bf16[128,512]{1,0:T(8,128)(2,1)S(1)} %collective-permute-done.3.refs_0_, bf16[128,512]{1,0:T(8,128)(2,1)S(1)} %collective-permute-done.4.refs_1_, bf16[128,512]{1,0:T(8,128)(2,1)S(1)} %collective-permute-done.5.refs_1_.refs_2_, ...), custom_call_target="tpu_custom_call" | custom-call | bytes 2097152 | tf_op jit(solution)/shard_map/pallas_call | solution.py:107
  (1 shorter events, 0.0 us)
Async XLA Ops:
  3.4 55.5 %all-to-all-start.1 = ((bf16[8,4,128,256]{3,2,1,0:T(8,128)(2,1)}), bf16[8,4,128,256]{3,2,1,0:T(8,128)(2,1)S(1)}, u32[]{:S(2)}, u32[]{:S(2)}) async-start(bf16[8,4,128,256]{3,2,1,0:T(8,128)(2,1)} %shard_map.86.refs_2_), calls=%async_computation.1 | async-start | bytes 4194304 | tf_op jit(solution)/shard_map/all_to_all | solution.py:88
  14.0 70.0 %copy-start = (s32[8,4]{0,1:T(4,128)S(1)}, s32[8,4]{0,1:T(4,128)}, u32[]{:S(2)}) copy-start(s32[8,4]{0,1:T(4,128)} %param.13) | copy-start | bytes 388
  60.0 24.1 %collective-permute-start = (bf16[4,4,128,256]{3,2,1,0:T(8,128)(2,1)}, bf16[4,4,128,256]{3,2,1,0:T(8,128)(2,1)}, u32[]{:S(2)}, u32[]{:S(2)}) collective-permute-start(bf16[4,4,128,256]{3,2,1,0:T(8,128)(2,1)} %constant_dynamic-slice_fusion), channel_id=1, source_target_pairs={{0,1},{1,0},{2,3},{3,2},{4,5},{5,4},{6,7},{7,6},{8,9},{9,8},{10,11... | collective-permute-start | bytes 3145736 | tf_op jit(solution)/shard_map/ppermute | solution.py:255
  61.5 30.2 %collective-permute-start.1 = (bf16[8,4,128,256]{3,2,1,0:T(8,128)(2,1)S(1)}, bf16[8,4,128,256]{3,2,1,0:T(8,128)(2,1)}, u32[]{:S(2)}, u32[]{:S(2)}) collective-permute-start(bf16[8,4,128,256]{3,2,1,0:T(8,128)(2,1)S(1)} %all-to-all-done.1.refs_0_), channel_id=1, source_target_pairs={{0,2},{2,0},{4,6},{6,4},{8,10},{10,8},{12,14},{14,12},{16,18},{18,... | collective-permute-start | bytes 6291464 | tf_op jit(solution)/shard_map/ppermute | solution.py:256
  61.5 30.2 %all-to-all-start = ((bf16[8,2,128,256]{3,2,1,0:T(8,128)(2,1)}), bf16[8,2,128,256]{3,2,1,0:T(8,128)(2,1)S(1)}, u32[]{:S(2)}, u32[]{:S(2)}) async-start(bf16[8,2,128,256]{3,2,1,0:T(8,128)(2,1)} %get-tuple-element.13), calls=%async_computation | async-start | bytes 2097152 | tf_op jit(solution)/shard_map/all_to_all | solution.py:88
  84.0 7.7 %collective-permute-start.2 = (bf16[4,4,128,256]{3,2,1,0:T(8,128)(2,1)}, bf16[4,4,128,256]{3,2,1,0:T(8,128)(2,1)}, u32[]{:S(2)}, u32[]{:S(2)}) collective-permute-start(bf16[4,4,128,256]{3,2,1,0:T(8,128)(2,1)} %collective-permute-done.refs_1_), channel_id=1, source_target_pairs={{0,2},{2,0},{4,6},{6,4},{8,10},{10,8},{12,14},{14,12},{16,18},{18,... | collective-permute-start | bytes 3145736 | tf_op jit(solution)/shard_map/ppermute | solution.py:256
  97.2 5.0 %collective-permute-start.5 = (bf16[128,512]{1,0:T(8,128)(2,1)S(1)}, bf16[128,512]{1,0:T(8,128)(2,1)S(1)}, u32[]{:S(2)}, u32[]{:S(2)}) collective-permute-start(bf16[128,512]{1,0:T(8,128)(2,1)S(1)} %get-tuple-element.17), channel_id=1, source_target_pairs={{0,4},{2,6},{4,0},{6,2},{8,12},{10,14},{12,8},{14,10},{16,20},{18,... | collective-permute-start | bytes 393224 | tf_op jit(solution)/shard_map/ppermute | solution.py:266
  98.7 12.7 %collective-permute-start.3 = (bf16[128,512]{1,0:T(8,128)(2,1)S(1)}, bf16[128,512]{1,0:T(8,128)(2,1)S(1)}, u32[]{:S(2)}, u32[]{:S(2)}) collective-permute-start(bf16[128,512]{1,0:T(8,128)(2,1)S(1)} %get-tuple-element.15), channel_id=1, source_target_pairs={{0,16},{2,18},{4,20},{6,22},{8,24},{10,26},{12,28},{14,30},{16,0},... | collective-permute-start | bytes 393224 | tf_op jit(solution)/shard_map/ppermute | solution.py:266
  98.7 19.9 %collective-permute-start.4 = (bf16[128,512]{1,0:T(8,128)(2,1)S(1)}, bf16[128,512]{1,0:T(8,128)(2,1)S(1)}, u32[]{:S(2)}, u32[]{:S(2)}) collective-permute-start(bf16[128,512]{1,0:T(8,128)(2,1)S(1)} %get-tuple-element.16), channel_id=1, source_target_pairs={{0,20},{2,22},{4,16},{6,18},{8,28},{10,30},{12,24},{14,26},{16,4},... | collective-permute-start | bytes 393224 | tf_op jit(solution)/shard_map/ppermute | solution.py:266
  106.6 12.0 %collective-permute-start.6 = (bf16[128,512]{1,0:T(8,128)(2,1)S(1)}, bf16[128,512]{1,0:T(8,128)(2,1)S(1)}, u32[]{:S(2)}, u32[]{:S(2)}) collective-permute-start(bf16[128,512]{1,0:T(8,128)(2,1)S(1)} %get-tuple-element.19), channel_id=1, source_target_pairs={{0,24},{2,26},{4,28},{6,30},{8,16},{10,18},{12,20},{14,22},{16,8},... | collective-permute-start | bytes 393224 | tf_op jit(solution)/shard_map/ppermute | solution.py:266
  109.4 9.2 %collective-permute-start.7 = (bf16[128,512]{1,0:T(8,128)(2,1)S(1)}, bf16[128,512]{1,0:T(8,128)(2,1)S(1)}, u32[]{:S(2)}, u32[]{:S(2)}) collective-permute-start(bf16[128,512]{1,0:T(8,128)(2,1)S(1)} %get-tuple-element.20), channel_id=1, source_target_pairs={{0,28},{2,30},{4,24},{6,26},{8,20},{10,22},{12,16},{14,18},{16,12}... | collective-permute-start | bytes 393224 | tf_op jit(solution)/shard_map/ppermute | solution.py:266
  111.4 9.2 %collective-permute-start.8 = (bf16[128,512]{1,0:T(8,128)(2,1)S(1)}, bf16[128,512]{1,0:T(8,128)(2,1)S(1)}, u32[]{:S(2)}, u32[]{:S(2)}) collective-permute-start(bf16[128,512]{1,0:T(8,128)(2,1)S(1)} %get-tuple-element.21), channel_id=1, source_target_pairs={{0,8},{2,10},{4,12},{6,14},{8,0},{10,2},{12,4},{14,6},{16,24},{18,... | collective-permute-start | bytes 393224 | tf_op jit(solution)/shard_map/ppermute | solution.py:266
  111.4 12.6 %collective-permute-start.9 = (bf16[128,512]{1,0:T(8,128)(2,1)S(1)}, bf16[128,512]{1,0:T(8,128)(2,1)S(1)}, u32[]{:S(2)}, u32[]{:S(2)}) collective-permute-start(bf16[128,512]{1,0:T(8,128)(2,1)S(1)} %get-tuple-element.22), channel_id=1, source_target_pairs={{0,12},{2,14},{4,8},{6,10},{8,4},{10,6},{12,0},{14,2},{16,28},{18,... | collective-permute-start | bytes 393224 | tf_op jit(solution)/shard_map/ppermute | solution.py:266

commit v18 on v17

--- a/solution.py
+++ b/solution.py
@@ -12,6 +12,8 @@
 WK = 4
 HB = 4
 PAIR = 2
+STEP = 2
+LEAD = 16
 PARAMS = pltpu.CompilerParams(vmem_limit_bytes=32 * 1024 * 1024)
 ANY = pl.BlockSpec(memory_space=pl.ANY)
 HBM = pl.BlockSpec(memory_space=pltpu.HBM)
@@ -27,56 +29,53 @@
     return pl.CostEstimate(flops=0, bytes_accessed=size, transcendentals=0)
 
 
-def pack_kernel(*refs, count, before, chunks):
+def pack_kernel(*refs, count, before):
     arrays, out = refs[:count], refs[count + before]
     held, staged, sems, out_sems = refs[-4:]
     if before:
         refs[count + before + 1][0] = 0
     chips, columns = out.shape[0], held.shape[2]
-    hd, some, step = columns // chips // PAIR, chips // chunks, columns // chunks
-    copies = {}
-    for c in range(chunks):
-        lanes = pl.ds(c * step, step)
-        for a, array in enumerate(arrays):
-            copies[c, a] = pltpu.make_async_copy(
-                array.at[:, lanes], held.at[a, :, lanes], sems.at[c, a]
-            )
-            copies[c, a].start()
+    hd = columns // chips // PAIR
+    copies = [pltpu.make_async_copy(a, held.at[i], sems.at[i]) for i, a in enumerate(arrays)]
+    for copy in copies:
+        copy.start()
     sends = []
-    for c in range(chunks):
-        for a in range(count):
-            copies[c, a].wait()
-        for chip in range(c * some, (c + 1) * some):
-            for h in range(PAIR):
+    for stage in range(count // 2):
+        pair = (2 * stage, 2 * stage + 1)
+        for a in pair:
+            copies[a].wait()
+        for h in range(PAIR):
+            group = h * (count // 2) + stage
+            for chip in range(chips):
                 source = (chip * PAIR + h) * hd
-                for a in range(count):
-                    group, target = h * (count // 2) + a // 2, a % 2 * hd
-                    staged[chip, group, :, target : target + hd] = held[
+                for i, a in enumerate(pair):
+                    staged[group, chip, :, i * hd : (i + 1) * hd] = held[
                         a, :, source : source + hd
                     ]
-        part = pl.ds(c * some, some)
-        sends.append(pltpu.make_async_copy(staged.at[part], out.at[part], out_sems.at[c]))
-        sends[-1].start()
+            sends.append(
+                pltpu.make_async_copy(staged.at[group], out.at[:, group], out_sems.at[group])
+            )
+            sends[-1].start()
     for send in sends:
         send.wait()
 
 
-def to_chips(arrays, devices, before=(), chunks=8):
+def to_chips(arrays, devices, before=()):
     tokens, columns = arrays[0].shape
     count, chips, hd = len(arrays), devices // PAIR, columns // devices
     shape = (chips, PAIR * count // 2, tokens, 2 * hd)
     more = min(len(before), 1)
     return pl.pallas_call(
-        functools.partial(pack_kernel, count=count, before=len(before), chunks=chunks),
+        functools.partial(pack_kernel, count=count, before=len(before)),
         in_specs=[HBM] * (count + len(before)),
         out_specs=[HBM] + [SMEM] * more,
         out_shape=[pltpu.HBM(shape, jnp.bfloat16)]
         + [jax.ShapeDtypeStruct((1,), jnp.int32)] * more,
         scratch_shapes=[
             pltpu.VMEM((count, tokens, columns), jnp.bfloat16),
-            pltpu.VMEM(shape, jnp.bfloat16),
-            pltpu.SemaphoreType.DMA((chunks, count)),
-            pltpu.SemaphoreType.DMA((chunks,)),
+            pltpu.VMEM((shape[1], chips, tokens, 2 * hd), jnp.bfloat16),
+            pltpu.SemaphoreType.DMA((count,)),
+            pltpu.SemaphoreType.DMA((shape[1],)),
         ],
         compiler_params=PARAMS,
         cost_estimate=moves(4 * count * tokens * columns),
@@ -118,28 +117,22 @@
     tokens = q_ref.shape[2]
     if sources:
         parts, sems, kv = refs[: PAIR * sources], refs[-1], refs[-2]
-        outs = refs[PAIR * sources + later : -2]
+        outs = refs[PAIR * sources + later : -3]
     else:
         kv, outs = refs[0], refs[1 + later :]
-    groups = []
-    for g in range(2 * PAIR if sources else 0):
-        copies = []
-        for n, ref in enumerate(parts):
-            core, row = n // sources, 0 if n % sources == 0 else parts[0].shape[0]
-            row += max(n % sources - 1, 0) * HB
-            target = kv.at[pl.ds(row, ref.shape[0]), core, g]
-            copies.append(pltpu.make_async_copy(ref.at[:, g], target, sems.at[g, n]))
-        groups.append(copies)
-
-    def start(*group):
-        for g in group:
-            for copy in groups[g] if sources else []:
-                copy.start()
-
-    def wait(*group):
-        for g in group:
-            for copy in groups[g] if sources else []:
-                copy.wait()
+    copies = []
+    for n, ref in enumerate(parts if sources else ()):
+        core, row = n // sources, 0 if n % sources == 0 else parts[0].shape[0]
+        row += max(n % sources - 1, 0) * HB
+        for i in range(0, ref.shape[0], STEP):
+            target = kv.at[pl.ds(row + i, STEP), core]
+            copies.append(
+                pltpu.make_async_copy(ref.at[pl.ds(i, STEP)], target, sems.at[n, i // STEP])
+            )
+    for copy in copies:
+        copy.start()
+    for copy in copies:
+        copy.wait()
 
     scale = hd ** (-0.5)
     factor = scale * math.log2(math.e)
@@ -180,19 +173,15 @@
         ref[:, 2 * h * hd : (2 * h + 1) * hd] = out.astype(jnp.bfloat16)
         ref[:, (2 * h + 1) * hd : 2 * (h + 1) * hd] = tan.astype(jnp.bfloat16)
 
-    units = [(k, h) for h in range(PAIR) for k in places]
-    start(0, 1)
-    wait(0)
+    units = [(k, h) for k in places for h in range(PAIR)]
     ahead = products(*units[0])
-    wait(1)
-    start(2, 3)
     for unit, following in zip(units, units[1:] + [None]):
         current = ahead
         if following is not None:
-            if following[1] > unit[1]:
-                wait(2, 3)
             ahead = products(*following)
         finish(*unit, *current)
+    if sources:
+        refs[-3][...] = outs[0][:LEAD]
 
 
 def attend(chip, table, queries, sources, later, places):
@@ -203,8 +192,10 @@
     scratch, total = [], 0
     if joins:
         total = sum(a.shape[0] for a in sources) // PAIR
+        outs.append(jax.ShapeDtypeStruct((LEAD, width), jnp.bfloat16))
         outs.append(jax.ShapeDtypeStruct((total, PAIR, 2 * PAIR, tokens, pair), jnp.bfloat16))
-        scratch.append(pltpu.SemaphoreType.DMA((2 * PAIR, len(sources))))
+        most = max(a.shape[0] for a in sources)
+        scratch.append(pltpu.SemaphoreType.DMA((len(sources), most // STEP)))
     return pl.pallas_call(
         functools.partial(
             attend_kernel,
@@ -259,12 +250,14 @@
     table = locate(neighbors, frame, blocks)
     half, middle = blocks // 2, blocks // 2 + blocks // 4
     back, later, sources = {}, [], mine + other
-    for part in ([*range(half, middle), 1], [*range(middle, blocks), *range(2, half), 0]):
-        pieces = attend(chip, table, queries, sources, later, part)
+    for part in (range(half, middle), [*range(middle, blocks), *range(1, half), 0]):
+        pieces = attend(chip, table, queries, sources, later, list(part))
         for k, piece in zip(part, pieces):
             pairs = [(d, d ^ (k * PAIR)) for d in range(devices)]
             back[k] = lax.ppermute(piece, "heads", pairs) if k else piece
-        later, sources = [back[1]], pieces[len(part) :]
+        if not later:
+            later = [lax.ppermute(pieces[-2], "heads", swap)]
+            sources = pieces[-1:]
     return unpack(chip, back, 2)
 
 

time: 126 us -> 125 us (level)
  starting transfers between devices: 23.7 us -> 21.7 us
  waiting for transfers between devices: 82.4 us -> 83.7 us
    ppermute x7, starting transfers between devices: 11.3 us -> 9.2 us  [per_device(): back[k] = lax.ppermute(piece, 'heads', pairs) if k else piece]
    ppermute x7, waiting for transfers between devices: 11.1 us -> 12.6 us  [per_device(): back[k] = lax.ppermute(piece, 'heads', pairs) if k else piece]
  transfers between devices with their start and end apart: 12 -> 13, of which waited for: 7 -> 7; matrix products, arithmetic and copies ran while one was open for 0% -> 0% of each run, Pallas kernels for 6% -> 6%
where the time goes in v18:
time: 125 us
  waiting for transfers between devices  83.7 us (67%)
  starting transfers between devices  21.7 us (17%)
  Pallas kernels  16.7 us (13%)
  between operations  1.35 us (1%)
    all_to_all x2, waiting for transfers between devices, exchange(): lax.all_to_all(pieces, 'heads', split_axis=0, concat_axis=0, axis_index_g...  52.2 us
    ppermute x1, waiting for transfers between devices, per_device(): lax.ppermute(edge, 'frames', pairs + [(j, i) for i, j in pairs])  18.9 us
    ppermute x7, waiting for transfers between devices, per_device(): back[k] = lax.ppermute(piece, 'heads', pairs) if k else piece  12.6 us
    all_to_all x2, starting transfers between devices, exchange(): lax.all_to_all(pieces, 'heads', split_axis=0, concat_axis=0, axis_index_g...  10.9 us
    pallas_call x2, Pallas kernels, attend(): pl.pallas_call(functools.partial(attend_kernel, sources=len(sources) // P...  9.9 us
    ppermute x7, starting transfers between devices, per_device(): back[k] = lax.ppermute(piece, 'heads', pairs) if k else piece  9.2 us
    pallas_call x2, Pallas kernels, to_chips(): pl.pallas_call(functools.partial(pack_kernel, count=count, before=len(bef...  5.51 us
  transfers between devices with their start and end apart: 13, of which 7 were waited for; matrix products, arithmetic and copies ran while one was open for 0% of the time, Pallas kernels for 6%

profile of v18, /device:TPU:0, one launch (start us, length us, event | category | flops | bytes accessed | tf_op | source)
XLA Modules:
  0.0 124.7 jit_solution(192785632101118899)
XLA Ops:
  0.6 2.7 %shard_map.86.refs_2_ = bf16[8,4,128,256]{3,2,1,0:T(8,128)(2,1)} custom-call(bf16[128,2048]{1,0:T(8,128)(2,1)} %refs_0_.2, bf16[128,2048]{1,0:T(8,128)(2,1)} %refs_1_.2, bf16[128,2048]{1,0:T(8,128)(2,1)} %refs_2_.1, bf16[128,2048]{1,0:T(8,128)(2,1)} %refs_3_.1), custom_call_target="tpu_custom_call" | custom-call | bytes 4194304 | tf_op jit(solution)/shard_map/pallas_call | solution.py:68
  3.3 7.3 %all-to-all-start.1 = ((bf16[8,4,128,256]{3,2,1,0:T(8,128)(2,1)}), bf16[8,4,128,256]{3,2,1,0:T(8,128)(2,1)S(1)}, u32[]{:S(2)}, u32[]{:S(2)}) async-start(bf16[8,4,128,256]{3,2,1,0:T(8,128)(2,1)} %shard_map.86.refs_2_), calls=%async_computation.1 | async-start | bytes 4194304 | tf_op jit(solution)/shard_map/all_to_all | solution.py:87
  10.6 2.8 %shard_map.87 = (bf16[8,2,128,256]{3,2,1,0:T(8,128)(2,1)}, s32[1]{0:T(128)}) custom-call(bf16[128,2048]{1,0:T(8,128)(2,1)} %refs_0_.3, bf16[128,2048]{1,0:T(8,128)(2,1)} %refs_1_.3, bf16[8,4,128,256]{3,2,1,0:T(8,128)(2,1)} %shard_map.86.refs_2_), custom_call_target="tpu_custom_call" | custom-call | bytes 2097152 | tf_op jit(solution)/shard_map/pallas_call | solution.py:68
  14.1 0.0 copy-start
  14.1 44.7 %all-to-all-done.1.refs_0_ = bf16[8,4,128,256]{3,2,1,0:T(8,128)(2,1)S(1)} async-done(((bf16[8,4,128,256]{3,2,1,0:T(8,128)(2,1)}), bf16[8,4,128,256]{3,2,1,0:T(8,128)(2,1)S(1)}, u32[]{:S(2)}, u32[]{:S(2)}) %all-to-all-start.1) | async-done | bytes 2097184 | tf_op jit(solution)/shard_map/all_to_all | solution.py:87
  58.8 1.1 constant_dynamic-slice_fusion
  59.9 1.5 %collective-permute-start = (bf16[4,4,128,256]{3,2,1,0:T(8,128)(2,1)}, bf16[4,4,128,256]{3,2,1,0:T(8,128)(2,1)}, u32[]{:S(2)}, u32[]{:S(2)}) collective-permute-start(bf16[4,4,128,256]{3,2,1,0:T(8,128)(2,1)} %constant_dynamic-slice_fusion), channel_id=1, source_target_pairs={{0,1},{1,0},{2,3},{3,2},{4,5},{5,4},{6,7},{7,6},{8,9},{9,8},{10,11... | collective-permute-start | bytes 3145736 | tf_op jit(solution)/shard_map/ppermute | solution.py:246
  61.4 0.0 collective-permute-start.1
  61.4 3.6 %all-to-all-start = ((bf16[8,2,128,256]{3,2,1,0:T(8,128)(2,1)}), bf16[8,2,128,256]{3,2,1,0:T(8,128)(2,1)S(1)}, u32[]{:S(2)}, u32[]{:S(2)}) async-start(bf16[8,2,128,256]{3,2,1,0:T(8,128)(2,1)} %get-tuple-element.14), calls=%async_computation | async-start | bytes 2097152 | tf_op jit(solution)/shard_map/all_to_all | solution.py:87
  65.1 18.9 %collective-permute-done.refs_1_ = bf16[4,4,128,256]{3,2,1,0:T(8,128)(2,1)} collective-permute-done((bf16[4,4,128,256]{3,2,1,0:T(8,128)(2,1)}, bf16[4,4,128,256]{3,2,1,0:T(8,128)(2,1)}, u32[]{:S(2)}, u32[]{:S(2)}) %collective-permute-start) | collective-permute-done | bytes 1048608 | tf_op jit(solution)/shard_map/ppermute | solution.py:246
  84.0 0.0 collective-permute-start.2
  84.0 0.0 copy-done
  84.0 0.1 copy.10
  84.1 0.1 reshape.11.table
  84.2 7.5 %all-to-all-done.q_ref = bf16[8,2,128,256]{3,2,1,0:T(8,128)(2,1)S(1)} async-done(((bf16[8,2,128,256]{3,2,1,0:T(8,128)(2,1)}), bf16[8,2,128,256]{3,2,1,0:T(8,128)(2,1)S(1)}, u32[]{:S(2)}, u32[]{:S(2)}) %all-to-all-start) | async-done | bytes 1048608 | tf_op jit(solution)/shard_map/all_to_all | solution.py:87
  91.6 0.0 collective-permute-done.2.refs_3_
  91.6 0.0 collective-permute-done.1.refs_2_
  91.6 4.8 %shard_map.88 = (bf16[128,512]{1,0:T(8,128)(2,1)S(1)}, bf16[128,512]{1,0:T(8,128)(2,1)S(1)}, bf16[16,512]{1,0:T(8,128)(2,1)S(1)}, bf16[12,2,4,128,256]{4,3,2,1,0:T(8,128)(2,1)S(1)}) custom-call(s32[1]{0:T(128)} %bitcast.chip, s32[32]{0:T(128)S(1)} %reshape.11.table, bf16[8,2,128,256]{3,2,1,0:T(8,128)(2,1)S(1)} %all-to-all-done.q_ref, ...), custom_call_target="tpu_custom_call" | custom-call | flops 805306368 | bytes 6291456 | tf_op jit(solution)/shard_map/pallas_call | solution.py:199
  96.4 0.1 collective-permute-start.5
  96.5 0.1 collective-permute-start.3
  96.6 3.8 %collective-permute-start.4 = (bf16[128,512]{1,0:T(8,128)(2,1)S(1)}, bf16[128,512]{1,0:T(8,128)(2,1)S(1)}, u32[]{:S(2)}, u32[]{:S(2)}) collective-permute-start(bf16[128,512]{1,0:T(8,128)(2,1)S(1)} %get-tuple-element.17), channel_id=1, source_target_pairs={{0,20},{2,22},{4,16},{6,18},{8,28},{10,30},{12,24},{14,26},{16,4},... | collective-permute-start | bytes 393224 | tf_op jit(solution)/shard_map/ppermute | solution.py:257
  100.3 0.0 collective-permute-done.5.refs_1_
  100.3 5.1 %shard_map.89 = (bf16[128,512]{1,0:T(8,128)(2,1)S(1)}, bf16[128,512]{1,0:T(8,128)(2,1)S(1)}, bf16[128,512]{1,0:T(8,128)(2,1)S(1)}, bf16[128,512]{1,0:T(8,128)(2,...) custom-call(s32[1]{0:T(128)} %bitcast.chip, s32[32]{0:T(128)S(1)} %reshape.11.table, ...), custom_call_target="tpu_custom_call" | custom-call | flops 2415919104 | tf_op jit(solution)/shard_map/pallas_call | solution.py:199
  105.5 1.5 %collective-permute-start.6 = (bf16[128,512]{1,0:T(8,128)(2,1)S(1)}, bf16[128,512]{1,0:T(8,128)(2,1)S(1)}, u32[]{:S(2)}, u32[]{:S(2)}) collective-permute-start(bf16[128,512]{1,0:T(8,128)(2,1)S(1)} %get-tuple-element.20), channel_id=1, source_target_pairs={{0,24},{2,26},{4,28},{6,30},{8,16},{10,18},{12,20},{14,22},{16,8},... | collective-permute-start | bytes 393224 | tf_op jit(solution)/shard_map/ppermute | solution.py:257
  107.0 2.4 %collective-permute-start.7 = (bf16[128,512]{1,0:T(8,128)(2,1)S(1)}, bf16[128,512]{1,0:T(8,128)(2,1)S(1)}, u32[]{:S(2)}, u32[]{:S(2)}) collective-permute-start(bf16[128,512]{1,0:T(8,128)(2,1)S(1)} %get-tuple-element.21), channel_id=1, source_target_pairs={{0,28},{2,30},{4,24},{6,26},{8,20},{10,22},{12,16},{14,18},{16,12}... | collective-permute-start | bytes 393224 | tf_op jit(solution)/shard_map/ppermute | solution.py:257
  109.4 1.4 %collective-permute-start.8 = (bf16[128,512]{1,0:T(8,128)(2,1)S(1)}, bf16[128,512]{1,0:T(8,128)(2,1)S(1)}, u32[]{:S(2)}, u32[]{:S(2)}) collective-permute-start(bf16[128,512]{1,0:T(8,128)(2,1)S(1)} %get-tuple-element.22), channel_id=1, source_target_pairs={{0,4},{2,6},{4,0},{6,2},{8,12},{10,14},{12,8},{14,10},{16,20},{18,... | collective-permute-start | bytes 393224 | tf_op jit(solution)/shard_map/ppermute | solution.py:257
  110.8 0.0 collective-permute-done.3.refs_0_
  110.8 0.0 collective-permute-start.9
  110.8 6.4 %collective-permute-done.4.refs_1_ = bf16[128,512]{1,0:T(8,128)(2,1)S(1)} collective-permute-done((bf16[128,512]{1,0:T(8,128)(2,1)S(1)}, bf16[128,512]{1,0:T(8,128)(2,1)S(1)}, u32[]{:S(2)}, u32[]{:S(2)}) %collective-permute-start.4) | collective-permute-done | bytes 131104 | tf_op jit(solution)/shard_map/ppermute | solution.py:257
  117.2 0.0 collective-permute-start.10
  117.2 0.0 collective-permute-done.6.refs_2_
  117.2 0.0 collective-permute-done.7.refs_3_
  117.2 1.2 collective-permute-done.8.refs_4_
  118.4 1.4 %collective-permute-done.9.refs_5_ = bf16[128,512]{1,0:T(8,128)(2,1)S(1)} collective-permute-done((bf16[128,512]{1,0:T(8,128)(2,1)S(1)}, bf16[128,512]{1,0:T(8,128)(2,1)S(1)}, u32[]{:S(2)}, u32[]{:S(2)}) %collective-permute-start.9) | collective-permute-done | bytes 131104 | tf_op jit(solution)/shard_map/ppermute | solution.py:257
  119.8 3.7 %collective-permute-done.10.refs_6_ = bf16[128,512]{1,0:T(8,128)(2,1)S(1)} collective-permute-done((bf16[128,512]{1,0:T(8,128)(2,1)S(1)}, bf16[128,512]{1,0:T(8,128)(2,1)S(1)}, u32[]{:S(2)}, u32[]{:S(2)}) %collective-permute-start.10) | collective-permute-done | bytes 131104 | tf_op jit(solution)/shard_map/ppermute | solution.py:257
  123.4 1.3 %shard_map.90 = (bf16[128,2048]{1,0:T(8,128)(2,1)}, bf16[128,2048]{1,0:T(8,128)(2,1)}) custom-call(s32[1]{0:T(128)} %bitcast.chip, bf16[128,512]{1,0:T(8,128)(2,1)S(1)} %collective-permute-done.3.refs_0_, bf16[128,512]{1,0:T(8,128)(2,1)S(1)} %collective-permute-done.4.refs_1_, bf16[128,512]{1,0:T(8,128)(2,1)S(1)} %collective-permute-done.6.refs_2_, ...), custom_call_target="tpu_custom_call" | custom-call | bytes 2097152 | tf_op jit(solution)/shard_map/pallas_call | solution.py:106
  (1 shorter events, 0.0 us)
Async XLA Ops:
  3.3 55.5 %all-to-all-start.1 = ((bf16[8,4,128,256]{3,2,1,0:T(8,128)(2,1)}), bf16[8,4,128,256]{3,2,1,0:T(8,128)(2,1)S(1)}, u32[]{:S(2)}, u32[]{:S(2)}) async-start(bf16[8,4,128,256]{3,2,1,0:T(8,128)(2,1)} %shard_map.86.refs_2_), calls=%async_computation.1 | async-start | bytes 4194304 | tf_op jit(solution)/shard_map/all_to_all | solution.py:87
  14.1 69.9 %copy-start = (s32[8,4]{0,1:T(4,128)S(1)}, s32[8,4]{0,1:T(4,128)}, u32[]{:S(2)}) copy-start(s32[8,4]{0,1:T(4,128)} %param.13) | copy-start | bytes 388
  59.9 24.1 %collective-permute-start = (bf16[4,4,128,256]{3,2,1,0:T(8,128)(2,1)}, bf16[4,4,128,256]{3,2,1,0:T(8,128)(2,1)}, u32[]{:S(2)}, u32[]{:S(2)}) collective-permute-start(bf16[4,4,128,256]{3,2,1,0:T(8,128)(2,1)} %constant_dynamic-slice_fusion), channel_id=1, source_target_pairs={{0,1},{1,0},{2,3},{3,2},{4,5},{5,4},{6,7},{7,6},{8,9},{9,8},{10,11... | collective-permute-start | bytes 3145736 | tf_op jit(solution)/shard_map/ppermute | solution.py:246
  61.4 30.2 %collective-permute-start.1 = (bf16[8,4,128,256]{3,2,1,0:T(8,128)(2,1)S(1)}, bf16[8,4,128,256]{3,2,1,0:T(8,128)(2,1)}, u32[]{:S(2)}, u32[]{:S(2)}) collective-permute-start(bf16[8,4,128,256]{3,2,1,0:T(8,128)(2,1)S(1)} %all-to-all-done.1.refs_0_), channel_id=1, source_target_pairs={{0,2},{2,0},{4,6},{6,4},{8,10},{10,8},{12,14},{14,12},{16,18},{18,... | collective-permute-start | bytes 6291464 | tf_op jit(solution)/shard_map/ppermute | solution.py:247
  61.4 30.2 %all-to-all-start = ((bf16[8,2,128,256]{3,2,1,0:T(8,128)(2,1)}), bf16[8,2,128,256]{3,2,1,0:T(8,128)(2,1)S(1)}, u32[]{:S(2)}, u32[]{:S(2)}) async-start(bf16[8,2,128,256]{3,2,1,0:T(8,128)(2,1)} %get-tuple-element.14), calls=%async_computation | async-start | bytes 2097152 | tf_op jit(solution)/shard_map/all_to_all | solution.py:87
  84.0 7.7 %collective-permute-start.2 = (bf16[4,4,128,256]{3,2,1,0:T(8,128)(2,1)}, bf16[4,4,128,256]{3,2,1,0:T(8,128)(2,1)}, u32[]{:S(2)}, u32[]{:S(2)}) collective-permute-start(bf16[4,4,128,256]{3,2,1,0:T(8,128)(2,1)} %collective-permute-done.refs_1_), channel_id=1, source_target_pairs={{0,2},{2,0},{4,6},{6,4},{8,10},{10,8},{12,14},{14,12},{16,18},{18,... | collective-permute-start | bytes 3145736 | tf_op jit(solution)/shard_map/ppermute | solution.py:247
  96.4 3.9 %collective-permute-start.5 = (bf16[16,512]{1,0:T(8,128)(2,1)S(1)}, bf16[16,512]{1,0:T(8,128)(2,1)S(1)}, u32[]{:S(2)}, u32[]{:S(2)}) collective-permute-start(bf16[16,512]{1,0:T(8,128)(2,1)S(1)} %get-tuple-element.19), channel_id=1, source_target_pairs={{0,2},{2,0},{4,6},{6,4},{8,10},{10,8},{12,14},{14,12},{16,18},{18,... | collective-permute-start | bytes 49160 | tf_op jit(solution)/shard_map/ppermute | solution.py:259
  96.5 14.3 %collective-permute-start.3 = (bf16[128,512]{1,0:T(8,128)(2,1)S(1)}, bf16[128,512]{1,0:T(8,128)(2,1)S(1)}, u32[]{:S(2)}, u32[]{:S(2)}) collective-permute-start(bf16[128,512]{1,0:T(8,128)(2,1)S(1)} %get-tuple-element.16), channel_id=1, source_target_pairs={{0,16},{2,18},{4,20},{6,22},{8,24},{10,26},{12,28},{14,30},{16,0},... | collective-permute-start | bytes 393224 | tf_op jit(solution)/shard_map/ppermute | solution.py:257
  96.6 20.6 %collective-permute-start.4 = (bf16[128,512]{1,0:T(8,128)(2,1)S(1)}, bf16[128,512]{1,0:T(8,128)(2,1)S(1)}, u32[]{:S(2)}, u32[]{:S(2)}) collective-permute-start(bf16[128,512]{1,0:T(8,128)(2,1)S(1)} %get-tuple-element.17), channel_id=1, source_target_pairs={{0,20},{2,22},{4,16},{6,18},{8,28},{10,30},{12,24},{14,26},{16,4},... | collective-permute-start | bytes 393224 | tf_op jit(solution)/shard_map/ppermute | solution.py:257
  105.5 11.7 %collective-permute-start.6 = (bf16[128,512]{1,0:T(8,128)(2,1)S(1)}, bf16[128,512]{1,0:T(8,128)(2,1)S(1)}, u32[]{:S(2)}, u32[]{:S(2)}) collective-permute-start(bf16[128,512]{1,0:T(8,128)(2,1)S(1)} %get-tuple-element.20), channel_id=1, source_target_pairs={{0,24},{2,26},{4,28},{6,30},{8,16},{10,18},{12,20},{14,22},{16,8},... | collective-permute-start | bytes 393224 | tf_op jit(solution)/shard_map/ppermute | solution.py:257
  107.0 10.2 %collective-permute-start.7 = (bf16[128,512]{1,0:T(8,128)(2,1)S(1)}, bf16[128,512]{1,0:T(8,128)(2,1)S(1)}, u32[]{:S(2)}, u32[]{:S(2)}) collective-permute-start(bf16[128,512]{1,0:T(8,128)(2,1)S(1)} %get-tuple-element.21), channel_id=1, source_target_pairs={{0,28},{2,30},{4,24},{6,26},{8,20},{10,22},{12,16},{14,18},{16,12}... | collective-permute-start | bytes 393224 | tf_op jit(solution)/shard_map/ppermute | solution.py:257
  109.4 9.0 %collective-permute-start.8 = (bf16[128,512]{1,0:T(8,128)(2,1)S(1)}, bf16[128,512]{1,0:T(8,128)(2,1)S(1)}, u32[]{:S(2)}, u32[]{:S(2)}) collective-permute-start(bf16[128,512]{1,0:T(8,128)(2,1)S(1)} %get-tuple-element.22), channel_id=1, source_target_pairs={{0,4},{2,6},{4,0},{6,2},{8,12},{10,14},{12,8},{14,10},{16,20},{18,... | collective-permute-start | bytes 393224 | tf_op jit(solution)/shard_map/ppermute | solution.py:257
  110.8 8.9 %collective-permute-start.9 = (bf16[128,512]{1,0:T(8,128)(2,1)S(1)}, bf16[128,512]{1,0:T(8,128)(2,1)S(1)}, u32[]{:S(2)}, u32[]{:S(2)}) collective-permute-start(bf16[128,512]{1,0:T(8,128)(2,1)S(1)} %get-tuple-element.23), channel_id=1, source_target_pairs={{0,8},{2,10},{4,12},{6,14},{8,0},{10,2},{12,4},{14,6},{16,24},{18,... | collective-permute-start | bytes 393224 | tf_op jit(solution)/shard_map/ppermute | solution.py:257
  117.2 6.3 %collective-permute-start.10 = (bf16[128,512]{1,0:T(8,128)(2,1)S(1)}, bf16[128,512]{1,0:T(8,128)(2,1)S(1)}, u32[]{:S(2)}, u32[]{:S(2)}) collective-permute-start(bf16[128,512]{1,0:T(8,128)(2,1)S(1)} %get-tuple-element.24), channel_id=1, source_target_pairs={{0,12},{2,14},{4,8},{6,10},{8,4},{10,6},{12,0},{14,2},{16,28},{18,... | collective-permute-start | bytes 393224 | tf_op jit(solution)/shard_map/ppermute | solution.py:257

commit v19 on v18

--- a/solution.py
+++ b/solution.py
@@ -113,26 +113,56 @@
     )(chip, *pieces.values())
 
 
-def attend_kernel(chip, table, q_ref, *refs, sources, later, places, hd):
-    tokens = q_ref.shape[2]
-    if sources:
-        parts, sems, kv = refs[: PAIR * sources], refs[-1], refs[-2]
-        outs = refs[PAIR * sources + later : -3]
-    else:
-        kv, outs = refs[0], refs[1 + later :]
+def edge_kernel(start, kv, out, sems):
     copies = []
-    for n, ref in enumerate(parts if sources else ()):
-        core, row = n // sources, 0 if n % sources == 0 else parts[0].shape[0]
-        row += max(n % sources - 1, 0) * HB
-        for i in range(0, ref.shape[0], STEP):
-            target = kv.at[pl.ds(row + i, STEP), core]
-            copies.append(
-                pltpu.make_async_copy(ref.at[pl.ds(i, STEP)], target, sems.at[n, i // STEP])
-            )
+    for i in range(HB):
+        copies.append(pltpu.make_async_copy(kv.at[start[0] + i], out.at[i], sems.at[i]))
     for copy in copies:
         copy.start()
     for copy in copies:
         copy.wait()
+
+
+def edge(start, kv):
+    shape = (HB, *kv.shape[1:])
+    return pl.pallas_call(
+        edge_kernel,
+        in_specs=[SMEM, VMEM],
+        out_specs=HBM,
+        out_shape=pltpu.HBM(shape, jnp.bfloat16),
+        scratch_shapes=[pltpu.SemaphoreType.DMA((HB,))],
+        compiler_params=PARAMS,
+        cost_estimate=moves(4 * math.prod(shape)),
+    )(start, kv)
+
+
+def attend_kernel(chip, table, q_ref, *refs, sources, halos, later, places, hd):
+    tokens = q_ref.shape[2]
+    own, refs = refs[0], refs[1:]
+    blocks = own.shape[0]
+    if sources:
+        parts, sems, halo, rest = refs[:sources], refs[-1], refs[-3], refs[-2]
+        outs = refs[sources + later : -4]
+        copies, row = [], {0: 0, 1: 0}
+        for n, ref in enumerate(parts):
+            target, core = (halo, 0) if n < halos else (rest, 1)
+            for i in range(0, ref.shape[0], STEP):
+                place = target.at[pl.ds(row[core] + i, STEP)]
+                copies.append(
+                    pltpu.make_async_copy(ref.at[pl.ds(i, STEP)], place, sems.at[n, i // STEP])
+                )
+            row[core] += ref.shape[0]
+        for copy in copies:
+            copy.start()
+        for copy in copies:
+            copy.wait()
+    else:
+        halo, rest, outs = refs[0], refs[1], refs[2 + later :]
+
+    def rows(index, group):
+        here = own[jnp.minimum(index, blocks - 1), group]
+        there = halo[jnp.maximum(index - blocks, 0), group]
+        return jnp.concatenate([jnp.where(index < blocks, here, there), rest[index, group]], axis=0)
 
     scale = hd ** (-0.5)
     factor = scale * math.log2(math.e)
@@ -147,7 +177,7 @@
         window = [table[block * WK + w] for w in range(WK)]
         scores, tans = [], []
         for index in window:
-            keys = kv[index, :, 2 * h].reshape(BQ, 2 * hd)
+            keys = rows(index, 2 * h)
             product = lax.dot_general(left, keys, trans, preferred_element_type=jnp.float32)
             scores.append(product[:tokens])
             tans.append(product[tokens:])
@@ -162,7 +192,7 @@
         mean = jnp.sum(functools.reduce(jnp.add, weighted), axis=1, keepdims=True)
         mixed = jnp.zeros((2 * tokens, 2 * hd), jnp.float32)
         for index, p, w in zip(window, probs, weighted):
-            vals = kv[index, :, 2 * h + 1].reshape(BQ, 2 * hd)
+            vals = rows(index, 2 * h + 1)
             right = jnp.concatenate([p.astype(jnp.bfloat16), w.astype(jnp.bfloat16)], axis=0)
             mixed += jnp.dot(right, vals, preferred_element_type=jnp.float32)
         inverse = 1.0 / total
@@ -181,31 +211,35 @@
             ahead = products(*following)
         finish(*unit, *current)
     if sources:
-        refs[-3][...] = outs[0][:LEAD]
-
-
-def attend(chip, table, queries, sources, later, places):
+        refs[-4][...] = outs[0][:LEAD]
+
+
+def attend(chip, table, queries, own, sources, halos, later, places, first):
     _, _, tokens, pair = queries.shape
-    hd, joins, width = pair // 2, len(sources) > 1, PAIR * pair
+    hd, width = pair // 2, PAIR * pair
     elements = len(places) * BQ * WK * BQ
     outs = [jax.ShapeDtypeStruct((tokens, width), jnp.bfloat16)] * len(places)
     scratch, total = [], 0
-    if joins:
-        total = sum(a.shape[0] for a in sources) // PAIR
+    if first:
+        count = halos
+        total = sum(a.shape[0] for a in sources)
         outs.append(jax.ShapeDtypeStruct((LEAD, width), jnp.bfloat16))
-        outs.append(jax.ShapeDtypeStruct((total, PAIR, 2 * PAIR, tokens, pair), jnp.bfloat16))
+        for group in (sources[:count], sources[count:]):
+            shape = (sum(a.shape[0] for a in group), *own.shape[1:])
+            outs.append(jax.ShapeDtypeStruct(shape, jnp.bfloat16))
         most = max(a.shape[0] for a in sources)
         scratch.append(pltpu.SemaphoreType.DMA((len(sources), most // STEP)))
     return pl.pallas_call(
         functools.partial(
             attend_kernel,
-            sources=len(sources) // PAIR if joins else 0,
+            sources=len(sources) if first else 0,
+            halos=halos,
             later=len(later),
             places=places,
             hd=hd,
         ),
-        in_specs=[SMEM, SMEM, VMEM]
-        + [ANY if joins else VMEM] * len(sources)
+        in_specs=[SMEM, SMEM, VMEM, VMEM]
+        + [ANY if first else VMEM] * len(sources)
         + [ANY] * len(later),
         out_specs=[VMEM] * len(outs),
         out_shape=outs,
@@ -213,10 +247,10 @@
         compiler_params=PARAMS,
         cost_estimate=pl.CostEstimate(
             flops=12 * elements * hd,
-            bytes_accessed=8 * total * tokens * width,
+            bytes_accessed=4 * total * tokens * width,
             transcendentals=elements,
         ),
-    )(chip, table, queries, *sources, *later)
+    )(chip, table, queries, own, *sources, *later)
 
 
 def locate(neighbors, frame, blocks):
@@ -237,27 +271,27 @@
     q_sent, zero = to_chips([query, query_tan], devices, [kv_sent])
     kv = exchange(kv_sent, devices)
 
-    mine = [kv]
+    mine, rounds = [kv], []
     for first in (0, 1):
         pairs = [(i, i + 1) for i in range(first, frames - 1, 2)]
         if pairs:
-            start = jnp.where(frame % 2 == first, blocks - HB, 0) + zero[0]
-            edge = lax.dynamic_slice_in_dim(kv, start, HB, axis=0)
-            mine.append(lax.ppermute(edge, "frames", pairs + [(j, i) for i, j in pairs]))
+            rounds.append(pairs + [(j, i) for i, j in pairs])
+            start = jnp.where(frame % 2 == first, blocks - HB, 0).astype(jnp.int32) + zero
+            mine.append(lax.ppermute(edge(start, kv), "frames", rounds[-1]))
     other = [lax.ppermute(a, "heads", swap) for a in mine]
 
     queries = exchange(q_sent, devices)
     table = locate(neighbors, frame, blocks)
     half, middle = blocks // 2, blocks // 2 + blocks // 4
-    back, later, sources = {}, [], mine + other
+    back, later, sources = {}, [], mine[1:] + other
     for part in (range(half, middle), [*range(middle, blocks), *range(1, half), 0]):
-        pieces = attend(chip, table, queries, sources, later, list(part))
+        pieces = attend(chip, table, queries, kv, sources, len(rounds), later, list(part), not later)
         for k, piece in zip(part, pieces):
             pairs = [(d, d ^ (k * PAIR)) for d in range(devices)]
             back[k] = lax.ppermute(piece, "heads", pairs) if k else piece
         if not later:
-            later = [lax.ppermute(pieces[-2], "heads", swap)]
-            sources = pieces[-1:]
+            later = [lax.ppermute(pieces[-3], "heads", swap)]
+            sources = pieces[-2:]
     return unpack(chip, back, 2)
 
 

time: 125 us -> 125 us (level)
    pallas_call x2 -> x3, Pallas kernels: 9.9 us -> 10.5 us  [the longest x2 9.51 us: attend(): pl.pallas_call(functools.partial(attend_kernel, sources=len(sources) if f...]
where the time goes in v19:
time: 125 us
  waiting for transfers between devices  84 us (67%)
  starting transfers between devices  21.8 us (17%)
  Pallas kernels  17.3 us (14%)
  between operations  1.36 us (1%)
    all_to_all x2, waiting for transfers between devices, exchange(): lax.all_to_all(pieces, 'heads', split_axis=0, concat_axis=0, axis_index_g...  52.2 us
    ppermute x1, waiting for transfers between devices, per_device(): mine.append(lax.ppermute(edge(start, kv), 'frames', rounds[-1]))  18.9 us
    ppermute x7, waiting for transfers between devices, per_device(): back[k] = lax.ppermute(piece, 'heads', pairs) if k else piece  12.8 us
    all_to_all x2, starting transfers between devices, exchange(): lax.all_to_all(pieces, 'heads', split_axis=0, concat_axis=0, axis_index_g...  10.9 us
    pallas_call x2, Pallas kernels, attend(): pl.pallas_call(functools.partial(attend_kernel, sources=len(sources) if f...  9.51 us
    ppermute x7, starting transfers between devices, per_device(): back[k] = lax.ppermute(piece, 'heads', pairs) if k else piece  9.21 us
    pallas_call x2, Pallas kernels, to_chips(): pl.pallas_call(functools.partial(pack_kernel, count=count, before=len(bef...  5.51 us
  transfers between devices with their start and end apart: 13, of which 7 were waited for; matrix products, arithmetic and copies ran while one was open for 0% of the time, Pallas kernels for 6%

profile of v19, /device:TPU:0, one launch (start us, length us, event | category | flops | bytes accessed | tf_op | source)
XLA Modules:
  0.0 124.6 jit_solution(1218210698794626438)
XLA Ops:
  0.6 2.7 %shard_map.86.refs_2_ = bf16[8,4,128,256]{3,2,1,0:T(8,128)(2,1)} custom-call(bf16[128,2048]{1,0:T(8,128)(2,1)} %refs_0_.2, bf16[128,2048]{1,0:T(8,128)(2,1)} %refs_1_.2, bf16[128,2048]{1,0:T(8,128)(2,1)} %refs_2_.1, bf16[128,2048]{1,0:T(8,128)(2,1)} %refs_3_.1), custom_call_target="tpu_custom_call" | custom-call | bytes 4194304 | tf_op jit(solution)/shard_map/pallas_call | solution.py:68
  3.3 7.3 %all-to-all-start.1 = ((bf16[8,4,128,256]{3,2,1,0:T(8,128)(2,1)}), bf16[8,4,128,256]{3,2,1,0:T(8,128)(2,1)S(1)}, u32[]{:S(2)}, u32[]{:S(2)}) async-start(bf16[8,4,128,256]{3,2,1,0:T(8,128)(2,1)} %shard_map.86.refs_2_), calls=%async_computation.1 | async-start | bytes 4194304 | tf_op jit(solution)/shard_map/all_to_all | solution.py:87
  10.6 2.8 %shard_map.87 = (bf16[8,2,128,256]{3,2,1,0:T(8,128)(2,1)}, s32[1]{0:T(128)}) custom-call(bf16[128,2048]{1,0:T(8,128)(2,1)} %refs_0_.3, bf16[128,2048]{1,0:T(8,128)(2,1)} %refs_1_.3, bf16[8,4,128,256]{3,2,1,0:T(8,128)(2,1)} %shard_map.86.refs_2_), custom_call_target="tpu_custom_call" | custom-call | bytes 2097152 | tf_op jit(solution)/shard_map/pallas_call | solution.py:68
  14.1 0.0 copy-start
  14.1 44.7 %all-to-all-done.1.kv.refs_0_ = bf16[8,4,128,256]{3,2,1,0:T(8,128)(2,1)S(1)} async-done(((bf16[8,4,128,256]{3,2,1,0:T(8,128)(2,1)}), bf16[8,4,128,256]{3,2,1,0:T(8,128)(2,1)S(1)}, u32[]{:S(2)}, u32[]{:S(2)}) %all-to-all-start.1) | async-done | bytes 2097184 | tf_op jit(solution)/shard_map/all_to_all | solution.py:87
  58.8 1.0 shard_map.88
  59.8 1.6 %collective-permute-start = (bf16[4,4,128,256]{3,2,1,0:T(8,128)(2,1)}, bf16[4,4,128,256]{3,2,1,0:T(8,128)(2,1)}, u32[]{:S(2)}, u32[]{:S(2)}) collective-permute-start(bf16[4,4,128,256]{3,2,1,0:T(8,128)(2,1)} %shard_map.88), channel_id=1, source_target_pairs={{0,1},{1,0},{2,3},{3,2},{4,5},{5,4},{6,7},{7,6},{8,9},{9,8},{10,11... | collective-permute-start | bytes 3145736 | tf_op jit(solution)/shard_map/ppermute | solution.py:280
  61.4 0.0 collective-permute-start.1
  61.4 3.6 %all-to-all-start = ((bf16[8,2,128,256]{3,2,1,0:T(8,128)(2,1)}), bf16[8,2,128,256]{3,2,1,0:T(8,128)(2,1)S(1)}, u32[]{:S(2)}, u32[]{:S(2)}) async-start(bf16[8,2,128,256]{3,2,1,0:T(8,128)(2,1)} %get-tuple-element.15), calls=%async_computation | async-start | bytes 2097152 | tf_op jit(solution)/shard_map/all_to_all | solution.py:87
  65.1 18.9 %collective-permute-done.refs_1_ = bf16[4,4,128,256]{3,2,1,0:T(8,128)(2,1)} collective-permute-done((bf16[4,4,128,256]{3,2,1,0:T(8,128)(2,1)}, bf16[4,4,128,256]{3,2,1,0:T(8,128)(2,1)}, u32[]{:S(2)}, u32[]{:S(2)}) %collective-permute-start) | collective-permute-done | bytes 1048608 | tf_op jit(solution)/shard_map/ppermute | solution.py:280
  84.0 0.0 collective-permute-start.2
  84.0 0.0 copy-done
  84.0 0.1 copy.10
  84.1 0.1 reshape.11.table
  84.2 7.5 %all-to-all-done.q_ref = bf16[8,2,128,256]{3,2,1,0:T(8,128)(2,1)S(1)} async-done(((bf16[8,2,128,256]{3,2,1,0:T(8,128)(2,1)}), bf16[8,2,128,256]{3,2,1,0:T(8,128)(2,1)S(1)}, u32[]{:S(2)}, u32[]{:S(2)}) %all-to-all-start) | async-done | bytes 1048608 | tf_op jit(solution)/shard_map/all_to_all | solution.py:87
  91.6 0.0 collective-permute-done.2.refs_3_
  91.6 0.0 collective-permute-done.1.refs_2_
  91.6 4.6 %shard_map.89 = (bf16[128,512]{1,0:T(8,128)(2,1)S(1)}, bf16[128,512]{1,0:T(8,128)(2,1)S(1)}, bf16[16,512]{1,0:T(8,128)(2,1)S(1)}, bf16[4,4,128,256]{3,2,1,0:T(8,128)(2,1)S(1)}, bf16[12,4,128,256]{3,2,1,0:T(8,128)(2,1)S(1)}) custom-call(s32[1]{0:T(128)} %bitcast.chip, s32[32]{0:T(128)S(1)} %reshape.11.table, bf16[8,2,128,256]{3,2,1,0:T(8,128)(2,1)S(1)} %all-to-all-done.q_ref, ...), custom_call_target="tpu_custom_call" | custom-call | flops 805306368 | bytes 4194304 | tf_op jit(solution)/shard_map/pallas_call | solution.py:232
  96.3 0.1 collective-permute-start.5
  96.4 0.1 collective-permute-start.3
  96.4 3.8 %collective-permute-start.4 = (bf16[128,512]{1,0:T(8,128)(2,1)S(1)}, bf16[128,512]{1,0:T(8,128)(2,1)S(1)}, u32[]{:S(2)}, u32[]{:S(2)}) collective-permute-start(bf16[128,512]{1,0:T(8,128)(2,1)S(1)} %get-tuple-element.18), channel_id=1, source_target_pairs={{0,20},{2,22},{4,16},{6,18},{8,28},{10,30},{12,24},{14,26},{16,4},... | collective-permute-start | bytes 393224 | tf_op jit(solution)/shard_map/ppermute | solution.py:291
  100.2 0.0 collective-permute-done.5.refs_3_
  100.2 4.9 %shard_map.90 = (bf16[128,512]{1,0:T(8,128)(2,1)S(1)}, bf16[128,512]{1,0:T(8,128)(2,1)S(1)}, bf16[128,512]{1,0:T(8,128)(2,1)S(1)}, bf16[128,512]{1,0:T(8,128)(2,...) custom-call(s32[1]{0:T(128)} %bitcast.chip, s32[32]{0:T(128)S(1)} %reshape.11.table, ...), custom_call_target="tpu_custom_call" | custom-call | flops 2415919104 | tf_op jit(solution)/shard_map/pallas_call | solution.py:232
  105.1 1.5 %collective-permute-start.6 = (bf16[128,512]{1,0:T(8,128)(2,1)S(1)}, bf16[128,512]{1,0:T(8,128)(2,1)S(1)}, u32[]{:S(2)}, u32[]{:S(2)}) collective-permute-start(bf16[128,512]{1,0:T(8,128)(2,1)S(1)} %get-tuple-element.22), channel_id=1, source_target_pairs={{0,24},{2,26},{4,28},{6,30},{8,16},{10,18},{12,20},{14,22},{16,8},... | collective-permute-start | bytes 393224 | tf_op jit(solution)/shard_map/ppermute | solution.py:291
  106.6 2.4 %collective-permute-start.7 = (bf16[128,512]{1,0:T(8,128)(2,1)S(1)}, bf16[128,512]{1,0:T(8,128)(2,1)S(1)}, u32[]{:S(2)}, u32[]{:S(2)}) collective-permute-start(bf16[128,512]{1,0:T(8,128)(2,1)S(1)} %get-tuple-element.23), channel_id=1, source_target_pairs={{0,28},{2,30},{4,24},{6,26},{8,20},{10,22},{12,16},{14,18},{16,12}... | collective-permute-start | bytes 393224 | tf_op jit(solution)/shard_map/ppermute | solution.py:291
  109.0 1.4 %collective-permute-start.8 = (bf16[128,512]{1,0:T(8,128)(2,1)S(1)}, bf16[128,512]{1,0:T(8,128)(2,1)S(1)}, u32[]{:S(2)}, u32[]{:S(2)}) collective-permute-start(bf16[128,512]{1,0:T(8,128)(2,1)S(1)} %get-tuple-element.24), channel_id=1, source_target_pairs={{0,4},{2,6},{4,0},{6,2},{8,12},{10,14},{12,8},{14,10},{16,20},{18,... | collective-permute-start | bytes 393224 | tf_op jit(solution)/shard_map/ppermute | solution.py:291
  110.5 0.0 collective-permute-done.3.refs_0_
  110.5 0.0 collective-permute-start.9
  110.5 6.6 %collective-permute-done.4.refs_1_ = bf16[128,512]{1,0:T(8,128)(2,1)S(1)} collective-permute-done((bf16[128,512]{1,0:T(8,128)(2,1)S(1)}, bf16[128,512]{1,0:T(8,128)(2,1)S(1)}, u32[]{:S(2)}, u32[]{:S(2)}) %collective-permute-start.4) | collective-permute-done | bytes 131104 | tf_op jit(solution)/shard_map/ppermute | solution.py:291
  117.1 0.0 collective-permute-start.10
  117.1 0.0 collective-permute-done.6.refs_2_
  117.1 0.0 collective-permute-done.7.refs_3_
  117.1 1.2 collective-permute-done.8.refs_4_
  118.3 1.4 %collective-permute-done.9.refs_5_ = bf16[128,512]{1,0:T(8,128)(2,1)S(1)} collective-permute-done((bf16[128,512]{1,0:T(8,128)(2,1)S(1)}, bf16[128,512]{1,0:T(8,128)(2,1)S(1)}, u32[]{:S(2)}, u32[]{:S(2)}) %collective-permute-start.9) | collective-permute-done | bytes 131104 | tf_op jit(solution)/shard_map/ppermute | solution.py:291
  119.7 3.7 %collective-permute-done.10.refs_6_ = bf16[128,512]{1,0:T(8,128)(2,1)S(1)} collective-permute-done((bf16[128,512]{1,0:T(8,128)(2,1)S(1)}, bf16[128,512]{1,0:T(8,128)(2,1)S(1)}, u32[]{:S(2)}, u32[]{:S(2)}) %collective-permute-start.10) | collective-permute-done | bytes 131104 | tf_op jit(solution)/shard_map/ppermute | solution.py:291
  123.3 1.3 %shard_map.91 = (bf16[128,2048]{1,0:T(8,128)(2,1)}, bf16[128,2048]{1,0:T(8,128)(2,1)}) custom-call(s32[1]{0:T(128)} %bitcast.chip, bf16[128,512]{1,0:T(8,128)(2,1)S(1)} %collective-permute-done.3.refs_0_, bf16[128,512]{1,0:T(8,128)(2,1)S(1)} %collective-permute-done.4.refs_1_, bf16[128,512]{1,0:T(8,128)(2,1)S(1)} %collective-permute-done.6.refs_2_, ...), custom_call_target="tpu_custom_call" | custom-call | bytes 2097152 | tf_op jit(solution)/shard_map/pallas_call | solution.py:106
  (1 shorter events, 0.0 us)
Async XLA Ops:
  3.3 55.5 %all-to-all-start.1 = ((bf16[8,4,128,256]{3,2,1,0:T(8,128)(2,1)}), bf16[8,4,128,256]{3,2,1,0:T(8,128)(2,1)S(1)}, u32[]{:S(2)}, u32[]{:S(2)}) async-start(bf16[8,4,128,256]{3,2,1,0:T(8,128)(2,1)} %shard_map.86.refs_2_), calls=%async_computation.1 | async-start | bytes 4194304 | tf_op jit(solution)/shard_map/all_to_all | solution.py:87
  14.1 69.9 %copy-start = (s32[8,4]{0,1:T(4,128)S(1)}, s32[8,4]{0,1:T(4,128)}, u32[]{:S(2)}) copy-start(s32[8,4]{0,1:T(4,128)} %param.13) | copy-start | bytes 388
  59.8 24.1 %collective-permute-start = (bf16[4,4,128,256]{3,2,1,0:T(8,128)(2,1)}, bf16[4,4,128,256]{3,2,1,0:T(8,128)(2,1)}, u32[]{:S(2)}, u32[]{:S(2)}) collective-permute-start(bf16[4,4,128,256]{3,2,1,0:T(8,128)(2,1)} %shard_map.88), channel_id=1, source_target_pairs={{0,1},{1,0},{2,3},{3,2},{4,5},{5,4},{6,7},{7,6},{8,9},{9,8},{10,11... | collective-permute-start | bytes 3145736 | tf_op jit(solution)/shard_map/ppermute | solution.py:280
  61.4 30.2 %collective-permute-start.1 = (bf16[8,4,128,256]{3,2,1,0:T(8,128)(2,1)S(1)}, bf16[8,4,128,256]{3,2,1,0:T(8,128)(2,1)}, u32[]{:S(2)}, u32[]{:S(2)}) collective-permute-start(bf16[8,4,128,256]{3,2,1,0:T(8,128)(2,1)S(1)} %all-to-all-done.1.kv.refs_0_), channel_id=1, source_target_pairs={{0,2},{2,0},{4,6},{6,4},{8,10},{10,8},{12,14},{14,12},{16,18},{18,... | collective-permute-start | bytes 6291464 | tf_op jit(solution)/shard_map/ppermute | solution.py:281
  61.4 30.2 %all-to-all-start = ((bf16[8,2,128,256]{3,2,1,0:T(8,128)(2,1)}), bf16[8,2,128,256]{3,2,1,0:T(8,128)(2,1)S(1)}, u32[]{:S(2)}, u32[]{:S(2)}) async-start(bf16[8,2,128,256]{3,2,1,0:T(8,128)(2,1)} %get-tuple-element.15), calls=%async_computation | async-start | bytes 2097152 | tf_op jit(solution)/shard_map/all_to_all | solution.py:87
  84.0 7.7 %collective-permute-start.2 = (bf16[4,4,128,256]{3,2,1,0:T(8,128)(2,1)}, bf16[4,4,128,256]{3,2,1,0:T(8,128)(2,1)}, u32[]{:S(2)}, u32[]{:S(2)}) collective-permute-start(bf16[4,4,128,256]{3,2,1,0:T(8,128)(2,1)} %collective-permute-done.refs_1_), channel_id=1, source_target_pairs={{0,2},{2,0},{4,6},{6,4},{8,10},{10,8},{12,14},{14,12},{16,18},{18,... | collective-permute-start | bytes 3145736 | tf_op jit(solution)/shard_map/ppermute | solution.py:281
  96.3 3.9 %collective-permute-start.5 = (bf16[16,512]{1,0:T(8,128)(2,1)S(1)}, bf16[16,512]{1,0:T(8,128)(2,1)S(1)}, u32[]{:S(2)}, u32[]{:S(2)}) collective-permute-start(bf16[16,512]{1,0:T(8,128)(2,1)S(1)} %get-tuple-element.21), channel_id=1, source_target_pairs={{0,2},{2,0},{4,6},{6,4},{8,10},{10,8},{12,14},{14,12},{16,18},{18,... | collective-permute-start | bytes 49160 | tf_op jit(solution)/shard_map/ppermute | solution.py:293
  96.4 14.1 %collective-permute-start.3 = (bf16[128,512]{1,0:T(8,128)(2,1)S(1)}, bf16[128,512]{1,0:T(8,128)(2,1)S(1)}, u32[]{:S(2)}, u32[]{:S(2)}) collective-permute-start(bf16[128,512]{1,0:T(8,128)(2,1)S(1)} %get-tuple-element.17), channel_id=1, source_target_pairs={{0,16},{2,18},{4,20},{6,22},{8,24},{10,26},{12,28},{14,30},{16,0},... | collective-permute-start | bytes 393224 | tf_op jit(solution)/shard_map/ppermute | solution.py:291
  96.4 20.6 %collective-permute-start.4 = (bf16[128,512]{1,0:T(8,128)(2,1)S(1)}, bf16[128,512]{1,0:T(8,128)(2,1)S(1)}, u32[]{:S(2)}, u32[]{:S(2)}) collective-permute-start(bf16[128,512]{1,0:T(8,128)(2,1)S(1)} %get-tuple-element.18), channel_id=1, source_target_pairs={{0,20},{2,22},{4,16},{6,18},{8,28},{10,30},{12,24},{14,26},{16,4},... | collective-permute-start | bytes 393224 | tf_op jit(solution)/shard_map/ppermute | solution.py:291
  105.1 12.0 %collective-permute-start.6 = (bf16[128,512]{1,0:T(8,128)(2,1)S(1)}, bf16[128,512]{1,0:T(8,128)(2,1)S(1)}, u32[]{:S(2)}, u32[]{:S(2)}) collective-permute-start(bf16[128,512]{1,0:T(8,128)(2,1)S(1)} %get-tuple-element.22), channel_id=1, source_target_pairs={{0,24},{2,26},{4,28},{6,30},{8,16},{10,18},{12,20},{14,22},{16,8},... | collective-permute-start | bytes 393224 | tf_op jit(solution)/shard_map/ppermute | solution.py:291
  106.6 10.4 %collective-permute-start.7 = (bf16[128,512]{1,0:T(8,128)(2,1)S(1)}, bf16[128,512]{1,0:T(8,128)(2,1)S(1)}, u32[]{:S(2)}, u32[]{:S(2)}) collective-permute-start(bf16[128,512]{1,0:T(8,128)(2,1)S(1)} %get-tuple-element.23), channel_id=1, source_target_pairs={{0,28},{2,30},{4,24},{6,26},{8,20},{10,22},{12,16},{14,18},{16,12}... | collective-permute-start | bytes 393224 | tf_op jit(solution)/shard_map/ppermute | solution.py:291
  109.0 9.2 %collective-permute-start.8 = (bf16[128,512]{1,0:T(8,128)(2,1)S(1)}, bf16[128,512]{1,0:T(8,128)(2,1)S(1)}, u32[]{:S(2)}, u32[]{:S(2)}) collective-permute-start(bf16[128,512]{1,0:T(8,128)(2,1)S(1)} %get-tuple-element.24), channel_id=1, source_target_pairs={{0,4},{2,6},{4,0},{6,2},{8,12},{10,14},{12,8},{14,10},{16,20},{18,... | collective-permute-start | bytes 393224 | tf_op jit(solution)/shard_map/ppermute | solution.py:291
  110.5 9.2 %collective-permute-start.9 = (bf16[128,512]{1,0:T(8,128)(2,1)S(1)}, bf16[128,512]{1,0:T(8,128)(2,1)S(1)}, u32[]{:S(2)}, u32[]{:S(2)}) collective-permute-start(bf16[128,512]{1,0:T(8,128)(2,1)S(1)} %get-tuple-element.25), channel_id=1, source_target_pairs={{0,8},{2,10},{4,12},{6,14},{8,0},{10,2},{12,4},{14,6},{16,24},{18,... | collective-permute-start | bytes 393224 | tf_op jit(solution)/shard_map/ppermute | solution.py:291
  117.1 6.3 %collective-permute-start.10 = (bf16[128,512]{1,0:T(8,128)(2,1)S(1)}, bf16[128,512]{1,0:T(8,128)(2,1)S(1)}, u32[]{:S(2)}, u32[]{:S(2)}) collective-permute-start(bf16[128,512]{1,0:T(8,128)(2,1)S(1)} %get-tuple-element.26), channel_id=1, source_target_pairs={{0,12},{2,14},{4,8},{6,10},{8,4},{10,6},{12,0},{14,2},{16,28},{18,... | collective-permute-start | bytes 393224 | tf_op jit(solution)/shard_map/ppermute | solution.py:291

commit v20 on v19

--- a/solution.py
+++ b/solution.py
@@ -90,14 +90,17 @@
 
 
 def unpack_kernel(chip, *refs, order):
-    pieces, arrays = refs[: len(order)], refs[len(order) :]
-    hd = pieces[0].shape[1] // len(arrays) // PAIR
+    pieces, arrays, sems = refs[: len(order)], refs[len(order) : -1], refs[-1]
+    width = pieces[0].shape[1] // len(arrays)
+    copies = []
     for k, piece in zip(order, pieces):
-        for h in range(PAIR):
-            columns = pl.ds(pl.multiple_of(((chip[0] ^ k) * PAIR + h) * hd, hd), hd)
-            for a, array in enumerate(arrays):
-                source = (h * len(arrays) + a) * hd
-                array[:, columns] = piece[:, source : source + hd]
+        columns = pl.ds(pl.multiple_of((chip[0] ^ k) * width, width), width)
+        for a, array in enumerate(arrays):
+            source = piece.at[:, a * width : (a + 1) * width]
+            copies.append(pltpu.make_async_copy(source, array.at[:, columns], sems.at[k, a]))
+            copies[-1].start()
+    for copy in copies:
+        copy.wait()
 
 
 def unpack(chip, pieces, count):
@@ -106,8 +109,9 @@
     return pl.pallas_call(
         functools.partial(unpack_kernel, order=list(pieces)),
         in_specs=[SMEM] + [VMEM] * len(pieces),
-        out_specs=[VMEM] * count,
-        out_shape=[jax.ShapeDtypeStruct((tokens, columns), jnp.bfloat16)] * count,
+        out_specs=[HBM] * count,
+        out_shape=[pltpu.HBM((tokens, columns), jnp.bfloat16)] * count,
+        scratch_shapes=[pltpu.SemaphoreType.DMA((len(pieces), count))],
         compiler_params=PARAMS,
         cost_estimate=moves(4 * len(pieces) * tokens * width),
     )(chip, *pieces.values())
@@ -143,21 +147,21 @@
     if sources:
         parts, sems, halo, rest = refs[:sources], refs[-1], refs[-3], refs[-2]
         outs = refs[sources + later : -4]
-        copies, row = [], {0: 0, 1: 0}
+        copies, row = [[] for _ in range(PAIR)], {0: 0, 1: 0}
         for n, ref in enumerate(parts):
             target, core = (halo, 0) if n < halos else (rest, 1)
             for i in range(0, ref.shape[0], STEP):
-                place = target.at[pl.ds(row[core] + i, STEP)]
-                copies.append(
-                    pltpu.make_async_copy(ref.at[pl.ds(i, STEP)], place, sems.at[n, i // STEP])
-                )
+                for h in range(PAIR):
+                    half = pl.ds(2 * h, 2)
+                    place = target.at[pl.ds(row[core] + i, STEP), half]
+                    source = ref.at[pl.ds(i, STEP), half]
+                    copies[h].append(
+                        pltpu.make_async_copy(source, place, sems.at[h, n, i // STEP])
+                    )
             row[core] += ref.shape[0]
-        for copy in copies:
-            copy.start()
-        for copy in copies:
-            copy.wait()
     else:
         halo, rest, outs = refs[0], refs[1], refs[2 + later :]
+        copies = [[] for _ in range(PAIR)]
 
     def rows(index, group):
         here = own[jnp.minimum(index, blocks - 1), group]
@@ -200,14 +204,28 @@
         tan = (mixed[:tokens, hd:] + scale * mixed[tokens:, :hd]) * inverse
         tan = tan - (scale * mean * inverse) * out
         ref = outs[places.index(k)]
-        ref[:, 2 * h * hd : (2 * h + 1) * hd] = out.astype(jnp.bfloat16)
-        ref[:, (2 * h + 1) * hd : 2 * (h + 1) * hd] = tan.astype(jnp.bfloat16)
-
-    units = [(k, h) for k in places for h in range(PAIR)]
+        ref[:, h * hd : (h + 1) * hd] = out.astype(jnp.bfloat16)
+        ref[:, (PAIR + h) * hd : (PAIR + h + 1) * hd] = tan.astype(jnp.bfloat16)
+
+    def start(h):
+        for copy in copies[h]:
+            copy.start()
+
+    def wait(h):
+        for copy in copies[h]:
+            copy.wait()
+
+    units = [(k, h) for h in range(PAIR) for k in places]
+    start(0)
+    wait(0)
+    for h in range(1, PAIR):
+        start(h)
     ahead = products(*units[0])
     for unit, following in zip(units, units[1:] + [None]):
         current = ahead
         if following is not None:
+            if following[1] > unit[1]:
+                wait(following[1])
             ahead = products(*following)
         finish(*unit, *current)
     if sources:
@@ -228,7 +246,7 @@
             shape = (sum(a.shape[0] for a in group), *own.shape[1:])
             outs.append(jax.ShapeDtypeStruct(shape, jnp.bfloat16))
         most = max(a.shape[0] for a in sources)
-        scratch.append(pltpu.SemaphoreType.DMA((len(sources), most // STEP)))
+        scratch.append(pltpu.SemaphoreType.DMA((PAIR, len(sources), most // STEP)))
     return pl.pallas_call(
         functools.partial(
             attend_kernel,

time: 125 us -> 125 us (level)
  no operation moved by 1% of the time
where the time goes in v20:
time: 125 us
  waiting for transfers between devices  84 us (67%)
  starting transfers between devices  21.8 us (17%)
  Pallas kernels  17.6 us (14%)
  between operations  1.36 us (1%)
    all_to_all x2, waiting for transfers between devices, exchange(): lax.all_to_all(pieces, 'heads', split_axis=0, concat_axis=0, axis_index_g...  52.2 us
    ppermute x1, waiting for transfers between devices, per_device(): mine.append(lax.ppermute(edge(start, kv), 'frames', rounds[-1]))  18.9 us
    ppermute x7, waiting for transfers between devices, per_device(): back[k] = lax.ppermute(piece, 'heads', pairs) if k else piece  12.9 us
    all_to_all x2, starting transfers between devices, exchange(): lax.all_to_all(pieces, 'heads', split_axis=0, concat_axis=0, axis_index_g...  10.9 us
    pallas_call x2, Pallas kernels, attend(): pl.pallas_call(functools.partial(attend_kernel, sources=len(sources) if f...  9.97 us
    ppermute x7, starting transfers between devices, per_device(): back[k] = lax.ppermute(piece, 'heads', pairs) if k else piece  9.2 us
    pallas_call x2, Pallas kernels, to_chips(): pl.pallas_call(functools.partial(pack_kernel, count=count, before=len(bef...  5.51 us
  transfers between devices with their start and end apart: 13, of which 7 were waited for; matrix products, arithmetic and copies ran while one was open for 0% of the time, Pallas kernels for 6%

profile of v20, /device:TPU:0, one launch (start us, length us, event | category | flops | bytes accessed | tf_op | source)
XLA Modules:
  0.0 124.9 jit_solution(15573265967931713854)
XLA Ops:
  0.6 2.7 %shard_map.86.refs_2_ = bf16[8,4,128,256]{3,2,1,0:T(8,128)(2,1)} custom-call(bf16[128,2048]{1,0:T(8,128)(2,1)} %refs_0_.2, bf16[128,2048]{1,0:T(8,128)(2,1)} %refs_1_.2, bf16[128,2048]{1,0:T(8,128)(2,1)} %refs_2_.1, bf16[128,2048]{1,0:T(8,128)(2,1)} %refs_3_.1), custom_call_target="tpu_custom_call" | custom-call | bytes 4194304 | tf_op jit(solution)/shard_map/pallas_call | solution.py:68
  3.3 7.3 %all-to-all-start.1 = ((bf16[8,4,128,256]{3,2,1,0:T(8,128)(2,1)}), bf16[8,4,128,256]{3,2,1,0:T(8,128)(2,1)S(1)}, u32[]{:S(2)}, u32[]{:S(2)}) async-start(bf16[8,4,128,256]{3,2,1,0:T(8,128)(2,1)} %shard_map.86.refs_2_), calls=%async_computation.1 | async-start | bytes 4194304 | tf_op jit(solution)/shard_map/all_to_all | solution.py:87
  10.6 2.8 %shard_map.87 = (bf16[8,2,128,256]{3,2,1,0:T(8,128)(2,1)}, s32[1]{0:T(128)}) custom-call(bf16[128,2048]{1,0:T(8,128)(2,1)} %refs_0_.3, bf16[128,2048]{1,0:T(8,128)(2,1)} %refs_1_.3, bf16[8,4,128,256]{3,2,1,0:T(8,128)(2,1)} %shard_map.86.refs_2_), custom_call_target="tpu_custom_call" | custom-call | bytes 2097152 | tf_op jit(solution)/shard_map/pallas_call | solution.py:68
  14.1 0.0 copy-start
  14.1 44.7 %all-to-all-done.1.kv.refs_0_ = bf16[8,4,128,256]{3,2,1,0:T(8,128)(2,1)S(1)} async-done(((bf16[8,4,128,256]{3,2,1,0:T(8,128)(2,1)}), bf16[8,4,128,256]{3,2,1,0:T(8,128)(2,1)S(1)}, u32[]{:S(2)}, u32[]{:S(2)}) %all-to-all-start.1) | async-done | bytes 2097184 | tf_op jit(solution)/shard_map/all_to_all | solution.py:87
  58.8 1.0 shard_map.88
  59.8 1.6 %collective-permute-start = (bf16[4,4,128,256]{3,2,1,0:T(8,128)(2,1)}, bf16[4,4,128,256]{3,2,1,0:T(8,128)(2,1)}, u32[]{:S(2)}, u32[]{:S(2)}) collective-permute-start(bf16[4,4,128,256]{3,2,1,0:T(8,128)(2,1)} %shard_map.88), channel_id=1, source_target_pairs={{0,1},{1,0},{2,3},{3,2},{4,5},{5,4},{6,7},{7,6},{8,9},{9,8},{10,11... | collective-permute-start | bytes 3145736 | tf_op jit(solution)/shard_map/ppermute | solution.py:298
  61.4 0.0 collective-permute-start.1
  61.4 3.6 %all-to-all-start = ((bf16[8,2,128,256]{3,2,1,0:T(8,128)(2,1)}), bf16[8,2,128,256]{3,2,1,0:T(8,128)(2,1)S(1)}, u32[]{:S(2)}, u32[]{:S(2)}) async-start(bf16[8,2,128,256]{3,2,1,0:T(8,128)(2,1)} %get-tuple-element.15), calls=%async_computation | async-start | bytes 2097152 | tf_op jit(solution)/shard_map/all_to_all | solution.py:87
  65.1 18.9 %collective-permute-done.refs_1_ = bf16[4,4,128,256]{3,2,1,0:T(8,128)(2,1)} collective-permute-done((bf16[4,4,128,256]{3,2,1,0:T(8,128)(2,1)}, bf16[4,4,128,256]{3,2,1,0:T(8,128)(2,1)}, u32[]{:S(2)}, u32[]{:S(2)}) %collective-permute-start) | collective-permute-done | bytes 1048608 | tf_op jit(solution)/shard_map/ppermute | solution.py:298
  84.0 0.0 collective-permute-start.2
  84.0 0.0 copy-done
  84.0 0.1 copy.10
  84.1 0.1 reshape.11.table
  84.2 7.5 %all-to-all-done.q_ref = bf16[8,2,128,256]{3,2,1,0:T(8,128)(2,1)S(1)} async-done(((bf16[8,2,128,256]{3,2,1,0:T(8,128)(2,1)}), bf16[8,2,128,256]{3,2,1,0:T(8,128)(2,1)S(1)}, u32[]{:S(2)}, u32[]{:S(2)}) %all-to-all-start) | async-done | bytes 1048608 | tf_op jit(solution)/shard_map/all_to_all | solution.py:87
  91.6 0.0 collective-permute-done.2.refs_3_
  91.6 0.0 collective-permute-done.1.refs_2_
  91.6 5.1 %shard_map.89 = (bf16[128,512]{1,0:T(8,128)(2,1)S(1)}, bf16[128,512]{1,0:T(8,128)(2,1)S(1)}, bf16[16,512]{1,0:T(8,128)(2,1)S(1)}, bf16[4,4,128,256]{3,2,1,0:T(8,128)(2,1)S(1)}, bf16[12,4,128,256]{3,2,1,0:T(8,128)(2,1)S(1)}) custom-call(s32[1]{0:T(128)} %bitcast.chip, s32[32]{0:T(128)S(1)} %reshape.11.table, bf16[8,2,128,256]{3,2,1,0:T(8,128)(2,1)S(1)} %all-to-all-done.q_ref, ...), custom_call_target="tpu_custom_call" | custom-call | flops 805306368 | bytes 4194304 | tf_op jit(solution)/shard_map/pallas_call | solution.py:250
  96.8 0.1 collective-permute-start.5
  96.8 0.1 collective-permute-start.3
  96.9 3.8 %collective-permute-start.4 = (bf16[128,512]{1,0:T(8,128)(2,1)S(1)}, bf16[128,512]{1,0:T(8,128)(2,1)S(1)}, u32[]{:S(2)}, u32[]{:S(2)}) collective-permute-start(bf16[128,512]{1,0:T(8,128)(2,1)S(1)} %get-tuple-element.18), channel_id=1, source_target_pairs={{0,20},{2,22},{4,16},{6,18},{8,28},{10,30},{12,24},{14,26},{16,4},... | collective-permute-start | bytes 393224 | tf_op jit(solution)/shard_map/ppermute | solution.py:309
  100.7 0.0 collective-permute-done.5.refs_3_
  100.7 4.9 %shard_map.90 = (bf16[128,512]{1,0:T(8,128)(2,1)S(1)}, bf16[128,512]{1,0:T(8,128)(2,1)S(1)}, bf16[128,512]{1,0:T(8,128)(2,1)S(1)}, bf16[128,512]{1,0:T(8,128)(2,...) custom-call(s32[1]{0:T(128)} %bitcast.chip, s32[32]{0:T(128)S(1)} %reshape.11.table, ...), custom_call_target="tpu_custom_call" | custom-call | flops 2415919104 | tf_op jit(solution)/shard_map/pallas_call | solution.py:250
  105.6 1.5 %collective-permute-start.6 = (bf16[128,512]{1,0:T(8,128)(2,1)S(1)}, bf16[128,512]{1,0:T(8,128)(2,1)S(1)}, u32[]{:S(2)}, u32[]{:S(2)}) collective-permute-start(bf16[128,512]{1,0:T(8,128)(2,1)S(1)} %get-tuple-element.22), channel_id=1, source_target_pairs={{0,24},{2,26},{4,28},{6,30},{8,16},{10,18},{12,20},{14,22},{16,8},... | collective-permute-start | bytes 393224 | tf_op jit(solution)/shard_map/ppermute | solution.py:309
  107.1 2.4 %collective-permute-start.7 = (bf16[128,512]{1,0:T(8,128)(2,1)S(1)}, bf16[128,512]{1,0:T(8,128)(2,1)S(1)}, u32[]{:S(2)}, u32[]{:S(2)}) collective-permute-start(bf16[128,512]{1,0:T(8,128)(2,1)S(1)} %get-tuple-element.23), channel_id=1, source_target_pairs={{0,28},{2,30},{4,24},{6,26},{8,20},{10,22},{12,16},{14,18},{16,12}... | collective-permute-start | bytes 393224 | tf_op jit(solution)/shard_map/ppermute | solution.py:309
  109.5 1.4 %collective-permute-start.8 = (bf16[128,512]{1,0:T(8,128)(2,1)S(1)}, bf16[128,512]{1,0:T(8,128)(2,1)S(1)}, u32[]{:S(2)}, u32[]{:S(2)}) collective-permute-start(bf16[128,512]{1,0:T(8,128)(2,1)S(1)} %get-tuple-element.24), channel_id=1, source_target_pairs={{0,4},{2,6},{4,0},{6,2},{8,12},{10,14},{12,8},{14,10},{16,20},{18,... | collective-permute-start | bytes 393224 | tf_op jit(solution)/shard_map/ppermute | solution.py:309
  110.9 0.0 collective-permute-done.3.refs_0_
  110.9 0.0 collective-permute-start.9
  110.9 6.6 %collective-permute-done.4.refs_1_ = bf16[128,512]{1,0:T(8,128)(2,1)S(1)} collective-permute-done((bf16[128,512]{1,0:T(8,128)(2,1)S(1)}, bf16[128,512]{1,0:T(8,128)(2,1)S(1)}, u32[]{:S(2)}, u32[]{:S(2)}) %collective-permute-start.4) | collective-permute-done | bytes 131104 | tf_op jit(solution)/shard_map/ppermute | solution.py:309
  117.5 0.0 collective-permute-start.10
  117.5 0.0 collective-permute-done.6.refs_2_
  117.5 0.0 collective-permute-done.7.refs_3_
  117.5 1.2 collective-permute-done.8.refs_4_
  118.7 1.4 %collective-permute-done.9.refs_5_ = bf16[128,512]{1,0:T(8,128)(2,1)S(1)} collective-permute-done((bf16[128,512]{1,0:T(8,128)(2,1)S(1)}, bf16[128,512]{1,0:T(8,128)(2,1)S(1)}, u32[]{:S(2)}, u32[]{:S(2)}) %collective-permute-start.9) | collective-permute-done | bytes 131104 | tf_op jit(solution)/shard_map/ppermute | solution.py:309
  120.1 3.7 %collective-permute-done.10.refs_6_ = bf16[128,512]{1,0:T(8,128)(2,1)S(1)} collective-permute-done((bf16[128,512]{1,0:T(8,128)(2,1)S(1)}, bf16[128,512]{1,0:T(8,128)(2,1)S(1)}, u32[]{:S(2)}, u32[]{:S(2)}) %collective-permute-start.10) | collective-permute-done | bytes 131104 | tf_op jit(solution)/shard_map/ppermute | solution.py:309
  123.8 1.1 shard_map.91
  (1 shorter events, 0.0 us)
Async XLA Ops:
  3.3 55.5 %all-to-all-start.1 = ((bf16[8,4,128,256]{3,2,1,0:T(8,128)(2,1)}), bf16[8,4,128,256]{3,2,1,0:T(8,128)(2,1)S(1)}, u32[]{:S(2)}, u32[]{:S(2)}) async-start(bf16[8,4,128,256]{3,2,1,0:T(8,128)(2,1)} %shard_map.86.refs_2_), calls=%async_computation.1 | async-start | bytes 4194304 | tf_op jit(solution)/shard_map/all_to_all | solution.py:87
  14.1 69.9 %copy-start = (s32[8,4]{0,1:T(4,128)S(1)}, s32[8,4]{0,1:T(4,128)}, u32[]{:S(2)}) copy-start(s32[8,4]{0,1:T(4,128)} %param.13) | copy-start | bytes 388
  59.8 24.1 %collective-permute-start = (bf16[4,4,128,256]{3,2,1,0:T(8,128)(2,1)}, bf16[4,4,128,256]{3,2,1,0:T(8,128)(2,1)}, u32[]{:S(2)}, u32[]{:S(2)}) collective-permute-start(bf16[4,4,128,256]{3,2,1,0:T(8,128)(2,1)} %shard_map.88), channel_id=1, source_target_pairs={{0,1},{1,0},{2,3},{3,2},{4,5},{5,4},{6,7},{7,6},{8,9},{9,8},{10,11... | collective-permute-start | bytes 3145736 | tf_op jit(solution)/shard_map/ppermute | solution.py:298
  61.4 30.2 %collective-permute-start.1 = (bf16[8,4,128,256]{3,2,1,0:T(8,128)(2,1)S(1)}, bf16[8,4,128,256]{3,2,1,0:T(8,128)(2,1)}, u32[]{:S(2)}, u32[]{:S(2)}) collective-permute-start(bf16[8,4,128,256]{3,2,1,0:T(8,128)(2,1)S(1)} %all-to-all-done.1.kv.refs_0_), channel_id=1, source_target_pairs={{0,2},{2,0},{4,6},{6,4},{8,10},{10,8},{12,14},{14,12},{16,18},{18,... | collective-permute-start | bytes 6291464 | tf_op jit(solution)/shard_map/ppermute | solution.py:299
  61.4 30.2 %all-to-all-start = ((bf16[8,2,128,256]{3,2,1,0:T(8,128)(2,1)}), bf16[8,2,128,256]{3,2,1,0:T(8,128)(2,1)S(1)}, u32[]{:S(2)}, u32[]{:S(2)}) async-start(bf16[8,2,128,256]{3,2,1,0:T(8,128)(2,1)} %get-tuple-element.15), calls=%async_computation | async-start | bytes 2097152 | tf_op jit(solution)/shard_map/all_to_all | solution.py:87
  84.0 7.7 %collective-permute-start.2 = (bf16[4,4,128,256]{3,2,1,0:T(8,128)(2,1)}, bf16[4,4,128,256]{3,2,1,0:T(8,128)(2,1)}, u32[]{:S(2)}, u32[]{:S(2)}) collective-permute-start(bf16[4,4,128,256]{3,2,1,0:T(8,128)(2,1)} %collective-permute-done.refs_1_), channel_id=1, source_target_pairs={{0,2},{2,0},{4,6},{6,4},{8,10},{10,8},{12,14},{14,12},{16,18},{18,... | collective-permute-start | bytes 3145736 | tf_op jit(solution)/shard_map/ppermute | solution.py:299
  96.8 3.9 %collective-permute-start.5 = (bf16[16,512]{1,0:T(8,128)(2,1)S(1)}, bf16[16,512]{1,0:T(8,128)(2,1)S(1)}, u32[]{:S(2)}, u32[]{:S(2)}) collective-permute-start(bf16[16,512]{1,0:T(8,128)(2,1)S(1)} %get-tuple-element.21), channel_id=1, source_target_pairs={{0,2},{2,0},{4,6},{6,4},{8,10},{10,8},{12,14},{14,12},{16,18},{18,... | collective-permute-start | bytes 49160 | tf_op jit(solution)/shard_map/ppermute | solution.py:311
  96.8 14.1 %collective-permute-start.3 = (bf16[128,512]{1,0:T(8,128)(2,1)S(1)}, bf16[128,512]{1,0:T(8,128)(2,1)S(1)}, u32[]{:S(2)}, u32[]{:S(2)}) collective-permute-start(bf16[128,512]{1,0:T(8,128)(2,1)S(1)} %get-tuple-element.17), channel_id=1, source_target_pairs={{0,16},{2,18},{4,20},{6,22},{8,24},{10,26},{12,28},{14,30},{16,0},... | collective-permute-start | bytes 393224 | tf_op jit(solution)/shard_map/ppermute | solution.py:309
  96.9 20.6 %collective-permute-start.4 = (bf16[128,512]{1,0:T(8,128)(2,1)S(1)}, bf16[128,512]{1,0:T(8,128)(2,1)S(1)}, u32[]{:S(2)}, u32[]{:S(2)}) collective-permute-start(bf16[128,512]{1,0:T(8,128)(2,1)S(1)} %get-tuple-element.18), channel_id=1, source_target_pairs={{0,20},{2,22},{4,16},{6,18},{8,28},{10,30},{12,24},{14,26},{16,4},... | collective-permute-start | bytes 393224 | tf_op jit(solution)/shard_map/ppermute | solution.py:309
  105.6 12.0 %collective-permute-start.6 = (bf16[128,512]{1,0:T(8,128)(2,1)S(1)}, bf16[128,512]{1,0:T(8,128)(2,1)S(1)}, u32[]{:S(2)}, u32[]{:S(2)}) collective-permute-start(bf16[128,512]{1,0:T(8,128)(2,1)S(1)} %get-tuple-element.22), channel_id=1, source_target_pairs={{0,24},{2,26},{4,28},{6,30},{8,16},{10,18},{12,20},{14,22},{16,8},... | collective-permute-start | bytes 393224 | tf_op jit(solution)/shard_map/ppermute | solution.py:309
  107.1 10.4 %collective-permute-start.7 = (bf16[128,512]{1,0:T(8,128)(2,1)S(1)}, bf16[128,512]{1,0:T(8,128)(2,1)S(1)}, u32[]{:S(2)}, u32[]{:S(2)}) collective-permute-start(bf16[128,512]{1,0:T(8,128)(2,1)S(1)} %get-tuple-element.23), channel_id=1, source_target_pairs={{0,28},{2,30},{4,24},{6,26},{8,20},{10,22},{12,16},{14,18},{16,12}... | collective-permute-start | bytes 393224 | tf_op jit(solution)/shard_map/ppermute | solution.py:309
  109.5 9.3 %collective-permute-start.8 = (bf16[128,512]{1,0:T(8,128)(2,1)S(1)}, bf16[128,512]{1,0:T(8,128)(2,1)S(1)}, u32[]{:S(2)}, u32[]{:S(2)}) collective-permute-start(bf16[128,512]{1,0:T(8,128)(2,1)S(1)} %get-tuple-element.24), channel_id=1, source_target_pairs={{0,4},{2,6},{4,0},{6,2},{8,12},{10,14},{12,8},{14,10},{16,20},{18,... | collective-permute-start | bytes 393224 | tf_op jit(solution)/shard_map/ppermute | solution.py:309
  110.9 9.2 %collective-permute-start.9 = (bf16[128,512]{1,0:T(8,128)(2,1)S(1)}, bf16[128,512]{1,0:T(8,128)(2,1)S(1)}, u32[]{:S(2)}, u32[]{:S(2)}) collective-permute-start(bf16[128,512]{1,0:T(8,128)(2,1)S(1)} %get-tuple-element.25), channel_id=1, source_target_pairs={{0,8},{2,10},{4,12},{6,14},{8,0},{10,2},{12,4},{14,6},{16,24},{18,... | collective-permute-start | bytes 393224 | tf_op jit(solution)/shard_map/ppermute | solution.py:309
  117.5 6.3 %collective-permute-start.10 = (bf16[128,512]{1,0:T(8,128)(2,1)S(1)}, bf16[128,512]{1,0:T(8,128)(2,1)S(1)}, u32[]{:S(2)}, u32[]{:S(2)}) collective-permute-start(bf16[128,512]{1,0:T(8,128)(2,1)S(1)} %get-tuple-element.26), channel_id=1, source_target_pairs={{0,12},{2,14},{4,8},{6,10},{8,4},{10,6},{12,0},{14,2},{16,28},{18,... | collective-permute-start | bytes 393224 | tf_op jit(solution)/shard_map/ppermute | solution.py:309

commit v21 on v20

--- a/solution.py
+++ b/solution.py
@@ -12,7 +12,6 @@
 WK = 4
 HB = 4
 PAIR = 2
-STEP = 2
 LEAD = 16
 PARAMS = pltpu.CompilerParams(vmem_limit_bytes=32 * 1024 * 1024)
 ANY = pl.BlockSpec(memory_space=pl.ANY)
@@ -147,21 +146,18 @@
     if sources:
         parts, sems, halo, rest = refs[:sources], refs[-1], refs[-3], refs[-2]
         outs = refs[sources + later : -4]
-        copies, row = [[] for _ in range(PAIR)], {0: 0, 1: 0}
+        copies, row = [], {0: 0, 1: 0}
         for n, ref in enumerate(parts):
             target, core = (halo, 0) if n < halos else (rest, 1)
-            for i in range(0, ref.shape[0], STEP):
-                for h in range(PAIR):
-                    half = pl.ds(2 * h, 2)
-                    place = target.at[pl.ds(row[core] + i, STEP), half]
-                    source = ref.at[pl.ds(i, STEP), half]
-                    copies[h].append(
-                        pltpu.make_async_copy(source, place, sems.at[h, n, i // STEP])
-                    )
+            place = target.at[pl.ds(row[core], ref.shape[0])]
+            copies.append(pltpu.make_async_copy(ref, place, sems.at[n]))
             row[core] += ref.shape[0]
+        for copy in copies:
+            copy.start()
+        for copy in copies:
+            copy.wait()
     else:
         halo, rest, outs = refs[0], refs[1], refs[2 + later :]
-        copies = [[] for _ in range(PAIR)]
 
     def rows(index, group):
         here = own[jnp.minimum(index, blocks - 1), group]
@@ -207,25 +203,11 @@
         ref[:, h * hd : (h + 1) * hd] = out.astype(jnp.bfloat16)
         ref[:, (PAIR + h) * hd : (PAIR + h + 1) * hd] = tan.astype(jnp.bfloat16)
 
-    def start(h):
-        for copy in copies[h]:
-            copy.start()
-
-    def wait(h):
-        for copy in copies[h]:
-            copy.wait()
-
-    units = [(k, h) for h in range(PAIR) for k in places]
-    start(0)
-    wait(0)
-    for h in range(1, PAIR):
-        start(h)
+    units = [(k, h) for k in places for h in range(PAIR)]
     ahead = products(*units[0])
     for unit, following in zip(units, units[1:] + [None]):
         current = ahead
         if following is not None:
-            if following[1] > unit[1]:
-                wait(following[1])
             ahead = products(*following)
         finish(*unit, *current)
     if sources:
@@ -245,8 +227,7 @@
         for group in (sources[:count], sources[count:]):
             shape = (sum(a.shape[0] for a in group), *own.shape[1:])
             outs.append(jax.ShapeDtypeStruct(shape, jnp.bfloat16))
-        most = max(a.shape[0] for a in sources)
-        scratch.append(pltpu.SemaphoreType.DMA((PAIR, len(sources), most // STEP)))
+        scratch.append(pltpu.SemaphoreType.DMA((len(sources),)))
     return pl.pallas_call(
         functools.partial(
             attend_kernel,
@@ -302,14 +283,21 @@
     table = locate(neighbors, frame, blocks)
     half, middle = blocks // 2, blocks // 2 + blocks // 4
     back, later, sources = {}, [], mine[1:] + other
-    for part in (range(half, middle), [*range(middle, blocks), *range(1, half), 0]):
-        pieces = attend(chip, table, queries, kv, sources, len(rounds), later, list(part), not later)
+    calls = (
+        range(half, half + 1),
+        range(half + 1, middle + 1),
+        [*range(middle + 1, blocks), *range(1, half), 0],
+    )
+    for n, part in enumerate(calls):
+        pieces = attend(chip, table, queries, kv, sources, len(rounds), later, list(part), n == 0)
         for k, piece in zip(part, pieces):
             pairs = [(d, d ^ (k * PAIR)) for d in range(devices)]
             back[k] = lax.ppermute(piece, "heads", pairs) if k else piece
-        if not later:
+        if n == 0:
             later = [lax.ppermute(pieces[-3], "heads", swap)]
             sources = pieces[-2:]
+        else:
+            later = [back[half]]
     return unpack(chip, back, 2)
 
 

time: 125 us -> 124 us (level)
  waiting for transfers between devices: 84 us -> 80.5 us
  starting transfers between devices: 21.8 us -> 23.3 us
    ppermute x7, waiting for transfers between devices: 12.9 us -> 8.13 us  [per_device(): back[k] = lax.ppermute(piece, 'heads', pairs) if k else piece]
    ppermute x7, starting transfers between devices: 9.2 us -> 10.7 us  [per_device(): back[k] = lax.ppermute(piece, 'heads', pairs) if k else piece]
    pallas_call x2 -> x3, Pallas kernels: 9.97 us -> 10.4 us  [attend(): pl.pallas_call(functools.partial(attend_kernel, sources=len(sources) if f...]
  transfers between devices with their start and end apart: 13 -> 13, of which waited for: 7 -> 9; matrix products, arithmetic and copies ran while one was open for 0% -> 0% of each run, Pallas kernels for 6% -> 8%
where the time goes in v21:
time: 124 us; the launch traced here: 123 us
  waiting for transfers between devices  80.5 us (65%)
  starting transfers between devices  23.3 us (19%)
  Pallas kernels  18 us (15%)
  between operations  1.36 us (1%)
    all_to_all x2, waiting for transfers between devices, exchange(): lax.all_to_all(pieces, 'heads', split_axis=0, concat_axis=0, axis_index_g...  52.2 us
    ppermute x1, waiting for transfers between devices, per_device(): mine.append(lax.ppermute(edge(start, kv), 'frames', rounds[-1]))  18.9 us
    all_to_all x2, starting transfers between devices, exchange(): lax.all_to_all(pieces, 'heads', split_axis=0, concat_axis=0, axis_index_g...  10.9 us
    ppermute x7, starting transfers between devices, per_device(): back[k] = lax.ppermute(piece, 'heads', pairs) if k else piece  10.7 us
    pallas_call x3, Pallas kernels, attend(): pl.pallas_call(functools.partial(attend_kernel, sources=len(sources) if f...  10.4 us
    ppermute x7, waiting for transfers between devices, per_device(): back[k] = lax.ppermute(piece, 'heads', pairs) if k else piece  8.13 us
    pallas_call x2, Pallas kernels, to_chips(): pl.pallas_call(functools.partial(pack_kernel, count=count, before=len(bef...  5.51 us
  transfers between devices with their start and end apart: 13, of which 9 were waited for; matrix products, arithmetic and copies ran while one was open for 0% of the time, Pallas kernels for 8%

profile of v21, /device:TPU:0, one launch (start us, length us, event | category | flops | bytes accessed | tf_op | source)
XLA Modules:
  0.0 123.3 jit_solution(9969633755910901326)
XLA Ops:
  0.6 2.7 %shard_map.86.refs_2_ = bf16[8,4,128,256]{3,2,1,0:T(8,128)(2,1)} custom-call(bf16[128,2048]{1,0:T(8,128)(2,1)} %refs_0_.2, bf16[128,2048]{1,0:T(8,128)(2,1)} %refs_1_.2, bf16[128,2048]{1,0:T(8,128)(2,1)} %refs_2_.1, bf16[128,2048]{1,0:T(8,128)(2,1)} %refs_3_.1), custom_call_target="tpu_custom_call" | custom-call | bytes 4194304 | tf_op jit(solution)/shard_map/pallas_call | solution.py:67
  3.3 7.3 %all-to-all-start.1 = ((bf16[8,4,128,256]{3,2,1,0:T(8,128)(2,1)}), bf16[8,4,128,256]{3,2,1,0:T(8,128)(2,1)S(1)}, u32[]{:S(2)}, u32[]{:S(2)}) async-start(bf16[8,4,128,256]{3,2,1,0:T(8,128)(2,1)} %shard_map.86.refs_2_), calls=%async_computation.1 | async-start | bytes 4194304 | tf_op jit(solution)/shard_map/all_to_all | solution.py:86
  10.6 2.8 %shard_map.87 = (bf16[8,2,128,256]{3,2,1,0:T(8,128)(2,1)}, s32[1]{0:T(128)}) custom-call(bf16[128,2048]{1,0:T(8,128)(2,1)} %refs_0_.3, bf16[128,2048]{1,0:T(8,128)(2,1)} %refs_1_.3, bf16[8,4,128,256]{3,2,1,0:T(8,128)(2,1)} %shard_map.86.refs_2_), custom_call_target="tpu_custom_call" | custom-call | bytes 2097152 | tf_op jit(solution)/shard_map/pallas_call | solution.py:67
  14.1 0.0 copy-start
  14.1 44.8 %all-to-all-done.1.kv.refs_0_ = bf16[8,4,128,256]{3,2,1,0:T(8,128)(2,1)S(1)} async-done(((bf16[8,4,128,256]{3,2,1,0:T(8,128)(2,1)}), bf16[8,4,128,256]{3,2,1,0:T(8,128)(2,1)S(1)}, u32[]{:S(2)}, u32[]{:S(2)}) %all-to-all-start.1) | async-done | bytes 2097184 | tf_op jit(solution)/shard_map/all_to_all | solution.py:86
  58.9 1.0 shard_map.88
  59.9 1.6 %collective-permute-start = (bf16[4,4,128,256]{3,2,1,0:T(8,128)(2,1)}, bf16[4,4,128,256]{3,2,1,0:T(8,128)(2,1)}, u32[]{:S(2)}, u32[]{:S(2)}) collective-permute-start(bf16[4,4,128,256]{3,2,1,0:T(8,128)(2,1)} %shard_map.88), channel_id=1, source_target_pairs={{0,1},{1,0},{2,3},{3,2},{4,5},{5,4},{6,7},{7,6},{8,9},{9,8},{10,11... | collective-permute-start | bytes 3145736 | tf_op jit(solution)/shard_map/ppermute | solution.py:279
  61.4 0.0 collective-permute-start.1
  61.5 3.6 %all-to-all-start = ((bf16[8,2,128,256]{3,2,1,0:T(8,128)(2,1)}), bf16[8,2,128,256]{3,2,1,0:T(8,128)(2,1)S(1)}, u32[]{:S(2)}, u32[]{:S(2)}) async-start(bf16[8,2,128,256]{3,2,1,0:T(8,128)(2,1)} %get-tuple-element.15), calls=%async_computation | async-start | bytes 2097152 | tf_op jit(solution)/shard_map/all_to_all | solution.py:86
  65.1 18.9 %collective-permute-done.refs_1_ = bf16[4,4,128,256]{3,2,1,0:T(8,128)(2,1)} collective-permute-done((bf16[4,4,128,256]{3,2,1,0:T(8,128)(2,1)}, bf16[4,4,128,256]{3,2,1,0:T(8,128)(2,1)}, u32[]{:S(2)}, u32[]{:S(2)}) %collective-permute-start) | collective-permute-done | bytes 1048608 | tf_op jit(solution)/shard_map/ppermute | solution.py:279
  84.0 0.0 collective-permute-start.2
  84.0 0.0 copy-done
  84.0 0.1 copy.10
  84.1 0.1 reshape.11.table
  84.2 7.5 %all-to-all-done.q_ref = bf16[8,2,128,256]{3,2,1,0:T(8,128)(2,1)S(1)} async-done(((bf16[8,2,128,256]{3,2,1,0:T(8,128)(2,1)}), bf16[8,2,128,256]{3,2,1,0:T(8,128)(2,1)S(1)}, u32[]{:S(2)}, u32[]{:S(2)}) %all-to-all-start) | async-done | bytes 1048608 | tf_op jit(solution)/shard_map/all_to_all | solution.py:86
  91.7 0.0 collective-permute-done.2.refs_3_
  91.7 0.0 collective-permute-done.1.refs_2_
  91.7 3.8 %shard_map.89 = (bf16[128,512]{1,0:T(8,128)(2,1)S(1)}, bf16[16,512]{1,0:T(8,128)(2,1)S(1)}, bf16[4,4,128,256]{3,2,1,0:T(8,128)(2,1)S(1)}, bf16[12,4,128,256]{3,2,1,0:T(8,128)(2,1)S(1)}) custom-call(s32[1]{0:T(128)} %bitcast.chip, s32[32]{0:T(128)S(1)} %reshape.11.table, bf16[8,2,128,256]{3,2,1,0:T(8,128)(2,1)S(1)} %all-to-all-done.q_ref, ...), custom_call_target="tpu_custom_call" | custom-call | flops 402653184 | bytes 4194304 | tf_op jit(solution)/shard_map/pallas_call | solution.py:231
  95.5 0.1 collective-permute-start.3
  95.6 0.1 collective-permute-start.4
  95.6 1.2 collective-permute-done.4.refs_3_
  96.8 2.4 %shard_map.90 = (bf16[128,512]{1,0:T(8,128)(2,1)S(1)}, bf16[128,512]{1,0:T(8,128)(2,1)S(1)}) custom-call(s32[1]{0:T(128)} %bitcast.chip, s32[32]{0:T(128)S(1)} %reshape.11.table, bf16[8,2,128,256]{3,2,1,0:T(8,128)(2,1)S(1)} %all-to-all-done.q_ref, bf16[8,4,128,256]{3,2,1,0:T(8,128)(2,1)S(1)} %all-to-all-done.1.kv.refs_0_, ...), custom_call_target="tpu_custom_call" | custom-call | flops 805306368 | tf_op jit(solution)/shard_map/pallas_call | solution.py:231
  99.2 3.8 %collective-permute-start.5 = (bf16[128,512]{1,0:T(8,128)(2,1)S(1)}, bf16[128,512]{1,0:T(8,128)(2,1)S(1)}, u32[]{:S(2)}, u32[]{:S(2)}) collective-permute-start(bf16[128,512]{1,0:T(8,128)(2,1)S(1)} %get-tuple-element.21), channel_id=1, source_target_pairs={{0,20},{2,22},{4,16},{6,18},{8,28},{10,30},{12,24},{14,26},{16,4},... | collective-permute-start | bytes 393224 | tf_op jit(solution)/shard_map/ppermute | solution.py:295
  103.0 1.5 %collective-permute-start.6 = (bf16[128,512]{1,0:T(8,128)(2,1)S(1)}, bf16[128,512]{1,0:T(8,128)(2,1)S(1)}, u32[]{:S(2)}, u32[]{:S(2)}) collective-permute-start(bf16[128,512]{1,0:T(8,128)(2,1)S(1)} %get-tuple-element.22), channel_id=1, source_target_pairs={{0,24},{2,26},{4,28},{6,30},{8,16},{10,18},{12,20},{14,22},{16,8},... | collective-permute-start | bytes 393224 | tf_op jit(solution)/shard_map/ppermute | solution.py:295
  104.5 0.0 collective-permute-done.3.refs_3_.refs_0_
  104.5 4.2 %shard_map.91 = (bf16[128,512]{1,0:T(8,128)(2,1)S(1)}, bf16[128,512]{1,0:T(8,128)(2,1)S(1)}, bf16[128,512]{1,0:T(8,128)(2,1)S(1)}, bf16[128,512]{1,0:T(8,128)(2,1)S(1)}, bf16[128,512]{1,0:T(8,128)(2,1)S(1)}) custom-call(s32[1]{0:T(128)} %bitcast.chip, s32[32]{0:T(128)S(1)} %reshape.11.table, bf16[8,2,128,256]{3,2,1,0:T(8,128)(2,1)S(1)} %all-to-all-done.q_ref, ...), custom_call_target="tpu_custom_call" | custom-call | flops 2013265920 | tf_op jit(solution)/shard_map/pallas_call | solution.py:231
  108.7 2.5 %collective-permute-start.7 = (bf16[128,512]{1,0:T(8,128)(2,1)S(1)}, bf16[128,512]{1,0:T(8,128)(2,1)S(1)}, u32[]{:S(2)}, u32[]{:S(2)}) collective-permute-start(bf16[128,512]{1,0:T(8,128)(2,1)S(1)} %get-tuple-element.23), channel_id=1, source_target_pairs={{0,28},{2,30},{4,24},{6,26},{8,20},{10,22},{12,16},{14,18},{16,12}... | collective-permute-start | bytes 393224 | tf_op jit(solution)/shard_map/ppermute | solution.py:295
  111.1 1.4 %collective-permute-start.8 = (bf16[128,512]{1,0:T(8,128)(2,1)S(1)}, bf16[128,512]{1,0:T(8,128)(2,1)S(1)}, u32[]{:S(2)}, u32[]{:S(2)}) collective-permute-start(bf16[128,512]{1,0:T(8,128)(2,1)S(1)} %get-tuple-element.24), channel_id=1, source_target_pairs={{0,4},{2,6},{4,0},{6,2},{8,12},{10,14},{12,8},{14,10},{16,20},{18,... | collective-permute-start | bytes 393224 | tf_op jit(solution)/shard_map/ppermute | solution.py:295
  112.5 0.0 collective-permute-start.9
  112.5 0.6 collective-permute-done.5.refs_1_
  113.1 1.5 %collective-permute-start.10 = (bf16[128,512]{1,0:T(8,128)(2,1)S(1)}, bf16[128,512]{1,0:T(8,128)(2,1)S(1)}, u32[]{:S(2)}, u32[]{:S(2)}) collective-permute-start(bf16[128,512]{1,0:T(8,128)(2,1)S(1)} %get-tuple-element.26), channel_id=1, source_target_pairs={{0,12},{2,14},{4,8},{6,10},{8,4},{10,6},{12,0},{14,2},{16,28},{18,... | collective-permute-start | bytes 393224 | tf_op jit(solution)/shard_map/ppermute | solution.py:295
  114.6 0.0 collective-permute-done.6.refs_2_
  114.6 3.2 %collective-permute-done.7.refs_3_ = bf16[128,512]{1,0:T(8,128)(2,1)S(1)} collective-permute-done((bf16[128,512]{1,0:T(8,128)(2,1)S(1)}, bf16[128,512]{1,0:T(8,128)(2,1)S(1)}, u32[]{:S(2)}, u32[]{:S(2)}) %collective-permute-start.7) | collective-permute-done | bytes 131104 | tf_op jit(solution)/shard_map/ppermute | solution.py:295
  117.8 0.8 collective-permute-done.8.refs_4_
  118.7 1.1 collective-permute-done.9.refs_5_
  119.8 2.4 %collective-permute-done.10.refs_6_ = bf16[128,512]{1,0:T(8,128)(2,1)S(1)} collective-permute-done((bf16[128,512]{1,0:T(8,128)(2,1)S(1)}, bf16[128,512]{1,0:T(8,128)(2,1)S(1)}, u32[]{:S(2)}, u32[]{:S(2)}) %collective-permute-start.10) | collective-permute-done | bytes 131104 | tf_op jit(solution)/shard_map/ppermute | solution.py:295
  122.2 1.1 shard_map.92
  (1 shorter events, 0.0 us)
Async XLA Ops:
  3.3 55.5 %all-to-all-start.1 = ((bf16[8,4,128,256]{3,2,1,0:T(8,128)(2,1)}), bf16[8,4,128,256]{3,2,1,0:T(8,128)(2,1)S(1)}, u32[]{:S(2)}, u32[]{:S(2)}) async-start(bf16[8,4,128,256]{3,2,1,0:T(8,128)(2,1)} %shard_map.86.refs_2_), calls=%async_computation.1 | async-start | bytes 4194304 | tf_op jit(solution)/shard_map/all_to_all | solution.py:86
  14.1 69.9 %copy-start = (s32[8,4]{0,1:T(4,128)S(1)}, s32[8,4]{0,1:T(4,128)}, u32[]{:S(2)}) copy-start(s32[8,4]{0,1:T(4,128)} %param.13) | copy-start | bytes 388
  59.9 24.1 %collective-permute-start = (bf16[4,4,128,256]{3,2,1,0:T(8,128)(2,1)}, bf16[4,4,128,256]{3,2,1,0:T(8,128)(2,1)}, u32[]{:S(2)}, u32[]{:S(2)}) collective-permute-start(bf16[4,4,128,256]{3,2,1,0:T(8,128)(2,1)} %shard_map.88), channel_id=1, source_target_pairs={{0,1},{1,0},{2,3},{3,2},{4,5},{5,4},{6,7},{7,6},{8,9},{9,8},{10,11... | collective-permute-start | bytes 3145736 | tf_op jit(solution)/shard_map/ppermute | solution.py:279
  61.4 30.2 %collective-permute-start.1 = (bf16[8,4,128,256]{3,2,1,0:T(8,128)(2,1)S(1)}, bf16[8,4,128,256]{3,2,1,0:T(8,128)(2,1)}, u32[]{:S(2)}, u32[]{:S(2)}) collective-permute-start(bf16[8,4,128,256]{3,2,1,0:T(8,128)(2,1)S(1)} %all-to-all-done.1.kv.refs_0_), channel_id=1, source_target_pairs={{0,2},{2,0},{4,6},{6,4},{8,10},{10,8},{12,14},{14,12},{16,18},{18,... | collective-permute-start | bytes 6291464 | tf_op jit(solution)/shard_map/ppermute | solution.py:280
  61.5 30.2 %all-to-all-start = ((bf16[8,2,128,256]{3,2,1,0:T(8,128)(2,1)}), bf16[8,2,128,256]{3,2,1,0:T(8,128)(2,1)S(1)}, u32[]{:S(2)}, u32[]{:S(2)}) async-start(bf16[8,2,128,256]{3,2,1,0:T(8,128)(2,1)} %get-tuple-element.15), calls=%async_computation | async-start | bytes 2097152 | tf_op jit(solution)/shard_map/all_to_all | solution.py:86
  84.0 7.7 %collective-permute-start.2 = (bf16[4,4,128,256]{3,2,1,0:T(8,128)(2,1)}, bf16[4,4,128,256]{3,2,1,0:T(8,128)(2,1)}, u32[]{:S(2)}, u32[]{:S(2)}) collective-permute-start(bf16[4,4,128,256]{3,2,1,0:T(8,128)(2,1)} %collective-permute-done.refs_1_), channel_id=1, source_target_pairs={{0,2},{2,0},{4,6},{6,4},{8,10},{10,8},{12,14},{14,12},{16,18},{18,... | collective-permute-start | bytes 3145736 | tf_op jit(solution)/shard_map/ppermute | solution.py:280
  95.5 9.0 %collective-permute-start.3 = (bf16[128,512]{1,0:T(8,128)(2,1)S(1)}, bf16[128,512]{1,0:T(8,128)(2,1)S(1)}, u32[]{:S(2)}, u32[]{:S(2)}) collective-permute-start(bf16[128,512]{1,0:T(8,128)(2,1)S(1)} %get-tuple-element.17), channel_id=1, source_target_pairs={{0,16},{2,18},{4,20},{6,22},{8,24},{10,26},{12,28},{14,30},{16,0},... | collective-permute-start | bytes 393224 | tf_op jit(solution)/shard_map/ppermute | solution.py:295
  95.6 1.2 %collective-permute-start.4 = (bf16[16,512]{1,0:T(8,128)(2,1)S(1)}, bf16[16,512]{1,0:T(8,128)(2,1)S(1)}, u32[]{:S(2)}, u32[]{:S(2)}) collective-permute-start(bf16[16,512]{1,0:T(8,128)(2,1)S(1)} %get-tuple-element.20), channel_id=1, source_target_pairs={{0,2},{2,0},{4,6},{6,4},{8,10},{10,8},{12,14},{14,12},{16,18},{18,... | collective-permute-start | bytes 49160 | tf_op jit(solution)/shard_map/ppermute | solution.py:297
  99.2 13.9 %collective-permute-start.5 = (bf16[128,512]{1,0:T(8,128)(2,1)S(1)}, bf16[128,512]{1,0:T(8,128)(2,1)S(1)}, u32[]{:S(2)}, u32[]{:S(2)}) collective-permute-start(bf16[128,512]{1,0:T(8,128)(2,1)S(1)} %get-tuple-element.21), channel_id=1, source_target_pairs={{0,20},{2,22},{4,16},{6,18},{8,28},{10,30},{12,24},{14,26},{16,4},... | collective-permute-start | bytes 393224 | tf_op jit(solution)/shard_map/ppermute | solution.py:295
  103.0 11.7 %collective-permute-start.6 = (bf16[128,512]{1,0:T(8,128)(2,1)S(1)}, bf16[128,512]{1,0:T(8,128)(2,1)S(1)}, u32[]{:S(2)}, u32[]{:S(2)}) collective-permute-start(bf16[128,512]{1,0:T(8,128)(2,1)S(1)} %get-tuple-element.22), channel_id=1, source_target_pairs={{0,24},{2,26},{4,28},{6,30},{8,16},{10,18},{12,20},{14,22},{16,8},... | collective-permute-start | bytes 393224 | tf_op jit(solution)/shard_map/ppermute | solution.py:295
  108.7 9.2 %collective-permute-start.7 = (bf16[128,512]{1,0:T(8,128)(2,1)S(1)}, bf16[128,512]{1,0:T(8,128)(2,1)S(1)}, u32[]{:S(2)}, u32[]{:S(2)}) collective-permute-start(bf16[128,512]{1,0:T(8,128)(2,1)S(1)} %get-tuple-element.23), channel_id=1, source_target_pairs={{0,28},{2,30},{4,24},{6,26},{8,20},{10,22},{12,16},{14,18},{16,12}... | collective-permute-start | bytes 393224 | tf_op jit(solution)/shard_map/ppermute | solution.py:295
  111.1 7.6 %collective-permute-start.8 = (bf16[128,512]{1,0:T(8,128)(2,1)S(1)}, bf16[128,512]{1,0:T(8,128)(2,1)S(1)}, u32[]{:S(2)}, u32[]{:S(2)}) collective-permute-start(bf16[128,512]{1,0:T(8,128)(2,1)S(1)} %get-tuple-element.24), channel_id=1, source_target_pairs={{0,4},{2,6},{4,0},{6,2},{8,12},{10,14},{12,8},{14,10},{16,20},{18,... | collective-permute-start | bytes 393224 | tf_op jit(solution)/shard_map/ppermute | solution.py:295
  112.5 7.3 %collective-permute-start.9 = (bf16[128,512]{1,0:T(8,128)(2,1)S(1)}, bf16[128,512]{1,0:T(8,128)(2,1)S(1)}, u32[]{:S(2)}, u32[]{:S(2)}) collective-permute-start(bf16[128,512]{1,0:T(8,128)(2,1)S(1)} %get-tuple-element.25), channel_id=1, source_target_pairs={{0,8},{2,10},{4,12},{6,14},{8,0},{10,2},{12,4},{14,6},{16,24},{18,... | collective-permute-start | bytes 393224 | tf_op jit(solution)/shard_map/ppermute | solution.py:295
  113.1 9.1 %collective-permute-start.10 = (bf16[128,512]{1,0:T(8,128)(2,1)S(1)}, bf16[128,512]{1,0:T(8,128)(2,1)S(1)}, u32[]{:S(2)}, u32[]{:S(2)}) collective-permute-start(bf16[128,512]{1,0:T(8,128)(2,1)S(1)} %get-tuple-element.26), channel_id=1, source_target_pairs={{0,12},{2,14},{4,8},{6,10},{8,4},{10,6},{12,0},{14,2},{16,28},{18,... | collective-permute-start | bytes 393224 | tf_op jit(solution)/shard_map/ppermute | solution.py:295

commit v22 on v21

--- a/solution.py
+++ b/solution.py
@@ -139,30 +139,54 @@
     )(start, kv)
 
 
+def fetch(parts, halos, table, place, blocks, near, wide, sems):
+    for w in range(WK):
+        index = table[place + w]
+        low = {0: blocks, 1: 0}
+        for n, ref in enumerate(parts):
+            side, target = (0, near) if n < halos else (1, wide)
+            first, size = low[side], ref.shape[0]
+            low[side] += size
+
+            @pl.when((index >= first) & (index < first + size))
+            def copy(ref=ref, first=first, side=side, target=target, index=index, w=w):
+                pltpu.make_async_copy(ref.at[index - first], target.at[w], sems.at[side, w]).start()
+
+
+def arrive(part, table, place, blocks, near, wide, sems):
+    for w in range(WK):
+        pltpu.make_async_copy(part.at[0], wide.at[w], sems.at[1, w]).wait()
+
+        @pl.when(table[place + w] >= blocks)
+        def wait(w=w):
+            pltpu.make_async_copy(part.at[0], near.at[w], sems.at[0, w]).wait()
+
+
 def attend_kernel(chip, table, q_ref, *refs, sources, halos, later, places, hd):
     tokens = q_ref.shape[2]
     own, refs = refs[0], refs[1:]
     blocks = own.shape[0]
     if sources:
-        parts, sems, halo, rest = refs[:sources], refs[-1], refs[-3], refs[-2]
-        outs = refs[sources + later : -4]
+        parts, (halo, rest, near, wide, sems, marks) = refs[:sources], refs[-6:]
+        outs = refs[sources + later : -7]
         copies, row = [], {0: 0, 1: 0}
         for n, ref in enumerate(parts):
             target, core = (halo, 0) if n < halos else (rest, 1)
             place = target.at[pl.ds(row[core], ref.shape[0])]
             copies.append(pltpu.make_async_copy(ref, place, sems.at[n]))
             row[core] += ref.shape[0]
+        fetch(parts, halos, table, (chip[0] ^ places[0]) * WK, blocks, near, wide, marks)
         for copy in copies:
             copy.start()
-        for copy in copies:
-            copy.wait()
+        arrive(parts[0], table, (chip[0] ^ places[0]) * WK, blocks, near, wide, marks)
     else:
         halo, rest, outs = refs[0], refs[1], refs[2 + later :]
 
-    def rows(index, group):
+    def rows(w, index, group):
         here = own[jnp.minimum(index, blocks - 1), group]
-        there = halo[jnp.maximum(index - blocks, 0), group]
-        return jnp.concatenate([jnp.where(index < blocks, here, there), rest[index, group]], axis=0)
+        there = near[w, group] if sources else halo[jnp.maximum(index - blocks, 0), group]
+        other = wide[w, group] if sources else rest[index, group]
+        return jnp.concatenate([jnp.where(index < blocks, here, there), other], axis=0)
 
     scale = hd ** (-0.5)
     factor = scale * math.log2(math.e)
@@ -176,8 +200,8 @@
         left = jnp.concatenate([left, both], axis=0)
         window = [table[block * WK + w] for w in range(WK)]
         scores, tans = [], []
-        for index in window:
-            keys = rows(index, 2 * h)
+        for w, index in enumerate(window):
+            keys = rows(w, index, 2 * h)
             product = lax.dot_general(left, keys, trans, preferred_element_type=jnp.float32)
             scores.append(product[:tokens])
             tans.append(product[tokens:])
@@ -191,9 +215,9 @@
         total = jnp.sum(functools.reduce(jnp.add, probs), axis=1, keepdims=True)
         mean = jnp.sum(functools.reduce(jnp.add, weighted), axis=1, keepdims=True)
         mixed = jnp.zeros((2 * tokens, 2 * hd), jnp.float32)
-        for index, p, w in zip(window, probs, weighted):
-            vals = rows(index, 2 * h + 1)
-            right = jnp.concatenate([p.astype(jnp.bfloat16), w.astype(jnp.bfloat16)], axis=0)
+        for w, (index, p, t) in enumerate(zip(window, probs, weighted)):
+            vals = rows(w, index, 2 * h + 1)
+            right = jnp.concatenate([p.astype(jnp.bfloat16), t.astype(jnp.bfloat16)], axis=0)
             mixed += jnp.dot(right, vals, preferred_element_type=jnp.float32)
         inverse = 1.0 / total
         out = mixed[:tokens, :hd] * inverse
@@ -211,7 +235,9 @@
             ahead = products(*following)
         finish(*unit, *current)
     if sources:
-        refs[-4][...] = outs[0][:LEAD]
+        refs[-7][...] = outs[0][:LEAD]
+        for copy in copies:
+            copy.wait()
 
 
 def attend(chip, table, queries, own, sources, halos, later, places, first):
@@ -227,7 +253,8 @@
         for group in (sources[:count], sources[count:]):
             shape = (sum(a.shape[0] for a in group), *own.shape[1:])
             outs.append(jax.ShapeDtypeStruct(shape, jnp.bfloat16))
-        scratch.append(pltpu.SemaphoreType.DMA((len(sources),)))
+        scratch += [pltpu.VMEM((WK, *own.shape[1:]), jnp.bfloat16)] * 2
+        scratch += [pltpu.SemaphoreType.DMA((len(sources),)), pltpu.SemaphoreType.DMA((2, WK))]
     return pl.pallas_call(
         functools.partial(
             attend_kernel,

time: 124 us -> 123 us (level)
  transfers between devices with their start and end apart: 13 -> 13, of which waited for: 9 -> 10; matrix products, arithmetic and copies ran while one was open for 0% -> 0% of each run, Pallas kernels for 8% -> 8%
where the time goes in v22:
time: 123 us
  waiting for transfers between devices  80.5 us (65%)
  starting transfers between devices  23.2 us (19%)
  Pallas kernels  17.4 us (14%)
  between operations  1.36 us (1%)
    all_to_all x2, waiting for transfers between devices, exchange(): lax.all_to_all(pieces, 'heads', split_axis=0, concat_axis=0, axis_index_g...  52.2 us
    ppermute x1, waiting for transfers between devices, per_device(): mine.append(lax.ppermute(edge(start, kv), 'frames', rounds[-1]))  18.9 us
    all_to_all x2, starting transfers between devices, exchange(): lax.all_to_all(pieces, 'heads', split_axis=0, concat_axis=0, axis_index_g...  10.9 us
    ppermute x7, starting transfers between devices, per_device(): back[k] = lax.ppermute(piece, 'heads', pairs) if k else piece  10.6 us
    pallas_call x3, Pallas kernels, attend(): pl.pallas_call(functools.partial(attend_kernel, sources=len(sources) if f...  9.83 us
    ppermute x7, waiting for transfers between devices, per_device(): back[k] = lax.ppermute(piece, 'heads', pairs) if k else piece  8.2 us
    pallas_call x2, Pallas kernels, to_chips(): pl.pallas_call(functools.partial(pack_kernel, count=count, before=len(bef...  5.51 us
  transfers between devices with their start and end apart: 13, of which 10 were waited for; matrix products, arithmetic and copies ran while one was open for 0% of the time, Pallas kernels for 8%

profile of v22, /device:TPU:0, one launch (start us, length us, event | category | flops | bytes accessed | tf_op | source)
XLA Modules:
  0.0 122.7 jit_solution(6804033496000557002)
XLA Ops:
  0.6 2.7 %shard_map.86.refs_2_ = bf16[8,4,128,256]{3,2,1,0:T(8,128)(2,1)} custom-call(bf16[128,2048]{1,0:T(8,128)(2,1)} %refs_0_.2, bf16[128,2048]{1,0:T(8,128)(2,1)} %refs_1_.2, bf16[128,2048]{1,0:T(8,128)(2,1)} %refs_2_.1, bf16[128,2048]{1,0:T(8,128)(2,1)} %refs_3_.1), custom_call_target="tpu_custom_call" | custom-call | bytes 4194304 | tf_op jit(solution)/shard_map/pallas_call | solution.py:67
  3.3 7.3 %all-to-all-start.1 = ((bf16[8,4,128,256]{3,2,1,0:T(8,128)(2,1)}), bf16[8,4,128,256]{3,2,1,0:T(8,128)(2,1)S(1)}, u32[]{:S(2)}, u32[]{:S(2)}) async-start(bf16[8,4,128,256]{3,2,1,0:T(8,128)(2,1)} %shard_map.86.refs_2_), calls=%async_computation.1 | async-start | bytes 4194304 | tf_op jit(solution)/shard_map/all_to_all | solution.py:86
  10.6 2.8 %shard_map.87 = (bf16[8,2,128,256]{3,2,1,0:T(8,128)(2,1)}, s32[1]{0:T(128)}) custom-call(bf16[128,2048]{1,0:T(8,128)(2,1)} %refs_0_.3, bf16[128,2048]{1,0:T(8,128)(2,1)} %refs_1_.3, bf16[8,4,128,256]{3,2,1,0:T(8,128)(2,1)} %shard_map.86.refs_2_), custom_call_target="tpu_custom_call" | custom-call | bytes 2097152 | tf_op jit(solution)/shard_map/pallas_call | solution.py:67
  14.1 0.0 copy-start
  14.1 44.8 %all-to-all-done.1.kv.refs_0_ = bf16[8,4,128,256]{3,2,1,0:T(8,128)(2,1)S(1)} async-done(((bf16[8,4,128,256]{3,2,1,0:T(8,128)(2,1)}), bf16[8,4,128,256]{3,2,1,0:T(8,128)(2,1)S(1)}, u32[]{:S(2)}, u32[]{:S(2)}) %all-to-all-start.1) | async-done | bytes 2097184 | tf_op jit(solution)/shard_map/all_to_all | solution.py:86
  58.9 1.0 shard_map.88
  59.9 1.6 %collective-permute-start = (bf16[4,4,128,256]{3,2,1,0:T(8,128)(2,1)}, bf16[4,4,128,256]{3,2,1,0:T(8,128)(2,1)}, u32[]{:S(2)}, u32[]{:S(2)}) collective-permute-start(bf16[4,4,128,256]{3,2,1,0:T(8,128)(2,1)} %shard_map.88), channel_id=1, source_target_pairs={{0,1},{1,0},{2,3},{3,2},{4,5},{5,4},{6,7},{7,6},{8,9},{9,8},{10,11... | collective-permute-start | bytes 3145736 | tf_op jit(solution)/shard_map/ppermute | solution.py:306
  61.4 0.0 collective-permute-start.1
  61.5 3.6 %all-to-all-start = ((bf16[8,2,128,256]{3,2,1,0:T(8,128)(2,1)}), bf16[8,2,128,256]{3,2,1,0:T(8,128)(2,1)S(1)}, u32[]{:S(2)}, u32[]{:S(2)}) async-start(bf16[8,2,128,256]{3,2,1,0:T(8,128)(2,1)} %get-tuple-element.15), calls=%async_computation | async-start | bytes 2097152 | tf_op jit(solution)/shard_map/all_to_all | solution.py:86
  65.1 18.9 %collective-permute-done.refs_1_ = bf16[4,4,128,256]{3,2,1,0:T(8,128)(2,1)} collective-permute-done((bf16[4,4,128,256]{3,2,1,0:T(8,128)(2,1)}, bf16[4,4,128,256]{3,2,1,0:T(8,128)(2,1)}, u32[]{:S(2)}, u32[]{:S(2)}) %collective-permute-start) | collective-permute-done | bytes 1048608 | tf_op jit(solution)/shard_map/ppermute | solution.py:306
  84.0 0.0 collective-permute-start.2
  84.0 0.0 copy-done
  84.0 0.1 copy.10
  84.1 0.1 reshape.11.table
  84.2 7.5 %all-to-all-done.q_ref = bf16[8,2,128,256]{3,2,1,0:T(8,128)(2,1)S(1)} async-done(((bf16[8,2,128,256]{3,2,1,0:T(8,128)(2,1)}), bf16[8,2,128,256]{3,2,1,0:T(8,128)(2,1)S(1)}, u32[]{:S(2)}, u32[]{:S(2)}) %all-to-all-start) | async-done | bytes 1048608 | tf_op jit(solution)/shard_map/all_to_all | solution.py:86
  91.7 0.0 collective-permute-done.2.refs_3_
  91.7 0.0 collective-permute-done.1.refs_2_
  91.7 3.2 %shard_map.89 = (bf16[128,512]{1,0:T(8,128)(2,1)S(1)}, bf16[16,512]{1,0:T(8,128)(2,1)S(1)}, bf16[4,4,128,256]{3,2,1,0:T(8,128)(2,1)S(1)}, bf16[12,4,128,256]{3,2,1,0:T(8,128)(2,1)S(1)}) custom-call(s32[1]{0:T(128)} %bitcast.chip, s32[32]{0:T(128)S(1)} %reshape.11.table, bf16[8,2,128,256]{3,2,1,0:T(8,128)(2,1)S(1)} %all-to-all-done.q_ref, ...), custom_call_target="tpu_custom_call" | custom-call | flops 402653184 | bytes 4194304 | tf_op jit(solution)/shard_map/pallas_call | solution.py:258
  94.9 0.1 collective-permute-start.3
  95.0 0.1 collective-permute-start.4
  95.1 1.2 collective-permute-done.4.refs_3_
  96.2 2.4 %shard_map.90 = (bf16[128,512]{1,0:T(8,128)(2,1)S(1)}, bf16[128,512]{1,0:T(8,128)(2,1)S(1)}) custom-call(s32[1]{0:T(128)} %bitcast.chip, s32[32]{0:T(128)S(1)} %reshape.11.table, bf16[8,2,128,256]{3,2,1,0:T(8,128)(2,1)S(1)} %all-to-all-done.q_ref, bf16[8,4,128,256]{3,2,1,0:T(8,128)(2,1)S(1)} %all-to-all-done.1.kv.refs_0_, ...), custom_call_target="tpu_custom_call" | custom-call | flops 805306368 | tf_op jit(solution)/shard_map/pallas_call | solution.py:258
  98.6 3.8 %collective-permute-start.5 = (bf16[128,512]{1,0:T(8,128)(2,1)S(1)}, bf16[128,512]{1,0:T(8,128)(2,1)S(1)}, u32[]{:S(2)}, u32[]{:S(2)}) collective-permute-start(bf16[128,512]{1,0:T(8,128)(2,1)S(1)} %get-tuple-element.21), channel_id=1, source_target_pairs={{0,20},{2,22},{4,16},{6,18},{8,28},{10,30},{12,24},{14,26},{16,4},... | collective-permute-start | bytes 393224 | tf_op jit(solution)/shard_map/ppermute | solution.py:322
  102.4 1.5 %collective-permute-start.6 = (bf16[128,512]{1,0:T(8,128)(2,1)S(1)}, bf16[128,512]{1,0:T(8,128)(2,1)S(1)}, u32[]{:S(2)}, u32[]{:S(2)}) collective-permute-start(bf16[128,512]{1,0:T(8,128)(2,1)S(1)} %get-tuple-element.22), channel_id=1, source_target_pairs={{0,24},{2,26},{4,28},{6,30},{8,16},{10,18},{12,20},{14,22},{16,8},... | collective-permute-start | bytes 393224 | tf_op jit(solution)/shard_map/ppermute | solution.py:322
  103.9 0.1 collective-permute-done.3.refs_3_.refs_0_
  104.0 4.2 %shard_map.91 = (bf16[128,512]{1,0:T(8,128)(2,1)S(1)}, bf16[128,512]{1,0:T(8,128)(2,1)S(1)}, bf16[128,512]{1,0:T(8,128)(2,1)S(1)}, bf16[128,512]{1,0:T(8,128)(2,1)S(1)}, bf16[128,512]{1,0:T(8,128)(2,1)S(1)}) custom-call(s32[1]{0:T(128)} %bitcast.chip, s32[32]{0:T(128)S(1)} %reshape.11.table, bf16[8,2,128,256]{3,2,1,0:T(8,128)(2,1)S(1)} %all-to-all-done.q_ref, ...), custom_call_target="tpu_custom_call" | custom-call | flops 2013265920 | tf_op jit(solution)/shard_map/pallas_call | solution.py:258
  108.2 2.3 %collective-permute-start.7 = (bf16[128,512]{1,0:T(8,128)(2,1)S(1)}, bf16[128,512]{1,0:T(8,128)(2,1)S(1)}, u32[]{:S(2)}, u32[]{:S(2)}) collective-permute-start(bf16[128,512]{1,0:T(8,128)(2,1)S(1)} %get-tuple-element.23), channel_id=1, source_target_pairs={{0,28},{2,30},{4,24},{6,26},{8,20},{10,22},{12,16},{14,18},{16,12}... | collective-permute-start | bytes 393224 | tf_op jit(solution)/shard_map/ppermute | solution.py:322
  110.5 1.4 %collective-permute-start.8 = (bf16[128,512]{1,0:T(8,128)(2,1)S(1)}, bf16[128,512]{1,0:T(8,128)(2,1)S(1)}, u32[]{:S(2)}, u32[]{:S(2)}) collective-permute-start(bf16[128,512]{1,0:T(8,128)(2,1)S(1)} %get-tuple-element.24), channel_id=1, source_target_pairs={{0,4},{2,6},{4,0},{6,2},{8,12},{10,14},{12,8},{14,10},{16,20},{18,... | collective-permute-start | bytes 393224 | tf_op jit(solution)/shard_map/ppermute | solution.py:322
  112.0 0.0 collective-permute-start.9
  112.0 0.5 collective-permute-done.5.refs_1_
  112.5 1.5 %collective-permute-start.10 = (bf16[128,512]{1,0:T(8,128)(2,1)S(1)}, bf16[128,512]{1,0:T(8,128)(2,1)S(1)}, u32[]{:S(2)}, u32[]{:S(2)}) collective-permute-start(bf16[128,512]{1,0:T(8,128)(2,1)S(1)} %get-tuple-element.26), channel_id=1, source_target_pairs={{0,12},{2,14},{4,8},{6,10},{8,4},{10,6},{12,0},{14,2},{16,28},{18,... | collective-permute-start | bytes 393224 | tf_op jit(solution)/shard_map/ppermute | solution.py:322
  114.0 0.0 collective-permute-done.6.refs_2_
  114.0 3.4 %collective-permute-done.7.refs_3_ = bf16[128,512]{1,0:T(8,128)(2,1)S(1)} collective-permute-done((bf16[128,512]{1,0:T(8,128)(2,1)S(1)}, bf16[128,512]{1,0:T(8,128)(2,1)S(1)}, u32[]{:S(2)}, u32[]{:S(2)}) %collective-permute-start.7) | collective-permute-done | bytes 131104 | tf_op jit(solution)/shard_map/ppermute | solution.py:322
  117.4 0.7 collective-permute-done.8.refs_4_
  118.1 1.1 collective-permute-done.9.refs_5_
  119.2 2.3 %collective-permute-done.10.refs_6_ = bf16[128,512]{1,0:T(8,128)(2,1)S(1)} collective-permute-done((bf16[128,512]{1,0:T(8,128)(2,1)S(1)}, bf16[128,512]{1,0:T(8,128)(2,1)S(1)}, u32[]{:S(2)}, u32[]{:S(2)}) %collective-permute-start.10) | collective-permute-done | bytes 131104 | tf_op jit(solution)/shard_map/ppermute | solution.py:322
  121.6 1.1 shard_map.92
  (1 shorter events, 0.0 us)
Async XLA Ops:
  3.3 55.5 %all-to-all-start.1 = ((bf16[8,4,128,256]{3,2,1,0:T(8,128)(2,1)}), bf16[8,4,128,256]{3,2,1,0:T(8,128)(2,1)S(1)}, u32[]{:S(2)}, u32[]{:S(2)}) async-start(bf16[8,4,128,256]{3,2,1,0:T(8,128)(2,1)} %shard_map.86.refs_2_), calls=%async_computation.1 | async-start | bytes 4194304 | tf_op jit(solution)/shard_map/all_to_all | solution.py:86
  14.1 69.9 %copy-start = (s32[8,4]{0,1:T(4,128)S(1)}, s32[8,4]{0,1:T(4,128)}, u32[]{:S(2)}) copy-start(s32[8,4]{0,1:T(4,128)} %param.13) | copy-start | bytes 388
  59.9 24.1 %collective-permute-start = (bf16[4,4,128,256]{3,2,1,0:T(8,128)(2,1)}, bf16[4,4,128,256]{3,2,1,0:T(8,128)(2,1)}, u32[]{:S(2)}, u32[]{:S(2)}) collective-permute-start(bf16[4,4,128,256]{3,2,1,0:T(8,128)(2,1)} %shard_map.88), channel_id=1, source_target_pairs={{0,1},{1,0},{2,3},{3,2},{4,5},{5,4},{6,7},{7,6},{8,9},{9,8},{10,11... | collective-permute-start | bytes 3145736 | tf_op jit(solution)/shard_map/ppermute | solution.py:306
  61.4 30.2 %collective-permute-start.1 = (bf16[8,4,128,256]{3,2,1,0:T(8,128)(2,1)S(1)}, bf16[8,4,128,256]{3,2,1,0:T(8,128)(2,1)}, u32[]{:S(2)}, u32[]{:S(2)}) collective-permute-start(bf16[8,4,128,256]{3,2,1,0:T(8,128)(2,1)S(1)} %all-to-all-done.1.kv.refs_0_), channel_id=1, source_target_pairs={{0,2},{2,0},{4,6},{6,4},{8,10},{10,8},{12,14},{14,12},{16,18},{18,... | collective-permute-start | bytes 6291464 | tf_op jit(solution)/shard_map/ppermute | solution.py:307
  61.5 30.2 %all-to-all-start = ((bf16[8,2,128,256]{3,2,1,0:T(8,128)(2,1)}), bf16[8,2,128,256]{3,2,1,0:T(8,128)(2,1)S(1)}, u32[]{:S(2)}, u32[]{:S(2)}) async-start(bf16[8,2,128,256]{3,2,1,0:T(8,128)(2,1)} %get-tuple-element.15), calls=%async_computation | async-start | bytes 2097152 | tf_op jit(solution)/shard_map/all_to_all | solution.py:86
  84.0 7.7 %collective-permute-start.2 = (bf16[4,4,128,256]{3,2,1,0:T(8,128)(2,1)}, bf16[4,4,128,256]{3,2,1,0:T(8,128)(2,1)}, u32[]{:S(2)}, u32[]{:S(2)}) collective-permute-start(bf16[4,4,128,256]{3,2,1,0:T(8,128)(2,1)} %collective-permute-done.refs_1_), channel_id=1, source_target_pairs={{0,2},{2,0},{4,6},{6,4},{8,10},{10,8},{12,14},{14,12},{16,18},{18,... | collective-permute-start | bytes 3145736 | tf_op jit(solution)/shard_map/ppermute | solution.py:307
  94.9 9.1 %collective-permute-start.3 = (bf16[128,512]{1,0:T(8,128)(2,1)S(1)}, bf16[128,512]{1,0:T(8,128)(2,1)S(1)}, u32[]{:S(2)}, u32[]{:S(2)}) collective-permute-start(bf16[128,512]{1,0:T(8,128)(2,1)S(1)} %get-tuple-element.17), channel_id=1, source_target_pairs={{0,16},{2,18},{4,20},{6,22},{8,24},{10,26},{12,28},{14,30},{16,0},... | collective-permute-start | bytes 393224 | tf_op jit(solution)/shard_map/ppermute | solution.py:322
  95.0 1.2 %collective-permute-start.4 = (bf16[16,512]{1,0:T(8,128)(2,1)S(1)}, bf16[16,512]{1,0:T(8,128)(2,1)S(1)}, u32[]{:S(2)}, u32[]{:S(2)}) collective-permute-start(bf16[16,512]{1,0:T(8,128)(2,1)S(1)} %get-tuple-element.20), channel_id=1, source_target_pairs={{0,2},{2,0},{4,6},{6,4},{8,10},{10,8},{12,14},{14,12},{16,18},{18,... | collective-permute-start | bytes 49160 | tf_op jit(solution)/shard_map/ppermute | solution.py:324
  98.6 13.9 %collective-permute-start.5 = (bf16[128,512]{1,0:T(8,128)(2,1)S(1)}, bf16[128,512]{1,0:T(8,128)(2,1)S(1)}, u32[]{:S(2)}, u32[]{:S(2)}) collective-permute-start(bf16[128,512]{1,0:T(8,128)(2,1)S(1)} %get-tuple-element.21), channel_id=1, source_target_pairs={{0,20},{2,22},{4,16},{6,18},{8,28},{10,30},{12,24},{14,26},{16,4},... | collective-permute-start | bytes 393224 | tf_op jit(solution)/shard_map/ppermute | solution.py:322
  102.4 11.6 %collective-permute-start.6 = (bf16[128,512]{1,0:T(8,128)(2,1)S(1)}, bf16[128,512]{1,0:T(8,128)(2,1)S(1)}, u32[]{:S(2)}, u32[]{:S(2)}) collective-permute-start(bf16[128,512]{1,0:T(8,128)(2,1)S(1)} %get-tuple-element.22), channel_id=1, source_target_pairs={{0,24},{2,26},{4,28},{6,30},{8,16},{10,18},{12,20},{14,22},{16,8},... | collective-permute-start | bytes 393224 | tf_op jit(solution)/shard_map/ppermute | solution.py:322
  108.2 9.2 %collective-permute-start.7 = (bf16[128,512]{1,0:T(8,128)(2,1)S(1)}, bf16[128,512]{1,0:T(8,128)(2,1)S(1)}, u32[]{:S(2)}, u32[]{:S(2)}) collective-permute-start(bf16[128,512]{1,0:T(8,128)(2,1)S(1)} %get-tuple-element.23), channel_id=1, source_target_pairs={{0,28},{2,30},{4,24},{6,26},{8,20},{10,22},{12,16},{14,18},{16,12}... | collective-permute-start | bytes 393224 | tf_op jit(solution)/shard_map/ppermute | solution.py:322
  110.5 7.6 %collective-permute-start.8 = (bf16[128,512]{1,0:T(8,128)(2,1)S(1)}, bf16[128,512]{1,0:T(8,128)(2,1)S(1)}, u32[]{:S(2)}, u32[]{:S(2)}) collective-permute-start(bf16[128,512]{1,0:T(8,128)(2,1)S(1)} %get-tuple-element.24), channel_id=1, source_target_pairs={{0,4},{2,6},{4,0},{6,2},{8,12},{10,14},{12,8},{14,10},{16,20},{18,... | collective-permute-start | bytes 393224 | tf_op jit(solution)/shard_map/ppermute | solution.py:322
  112.0 7.3 %collective-permute-start.9 = (bf16[128,512]{1,0:T(8,128)(2,1)S(1)}, bf16[128,512]{1,0:T(8,128)(2,1)S(1)}, u32[]{:S(2)}, u32[]{:S(2)}) collective-permute-start(bf16[128,512]{1,0:T(8,128)(2,1)S(1)} %get-tuple-element.25), channel_id=1, source_target_pairs={{0,8},{2,10},{4,12},{6,14},{8,0},{10,2},{12,4},{14,6},{16,24},{18,... | collective-permute-start | bytes 393224 | tf_op jit(solution)/shard_map/ppermute | solution.py:322
  112.5 9.1 %collective-permute-start.10 = (bf16[128,512]{1,0:T(8,128)(2,1)S(1)}, bf16[128,512]{1,0:T(8,128)(2,1)S(1)}, u32[]{:S(2)}, u32[]{:S(2)}) collective-permute-start(bf16[128,512]{1,0:T(8,128)(2,1)S(1)} %get-tuple-element.26), channel_id=1, source_target_pairs={{0,12},{2,14},{4,8},{6,10},{8,4},{10,6},{12,0},{14,2},{16,28},{18,... | collective-permute-start | bytes 393224 | tf_op jit(solution)/shard_map/ppermute | solution.py:322

commit v23 on v22

--- a/solution.py
+++ b/solution.py
@@ -310,11 +310,9 @@
     table = locate(neighbors, frame, blocks)
     half, middle = blocks // 2, blocks // 2 + blocks // 4
     back, later, sources = {}, [], mine[1:] + other
-    calls = (
-        range(half, half + 1),
-        range(half + 1, middle + 1),
-        [*range(middle + 1, blocks), *range(1, half), 0],
-    )
+    far = [*range(middle, blocks), *range(half, middle)]
+    cut = 1 + (middle - half)
+    calls = (far[:1], far[1:cut], [*far[cut:], *range(1, half), 0])
     for n, part in enumerate(calls):
         pieces = attend(chip, table, queries, kv, sources, len(rounds), later, list(part), n == 0)
         for k, piece in zip(part, pieces):
@@ -324,7 +322,7 @@
             later = [lax.ppermute(pieces[-3], "heads", swap)]
             sources = pieces[-2:]
         else:
-            later = [back[half]]
+            later = [back[far[0]]]
     return unpack(chip, back, 2)
 
 

time: 123 us -> 125 us (1.016)
  waiting for transfers between devices: 80.5 us -> 82.3 us
    ppermute x7, waiting for transfers between devices: 8.2 us -> 9.93 us  [per_device(): back[k] = lax.ppermute(piece, 'heads', pairs) if k else piece]
  transfers between devices with their start and end apart: 13 -> 13, of which waited for: 10 -> 8; matrix products, arithmetic and copies ran while one was open for 0% -> 0% of each run, Pallas kernels for 8% -> 8%
where the time goes in v23:
time: 125 us
  waiting for transfers between devices  82.3 us (66%)
  starting transfers between devices  24 us (19%)
  Pallas kernels  17.4 us (14%)
  between operations  1.35 us (1%)
    all_to_all x2, waiting for transfers between devices, exchange(): lax.all_to_all(pieces, 'heads', split_axis=0, concat_axis=0, axis_index_g...  52.2 us
    ppermute x1, waiting for transfers between devices, per_device(): mine.append(lax.ppermute(edge(start, kv), 'frames', rounds[-1]))  18.9 us
    ppermute x7, starting transfers between devices, per_device(): back[k] = lax.ppermute(piece, 'heads', pairs) if k else piece  11.5 us
    all_to_all x2, starting transfers between devices, exchange(): lax.all_to_all(pieces, 'heads', split_axis=0, concat_axis=0, axis_index_g...  10.9 us
    ppermute x7, waiting for transfers between devices, per_device(): back[k] = lax.ppermute(piece, 'heads', pairs) if k else piece  9.93 us
    pallas_call x3, Pallas kernels, attend(): pl.pallas_call(functools.partial(attend_kernel, sources=len(sources) if f...  9.83 us
    pallas_call x2, Pallas kernels, to_chips(): pl.pallas_call(functools.partial(pack_kernel, count=count, before=len(bef...  5.51 us
  transfers between devices with their start and end apart: 13, of which 8 were waited for; matrix products, arithmetic and copies ran while one was open for 0% of the time, Pallas kernels for 8%

profile of v23, /device:TPU:0, one launch (start us, length us, event | category | flops | bytes accessed | tf_op | source)
XLA Modules:
  0.0 125.2 jit_solution(13177334799108832106)
XLA Ops:
  0.6 2.7 %shard_map.86.refs_2_ = bf16[8,4,128,256]{3,2,1,0:T(8,128)(2,1)} custom-call(bf16[128,2048]{1,0:T(8,128)(2,1)} %refs_0_.2, bf16[128,2048]{1,0:T(8,128)(2,1)} %refs_1_.2, bf16[128,2048]{1,0:T(8,128)(2,1)} %refs_2_.1, bf16[128,2048]{1,0:T(8,128)(2,1)} %refs_3_.1), custom_call_target="tpu_custom_call" | custom-call | bytes 4194304 | tf_op jit(solution)/shard_map/pallas_call | solution.py:67
  3.3 7.3 %all-to-all-start.1 = ((bf16[8,4,128,256]{3,2,1,0:T(8,128)(2,1)}), bf16[8,4,128,256]{3,2,1,0:T(8,128)(2,1)S(1)}, u32[]{:S(2)}, u32[]{:S(2)}) async-start(bf16[8,4,128,256]{3,2,1,0:T(8,128)(2,1)} %shard_map.86.refs_2_), calls=%async_computation.1 | async-start | bytes 4194304 | tf_op jit(solution)/shard_map/all_to_all | solution.py:86
  10.6 2.8 %shard_map.87 = (bf16[8,2,128,256]{3,2,1,0:T(8,128)(2,1)}, s32[1]{0:T(128)}) custom-call(bf16[128,2048]{1,0:T(8,128)(2,1)} %refs_0_.3, bf16[128,2048]{1,0:T(8,128)(2,1)} %refs_1_.3, bf16[8,4,128,256]{3,2,1,0:T(8,128)(2,1)} %shard_map.86.refs_2_), custom_call_target="tpu_custom_call" | custom-call | bytes 2097152 | tf_op jit(solution)/shard_map/pallas_call | solution.py:67
  14.1 0.0 copy-start
  14.1 44.8 %all-to-all-done.1.kv.refs_0_ = bf16[8,4,128,256]{3,2,1,0:T(8,128)(2,1)S(1)} async-done(((bf16[8,4,128,256]{3,2,1,0:T(8,128)(2,1)}), bf16[8,4,128,256]{3,2,1,0:T(8,128)(2,1)S(1)}, u32[]{:S(2)}, u32[]{:S(2)}) %all-to-all-start.1) | async-done | bytes 2097184 | tf_op jit(solution)/shard_map/all_to_all | solution.py:86
  58.9 1.0 shard_map.88
  59.9 1.6 %collective-permute-start = (bf16[4,4,128,256]{3,2,1,0:T(8,128)(2,1)}, bf16[4,4,128,256]{3,2,1,0:T(8,128)(2,1)}, u32[]{:S(2)}, u32[]{:S(2)}) collective-permute-start(bf16[4,4,128,256]{3,2,1,0:T(8,128)(2,1)} %shard_map.88), channel_id=1, source_target_pairs={{0,1},{1,0},{2,3},{3,2},{4,5},{5,4},{6,7},{7,6},{8,9},{9,8},{10,11... | collective-permute-start | bytes 3145736 | tf_op jit(solution)/shard_map/ppermute | solution.py:306
  61.4 0.0 collective-permute-start.1
  61.5 3.6 %all-to-all-start = ((bf16[8,2,128,256]{3,2,1,0:T(8,128)(2,1)}), bf16[8,2,128,256]{3,2,1,0:T(8,128)(2,1)S(1)}, u32[]{:S(2)}, u32[]{:S(2)}) async-start(bf16[8,2,128,256]{3,2,1,0:T(8,128)(2,1)} %get-tuple-element.15), calls=%async_computation | async-start | bytes 2097152 | tf_op jit(solution)/shard_map/all_to_all | solution.py:86
  65.1 18.9 %collective-permute-done.refs_1_ = bf16[4,4,128,256]{3,2,1,0:T(8,128)(2,1)} collective-permute-done((bf16[4,4,128,256]{3,2,1,0:T(8,128)(2,1)}, bf16[4,4,128,256]{3,2,1,0:T(8,128)(2,1)}, u32[]{:S(2)}, u32[]{:S(2)}) %collective-permute-start) | collective-permute-done | bytes 1048608 | tf_op jit(solution)/shard_map/ppermute | solution.py:306
  84.0 0.0 collective-permute-start.2
  84.0 0.0 copy-done
  84.0 0.1 copy.10
  84.1 0.1 reshape.11.table
  84.2 7.5 %all-to-all-done.q_ref = bf16[8,2,128,256]{3,2,1,0:T(8,128)(2,1)S(1)} async-done(((bf16[8,2,128,256]{3,2,1,0:T(8,128)(2,1)}), bf16[8,2,128,256]{3,2,1,0:T(8,128)(2,1)S(1)}, u32[]{:S(2)}, u32[]{:S(2)}) %all-to-all-start) | async-done | bytes 1048608 | tf_op jit(solution)/shard_map/all_to_all | solution.py:86
  91.7 0.0 collective-permute-done.2.refs_3_
  91.7 0.0 collective-permute-done.1.refs_2_
  91.7 3.2 %shard_map.89 = (bf16[128,512]{1,0:T(8,128)(2,1)S(1)}, bf16[16,512]{1,0:T(8,128)(2,1)S(1)}, bf16[4,4,128,256]{3,2,1,0:T(8,128)(2,1)S(1)}, bf16[12,4,128,256]{3,2,1,0:T(8,128)(2,1)S(1)}) custom-call(s32[1]{0:T(128)} %bitcast.chip, s32[32]{0:T(128)S(1)} %reshape.11.table, bf16[8,2,128,256]{3,2,1,0:T(8,128)(2,1)S(1)} %all-to-all-done.q_ref, ...), custom_call_target="tpu_custom_call" | custom-call | flops 402653184 | bytes 4194304 | tf_op jit(solution)/shard_map/pallas_call | solution.py:258
  94.9 2.3 %collective-permute-start.3 = (bf16[128,512]{1,0:T(8,128)(2,1)S(1)}, bf16[128,512]{1,0:T(8,128)(2,1)S(1)}, u32[]{:S(2)}, u32[]{:S(2)}) collective-permute-start(bf16[128,512]{1,0:T(8,128)(2,1)S(1)} %get-tuple-element.17), channel_id=1, source_target_pairs={{0,24},{2,26},{4,28},{6,30},{8,16},{10,18},{12,20},{14,22},{16,8},... | collective-permute-start | bytes 393224 | tf_op jit(solution)/shard_map/ppermute | solution.py:320
  97.2 0.0 collective-permute-start.4
  97.3 1.2 collective-permute-done.4.refs_3_
  98.4 2.4 %shard_map.90 = (bf16[128,512]{1,0:T(8,128)(2,1)S(1)}, bf16[128,512]{1,0:T(8,128)(2,1)S(1)}) custom-call(s32[1]{0:T(128)} %bitcast.chip, s32[32]{0:T(128)S(1)} %reshape.11.table, bf16[8,2,128,256]{3,2,1,0:T(8,128)(2,1)S(1)} %all-to-all-done.q_ref, bf16[8,4,128,256]{3,2,1,0:T(8,128)(2,1)S(1)} %all-to-all-done.1.kv.refs_0_, ...), custom_call_target="tpu_custom_call" | custom-call | flops 805306368 | tf_op jit(solution)/shard_map/pallas_call | solution.py:258
  100.8 3.3 %collective-permute-start.5 = (bf16[128,512]{1,0:T(8,128)(2,1)S(1)}, bf16[128,512]{1,0:T(8,128)(2,1)S(1)}, u32[]{:S(2)}, u32[]{:S(2)}) collective-permute-start(bf16[128,512]{1,0:T(8,128)(2,1)S(1)} %get-tuple-element.21), channel_id=1, source_target_pairs={{0,28},{2,30},{4,24},{6,26},{8,20},{10,22},{12,16},{14,18},{16,12}... | collective-permute-start | bytes 393224 | tf_op jit(solution)/shard_map/ppermute | solution.py:320
  104.1 0.0 collective-permute-start.6
  104.1 0.0 collective-permute-done.3.refs_3_.refs_0_
  104.1 4.2 %shard_map.91 = (bf16[128,512]{1,0:T(8,128)(2,1)S(1)}, bf16[128,512]{1,0:T(8,128)(2,1)S(1)}, bf16[128,512]{1,0:T(8,128)(2,1)S(1)}, bf16[128,512]{1,0:T(8,128)(2,1)S(1)}, bf16[128,512]{1,0:T(8,128)(2,1)S(1)}) custom-call(s32[1]{0:T(128)} %bitcast.chip, s32[32]{0:T(128)S(1)} %reshape.11.table, bf16[8,2,128,256]{3,2,1,0:T(8,128)(2,1)S(1)} %all-to-all-done.q_ref, ...), custom_call_target="tpu_custom_call" | custom-call | flops 2013265920 | tf_op jit(solution)/shard_map/pallas_call | solution.py:258
  108.3 2.2 %collective-permute-start.7 = (bf16[128,512]{1,0:T(8,128)(2,1)S(1)}, bf16[128,512]{1,0:T(8,128)(2,1)S(1)}, u32[]{:S(2)}, u32[]{:S(2)}) collective-permute-start(bf16[128,512]{1,0:T(8,128)(2,1)S(1)} %get-tuple-element.23), channel_id=1, source_target_pairs={{0,20},{2,22},{4,16},{6,18},{8,28},{10,30},{12,24},{14,26},{16,4},... | collective-permute-start | bytes 393224 | tf_op jit(solution)/shard_map/ppermute | solution.py:320
  110.5 2.2 %collective-permute-start.8 = (bf16[128,512]{1,0:T(8,128)(2,1)S(1)}, bf16[128,512]{1,0:T(8,128)(2,1)S(1)}, u32[]{:S(2)}, u32[]{:S(2)}) collective-permute-start(bf16[128,512]{1,0:T(8,128)(2,1)S(1)} %get-tuple-element.24), channel_id=1, source_target_pairs={{0,4},{2,6},{4,0},{6,2},{8,12},{10,14},{12,8},{14,10},{16,20},{18,... | collective-permute-start | bytes 393224 | tf_op jit(solution)/shard_map/ppermute | solution.py:320
  112.7 0.0 collective-permute-start.9
  112.8 0.0 collective-permute-done.5.refs_1_
  112.8 1.5 %collective-permute-start.10 = (bf16[128,512]{1,0:T(8,128)(2,1)S(1)}, bf16[128,512]{1,0:T(8,128)(2,1)S(1)}, u32[]{:S(2)}, u32[]{:S(2)}) collective-permute-start(bf16[128,512]{1,0:T(8,128)(2,1)S(1)} %get-tuple-element.26), channel_id=1, source_target_pairs={{0,12},{2,14},{4,8},{6,10},{8,4},{10,6},{12,0},{14,2},{16,28},{18,... | collective-permute-start | bytes 393224 | tf_op jit(solution)/shard_map/ppermute | solution.py:320
  114.2 2.2 %collective-permute-done.6.refs_2_ = bf16[128,512]{1,0:T(8,128)(2,1)S(1)} collective-permute-done((bf16[128,512]{1,0:T(8,128)(2,1)S(1)}, bf16[128,512]{1,0:T(8,128)(2,1)S(1)}, u32[]{:S(2)}, u32[]{:S(2)}) %collective-permute-start.6) | collective-permute-done | bytes 131104 | tf_op jit(solution)/shard_map/ppermute | solution.py:320
  116.4 4.1 %collective-permute-done.7.refs_3_ = bf16[128,512]{1,0:T(8,128)(2,1)S(1)} collective-permute-done((bf16[128,512]{1,0:T(8,128)(2,1)S(1)}, bf16[128,512]{1,0:T(8,128)(2,1)S(1)}, u32[]{:S(2)}, u32[]{:S(2)}) %collective-permute-start.7) | collective-permute-done | bytes 131104 | tf_op jit(solution)/shard_map/ppermute | solution.py:320
  120.5 0.0 collective-permute-done.8.refs_4_
  120.5 1.5 %collective-permute-done.9.refs_5_ = bf16[128,512]{1,0:T(8,128)(2,1)S(1)} collective-permute-done((bf16[128,512]{1,0:T(8,128)(2,1)S(1)}, bf16[128,512]{1,0:T(8,128)(2,1)S(1)}, u32[]{:S(2)}, u32[]{:S(2)}) %collective-permute-start.9) | collective-permute-done | bytes 131104 | tf_op jit(solution)/shard_map/ppermute | solution.py:320
  122.0 2.2 %collective-permute-done.10.refs_6_ = bf16[128,512]{1,0:T(8,128)(2,1)S(1)} collective-permute-done((bf16[128,512]{1,0:T(8,128)(2,1)S(1)}, bf16[128,512]{1,0:T(8,128)(2,1)S(1)}, u32[]{:S(2)}, u32[]{:S(2)}) %collective-permute-start.10) | collective-permute-done | bytes 131104 | tf_op jit(solution)/shard_map/ppermute | solution.py:320
  124.1 1.1 shard_map.92
  (1 shorter events, 0.0 us)
Async XLA Ops:
  3.3 55.5 %all-to-all-start.1 = ((bf16[8,4,128,256]{3,2,1,0:T(8,128)(2,1)}), bf16[8,4,128,256]{3,2,1,0:T(8,128)(2,1)S(1)}, u32[]{:S(2)}, u32[]{:S(2)}) async-start(bf16[8,4,128,256]{3,2,1,0:T(8,128)(2,1)} %shard_map.86.refs_2_), calls=%async_computation.1 | async-start | bytes 4194304 | tf_op jit(solution)/shard_map/all_to_all | solution.py:86
  14.1 69.9 %copy-start = (s32[8,4]{0,1:T(4,128)S(1)}, s32[8,4]{0,1:T(4,128)}, u32[]{:S(2)}) copy-start(s32[8,4]{0,1:T(4,128)} %param.13) | copy-start | bytes 388
  59.9 24.1 %collective-permute-start = (bf16[4,4,128,256]{3,2,1,0:T(8,128)(2,1)}, bf16[4,4,128,256]{3,2,1,0:T(8,128)(2,1)}, u32[]{:S(2)}, u32[]{:S(2)}) collective-permute-start(bf16[4,4,128,256]{3,2,1,0:T(8,128)(2,1)} %shard_map.88), channel_id=1, source_target_pairs={{0,1},{1,0},{2,3},{3,2},{4,5},{5,4},{6,7},{7,6},{8,9},{9,8},{10,11... | collective-permute-start | bytes 3145736 | tf_op jit(solution)/shard_map/ppermute | solution.py:306
  61.4 30.2 %collective-permute-start.1 = (bf16[8,4,128,256]{3,2,1,0:T(8,128)(2,1)S(1)}, bf16[8,4,128,256]{3,2,1,0:T(8,128)(2,1)}, u32[]{:S(2)}, u32[]{:S(2)}) collective-permute-start(bf16[8,4,128,256]{3,2,1,0:T(8,128)(2,1)S(1)} %all-to-all-done.1.kv.refs_0_), channel_id=1, source_target_pairs={{0,2},{2,0},{4,6},{6,4},{8,10},{10,8},{12,14},{14,12},{16,18},{18,... | collective-permute-start | bytes 6291464 | tf_op jit(solution)/shard_map/ppermute | solution.py:307
  61.5 30.2 %all-to-all-start = ((bf16[8,2,128,256]{3,2,1,0:T(8,128)(2,1)}), bf16[8,2,128,256]{3,2,1,0:T(8,128)(2,1)S(1)}, u32[]{:S(2)}, u32[]{:S(2)}) async-start(bf16[8,2,128,256]{3,2,1,0:T(8,128)(2,1)} %get-tuple-element.15), calls=%async_computation | async-start | bytes 2097152 | tf_op jit(solution)/shard_map/all_to_all | solution.py:86
  84.0 7.7 %collective-permute-start.2 = (bf16[4,4,128,256]{3,2,1,0:T(8,128)(2,1)}, bf16[4,4,128,256]{3,2,1,0:T(8,128)(2,1)}, u32[]{:S(2)}, u32[]{:S(2)}) collective-permute-start(bf16[4,4,128,256]{3,2,1,0:T(8,128)(2,1)} %collective-permute-done.refs_1_), channel_id=1, source_target_pairs={{0,2},{2,0},{4,6},{6,4},{8,10},{10,8},{12,14},{14,12},{16,18},{18,... | collective-permute-start | bytes 3145736 | tf_op jit(solution)/shard_map/ppermute | solution.py:307
  94.9 9.2 %collective-permute-start.3 = (bf16[128,512]{1,0:T(8,128)(2,1)S(1)}, bf16[128,512]{1,0:T(8,128)(2,1)S(1)}, u32[]{:S(2)}, u32[]{:S(2)}) collective-permute-start(bf16[128,512]{1,0:T(8,128)(2,1)S(1)} %get-tuple-element.17), channel_id=1, source_target_pairs={{0,24},{2,26},{4,28},{6,30},{8,16},{10,18},{12,20},{14,22},{16,8},... | collective-permute-start | bytes 393224 | tf_op jit(solution)/shard_map/ppermute | solution.py:320
  97.2 1.2 collective-permute-start.4
  100.8 11.9 %collective-permute-start.5 = (bf16[128,512]{1,0:T(8,128)(2,1)S(1)}, bf16[128,512]{1,0:T(8,128)(2,1)S(1)}, u32[]{:S(2)}, u32[]{:S(2)}) collective-permute-start(bf16[128,512]{1,0:T(8,128)(2,1)S(1)} %get-tuple-element.21), channel_id=1, source_target_pairs={{0,28},{2,30},{4,24},{6,26},{8,20},{10,22},{12,16},{14,18},{16,12}... | collective-permute-start | bytes 393224 | tf_op jit(solution)/shard_map/ppermute | solution.py:320
  104.1 12.4 %collective-permute-start.6 = (bf16[128,512]{1,0:T(8,128)(2,1)S(1)}, bf16[128,512]{1,0:T(8,128)(2,1)S(1)}, u32[]{:S(2)}, u32[]{:S(2)}) collective-permute-start(bf16[128,512]{1,0:T(8,128)(2,1)S(1)} %get-tuple-element.22), channel_id=1, source_target_pairs={{0,16},{2,18},{4,20},{6,22},{8,24},{10,26},{12,28},{14,30},{16,0},... | collective-permute-start | bytes 393224 | tf_op jit(solution)/shard_map/ppermute | solution.py:320
  108.3 12.2 %collective-permute-start.7 = (bf16[128,512]{1,0:T(8,128)(2,1)S(1)}, bf16[128,512]{1,0:T(8,128)(2,1)S(1)}, u32[]{:S(2)}, u32[]{:S(2)}) collective-permute-start(bf16[128,512]{1,0:T(8,128)(2,1)S(1)} %get-tuple-element.23), channel_id=1, source_target_pairs={{0,20},{2,22},{4,16},{6,18},{8,28},{10,30},{12,24},{14,26},{16,4},... | collective-permute-start | bytes 393224 | tf_op jit(solution)/shard_map/ppermute | solution.py:320
  110.5 10.0 %collective-permute-start.8 = (bf16[128,512]{1,0:T(8,128)(2,1)S(1)}, bf16[128,512]{1,0:T(8,128)(2,1)S(1)}, u32[]{:S(2)}, u32[]{:S(2)}) collective-permute-start(bf16[128,512]{1,0:T(8,128)(2,1)S(1)} %get-tuple-element.24), channel_id=1, source_target_pairs={{0,4},{2,6},{4,0},{6,2},{8,12},{10,14},{12,8},{14,10},{16,20},{18,... | collective-permute-start | bytes 393224 | tf_op jit(solution)/shard_map/ppermute | solution.py:320
  112.7 9.2 %collective-permute-start.9 = (bf16[128,512]{1,0:T(8,128)(2,1)S(1)}, bf16[128,512]{1,0:T(8,128)(2,1)S(1)}, u32[]{:S(2)}, u32[]{:S(2)}) collective-permute-start(bf16[128,512]{1,0:T(8,128)(2,1)S(1)} %get-tuple-element.25), channel_id=1, source_target_pairs={{0,8},{2,10},{4,12},{6,14},{8,0},{10,2},{12,4},{14,6},{16,24},{18,... | collective-permute-start | bytes 393224 | tf_op jit(solution)/shard_map/ppermute | solution.py:320
  112.8 11.4 %collective-permute-start.10 = (bf16[128,512]{1,0:T(8,128)(2,1)S(1)}, bf16[128,512]{1,0:T(8,128)(2,1)S(1)}, u32[]{:S(2)}, u32[]{:S(2)}) collective-permute-start(bf16[128,512]{1,0:T(8,128)(2,1)S(1)} %get-tuple-element.26), channel_id=1, source_target_pairs={{0,12},{2,14},{4,8},{6,10},{8,4},{10,6},{12,0},{14,2},{16,28},{18,... | collective-permute-start | bytes 393224 | tf_op jit(solution)/shard_map/ppermute | solution.py:320

commit v24 on v22

--- a/solution.py
+++ b/solution.py
@@ -313,7 +313,7 @@
     calls = (
         range(half, half + 1),
         range(half + 1, middle + 1),
-        [*range(middle + 1, blocks), *range(1, half), 0],
+        [*range(middle + 1, blocks), *range(half - 1, 0, -1), 0],
     )
     for n, part in enumerate(calls):
         pieces = attend(chip, table, queries, kv, sources, len(rounds), later, list(part), n == 0)

time: 123 us -> 123 us (level)
  transfers between devices with their start and end apart: 13 -> 13, of which waited for: 10 -> 9; matrix products, arithmetic and copies ran while one was open for 0% -> 0% of each run, Pallas kernels for 8% -> 8%
where the time goes in v24:
time: 123 us
  waiting for transfers between devices  80.2 us (65%)
  starting transfers between devices  23.7 us (19%)
  Pallas kernels  17.7 us (14%)
  between operations  1.36 us (1%)
    all_to_all x2, waiting for transfers between devices, exchange(): lax.all_to_all(pieces, 'heads', split_axis=0, concat_axis=0, axis_index_g...  52.2 us
    ppermute x1, waiting for transfers between devices, per_device(): mine.append(lax.ppermute(edge(start, kv), 'frames', rounds[-1]))  18.9 us
    ppermute x7, starting transfers between devices, per_device(): back[k] = lax.ppermute(piece, 'heads', pairs) if k else piece  11.1 us
    all_to_all x2, starting transfers between devices, exchange(): lax.all_to_all(pieces, 'heads', split_axis=0, concat_axis=0, axis_index_g...  10.9 us
    pallas_call x3, Pallas kernels, attend(): pl.pallas_call(functools.partial(attend_kernel, sources=len(sources) if f...  10.1 us
    ppermute x7, waiting for transfers between devices, per_device(): back[k] = lax.ppermute(piece, 'heads', pairs) if k else piece  7.83 us
    pallas_call x2, Pallas kernels, to_chips(): pl.pallas_call(functools.partial(pack_kernel, count=count, before=len(bef...  5.51 us
  transfers between devices with their start and end apart: 13, of which 9 were waited for; matrix products, arithmetic and copies ran while one was open for 0% of the time, Pallas kernels for 8%

profile of v24, /device:TPU:0, one launch (start us, length us, event | category | flops | bytes accessed | tf_op | source)
XLA Modules:
  0.0 123.0 jit_solution(14068772552888778163)
XLA Ops:
  0.6 2.7 %shard_map.86.refs_2_ = bf16[8,4,128,256]{3,2,1,0:T(8,128)(2,1)} custom-call(bf16[128,2048]{1,0:T(8,128)(2,1)} %refs_0_.2, bf16[128,2048]{1,0:T(8,128)(2,1)} %refs_1_.2, bf16[128,2048]{1,0:T(8,128)(2,1)} %refs_2_.1, bf16[128,2048]{1,0:T(8,128)(2,1)} %refs_3_.1), custom_call_target="tpu_custom_call" | custom-call | bytes 4194304 | tf_op jit(solution)/shard_map/pallas_call | solution.py:67
  3.3 7.3 %all-to-all-start.1 = ((bf16[8,4,128,256]{3,2,1,0:T(8,128)(2,1)}), bf16[8,4,128,256]{3,2,1,0:T(8,128)(2,1)S(1)}, u32[]{:S(2)}, u32[]{:S(2)}) async-start(bf16[8,4,128,256]{3,2,1,0:T(8,128)(2,1)} %shard_map.86.refs_2_), calls=%async_computation.1 | async-start | bytes 4194304 | tf_op jit(solution)/shard_map/all_to_all | solution.py:86
  10.6 2.8 %shard_map.87 = (bf16[8,2,128,256]{3,2,1,0:T(8,128)(2,1)}, s32[1]{0:T(128)}) custom-call(bf16[128,2048]{1,0:T(8,128)(2,1)} %refs_0_.3, bf16[128,2048]{1,0:T(8,128)(2,1)} %refs_1_.3, bf16[8,4,128,256]{3,2,1,0:T(8,128)(2,1)} %shard_map.86.refs_2_), custom_call_target="tpu_custom_call" | custom-call | bytes 2097152 | tf_op jit(solution)/shard_map/pallas_call | solution.py:67
  14.1 0.0 copy-start
  14.1 44.8 %all-to-all-done.1.kv.refs_0_ = bf16[8,4,128,256]{3,2,1,0:T(8,128)(2,1)S(1)} async-done(((bf16[8,4,128,256]{3,2,1,0:T(8,128)(2,1)}), bf16[8,4,128,256]{3,2,1,0:T(8,128)(2,1)S(1)}, u32[]{:S(2)}, u32[]{:S(2)}) %all-to-all-start.1) | async-done | bytes 2097184 | tf_op jit(solution)/shard_map/all_to_all | solution.py:86
  58.9 1.0 shard_map.88
  59.9 1.6 %collective-permute-start = (bf16[4,4,128,256]{3,2,1,0:T(8,128)(2,1)}, bf16[4,4,128,256]{3,2,1,0:T(8,128)(2,1)}, u32[]{:S(2)}, u32[]{:S(2)}) collective-permute-start(bf16[4,4,128,256]{3,2,1,0:T(8,128)(2,1)} %shard_map.88), channel_id=1, source_target_pairs={{0,1},{1,0},{2,3},{3,2},{4,5},{5,4},{6,7},{7,6},{8,9},{9,8},{10,11... | collective-permute-start | bytes 3145736 | tf_op jit(solution)/shard_map/ppermute | solution.py:306
  61.4 0.0 collective-permute-start.1
  61.5 3.6 %all-to-all-start = ((bf16[8,2,128,256]{3,2,1,0:T(8,128)(2,1)}), bf16[8,2,128,256]{3,2,1,0:T(8,128)(2,1)S(1)}, u32[]{:S(2)}, u32[]{:S(2)}) async-start(bf16[8,2,128,256]{3,2,1,0:T(8,128)(2,1)} %get-tuple-element.15), calls=%async_computation | async-start | bytes 2097152 | tf_op jit(solution)/shard_map/all_to_all | solution.py:86
  65.1 18.9 %collective-permute-done.refs_1_ = bf16[4,4,128,256]{3,2,1,0:T(8,128)(2,1)} collective-permute-done((bf16[4,4,128,256]{3,2,1,0:T(8,128)(2,1)}, bf16[4,4,128,256]{3,2,1,0:T(8,128)(2,1)}, u32[]{:S(2)}, u32[]{:S(2)}) %collective-permute-start) | collective-permute-done | bytes 1048608 | tf_op jit(solution)/shard_map/ppermute | solution.py:306
  84.0 0.0 collective-permute-start.2
  84.0 0.0 copy-done
  84.0 0.1 copy.10
  84.1 0.1 reshape.11.table
  84.2 7.5 %all-to-all-done.q_ref = bf16[8,2,128,256]{3,2,1,0:T(8,128)(2,1)S(1)} async-done(((bf16[8,2,128,256]{3,2,1,0:T(8,128)(2,1)}), bf16[8,2,128,256]{3,2,1,0:T(8,128)(2,1)S(1)}, u32[]{:S(2)}, u32[]{:S(2)}) %all-to-all-start) | async-done | bytes 1048608 | tf_op jit(solution)/shard_map/all_to_all | solution.py:86
  91.7 0.0 collective-permute-done.2.refs_3_
  91.7 0.0 collective-permute-done.1.refs_2_
  91.7 3.5 %shard_map.89 = (bf16[128,512]{1,0:T(8,128)(2,1)S(1)}, bf16[16,512]{1,0:T(8,128)(2,1)S(1)}, bf16[4,4,128,256]{3,2,1,0:T(8,128)(2,1)S(1)}, bf16[12,4,128,256]{3,2,1,0:T(8,128)(2,1)S(1)}) custom-call(s32[1]{0:T(128)} %bitcast.chip, s32[32]{0:T(128)S(1)} %reshape.11.table, bf16[8,2,128,256]{3,2,1,0:T(8,128)(2,1)S(1)} %all-to-all-done.q_ref, ...), custom_call_target="tpu_custom_call" | custom-call | flops 402653184 | bytes 4194304 | tf_op jit(solution)/shard_map/pallas_call | solution.py:258
  95.2 0.1 collective-permute-start.3
  95.2 0.1 collective-permute-start.4
  95.3 1.2 collective-permute-done.4.refs_3_
  96.5 2.4 %shard_map.90 = (bf16[128,512]{1,0:T(8,128)(2,1)S(1)}, bf16[128,512]{1,0:T(8,128)(2,1)S(1)}) custom-call(s32[1]{0:T(128)} %bitcast.chip, s32[32]{0:T(128)S(1)} %reshape.11.table, bf16[8,2,128,256]{3,2,1,0:T(8,128)(2,1)S(1)} %all-to-all-done.q_ref, bf16[8,4,128,256]{3,2,1,0:T(8,128)(2,1)S(1)} %all-to-all-done.1.kv.refs_0_, ...), custom_call_target="tpu_custom_call" | custom-call | flops 805306368 | tf_op jit(solution)/shard_map/pallas_call | solution.py:258
  98.9 3.5 %collective-permute-start.5 = (bf16[128,512]{1,0:T(8,128)(2,1)S(1)}, bf16[128,512]{1,0:T(8,128)(2,1)S(1)}, u32[]{:S(2)}, u32[]{:S(2)}) collective-permute-start(bf16[128,512]{1,0:T(8,128)(2,1)S(1)} %get-tuple-element.21), channel_id=1, source_target_pairs={{0,20},{2,22},{4,16},{6,18},{8,28},{10,30},{12,24},{14,26},{16,4},... | collective-permute-start | bytes 393224 | tf_op jit(solution)/shard_map/ppermute | solution.py:322
  102.4 1.5 %collective-permute-start.6 = (bf16[128,512]{1,0:T(8,128)(2,1)S(1)}, bf16[128,512]{1,0:T(8,128)(2,1)S(1)}, u32[]{:S(2)}, u32[]{:S(2)}) collective-permute-start(bf16[128,512]{1,0:T(8,128)(2,1)S(1)} %get-tuple-element.22), channel_id=1, source_target_pairs={{0,24},{2,26},{4,28},{6,30},{8,16},{10,18},{12,20},{14,22},{16,8},... | collective-permute-start | bytes 393224 | tf_op jit(solution)/shard_map/ppermute | solution.py:322
  103.9 0.2 collective-permute-done.3.refs_3_.refs_0_
  104.0 4.2 %shard_map.91 = (bf16[128,512]{1,0:T(8,128)(2,1)S(1)}, bf16[128,512]{1,0:T(8,128)(2,1)S(1)}, bf16[128,512]{1,0:T(8,128)(2,1)S(1)}, bf16[128,512]{1,0:T(8,128)(2,1)S(1)}, bf16[128,512]{1,0:T(8,128)(2,1)S(1)}) custom-call(s32[1]{0:T(128)} %bitcast.chip, s32[32]{0:T(128)S(1)} %reshape.11.table, bf16[8,2,128,256]{3,2,1,0:T(8,128)(2,1)S(1)} %all-to-all-done.q_ref, ...), custom_call_target="tpu_custom_call" | custom-call | flops 2013265920 | tf_op jit(solution)/shard_map/pallas_call | solution.py:258
  108.2 2.6 %collective-permute-start.7 = (bf16[128,512]{1,0:T(8,128)(2,1)S(1)}, bf16[128,512]{1,0:T(8,128)(2,1)S(1)}, u32[]{:S(2)}, u32[]{:S(2)}) collective-permute-start(bf16[128,512]{1,0:T(8,128)(2,1)S(1)} %get-tuple-element.23), channel_id=1, source_target_pairs={{0,28},{2,30},{4,24},{6,26},{8,20},{10,22},{12,16},{14,18},{16,12}... | collective-permute-start | bytes 393224 | tf_op jit(solution)/shard_map/ppermute | solution.py:322
  110.8 0.0 collective-permute-start.8
  110.8 2.6 %collective-permute-start.9 = (bf16[128,512]{1,0:T(8,128)(2,1)S(1)}, bf16[128,512]{1,0:T(8,128)(2,1)S(1)}, u32[]{:S(2)}, u32[]{:S(2)}) collective-permute-start(bf16[128,512]{1,0:T(8,128)(2,1)S(1)} %get-tuple-element.25), channel_id=1, source_target_pairs={{0,8},{2,10},{4,12},{6,14},{8,0},{10,2},{12,4},{14,6},{16,24},{18,... | collective-permute-start | bytes 393224 | tf_op jit(solution)/shard_map/ppermute | solution.py:322
  113.4 0.0 collective-permute-done.5.refs_1_
  113.4 0.9 collective-permute-start.10
  114.3 0.0 collective-permute-done.6.refs_2_
  114.3 3.2 %collective-permute-done.7.refs_3_ = bf16[128,512]{1,0:T(8,128)(2,1)S(1)} collective-permute-done((bf16[128,512]{1,0:T(8,128)(2,1)S(1)}, bf16[128,512]{1,0:T(8,128)(2,1)S(1)}, u32[]{:S(2)}, u32[]{:S(2)}) %collective-permute-start.7) | collective-permute-done | bytes 131104 | tf_op jit(solution)/shard_map/ppermute | solution.py:322
  117.4 1.8 %collective-permute-done.8.refs_4_ = bf16[128,512]{1,0:T(8,128)(2,1)S(1)} collective-permute-done((bf16[128,512]{1,0:T(8,128)(2,1)S(1)}, bf16[128,512]{1,0:T(8,128)(2,1)S(1)}, u32[]{:S(2)}, u32[]{:S(2)}) %collective-permute-start.8) | collective-permute-done | bytes 131104 | tf_op jit(solution)/shard_map/ppermute | solution.py:322
  119.3 2.4 %collective-permute-done.9.refs_5_ = bf16[128,512]{1,0:T(8,128)(2,1)S(1)} collective-permute-done((bf16[128,512]{1,0:T(8,128)(2,1)S(1)}, bf16[128,512]{1,0:T(8,128)(2,1)S(1)}, u32[]{:S(2)}, u32[]{:S(2)}) %collective-permute-start.9) | collective-permute-done | bytes 131104 | tf_op jit(solution)/shard_map/ppermute | solution.py:322
  121.7 0.3 collective-permute-done.10.refs_6_
  122.0 1.1 shard_map.92
  (1 shorter events, 0.0 us)
Async XLA Ops:
  3.3 55.5 %all-to-all-start.1 = ((bf16[8,4,128,256]{3,2,1,0:T(8,128)(2,1)}), bf16[8,4,128,256]{3,2,1,0:T(8,128)(2,1)S(1)}, u32[]{:S(2)}, u32[]{:S(2)}) async-start(bf16[8,4,128,256]{3,2,1,0:T(8,128)(2,1)} %shard_map.86.refs_2_), calls=%async_computation.1 | async-start | bytes 4194304 | tf_op jit(solution)/shard_map/all_to_all | solution.py:86
  14.1 69.9 %copy-start = (s32[8,4]{0,1:T(4,128)S(1)}, s32[8,4]{0,1:T(4,128)}, u32[]{:S(2)}) copy-start(s32[8,4]{0,1:T(4,128)} %param.13) | copy-start | bytes 388
  59.9 24.1 %collective-permute-start = (bf16[4,4,128,256]{3,2,1,0:T(8,128)(2,1)}, bf16[4,4,128,256]{3,2,1,0:T(8,128)(2,1)}, u32[]{:S(2)}, u32[]{:S(2)}) collective-permute-start(bf16[4,4,128,256]{3,2,1,0:T(8,128)(2,1)} %shard_map.88), channel_id=1, source_target_pairs={{0,1},{1,0},{2,3},{3,2},{4,5},{5,4},{6,7},{7,6},{8,9},{9,8},{10,11... | collective-permute-start | bytes 3145736 | tf_op jit(solution)/shard_map/ppermute | solution.py:306
  61.4 30.2 %collective-permute-start.1 = (bf16[8,4,128,256]{3,2,1,0:T(8,128)(2,1)S(1)}, bf16[8,4,128,256]{3,2,1,0:T(8,128)(2,1)}, u32[]{:S(2)}, u32[]{:S(2)}) collective-permute-start(bf16[8,4,128,256]{3,2,1,0:T(8,128)(2,1)S(1)} %all-to-all-done.1.kv.refs_0_), channel_id=1, source_target_pairs={{0,2},{2,0},{4,6},{6,4},{8,10},{10,8},{12,14},{14,12},{16,18},{18,... | collective-permute-start | bytes 6291464 | tf_op jit(solution)/shard_map/ppermute | solution.py:307
  61.5 30.2 %all-to-all-start = ((bf16[8,2,128,256]{3,2,1,0:T(8,128)(2,1)}), bf16[8,2,128,256]{3,2,1,0:T(8,128)(2,1)S(1)}, u32[]{:S(2)}, u32[]{:S(2)}) async-start(bf16[8,2,128,256]{3,2,1,0:T(8,128)(2,1)} %get-tuple-element.15), calls=%async_computation | async-start | bytes 2097152 | tf_op jit(solution)/shard_map/all_to_all | solution.py:86
  84.0 7.7 %collective-permute-start.2 = (bf16[4,4,128,256]{3,2,1,0:T(8,128)(2,1)}, bf16[4,4,128,256]{3,2,1,0:T(8,128)(2,1)}, u32[]{:S(2)}, u32[]{:S(2)}) collective-permute-start(bf16[4,4,128,256]{3,2,1,0:T(8,128)(2,1)} %collective-permute-done.refs_1_), channel_id=1, source_target_pairs={{0,2},{2,0},{4,6},{6,4},{8,10},{10,8},{12,14},{14,12},{16,18},{18,... | collective-permute-start | bytes 3145736 | tf_op jit(solution)/shard_map/ppermute | solution.py:307
  95.2 8.9 %collective-permute-start.3 = (bf16[128,512]{1,0:T(8,128)(2,1)S(1)}, bf16[128,512]{1,0:T(8,128)(2,1)S(1)}, u32[]{:S(2)}, u32[]{:S(2)}) collective-permute-start(bf16[128,512]{1,0:T(8,128)(2,1)S(1)} %get-tuple-element.17), channel_id=1, source_target_pairs={{0,16},{2,18},{4,20},{6,22},{8,24},{10,26},{12,28},{14,30},{16,0},... | collective-permute-start | bytes 393224 | tf_op jit(solution)/shard_map/ppermute | solution.py:322
  95.2 1.2 %collective-permute-start.4 = (bf16[16,512]{1,0:T(8,128)(2,1)S(1)}, bf16[16,512]{1,0:T(8,128)(2,1)S(1)}, u32[]{:S(2)}, u32[]{:S(2)}) collective-permute-start(bf16[16,512]{1,0:T(8,128)(2,1)S(1)} %get-tuple-element.20), channel_id=1, source_target_pairs={{0,2},{2,0},{4,6},{6,4},{8,10},{10,8},{12,14},{14,12},{16,18},{18,... | collective-permute-start | bytes 49160 | tf_op jit(solution)/shard_map/ppermute | solution.py:324
  98.9 14.6 %collective-permute-start.5 = (bf16[128,512]{1,0:T(8,128)(2,1)S(1)}, bf16[128,512]{1,0:T(8,128)(2,1)S(1)}, u32[]{:S(2)}, u32[]{:S(2)}) collective-permute-start(bf16[128,512]{1,0:T(8,128)(2,1)S(1)} %get-tuple-element.21), channel_id=1, source_target_pairs={{0,20},{2,22},{4,16},{6,18},{8,28},{10,30},{12,24},{14,26},{16,4},... | collective-permute-start | bytes 393224 | tf_op jit(solution)/shard_map/ppermute | solution.py:322
  102.4 11.9 %collective-permute-start.6 = (bf16[128,512]{1,0:T(8,128)(2,1)S(1)}, bf16[128,512]{1,0:T(8,128)(2,1)S(1)}, u32[]{:S(2)}, u32[]{:S(2)}) collective-permute-start(bf16[128,512]{1,0:T(8,128)(2,1)S(1)} %get-tuple-element.22), channel_id=1, source_target_pairs={{0,24},{2,26},{4,28},{6,30},{8,16},{10,18},{12,20},{14,22},{16,8},... | collective-permute-start | bytes 393224 | tf_op jit(solution)/shard_map/ppermute | solution.py:322
  108.2 9.2 %collective-permute-start.7 = (bf16[128,512]{1,0:T(8,128)(2,1)S(1)}, bf16[128,512]{1,0:T(8,128)(2,1)S(1)}, u32[]{:S(2)}, u32[]{:S(2)}) collective-permute-start(bf16[128,512]{1,0:T(8,128)(2,1)S(1)} %get-tuple-element.23), channel_id=1, source_target_pairs={{0,28},{2,30},{4,24},{6,26},{8,20},{10,22},{12,16},{14,18},{16,12}... | collective-permute-start | bytes 393224 | tf_op jit(solution)/shard_map/ppermute | solution.py:322
  110.8 8.5 %collective-permute-start.8 = (bf16[128,512]{1,0:T(8,128)(2,1)S(1)}, bf16[128,512]{1,0:T(8,128)(2,1)S(1)}, u32[]{:S(2)}, u32[]{:S(2)}) collective-permute-start(bf16[128,512]{1,0:T(8,128)(2,1)S(1)} %get-tuple-element.24), channel_id=1, source_target_pairs={{0,12},{2,14},{4,8},{6,10},{8,4},{10,6},{12,0},{14,2},{16,28},{18,... | collective-permute-start | bytes 393224 | tf_op jit(solution)/shard_map/ppermute | solution.py:322
  110.8 10.9 %collective-permute-start.9 = (bf16[128,512]{1,0:T(8,128)(2,1)S(1)}, bf16[128,512]{1,0:T(8,128)(2,1)S(1)}, u32[]{:S(2)}, u32[]{:S(2)}) collective-permute-start(bf16[128,512]{1,0:T(8,128)(2,1)S(1)} %get-tuple-element.25), channel_id=1, source_target_pairs={{0,8},{2,10},{4,12},{6,14},{8,0},{10,2},{12,4},{14,6},{16,24},{18,... | collective-permute-start | bytes 393224 | tf_op jit(solution)/shard_map/ppermute | solution.py:322
  113.4 8.5 %collective-permute-start.10 = (bf16[128,512]{1,0:T(8,128)(2,1)S(1)}, bf16[128,512]{1,0:T(8,128)(2,1)S(1)}, u32[]{:S(2)}, u32[]{:S(2)}) collective-permute-start(bf16[128,512]{1,0:T(8,128)(2,1)S(1)} %get-tuple-element.26), channel_id=1, source_target_pairs={{0,4},{2,6},{4,0},{6,2},{8,12},{10,14},{12,8},{14,10},{16,20},{18,... | collective-permute-start | bytes 393224 | tf_op jit(solution)/shard_map/ppermute | solution.py:322

commit v25 on v24

--- a/solution.py
+++ b/solution.py
@@ -312,8 +312,8 @@
     back, later, sources = {}, [], mine[1:] + other
     calls = (
         range(half, half + 1),
-        range(half + 1, middle + 1),
-        [*range(middle + 1, blocks), *range(half - 1, 0, -1), 0],
+        [*range(half + 1, middle + 1), half - 1],
+        [*range(middle + 1, blocks), *range(half - 2, 0, -1), 0],
     )
     for n, part in enumerate(calls):
         pieces = attend(chip, table, queries, kv, sources, len(rounds), later, list(part), n == 0)

time: 123 us -> 122 us (level)
  waiting for transfers between devices: 80.2 us -> 78.4 us
    ppermute x7, waiting for transfers between devices: 7.83 us -> 6.11 us  [per_device(): back[k] = lax.ppermute(piece, 'heads', pairs) if k else piece]
  transfers between devices with their start and end apart: 13 -> 13, of which waited for: 9 -> 7; matrix products, arithmetic and copies ran while one was open for 0% -> 0% of each run, Pallas kernels for 8% -> 8%
where the time goes in v25:
time: 122 us; the launch traced here: 121 us
  waiting for transfers between devices  78.4 us (64%)
  starting transfers between devices  23.8 us (20%)
  Pallas kernels  17.3 us (14%)
  between operations  1.36 us (1%)
    all_to_all x2, waiting for transfers between devices, exchange(): lax.all_to_all(pieces, 'heads', split_axis=0, concat_axis=0, axis_index_g...  52.2 us
    ppermute x1, waiting for transfers between devices, per_device(): mine.append(lax.ppermute(edge(start, kv), 'frames', rounds[-1]))  18.9 us
    ppermute x7, starting transfers between devices, per_device(): back[k] = lax.ppermute(piece, 'heads', pairs) if k else piece  11.2 us
    all_to_all x2, starting transfers between devices, exchange(): lax.all_to_all(pieces, 'heads', split_axis=0, concat_axis=0, axis_index_g...  10.9 us
    pallas_call x3, Pallas kernels, attend(): pl.pallas_call(functools.partial(attend_kernel, sources=len(sources) if f...  9.71 us
    ppermute x7, waiting for transfers between devices, per_device(): back[k] = lax.ppermute(piece, 'heads', pairs) if k else piece  6.11 us
    pallas_call x2, Pallas kernels, to_chips(): pl.pallas_call(functools.partial(pack_kernel, count=count, before=len(bef...  5.51 us
  transfers between devices with their start and end apart: 13, of which 7 were waited for; matrix products, arithmetic and copies ran while one was open for 0% of the time, Pallas kernels for 8%

profile of v25, /device:TPU:0, one launch (start us, length us, event | category | flops | bytes accessed | tf_op | source)
XLA Modules:
  0.0 121.1 jit_solution(4593007942673951596)
XLA Ops:
  0.6 2.7 %shard_map.86.refs_2_ = bf16[8,4,128,256]{3,2,1,0:T(8,128)(2,1)} custom-call(bf16[128,2048]{1,0:T(8,128)(2,1)} %refs_0_.2, bf16[128,2048]{1,0:T(8,128)(2,1)} %refs_1_.2, bf16[128,2048]{1,0:T(8,128)(2,1)} %refs_2_.1, bf16[128,2048]{1,0:T(8,128)(2,1)} %refs_3_.1), custom_call_target="tpu_custom_call" | custom-call | bytes 4194304 | tf_op jit(solution)/shard_map/pallas_call | solution.py:67
  3.3 7.3 %all-to-all-start.1 = ((bf16[8,4,128,256]{3,2,1,0:T(8,128)(2,1)}), bf16[8,4,128,256]{3,2,1,0:T(8,128)(2,1)S(1)}, u32[]{:S(2)}, u32[]{:S(2)}) async-start(bf16[8,4,128,256]{3,2,1,0:T(8,128)(2,1)} %shard_map.86.refs_2_), calls=%async_computation.1 | async-start | bytes 4194304 | tf_op jit(solution)/shard_map/all_to_all | solution.py:86
  10.6 2.8 %shard_map.87 = (bf16[8,2,128,256]{3,2,1,0:T(8,128)(2,1)}, s32[1]{0:T(128)}) custom-call(bf16[128,2048]{1,0:T(8,128)(2,1)} %refs_0_.3, bf16[128,2048]{1,0:T(8,128)(2,1)} %refs_1_.3, bf16[8,4,128,256]{3,2,1,0:T(8,128)(2,1)} %shard_map.86.refs_2_), custom_call_target="tpu_custom_call" | custom-call | bytes 2097152 | tf_op jit(solution)/shard_map/pallas_call | solution.py:67
  14.1 0.0 copy-start
  14.1 44.8 %all-to-all-done.1.kv.refs_0_ = bf16[8,4,128,256]{3,2,1,0:T(8,128)(2,1)S(1)} async-done(((bf16[8,4,128,256]{3,2,1,0:T(8,128)(2,1)}), bf16[8,4,128,256]{3,2,1,0:T(8,128)(2,1)S(1)}, u32[]{:S(2)}, u32[]{:S(2)}) %all-to-all-start.1) | async-done | bytes 2097184 | tf_op jit(solution)/shard_map/all_to_all | solution.py:86
  58.9 1.0 shard_map.88
  59.9 1.6 %collective-permute-start = (bf16[4,4,128,256]{3,2,1,0:T(8,128)(2,1)}, bf16[4,4,128,256]{3,2,1,0:T(8,128)(2,1)}, u32[]{:S(2)}, u32[]{:S(2)}) collective-permute-start(bf16[4,4,128,256]{3,2,1,0:T(8,128)(2,1)} %shard_map.88), channel_id=1, source_target_pairs={{0,1},{1,0},{2,3},{3,2},{4,5},{5,4},{6,7},{7,6},{8,9},{9,8},{10,11... | collective-permute-start | bytes 3145736 | tf_op jit(solution)/shard_map/ppermute | solution.py:306
  61.4 0.0 collective-permute-start.1
  61.5 3.6 %all-to-all-start = ((bf16[8,2,128,256]{3,2,1,0:T(8,128)(2,1)}), bf16[8,2,128,256]{3,2,1,0:T(8,128)(2,1)S(1)}, u32[]{:S(2)}, u32[]{:S(2)}) async-start(bf16[8,2,128,256]{3,2,1,0:T(8,128)(2,1)} %get-tuple-element.15), calls=%async_computation | async-start | bytes 2097152 | tf_op jit(solution)/shard_map/all_to_all | solution.py:86
  65.1 18.9 %collective-permute-done.refs_1_ = bf16[4,4,128,256]{3,2,1,0:T(8,128)(2,1)} collective-permute-done((bf16[4,4,128,256]{3,2,1,0:T(8,128)(2,1)}, bf16[4,4,128,256]{3,2,1,0:T(8,128)(2,1)}, u32[]{:S(2)}, u32[]{:S(2)}) %collective-permute-start) | collective-permute-done | bytes 1048608 | tf_op jit(solution)/shard_map/ppermute | solution.py:306
  84.0 0.0 collective-permute-start.2
  84.0 0.0 copy-done
  84.0 0.1 copy.10
  84.1 0.1 reshape.11.table
  84.2 7.5 %all-to-all-done.q_ref = bf16[8,2,128,256]{3,2,1,0:T(8,128)(2,1)S(1)} async-done(((bf16[8,2,128,256]{3,2,1,0:T(8,128)(2,1)}), bf16[8,2,128,256]{3,2,1,0:T(8,128)(2,1)S(1)}, u32[]{:S(2)}, u32[]{:S(2)}) %all-to-all-start) | async-done | bytes 1048608 | tf_op jit(solution)/shard_map/all_to_all | solution.py:86
  91.7 0.0 collective-permute-done.2.refs_3_
  91.7 0.0 collective-permute-done.1.refs_2_
  91.7 3.2 %shard_map.89 = (bf16[128,512]{1,0:T(8,128)(2,1)S(1)}, bf16[16,512]{1,0:T(8,128)(2,1)S(1)}, bf16[4,4,128,256]{3,2,1,0:T(8,128)(2,1)S(1)}, bf16[12,4,128,256]{3,2,1,0:T(8,128)(2,1)S(1)}) custom-call(s32[1]{0:T(128)} %bitcast.chip, s32[32]{0:T(128)S(1)} %reshape.11.table, bf16[8,2,128,256]{3,2,1,0:T(8,128)(2,1)S(1)} %all-to-all-done.q_ref, ...), custom_call_target="tpu_custom_call" | custom-call | flops 402653184 | bytes 4194304 | tf_op jit(solution)/shard_map/pallas_call | solution.py:258
  94.9 0.1 collective-permute-start.3
  95.0 0.1 collective-permute-start.4
  95.1 1.2 collective-permute-done.4.refs_3_
  96.2 2.9 %shard_map.90 = (bf16[128,512]{1,0:T(8,128)(2,1)S(1)}, bf16[128,512]{1,0:T(8,128)(2,1)S(1)}, bf16[128,512]{1,0:T(8,128)(2,1)S(1)}) custom-call(s32[1]{0:T(128)} %bitcast.chip, s32[32]{0:T(128)S(1)} %reshape.11.table, bf16[8,2,128,256]{3,2,1,0:T(8,128)(2,1)S(1)} %all-to-all-done.q_ref, bf16[8,4,128,256]{3,2,1,0:T(8,128)(2,1)S(1)} %all-to-all-done.1.kv.refs_0_, ...), custom_call_target="tpu_custom_call" | custom-call | flops 1207959552 | tf_op jit(solution)/shard_map/pallas_call | solution.py:258
  99.2 3.8 %collective-permute-start.5 = (bf16[128,512]{1,0:T(8,128)(2,1)S(1)}, bf16[128,512]{1,0:T(8,128)(2,1)S(1)}, u32[]{:S(2)}, u32[]{:S(2)}) collective-permute-start(bf16[128,512]{1,0:T(8,128)(2,1)S(1)} %get-tuple-element.21), channel_id=1, source_target_pairs={{0,20},{2,22},{4,16},{6,18},{8,28},{10,30},{12,24},{14,26},{16,4},... | collective-permute-start | bytes 393224 | tf_op jit(solution)/shard_map/ppermute | solution.py:322
  102.9 1.5 %collective-permute-start.6 = (bf16[128,512]{1,0:T(8,128)(2,1)S(1)}, bf16[128,512]{1,0:T(8,128)(2,1)S(1)}, u32[]{:S(2)}, u32[]{:S(2)}) collective-permute-start(bf16[128,512]{1,0:T(8,128)(2,1)S(1)} %get-tuple-element.22), channel_id=1, source_target_pairs={{0,24},{2,26},{4,28},{6,30},{8,16},{10,18},{12,20},{14,22},{16,8},... | collective-permute-start | bytes 393224 | tf_op jit(solution)/shard_map/ppermute | solution.py:322
  104.4 0.0 collective-permute-start.7
  104.4 0.0 collective-permute-done.3.refs_3_.refs_0_
  104.4 3.6 %shard_map.91 = (bf16[128,512]{1,0:T(8,128)(2,1)S(1)}, bf16[128,512]{1,0:T(8,128)(2,1)S(1)}, bf16[128,512]{1,0:T(8,128)(2,1)S(1)}, bf16[128,512]{1,0:T(8,128)(2,1)S(1)}) custom-call(s32[1]{0:T(128)} %bitcast.chip, s32[32]{0:T(128)S(1)} %reshape.11.table, bf16[8,2,128,256]{3,2,1,0:T(8,128)(2,1)S(1)} %all-to-all-done.q_ref, ...), custom_call_target="tpu_custom_call" | custom-call | flops 1610612736 | tf_op jit(solution)/shard_map/pallas_call | solution.py:258
  108.0 2.5 %collective-permute-start.8 = (bf16[128,512]{1,0:T(8,128)(2,1)S(1)}, bf16[128,512]{1,0:T(8,128)(2,1)S(1)}, u32[]{:S(2)}, u32[]{:S(2)}) collective-permute-start(bf16[128,512]{1,0:T(8,128)(2,1)S(1)} %get-tuple-element.24), channel_id=1, source_target_pairs={{0,28},{2,30},{4,24},{6,26},{8,20},{10,22},{12,16},{14,18},{16,12}... | collective-permute-start | bytes 393224 | tf_op jit(solution)/shard_map/ppermute | solution.py:322
  110.4 2.0 %collective-permute-start.9 = (bf16[128,512]{1,0:T(8,128)(2,1)S(1)}, bf16[128,512]{1,0:T(8,128)(2,1)S(1)}, u32[]{:S(2)}, u32[]{:S(2)}) collective-permute-start(bf16[128,512]{1,0:T(8,128)(2,1)S(1)} %get-tuple-element.25), channel_id=1, source_target_pairs={{0,8},{2,10},{4,12},{6,14},{8,0},{10,2},{12,4},{14,6},{16,24},{18,... | collective-permute-start | bytes 393224 | tf_op jit(solution)/shard_map/ppermute | solution.py:322
  112.4 0.6 collective-permute-done.5.refs_1_
  113.0 1.5 %collective-permute-start.10 = (bf16[128,512]{1,0:T(8,128)(2,1)S(1)}, bf16[128,512]{1,0:T(8,128)(2,1)S(1)}, u32[]{:S(2)}, u32[]{:S(2)}) collective-permute-start(bf16[128,512]{1,0:T(8,128)(2,1)S(1)} %get-tuple-element.26), channel_id=1, source_target_pairs={{0,4},{2,6},{4,0},{6,2},{8,12},{10,14},{12,8},{14,10},{16,20},{18,... | collective-permute-start | bytes 393224 | tf_op jit(solution)/shard_map/ppermute | solution.py:322
  114.5 0.0 collective-permute-done.6.refs_2_
  114.5 0.0 collective-permute-done.7.refs_3_
  114.5 3.8 %collective-permute-done.8.refs_4_ = bf16[128,512]{1,0:T(8,128)(2,1)S(1)} collective-permute-done((bf16[128,512]{1,0:T(8,128)(2,1)S(1)}, bf16[128,512]{1,0:T(8,128)(2,1)S(1)}, u32[]{:S(2)}, u32[]{:S(2)}) %collective-permute-start.8) | collective-permute-done | bytes 131104 | tf_op jit(solution)/shard_map/ppermute | solution.py:322
  118.2 1.8 %collective-permute-done.9.refs_5_ = bf16[128,512]{1,0:T(8,128)(2,1)S(1)} collective-permute-done((bf16[128,512]{1,0:T(8,128)(2,1)S(1)}, bf16[128,512]{1,0:T(8,128)(2,1)S(1)}, u32[]{:S(2)}, u32[]{:S(2)}) %collective-permute-start.9) | collective-permute-done | bytes 131104 | tf_op jit(solution)/shard_map/ppermute | solution.py:322
  120.0 0.0 collective-permute-done.10.refs_6_
  120.0 1.1 shard_map.92
  (1 shorter events, 0.0 us)
Async XLA Ops:
  3.3 55.5 %all-to-all-start.1 = ((bf16[8,4,128,256]{3,2,1,0:T(8,128)(2,1)}), bf16[8,4,128,256]{3,2,1,0:T(8,128)(2,1)S(1)}, u32[]{:S(2)}, u32[]{:S(2)}) async-start(bf16[8,4,128,256]{3,2,1,0:T(8,128)(2,1)} %shard_map.86.refs_2_), calls=%async_computation.1 | async-start | bytes 4194304 | tf_op jit(solution)/shard_map/all_to_all | solution.py:86
  14.1 69.9 %copy-start = (s32[8,4]{0,1:T(4,128)S(1)}, s32[8,4]{0,1:T(4,128)}, u32[]{:S(2)}) copy-start(s32[8,4]{0,1:T(4,128)} %param.13) | copy-start | bytes 388
  59.9 24.1 %collective-permute-start = (bf16[4,4,128,256]{3,2,1,0:T(8,128)(2,1)}, bf16[4,4,128,256]{3,2,1,0:T(8,128)(2,1)}, u32[]{:S(2)}, u32[]{:S(2)}) collective-permute-start(bf16[4,4,128,256]{3,2,1,0:T(8,128)(2,1)} %shard_map.88), channel_id=1, source_target_pairs={{0,1},{1,0},{2,3},{3,2},{4,5},{5,4},{6,7},{7,6},{8,9},{9,8},{10,11... | collective-permute-start | bytes 3145736 | tf_op jit(solution)/shard_map/ppermute | solution.py:306
  61.4 30.2 %collective-permute-start.1 = (bf16[8,4,128,256]{3,2,1,0:T(8,128)(2,1)S(1)}, bf16[8,4,128,256]{3,2,1,0:T(8,128)(2,1)}, u32[]{:S(2)}, u32[]{:S(2)}) collective-permute-start(bf16[8,4,128,256]{3,2,1,0:T(8,128)(2,1)S(1)} %all-to-all-done.1.kv.refs_0_), channel_id=1, source_target_pairs={{0,2},{2,0},{4,6},{6,4},{8,10},{10,8},{12,14},{14,12},{16,18},{18,... | collective-permute-start | bytes 6291464 | tf_op jit(solution)/shard_map/ppermute | solution.py:307
  61.5 30.2 %all-to-all-start = ((bf16[8,2,128,256]{3,2,1,0:T(8,128)(2,1)}), bf16[8,2,128,256]{3,2,1,0:T(8,128)(2,1)S(1)}, u32[]{:S(2)}, u32[]{:S(2)}) async-start(bf16[8,2,128,256]{3,2,1,0:T(8,128)(2,1)} %get-tuple-element.15), calls=%async_computation | async-start | bytes 2097152 | tf_op jit(solution)/shard_map/all_to_all | solution.py:86
  84.0 7.7 %collective-permute-start.2 = (bf16[4,4,128,256]{3,2,1,0:T(8,128)(2,1)}, bf16[4,4,128,256]{3,2,1,0:T(8,128)(2,1)}, u32[]{:S(2)}, u32[]{:S(2)}) collective-permute-start(bf16[4,4,128,256]{3,2,1,0:T(8,128)(2,1)} %collective-permute-done.refs_1_), channel_id=1, source_target_pairs={{0,2},{2,0},{4,6},{6,4},{8,10},{10,8},{12,14},{14,12},{16,18},{18,... | collective-permute-start | bytes 3145736 | tf_op jit(solution)/shard_map/ppermute | solution.py:307
  94.9 9.5 %collective-permute-start.3 = (bf16[128,512]{1,0:T(8,128)(2,1)S(1)}, bf16[128,512]{1,0:T(8,128)(2,1)S(1)}, u32[]{:S(2)}, u32[]{:S(2)}) collective-permute-start(bf16[128,512]{1,0:T(8,128)(2,1)S(1)} %get-tuple-element.17), channel_id=1, source_target_pairs={{0,16},{2,18},{4,20},{6,22},{8,24},{10,26},{12,28},{14,30},{16,0},... | collective-permute-start | bytes 393224 | tf_op jit(solution)/shard_map/ppermute | solution.py:322
  95.0 1.2 %collective-permute-start.4 = (bf16[16,512]{1,0:T(8,128)(2,1)S(1)}, bf16[16,512]{1,0:T(8,128)(2,1)S(1)}, u32[]{:S(2)}, u32[]{:S(2)}) collective-permute-start(bf16[16,512]{1,0:T(8,128)(2,1)S(1)} %get-tuple-element.20), channel_id=1, source_target_pairs={{0,2},{2,0},{4,6},{6,4},{8,10},{10,8},{12,14},{14,12},{16,18},{18,... | collective-permute-start | bytes 49160 | tf_op jit(solution)/shard_map/ppermute | solution.py:324
  99.2 13.8 %collective-permute-start.5 = (bf16[128,512]{1,0:T(8,128)(2,1)S(1)}, bf16[128,512]{1,0:T(8,128)(2,1)S(1)}, u32[]{:S(2)}, u32[]{:S(2)}) collective-permute-start(bf16[128,512]{1,0:T(8,128)(2,1)S(1)} %get-tuple-element.21), channel_id=1, source_target_pairs={{0,20},{2,22},{4,16},{6,18},{8,28},{10,30},{12,24},{14,26},{16,4},... | collective-permute-start | bytes 393224 | tf_op jit(solution)/shard_map/ppermute | solution.py:322
  102.9 11.5 %collective-permute-start.6 = (bf16[128,512]{1,0:T(8,128)(2,1)S(1)}, bf16[128,512]{1,0:T(8,128)(2,1)S(1)}, u32[]{:S(2)}, u32[]{:S(2)}) collective-permute-start(bf16[128,512]{1,0:T(8,128)(2,1)S(1)} %get-tuple-element.22), channel_id=1, source_target_pairs={{0,24},{2,26},{4,28},{6,30},{8,16},{10,18},{12,20},{14,22},{16,8},... | collective-permute-start | bytes 393224 | tf_op jit(solution)/shard_map/ppermute | solution.py:322
  104.4 10.1 %collective-permute-start.7 = (bf16[128,512]{1,0:T(8,128)(2,1)S(1)}, bf16[128,512]{1,0:T(8,128)(2,1)S(1)}, u32[]{:S(2)}, u32[]{:S(2)}) collective-permute-start(bf16[128,512]{1,0:T(8,128)(2,1)S(1)} %get-tuple-element.23), channel_id=1, source_target_pairs={{0,12},{2,14},{4,8},{6,10},{8,4},{10,6},{12,0},{14,2},{16,28},{18,... | collective-permute-start | bytes 393224 | tf_op jit(solution)/shard_map/ppermute | solution.py:322
  108.0 10.2 %collective-permute-start.8 = (bf16[128,512]{1,0:T(8,128)(2,1)S(1)}, bf16[128,512]{1,0:T(8,128)(2,1)S(1)}, u32[]{:S(2)}, u32[]{:S(2)}) collective-permute-start(bf16[128,512]{1,0:T(8,128)(2,1)S(1)} %get-tuple-element.24), channel_id=1, source_target_pairs={{0,28},{2,30},{4,24},{6,26},{8,20},{10,22},{12,16},{14,18},{16,12}... | collective-permute-start | bytes 393224 | tf_op jit(solution)/shard_map/ppermute | solution.py:322
  110.4 9.5 %collective-permute-start.9 = (bf16[128,512]{1,0:T(8,128)(2,1)S(1)}, bf16[128,512]{1,0:T(8,128)(2,1)S(1)}, u32[]{:S(2)}, u32[]{:S(2)}) collective-permute-start(bf16[128,512]{1,0:T(8,128)(2,1)S(1)} %get-tuple-element.25), channel_id=1, source_target_pairs={{0,8},{2,10},{4,12},{6,14},{8,0},{10,2},{12,4},{14,6},{16,24},{18,... | collective-permute-start | bytes 393224 | tf_op jit(solution)/shard_map/ppermute | solution.py:322
  113.0 7.0 %collective-permute-start.10 = (bf16[128,512]{1,0:T(8,128)(2,1)S(1)}, bf16[128,512]{1,0:T(8,128)(2,1)S(1)}, u32[]{:S(2)}, u32[]{:S(2)}) collective-permute-start(bf16[128,512]{1,0:T(8,128)(2,1)S(1)} %get-tuple-element.26), channel_id=1, source_target_pairs={{0,4},{2,6},{4,0},{6,2},{8,12},{10,14},{12,8},{14,10},{16,20},{18,... | collective-permute-start | bytes 393224 | tf_op jit(solution)/shard_map/ppermute | solution.py:322

commit v26 on v25

--- a/solution.py
+++ b/solution.py
@@ -312,8 +312,8 @@
     back, later, sources = {}, [], mine[1:] + other
     calls = (
         range(half, half + 1),
-        [*range(half + 1, middle + 1), half - 1],
-        [*range(middle + 1, blocks), *range(half - 2, 0, -1), 0],
+        [*range(half + 1, middle + 1), *range(half - 1, half // 2 - 1, -1)],
+        [*range(middle + 1, blocks), *range(half // 2 - 1, 0, -1), 0],
     )
     for n, part in enumerate(calls):
         pieces = attend(chip, table, queries, kv, sources, len(rounds), later, list(part), n == 0)

time: 122 us -> 123 us (level)
  starting transfers between devices: 23.8 us -> 25.2 us
    ppermute x7, starting transfers between devices: 11.2 us -> 12.7 us  [per_device(): back[k] = lax.ppermute(piece, 'heads', pairs) if k else piece]
  transfers between devices with their start and end apart: 13 -> 13, of which waited for: 7 -> 6; matrix products, arithmetic and copies ran while one was open for 0% -> 0% of each run, Pallas kernels for 8% -> 8%
where the time goes in v26:
time: 123 us; the launch traced here: 122 us
  waiting for transfers between devices  78.2 us (64%)
  starting transfers between devices  25.2 us (20%)
  Pallas kernels  17.3 us (14%)
  between operations  1.37 us (1%)
    all_to_all x2, waiting for transfers between devices, exchange(): lax.all_to_all(pieces, 'heads', split_axis=0, concat_axis=0, axis_index_g...  52.2 us
    ppermute x1, waiting for transfers between devices, per_device(): mine.append(lax.ppermute(edge(start, kv), 'frames', rounds[-1]))  18.9 us
    ppermute x7, starting transfers between devices, per_device(): back[k] = lax.ppermute(piece, 'heads', pairs) if k else piece  12.7 us
    all_to_all x2, starting transfers between devices, exchange(): lax.all_to_all(pieces, 'heads', split_axis=0, concat_axis=0, axis_index_g...  10.9 us
    pallas_call x3, Pallas kernels, attend(): pl.pallas_call(functools.partial(attend_kernel, sources=len(sources) if f...  9.71 us
    ppermute x7, waiting for transfers between devices, per_device(): back[k] = lax.ppermute(piece, 'heads', pairs) if k else piece  5.91 us
    pallas_call x2, Pallas kernels, to_chips(): pl.pallas_call(functools.partial(pack_kernel, count=count, before=len(bef...  5.51 us
  transfers between devices with their start and end apart: 13, of which 6 were waited for; matrix products, arithmetic and copies ran while one was open for 0% of the time, Pallas kernels for 8%

profile of v26, /device:TPU:0, one launch (start us, length us, event | category | flops | bytes accessed | tf_op | source)
XLA Modules:
  0.0 122.2 jit_solution(13037002490067768881)
XLA Ops:
  0.6 2.7 %shard_map.86.refs_2_ = bf16[8,4,128,256]{3,2,1,0:T(8,128)(2,1)} custom-call(bf16[128,2048]{1,0:T(8,128)(2,1)} %refs_0_.2, bf16[128,2048]{1,0:T(8,128)(2,1)} %refs_1_.2, bf16[128,2048]{1,0:T(8,128)(2,1)} %refs_2_.1, bf16[128,2048]{1,0:T(8,128)(2,1)} %refs_3_.1), custom_call_target="tpu_custom_call" | custom-call | bytes 4194304 | tf_op jit(solution)/shard_map/pallas_call | solution.py:67
  3.3 7.3 %all-to-all-start.1 = ((bf16[8,4,128,256]{3,2,1,0:T(8,128)(2,1)}), bf16[8,4,128,256]{3,2,1,0:T(8,128)(2,1)S(1)}, u32[]{:S(2)}, u32[]{:S(2)}) async-start(bf16[8,4,128,256]{3,2,1,0:T(8,128)(2,1)} %shard_map.86.refs_2_), calls=%async_computation.1 | async-start | bytes 4194304 | tf_op jit(solution)/shard_map/all_to_all | solution.py:86
  10.6 2.8 %shard_map.87 = (bf16[8,2,128,256]{3,2,1,0:T(8,128)(2,1)}, s32[1]{0:T(128)}) custom-call(bf16[128,2048]{1,0:T(8,128)(2,1)} %refs_0_.3, bf16[128,2048]{1,0:T(8,128)(2,1)} %refs_1_.3, bf16[8,4,128,256]{3,2,1,0:T(8,128)(2,1)} %shard_map.86.refs_2_), custom_call_target="tpu_custom_call" | custom-call | bytes 2097152 | tf_op jit(solution)/shard_map/pallas_call | solution.py:67
  14.1 0.0 copy-start
  14.1 44.8 %all-to-all-done.1.kv.refs_0_ = bf16[8,4,128,256]{3,2,1,0:T(8,128)(2,1)S(1)} async-done(((bf16[8,4,128,256]{3,2,1,0:T(8,128)(2,1)}), bf16[8,4,128,256]{3,2,1,0:T(8,128)(2,1)S(1)}, u32[]{:S(2)}, u32[]{:S(2)}) %all-to-all-start.1) | async-done | bytes 2097184 | tf_op jit(solution)/shard_map/all_to_all | solution.py:86
  58.9 1.0 shard_map.88
  59.9 1.6 %collective-permute-start = (bf16[4,4,128,256]{3,2,1,0:T(8,128)(2,1)}, bf16[4,4,128,256]{3,2,1,0:T(8,128)(2,1)}, u32[]{:S(2)}, u32[]{:S(2)}) collective-permute-start(bf16[4,4,128,256]{3,2,1,0:T(8,128)(2,1)} %shard_map.88), channel_id=1, source_target_pairs={{0,1},{1,0},{2,3},{3,2},{4,5},{5,4},{6,7},{7,6},{8,9},{9,8},{10,11... | collective-permute-start | bytes 3145736 | tf_op jit(solution)/shard_map/ppermute | solution.py:306
  61.4 0.0 collective-permute-start.1
  61.5 3.6 %all-to-all-start = ((bf16[8,2,128,256]{3,2,1,0:T(8,128)(2,1)}), bf16[8,2,128,256]{3,2,1,0:T(8,128)(2,1)S(1)}, u32[]{:S(2)}, u32[]{:S(2)}) async-start(bf16[8,2,128,256]{3,2,1,0:T(8,128)(2,1)} %get-tuple-element.15), calls=%async_computation | async-start | bytes 2097152 | tf_op jit(solution)/shard_map/all_to_all | solution.py:86
  65.1 18.9 %collective-permute-done.refs_1_ = bf16[4,4,128,256]{3,2,1,0:T(8,128)(2,1)} collective-permute-done((bf16[4,4,128,256]{3,2,1,0:T(8,128)(2,1)}, bf16[4,4,128,256]{3,2,1,0:T(8,128)(2,1)}, u32[]{:S(2)}, u32[]{:S(2)}) %collective-permute-start) | collective-permute-done | bytes 1048608 | tf_op jit(solution)/shard_map/ppermute | solution.py:306
  84.0 0.0 collective-permute-start.2
  84.0 0.0 copy-done
  84.0 0.1 copy.10
  84.1 0.1 reshape.11.table
  84.2 7.5 %all-to-all-done.q_ref = bf16[8,2,128,256]{3,2,1,0:T(8,128)(2,1)S(1)} async-done(((bf16[8,2,128,256]{3,2,1,0:T(8,128)(2,1)}), bf16[8,2,128,256]{3,2,1,0:T(8,128)(2,1)S(1)}, u32[]{:S(2)}, u32[]{:S(2)}) %all-to-all-start) | async-done | bytes 1048608 | tf_op jit(solution)/shard_map/all_to_all | solution.py:86
  91.7 0.0 collective-permute-done.2.refs_3_
  91.7 0.0 collective-permute-done.1.refs_2_
  91.7 3.2 %shard_map.89 = (bf16[128,512]{1,0:T(8,128)(2,1)S(1)}, bf16[16,512]{1,0:T(8,128)(2,1)S(1)}, bf16[4,4,128,256]{3,2,1,0:T(8,128)(2,1)S(1)}, bf16[12,4,128,256]{3,2,1,0:T(8,128)(2,1)S(1)}) custom-call(s32[1]{0:T(128)} %bitcast.chip, s32[32]{0:T(128)S(1)} %reshape.11.table, bf16[8,2,128,256]{3,2,1,0:T(8,128)(2,1)S(1)} %all-to-all-done.q_ref, ...), custom_call_target="tpu_custom_call" | custom-call | flops 402653184 | bytes 4194304 | tf_op jit(solution)/shard_map/pallas_call | solution.py:258
  94.9 0.1 collective-permute-start.4
  95.0 0.1 collective-permute-start.3
  95.1 1.1 collective-permute-done.4.refs_3_
  96.1 3.6 %shard_map.90 = (bf16[128,512]{1,0:T(8,128)(2,1)S(1)}, bf16[128,512]{1,0:T(8,128)(2,1)S(1)}, bf16[128,512]{1,0:T(8,128)(2,1)S(1)}, bf16[128,512]{1,0:T(8,128)(2,1)S(1)}) custom-call(s32[1]{0:T(128)} %bitcast.chip, s32[32]{0:T(128)S(1)} %reshape.11.table, bf16[8,2,128,256]{3,2,1,0:T(8,128)(2,1)S(1)} %all-to-all-done.q_ref, ...), custom_call_target="tpu_custom_call" | custom-call | flops 1610612736 | tf_op jit(solution)/shard_map/pallas_call | solution.py:258
  99.7 3.5 %collective-permute-start.5 = (bf16[128,512]{1,0:T(8,128)(2,1)S(1)}, bf16[128,512]{1,0:T(8,128)(2,1)S(1)}, u32[]{:S(2)}, u32[]{:S(2)}) collective-permute-start(bf16[128,512]{1,0:T(8,128)(2,1)S(1)} %get-tuple-element.21), channel_id=1, source_target_pairs={{0,20},{2,22},{4,16},{6,18},{8,28},{10,30},{12,24},{14,26},{16,4},... | collective-permute-start | bytes 393224 | tf_op jit(solution)/shard_map/ppermute | solution.py:322
  103.3 0.7 collective-permute-start.6
  103.9 0.2 collective-permute-start.7
  104.2 2.6 %collective-permute-start.8 = (bf16[128,512]{1,0:T(8,128)(2,1)S(1)}, bf16[128,512]{1,0:T(8,128)(2,1)S(1)}, u32[]{:S(2)}, u32[]{:S(2)}) collective-permute-start(bf16[128,512]{1,0:T(8,128)(2,1)S(1)} %get-tuple-element.24), channel_id=1, source_target_pairs={{0,8},{2,10},{4,12},{6,14},{8,0},{10,2},{12,4},{14,6},{16,24},{18,... | collective-permute-start | bytes 393224 | tf_op jit(solution)/shard_map/ppermute | solution.py:322
  106.8 0.0 collective-permute-done.3.refs_3_.refs_0_
  106.8 2.9 %shard_map.91 = (bf16[128,512]{1,0:T(8,128)(2,1)S(1)}, bf16[128,512]{1,0:T(8,128)(2,1)S(1)}, bf16[128,512]{1,0:T(8,128)(2,1)S(1)}) custom-call(s32[1]{0:T(128)} %bitcast.chip, s32[32]{0:T(128)S(1)} %reshape.11.table, bf16[8,2,128,256]{3,2,1,0:T(8,128)(2,1)S(1)} %all-to-all-done.q_ref, bf16[8,4,128,256]{3,2,1,0:T(8,128)(2,1)S(1)} %all-to-all-done.1.kv.refs_0_, ...), custom_call_target="tpu_custom_call" | custom-call | flops 1207959552 | tf_op jit(solution)/shard_map/pallas_call | solution.py:258
  109.7 5.5 %collective-permute-start.9 = (bf16[128,512]{1,0:T(8,128)(2,1)S(1)}, bf16[128,512]{1,0:T(8,128)(2,1)S(1)}, u32[]{:S(2)}, u32[]{:S(2)}) collective-permute-start(bf16[128,512]{1,0:T(8,128)(2,1)S(1)} %get-tuple-element.25), channel_id=1, source_target_pairs={{0,28},{2,30},{4,24},{6,26},{8,20},{10,22},{12,16},{14,18},{16,12}... | collective-permute-start | bytes 393224 | tf_op jit(solution)/shard_map/ppermute | solution.py:322
  115.2 0.0 collective-permute-done.5.refs_1_
  115.2 0.0 collective-permute-start.10
  115.2 0.0 collective-permute-done.6.refs_2_
  115.3 0.0 collective-permute-done.7.refs_3_
  115.3 5.7 %collective-permute-done.8.refs_4_ = bf16[128,512]{1,0:T(8,128)(2,1)S(1)} collective-permute-done((bf16[128,512]{1,0:T(8,128)(2,1)S(1)}, bf16[128,512]{1,0:T(8,128)(2,1)S(1)}, u32[]{:S(2)}, u32[]{:S(2)}) %collective-permute-start.8) | collective-permute-done | bytes 131104 | tf_op jit(solution)/shard_map/ppermute | solution.py:322
  120.9 0.0 collective-permute-done.9.refs_5_
  120.9 0.2 collective-permute-done.10.refs_6_
  121.2 1.1 shard_map.92
  (1 shorter events, 0.0 us)
Async XLA Ops:
  3.3 55.5 %all-to-all-start.1 = ((bf16[8,4,128,256]{3,2,1,0:T(8,128)(2,1)}), bf16[8,4,128,256]{3,2,1,0:T(8,128)(2,1)S(1)}, u32[]{:S(2)}, u32[]{:S(2)}) async-start(bf16[8,4,128,256]{3,2,1,0:T(8,128)(2,1)} %shard_map.86.refs_2_), calls=%async_computation.1 | async-start | bytes 4194304 | tf_op jit(solution)/shard_map/all_to_all | solution.py:86
  14.1 69.9 %copy-start = (s32[8,4]{0,1:T(4,128)S(1)}, s32[8,4]{0,1:T(4,128)}, u32[]{:S(2)}) copy-start(s32[8,4]{0,1:T(4,128)} %param.13) | copy-start | bytes 388
  59.9 24.1 %collective-permute-start = (bf16[4,4,128,256]{3,2,1,0:T(8,128)(2,1)}, bf16[4,4,128,256]{3,2,1,0:T(8,128)(2,1)}, u32[]{:S(2)}, u32[]{:S(2)}) collective-permute-start(bf16[4,4,128,256]{3,2,1,0:T(8,128)(2,1)} %shard_map.88), channel_id=1, source_target_pairs={{0,1},{1,0},{2,3},{3,2},{4,5},{5,4},{6,7},{7,6},{8,9},{9,8},{10,11... | collective-permute-start | bytes 3145736 | tf_op jit(solution)/shard_map/ppermute | solution.py:306
  61.4 30.2 %collective-permute-start.1 = (bf16[8,4,128,256]{3,2,1,0:T(8,128)(2,1)S(1)}, bf16[8,4,128,256]{3,2,1,0:T(8,128)(2,1)}, u32[]{:S(2)}, u32[]{:S(2)}) collective-permute-start(bf16[8,4,128,256]{3,2,1,0:T(8,128)(2,1)S(1)} %all-to-all-done.1.kv.refs_0_), channel_id=1, source_target_pairs={{0,2},{2,0},{4,6},{6,4},{8,10},{10,8},{12,14},{14,12},{16,18},{18,... | collective-permute-start | bytes 6291464 | tf_op jit(solution)/shard_map/ppermute | solution.py:307
  61.5 30.2 %all-to-all-start = ((bf16[8,2,128,256]{3,2,1,0:T(8,128)(2,1)}), bf16[8,2,128,256]{3,2,1,0:T(8,128)(2,1)S(1)}, u32[]{:S(2)}, u32[]{:S(2)}) async-start(bf16[8,2,128,256]{3,2,1,0:T(8,128)(2,1)} %get-tuple-element.15), calls=%async_computation | async-start | bytes 2097152 | tf_op jit(solution)/shard_map/all_to_all | solution.py:86
  84.0 7.7 %collective-permute-start.2 = (bf16[4,4,128,256]{3,2,1,0:T(8,128)(2,1)}, bf16[4,4,128,256]{3,2,1,0:T(8,128)(2,1)}, u32[]{:S(2)}, u32[]{:S(2)}) collective-permute-start(bf16[4,4,128,256]{3,2,1,0:T(8,128)(2,1)} %collective-permute-done.refs_1_), channel_id=1, source_target_pairs={{0,2},{2,0},{4,6},{6,4},{8,10},{10,8},{12,14},{14,12},{16,18},{18,... | collective-permute-start | bytes 3145736 | tf_op jit(solution)/shard_map/ppermute | solution.py:307
  94.9 1.2 %collective-permute-start.4 = (bf16[16,512]{1,0:T(8,128)(2,1)S(1)}, bf16[16,512]{1,0:T(8,128)(2,1)S(1)}, u32[]{:S(2)}, u32[]{:S(2)}) collective-permute-start(bf16[16,512]{1,0:T(8,128)(2,1)S(1)} %get-tuple-element.20), channel_id=1, source_target_pairs={{0,2},{2,0},{4,6},{6,4},{8,10},{10,8},{12,14},{14,12},{16,18},{18,... | collective-permute-start | bytes 49160 | tf_op jit(solution)/shard_map/ppermute | solution.py:324
  95.0 11.8 %collective-permute-start.3 = (bf16[128,512]{1,0:T(8,128)(2,1)S(1)}, bf16[128,512]{1,0:T(8,128)(2,1)S(1)}, u32[]{:S(2)}, u32[]{:S(2)}) collective-permute-start(bf16[128,512]{1,0:T(8,128)(2,1)S(1)} %get-tuple-element.17), channel_id=1, source_target_pairs={{0,16},{2,18},{4,20},{6,22},{8,24},{10,26},{12,28},{14,30},{16,0},... | collective-permute-start | bytes 393224 | tf_op jit(solution)/shard_map/ppermute | solution.py:322
  99.7 15.5 %collective-permute-start.5 = (bf16[128,512]{1,0:T(8,128)(2,1)S(1)}, bf16[128,512]{1,0:T(8,128)(2,1)S(1)}, u32[]{:S(2)}, u32[]{:S(2)}) collective-permute-start(bf16[128,512]{1,0:T(8,128)(2,1)S(1)} %get-tuple-element.21), channel_id=1, source_target_pairs={{0,20},{2,22},{4,16},{6,18},{8,28},{10,30},{12,24},{14,26},{16,4},... | collective-permute-start | bytes 393224 | tf_op jit(solution)/shard_map/ppermute | solution.py:322
  103.3 12.0 %collective-permute-start.6 = (bf16[128,512]{1,0:T(8,128)(2,1)S(1)}, bf16[128,512]{1,0:T(8,128)(2,1)S(1)}, u32[]{:S(2)}, u32[]{:S(2)}) collective-permute-start(bf16[128,512]{1,0:T(8,128)(2,1)S(1)} %get-tuple-element.22), channel_id=1, source_target_pairs={{0,24},{2,26},{4,28},{6,30},{8,16},{10,18},{12,20},{14,22},{16,8},... | collective-permute-start | bytes 393224 | tf_op jit(solution)/shard_map/ppermute | solution.py:322
  103.9 11.3 %collective-permute-start.7 = (bf16[128,512]{1,0:T(8,128)(2,1)S(1)}, bf16[128,512]{1,0:T(8,128)(2,1)S(1)}, u32[]{:S(2)}, u32[]{:S(2)}) collective-permute-start(bf16[128,512]{1,0:T(8,128)(2,1)S(1)} %get-tuple-element.23), channel_id=1, source_target_pairs={{0,12},{2,14},{4,8},{6,10},{8,4},{10,6},{12,0},{14,2},{16,28},{18,... | collective-permute-start | bytes 393224 | tf_op jit(solution)/shard_map/ppermute | solution.py:322
  104.2 16.8 %collective-permute-start.8 = (bf16[128,512]{1,0:T(8,128)(2,1)S(1)}, bf16[128,512]{1,0:T(8,128)(2,1)S(1)}, u32[]{:S(2)}, u32[]{:S(2)}) collective-permute-start(bf16[128,512]{1,0:T(8,128)(2,1)S(1)} %get-tuple-element.24), channel_id=1, source_target_pairs={{0,8},{2,10},{4,12},{6,14},{8,0},{10,2},{12,4},{14,6},{16,24},{18,... | collective-permute-start | bytes 393224 | tf_op jit(solution)/shard_map/ppermute | solution.py:322
  109.7 11.2 %collective-permute-start.9 = (bf16[128,512]{1,0:T(8,128)(2,1)S(1)}, bf16[128,512]{1,0:T(8,128)(2,1)S(1)}, u32[]{:S(2)}, u32[]{:S(2)}) collective-permute-start(bf16[128,512]{1,0:T(8,128)(2,1)S(1)} %get-tuple-element.25), channel_id=1, source_target_pairs={{0,28},{2,30},{4,24},{6,26},{8,20},{10,22},{12,16},{14,18},{16,12}... | collective-permute-start | bytes 393224 | tf_op jit(solution)/shard_map/ppermute | solution.py:322
  115.2 5.9 %collective-permute-start.10 = (bf16[128,512]{1,0:T(8,128)(2,1)S(1)}, bf16[128,512]{1,0:T(8,128)(2,1)S(1)}, u32[]{:S(2)}, u32[]{:S(2)}) collective-permute-start(bf16[128,512]{1,0:T(8,128)(2,1)S(1)} %get-tuple-element.26), channel_id=1, source_target_pairs={{0,4},{2,6},{4,0},{6,2},{8,12},{10,14},{12,8},{14,10},{16,20},{18,... | collective-permute-start | bytes 393224 | tf_op jit(solution)/shard_map/ppermute | solution.py:322
